TPU v7x, 32 devices: a whole 2x2x4 slice. The times are simulated.
32 devices in a mesh: tok: 8 (over z, x), wid: 4 (over y, core).
Axes of the slice: x: 2, y: 2, z: 4, core: 2. Of those that a mesh axis runs over, the one named last changes fastest.
Arguments:
- acts: bfloat16 [4096, 4096], P('tok', 'wid'), may hold values from -6 to 6
- grads: bfloat16 [4096, 11008], P('tok', 'wid'), may hold values from -6 to 6
- lengths: int32 [8], replicated, may hold values from 1 to 512, 3072 in all
Outputs:
- kernel_tiles: float32 [4096, 5, 512], P('tok', None, 'wid')
Inputs may be any that keep to these rules, and one draw needn't show every extreme that they name: One block has all 512 slots live; the lengths sum to 3072.
All inputs are finite; a program needn't handle non-finite values.
Results may differ from a plain program's by a relative error of at most 0.00075.
Values may be sent and summed in bfloat16 or wider, within the bound.
No kernel may reach another device: no remote copies, remote signals or barrier semaphores. Data moves between devices by JAX's collectives and lax.ppermute only.
A program may use at most 128 MiB of HBM per device.

v0:
```python
import jax
import jax.numpy as jnp
from jax import lax
from jax.sharding import PartitionSpec as P

D = 4096
FF = 11008
REACH = 2


def shifted(shard, axis, by):
    length = lax.axis_size(axis)
    return lax.ppermute(shard, axis, [(i, (i + by) % length) for i in range(length)])


def fetch_blocks(pair, signs):
    partners = {}
    for sign in signs:
        for step in (sign, 2 * sign):
            partners[step] = shifted((pair[0], pair[1]), "tok", step)
    return partners


def width_total(act_gram, grad_gram):
    return (
        lax.psum_scatter(act_gram, "wid", scatter_dimension=2, tiled=True),
        lax.psum_scatter(grad_gram, "wid", scatter_dimension=2, tiled=True),
    )


def gram_tiles(masked_acts, masked_grads, partners, order):
    act_tiles = []
    grad_tiles = []
    for step in order:
        other_acts, other_grads = partners[step]
        act_tiles.append(jnp.dot(masked_acts, other_acts.T, preferred_element_type=jnp.float32))
        grad_tiles.append(jnp.dot(masked_grads, other_grads.T, preferred_element_type=jnp.float32))
    return (jnp.stack(act_tiles, axis=1), jnp.stack(grad_tiles, axis=1))


def shards(acts, grads, lengths):
    rows = acts.shape[0]
    position = lax.axis_index("tok")
    count = lax.dynamic_index_in_dim(lengths, position, 0, keepdims=False)
    live = (jnp.arange(rows, dtype=jnp.int32) < count).astype(jnp.bfloat16)
    masked_acts = acts * live[:, None]
    masked_grads = grads * live[:, None]
    act_scale = jnp.sqrt(jnp.float32(D))
    grad_scale = jnp.sqrt(jnp.float32(FF))
    partners = fetch_blocks((masked_acts, masked_grads), (1, -1))
    partners[0] = (masked_acts, masked_grads)
    order = tuple((REACH - offset for offset in range(2 * REACH + 1)))
    act_gram, grad_gram = gram_tiles(masked_acts, masked_grads, partners, order)
    act_sum, grad_sum = width_total(act_gram, grad_gram)
    return act_sum / act_scale * (grad_sum / grad_scale)


def solution(mesh):
    return jax.shard_map(
        shards,
        mesh=mesh,
        in_specs=(P("tok", "wid"), P("tok", "wid"), P()),
        out_specs=P("tok", None, "wid"),
        check_vma=False,
    )
```

profile of v0, /device:TPU:0, one launch (start us, length us, event | category | flops | bytes accessed | tf_op | source)
XLA Modules:
  0.0 334.6 jit_solution(79793948317025200)
XLA Ops:
  9.8 3.1 collective-permute-start
  12.9 1.5 collective-permute-start.1
  14.4 3.2 collective-permute-start.2
  17.9 21.0 %collective-permute-done = bf16[512,1024]{1,0:T(8,128)(2,1)S(1)} collective-permute-done((bf16[512,1024]{1,0:T(8,128)(2,1)S(1)}, bf16[512,1024]{1,0:T(8,128)(2,1)S(1)}, u32[]{:S(2)}, u32[]{:S(2)}) %collective-permute-start) | collective-permute-done | bytes 1048608 | tf_op jit(solution)/shard_map/ppermute | solution.py:13
  38.9 1.7 fusion.9
  40.7 21.9 %collective-permute-done.1 = bf16[512,1024]{1,0:T(8,128)(2,1)S(1)} collective-permute-done((bf16[512,1024]{1,0:T(8,128)(2,1)S(1)}, bf16[512,1024]{1,0:T(8,128)(2,1)S(1)}, u32[]{:S(2)}, u32[]{:S(2)}) %collective-permute-start.1) | collective-permute-done | bytes 1048608 | tf_op jit(solution)/shard_map/ppermute | solution.py:13
  62.6 1.7 fusion.8
  64.3 1.8 fusion.7
  66.1 1.8 fusion.6
  67.9 15.1 %collective-permute-done.3 = bf16[512,1024]{1,0:T(8,128)(2,1)S(1)} collective-permute-done((bf16[512,1024]{1,0:T(8,128)(2,1)S(1)}, bf16[512,1024]{1,0:T(8,128)(2,1)S(1)}, u32[]{:S(2)}, u32[]{:S(2)}) %collective-permute-start.3) | collective-permute-done | bytes 1048608 | tf_op jit(solution)/shard_map/ppermute | solution.py:13
  83.0 1.7 fusion.5
  84.8 1.7 copy-done
  88.8 3.3 collective-permute-start.6
  92.1 6.4 %collective-permute-start.7 = (bf16[512,2752]{0,1:T(8,128)(2,1)S(1)}, bf16[512,2752]{0,1:T(8,128)(2,1)S(1)}, u32[]{:S(2)}, u32[]{:S(2)}) collective-permute-start(bf16[512,2752]{0,1:T(8,128)(2,1)S(1)} %broadcast_multiply_fusion), channel_id=1, source_target_pairs={{0,24},{4,28},{8,0},{12,4},{16,8},{20,12},{24,16},{28,20},{1,25},{... | collective-permute-start | bytes 8454152 | tf_op jit(solution)/shard_map/ppermute | solution.py:13
  98.5 59.0 %collective-permute-done.4 = bf16[512,2752]{0,1:T(8,128)(2,1)S(1)} collective-permute-done((bf16[512,2752]{0,1:T(8,128)(2,1)S(1)}, bf16[512,2752]{0,1:T(8,128)(2,1)S(1)}, u32[]{:S(2)}, u32[]{:S(2)}) %collective-permute-start.4) | collective-permute-done | bytes 2818080 | tf_op jit(solution)/shard_map/ppermute | solution.py:13
  157.5 2.6 fusion.4
  160.2 53.7 %collective-permute-done.5 = bf16[512,2752]{0,1:T(8,128)(2,1)S(1)} collective-permute-done((bf16[512,2752]{0,1:T(8,128)(2,1)S(1)}, bf16[512,2752]{0,1:T(8,128)(2,1)S(1)}, u32[]{:S(2)}, u32[]{:S(2)}) %collective-permute-start.5) | collective-permute-done | bytes 2818080 | tf_op jit(solution)/shard_map/ppermute | solution.py:13
  213.9 2.7 fusion.3
  216.6 2.7 fusion.2
  219.2 2.7 fusion.1
  221.9 49.9 %collective-permute-done.7 = bf16[512,2752]{0,1:T(8,128)(2,1)S(1)} collective-permute-done((bf16[512,2752]{0,1:T(8,128)(2,1)S(1)}, bf16[512,2752]{0,1:T(8,128)(2,1)S(1)}, u32[]{:S(2)}, u32[]{:S(2)}) %collective-permute-start.7) | collective-permute-done | bytes 2818080 | tf_op jit(solution)/shard_map/ppermute | solution.py:13
  271.8 2.7 fusion
  274.5 50.3 %reduce-scatter.5.cloned.1.call-done = f32[512,5,128]{2,0,1:T(8,128)} async-done(((f32[512,5,512]{2,0,1:T(8,128)}), f32[512,5,128]{2,0,1:T(8,128)}) %reduce-scatter.5.cloned.1.call-update) | async-done | bytes 1310736 | tf_op jit(solution)/shard_map/reduce_scatter | solution.py:27
  324.8 2.9 multiply_multiply_fusion
  (15 shorter events, 5.9 us)
Async XLA Ops:
  6.5 268.0 %reduce-scatter.3.cloned.1.call-start = ((), (), s32[]{:S(2)}) async-start(), calls=%async_computation.2 | async-start | bytes 6553600 | tf_op jit(solution)/shard_map/reduce_scatter | solution.py:26
  9.8 29.1 %collective-permute-start = (bf16[512,1024]{1,0:T(8,128)(2,1)S(1)}, bf16[512,1024]{1,0:T(8,128)(2,1)S(1)}, u32[]{:S(2)}, u32[]{:S(2)}) collective-permute-start(bf16[512,1024]{1,0:T(8,128)(2,1)S(1)} %broadcast_multiply_fusion.1), channel_id=1, source_target_pairs={{0,8},{4,12},{8,16},{12,20},{16,24},{20,28},{24,0},{28,4},{1,9},{5... | collective-permute-start | bytes 3145736 | tf_op jit(solution)/shard_map/ppermute | solution.py:13
  12.9 49.7 %collective-permute-start.1 = (bf16[512,1024]{1,0:T(8,128)(2,1)S(1)}, bf16[512,1024]{1,0:T(8,128)(2,1)S(1)}, u32[]{:S(2)}, u32[]{:S(2)}) collective-permute-start(bf16[512,1024]{1,0:T(8,128)(2,1)S(1)} %broadcast_multiply_fusion.1), channel_id=1, source_target_pairs={{0,4},{4,8},{8,12},{12,16},{16,20},{20,24},{24,28},{28,0},{1,5},{5... | collective-permute-start | bytes 3145736 | tf_op jit(solution)/shard_map/ppermute | solution.py:13
  14.4 51.7 %collective-permute-start.2 = (bf16[512,1024]{1,0:T(8,128)(2,1)S(1)}, bf16[512,1024]{1,0:T(8,128)(2,1)S(1)}, u32[]{:S(2)}, u32[]{:S(2)}) collective-permute-start(bf16[512,1024]{1,0:T(8,128)(2,1)S(1)} %broadcast_multiply_fusion.1), channel_id=1, source_target_pairs={{0,28},{4,0},{8,4},{12,8},{16,12},{20,16},{24,20},{28,24},{1,29},{... | collective-permute-start | bytes 3145736 | tf_op jit(solution)/shard_map/ppermute | solution.py:13
  17.6 65.4 %collective-permute-start.3 = (bf16[512,1024]{1,0:T(8,128)(2,1)S(1)}, bf16[512,1024]{1,0:T(8,128)(2,1)S(1)}, u32[]{:S(2)}, u32[]{:S(2)}) collective-permute-start(bf16[512,1024]{1,0:T(8,128)(2,1)S(1)} %broadcast_multiply_fusion.1), channel_id=1, source_target_pairs={{0,24},{4,28},{8,0},{12,4},{16,8},{20,12},{24,16},{28,20},{1,25},{... | collective-permute-start | bytes 3145736 | tf_op jit(solution)/shard_map/ppermute | solution.py:13
  84.7 1.8 copy-start
  84.7 240.1 %reduce-scatter.5.cloned.1.call-start = ((), (), s32[]{:S(2)}) async-start(), calls=%async_computation.3 | async-start | bytes 6553600 | tf_op jit(solution)/shard_map/reduce_scatter | solution.py:27
  86.7 70.8 %collective-permute-start.4 = (bf16[512,2752]{0,1:T(8,128)(2,1)S(1)}, bf16[512,2752]{0,1:T(8,128)(2,1)S(1)}, u32[]{:S(2)}, u32[]{:S(2)}) collective-permute-start(bf16[512,2752]{0,1:T(8,128)(2,1)S(1)} %broadcast_multiply_fusion), channel_id=1, source_target_pairs={{0,8},{4,12},{8,16},{12,20},{16,24},{20,28},{24,0},{28,4},{1,9},{5... | collective-permute-start | bytes 8454152 | tf_op jit(solution)/shard_map/ppermute | solution.py:13
  87.4 126.5 %collective-permute-start.5 = (bf16[512,2752]{0,1:T(8,128)(2,1)S(1)}, bf16[512,2752]{0,1:T(8,128)(2,1)S(1)}, u32[]{:S(2)}, u32[]{:S(2)}) collective-permute-start(bf16[512,2752]{0,1:T(8,128)(2,1)S(1)} %broadcast_multiply_fusion), channel_id=1, source_target_pairs={{0,4},{4,8},{8,12},{12,16},{16,20},{20,24},{24,28},{28,0},{1,5},{5... | collective-permute-start | bytes 8454152 | tf_op jit(solution)/shard_map/ppermute | solution.py:13
  88.8 130.4 %collective-permute-start.6 = (bf16[512,2752]{0,1:T(8,128)(2,1)S(1)}, bf16[512,2752]{0,1:T(8,128)(2,1)S(1)}, u32[]{:S(2)}, u32[]{:S(2)}) collective-permute-start(bf16[512,2752]{0,1:T(8,128)(2,1)S(1)} %broadcast_multiply_fusion), channel_id=1, source_target_pairs={{0,28},{4,0},{8,4},{12,8},{16,12},{20,16},{24,20},{28,24},{1,29},{... | collective-permute-start | bytes 8454152 | tf_op jit(solution)/shard_map/ppermute | solution.py:13
  92.1 179.7 %collective-permute-start.7 = (bf16[512,2752]{0,1:T(8,128)(2,1)S(1)}, bf16[512,2752]{0,1:T(8,128)(2,1)S(1)}, u32[]{:S(2)}, u32[]{:S(2)}) collective-permute-start(bf16[512,2752]{0,1:T(8,128)(2,1)S(1)} %broadcast_multiply_fusion), channel_id=1, source_target_pairs={{0,24},{4,28},{8,0},{12,4},{16,8},{20,12},{24,16},{28,20},{1,25},{... | collective-permute-start | bytes 8454152 | tf_op jit(solution)/shard_map/ppermute | solution.py:13
Sparse Core Ops, SparseCore 0:
  84.8 56.8 reduce-scatter.2
  274.6 50.1 reduce-scatter.4
where the time goes:
time: 335 us
  waiting for transfers between devices  271 us (81%)
  matrix products  22.1 us (7%)
  starting transfers between devices  19.9 us (6%)
  between operations  13.4 us (4%)
  other arithmetic  5.13 us (2%)
    ppermute x8, waiting for transfers between devices, shifted(): lax.ppermute(shard, axis, [(i, (i + by) % length) for i in range(length)])  221 us
    reduce_scatter x1, waiting for transfers between devices, width_total(): lax.psum_scatter(grad_gram, 'wid', scatter_dimension=2, tiled=True)  50.3 us
    ppermute x8, starting transfers between devices, shifted(): lax.ppermute(shard, axis, [(i, (i + by) % length) for i in range(length)])  19.9 us
    dot_general x5, matrix products, gram_tiles(): jnp.dot(masked_grads, other_grads.T, preferred_element_type=jnp.float32)  13.4 us
    dot_general x5, matrix products, gram_tiles(): jnp.dot(masked_acts, other_acts.T, preferred_element_type=jnp.float32)  8.72 us
  transfers between devices with their start and end apart: 10, of which 7 were waited for; matrix products, arithmetic and copies ran while one was open for 6% of the time, Pallas kernels for 0%

commit v1 on v0

v1 whole, which is shorter than its diff:
```python
import math

import jax
import jax.numpy as jnp
from jax import lax
from jax.experimental import pallas as pl
from jax.experimental.pallas import tpu as pltpu
from jax.sharding import PartitionSpec as P

D = 4096
FF = 11008
WID = 4
UNIT = 128
SUB = UNIT // WID


def gram(left, right):
    return lax.dot_general(left, right, (((1,), (1,)), ((), ())), preferred_element_type=jnp.float32)


def step_blocks(step, units):
    fresh = [(step, b) for b in range(step + 1)] + [(a, step) for a in range(step)]
    return (
        [("rt", a, step) for a in range(units)]
        + [("tt", b, a) for a, b in fresh]
        + [("tj", a, b) for a, b in fresh]
        + [("rj", step, b) for b in range(units)]
    )


def partial_kernel(names, units, place_ref, *refs):
    own, ring, other, (keep, send) = refs[:units], refs[units : 2 * units], refs[2 * units : -2], refs[-2:]
    even = place_ref[0] == 0
    core = place_ref[1]
    side = place_ref[2]
    spot = {name: i for i, name in enumerate(names)}

    def put(name, block):
        at = pl.ds(spot[name] * SUB, SUB)
        for quarter in range(WID):
            rows = block[quarter * SUB : (quarter + 1) * SUB]
            there = jnp.abs(side - quarter // 2)

            @pl.when(core == quarter % 2)
            def _():
                keep[there, at, :] = rows

            @pl.when(core != quarter % 2)
            def _():
                send[there, at, :] = rows

    for kind, a, b in names:
        if kind == "rj":
            block = gram(ring[a][...], own[b][...])
            put((kind, a, b), block)
            put(("rt", b, a), block.T)
        elif kind == "tj":
            chosen = jnp.where(even, ring[a][...], own[a][...])
            block = gram(chosen, other[b][...])
            put((kind, a, b), block)
            put(("tt", b, a), block.T)
        elif kind == "s":
            put((kind, a, b), gram(own[a][...], own[b][...]))


def partials(names, place, own, ring, other):
    units = len(own)
    shape = jax.ShapeDtypeStruct((2, len(names) * SUB, UNIT), jnp.float32)
    return pl.pallas_call(
        lambda *refs: partial_kernel(names, units, *refs),
        out_shape=(shape, shape),
        in_specs=[pl.BlockSpec(memory_space=pltpu.SMEM)] + [pl.BlockSpec(memory_space=pltpu.VMEM)] * (len(own) + len(ring) + len(other)),
        out_specs=(pl.BlockSpec(memory_space=pltpu.VMEM),) * 2,
        compiler_params=pltpu.CompilerParams(vmem_limit_bytes=40 << 20),
    )(place, *own, *ring, *other)


def wid_total(keep, send):
    arrived = lax.ppermute(send, "wid", [(w, w ^ 1) for w in range(WID)])
    across = lax.ppermute(keep[1] + arrived[1], "wid", [(w, w ^ 2) for w in range(WID)])
    return keep[0] + arrived[0] + across


def final_kernel(units, pieces, place_ref, lengths_ref, *refs):
    out = refs[-1]
    even = place_ref[0] == 0
    width = place_ref[3]
    token = place_ref[4]
    total = lengths_ref.shape[0]
    here = lengths_ref[token]
    for offset in range(5):
        there = lengths_ref[lax.rem(token + offset + total - 2, total)]
        for b in range(units):
            def piece(source):
                parts = []
                for a in range(units):
                    which, at = pieces[(source, a, b)]
                    parts.append(refs[which][at * SUB : (at + 1) * SUB, :])
                return jnp.concatenate(parts, axis=0)

            if offset == 1:
                tile = jnp.where(even, piece("ztt"), piece("tt"))
            else:
                tile = piece(("zrt", None, "s", "xtj", "rj")[offset])
            tile = tile.T
            columns = width * UNIT + lax.broadcasted_iota(jnp.int32, (SUB, UNIT), 1)
            for quarter in range(WID):
                first = quarter * UNIT + b * SUB
                rows = first + lax.broadcasted_iota(jnp.int32, (SUB, UNIT), 0)
                live = (rows < here) & (columns < there)
                out[first : first + SUB, offset, :] = jnp.where(live, tile[quarter * SUB : (quarter + 1) * SUB], 0.0)


def shards(acts, grads, lengths):
    rows = acts.shape[0]
    units = rows // UNIT
    length = lax.axis_size("tok")
    token = lax.axis_index("tok")
    width = lax.axis_index("wid")
    place = jnp.stack([token % 2, width % 2, width // 2, width, token]).astype(jnp.int32)
    swap = [(i, i ^ 1) for i in range(length)]
    down = [(i, (i - 2) % length) for i in range(length)]
    up = [(i, (i + 2) % length) for i in range(length)]

    def cut(x):
        x = x.reshape(WID, units, SUB, x.shape[1])
        return [x[:, c].reshape(UNIT, x.shape[3]) for c in range(units)]

    own_a = jnp.concatenate(cut(acts), axis=0)
    ring_a = lax.ppermute(own_a, "tok", down)
    other_a = lax.ppermute(own_a, "tok", swap)
    own_g = cut(grads)
    ring_g, other_g = [], []
    for c in range(units):
        chunk = own_g[c]
        if c >= 1:
            held = (ring_a, other_a) if c == 1 else (ring_g[c - 2], other_g[c - 2])
            chunk, first, second = lax.optimization_barrier((chunk, *held))
            if c == 1:
                ring_a, other_a = first, second
            else:
                ring_g[c - 2], other_g[c - 2] = first, second
        ring_g.append(lax.ppermute(chunk, "tok", down))
        other_g.append(lax.ppermute(chunk, "tok", swap))

    scale_a = 1.0 / jnp.sqrt(jnp.float32(D))
    scale_g = 1.0 / jnp.sqrt(jnp.float32(FF))
    pick = lambda x: [x[c * UNIT : (c + 1) * UNIT] for c in range(units)]

    self_names = [("s", a, b) for a in range(units) for b in range(units)]
    keep_a, send_a = partials(self_names, place, pick(own_a), [], [])
    keep_g, send_g = partials(self_names, place, own_g, [], [])
    both = wid_total(jnp.concatenate([keep_a, keep_g], axis=1), jnp.concatenate([send_a, send_g], axis=1))
    half = both.shape[0] // 2
    self_tile = (both[:half] * scale_a) * (both[half:] * scale_g)

    steps = [step_blocks(c, units) for c in range(units)]
    names = sum(steps, [])
    act_total = wid_total(*partials(names, place, pick(own_a), pick(ring_a), pick(other_a)))

    arrays, pieces = [self_tile], {("s", a, b): (0, i) for i, (_, a, b) in enumerate(self_names)}
    start = 0
    for c in range(units):
        size = len(steps[c])
        pad = lambda x: x[: c + 1] + [x[0]] * (units - c - 1)
        grad_total = wid_total(*partials(steps[c], place, own_g, pad(ring_g), pad(other_g)))
        tile = (act_total[start * SUB : (start + size) * SUB] * scale_a) * (grad_total * scale_g)
        start += size
        n_z, n_x = units + 2 * c + 1, 2 * c + 1
        arrays.append(tile)
        arrays.append(lax.ppermute(tile[: n_z * SUB], "tok", up))
        arrays.append(lax.ppermute(tile[n_z * SUB : (n_z + n_x) * SUB], "tok", swap))
        for i, (kind, a, b) in enumerate(steps[c]):
            if kind in ("rj", "tt"):
                pieces[(kind, a, b)] = (len(arrays) - 3, i)
            if kind in ("rt", "tt"):
                pieces[("z" + kind, a, b)] = (len(arrays) - 2, i)
            if kind == "tj":
                pieces[("xtj", a, b)] = (len(arrays) - 1, i - n_z)

    return pl.pallas_call(
        lambda *refs: final_kernel(units, pieces, *refs),
        out_shape=jax.ShapeDtypeStruct((rows, 5, UNIT), jnp.float32),
        in_specs=[pl.BlockSpec(memory_space=pltpu.SMEM)] * 2 + [pl.BlockSpec(memory_space=pltpu.VMEM)] * len(arrays),
        out_specs=pl.BlockSpec(memory_space=pltpu.VMEM),
        compiler_params=pltpu.CompilerParams(vmem_limit_bytes=32 << 20),
    )(place, lengths, *arrays)


def solution(mesh):
    return jax.shard_map(
        shards,
        mesh=mesh,
        in_specs=(P("tok", "wid"), P("tok", "wid"), P()),
        out_specs=P("tok", None, "wid"),
        check_vma=False,
    )
```

time: 335 us -> 212 us (0.63)
  waiting for transfers between devices: 271 us -> 54.5 us
  Pallas kernels: 0 us -> 54.7 us
  local copies, waits for them, and re-layouts: 2.96 us -> 56.3 us
  matrix products: 22.1 us -> 0 us
  between operations: 13.4 us -> 0.38 us
  other arithmetic: 5.13 us -> 18 us
  starting transfers between devices: 19.9 us -> 26.1 us
    ppermute x8 -> x30, waiting for transfers between devices: 221 us -> 54.5 us  [the longest x4 14.7 us: shards(): ring_g.append(lax.ppermute(chunk, 'tok', down))]
    pallas_call x0 -> x8, Pallas kernels: none -> 54.7 us  [the longest x7 53.2 us: partials(): pl.pallas_call(lambda *refs: partial_kernel(names, units, *refs), out_sha...]
    reduce_scatter x2 -> x0, waiting for transfers between devices: 50.3 us -> none  [the longest x1 50.3 us: width_total(): lax.psum_scatter(grad_gram, 'wid', scatter_dimension=2, tiled=True)]
    unnamed x2 -> x78, local copies, waits for them, and re-layouts: 1.72 us -> 28.1 us
    dot_general x10 -> x0, matrix products: 22.1 us -> none  [the longest x5 13.4 us: gram_tiles(): jnp.dot(masked_grads, other_grads.T, preferred_element_type=jnp.float32)]
    add x0 -> x8, other arithmetic: none -> 11.4 us  [the longest x6 8.05 us: wid_total(): keep[1] + arrived[1]]
    optimization_barrier x0 -> x7, local copies, waits for them, and re-layouts: none -> 10.7 us  [shards(): chunk, first, second = lax.optimization_barrier((chunk, *held))]
    ppermute x0 -> x4, local copies, waits for them, and re-layouts: none -> 9.05 us  [the longest x2 4.57 us: shards(): ring_g.append(lax.ppermute(chunk, 'tok', down))]
  transfers between devices with their start and end apart: 10 -> 30, of which waited for: 7 -> 9; matrix products, arithmetic and copies ran while one was open for 6% -> 22% of each run, Pallas kernels for 0% -> 18%
where the time goes in v1:
time: 212 us; the launch traced here: 210 us
  local copies, waits for them, and re-layouts  56.3 us (27%)
  Pallas kernels  54.7 us (26%)
  waiting for transfers between devices  54.5 us (26%)
  starting transfers between devices  26.1 us (12%)
  other arithmetic  18 us (8%)
    pallas_call x7, Pallas kernels, partials(): pl.pallas_call(lambda *refs: partial_kernel(names, units, *refs), out_sha...  53.2 us
    unnamed x78, local copies, waits for them, and re-layouts  28.1 us
    ppermute x4, waiting for transfers between devices, shards(): ring_g.append(lax.ppermute(chunk, 'tok', down))  14.7 us
    ppermute x1, waiting for transfers between devices, shards(): ring_a = lax.ppermute(own_a, 'tok', down)  14.6 us
    ppermute x6, waiting for transfers between devices, wid_total(): lax.ppermute(keep[1] + arrived[1], 'wid', [(w, w ^ 2) for w in range(WID)])  12.8 us
    optimization_barrier x7, local copies, waits for them, and re-layouts, shards(): chunk, first, second = lax.optimization_barrier((chunk, *held))  10.7 us
    ppermute x4, waiting for transfers between devices, shards(): arrays.append(lax.ppermute(tile[:n_z * SUB], 'tok', up))  8.14 us
    add x6, other arithmetic, wid_total(): keep[1] + arrived[1]  8.05 us
  transfers between devices with their start and end apart: 30, of which 9 were waited for; matrix products, arithmetic and copies ran while one was open for 22% of the time, Pallas kernels for 18%

profile of v1, /device:TPU:0, one launch (start us, length us, event | category | flops | bytes accessed | tf_op | source)
XLA Modules:
  0.0 210.0 jit_solution(2346393911258113969)
XLA Ops:
  3.1 5.0 %collective-permute-start.2 = (bf16[512,1024]{1,0:T(8,128)(2,1)}, bf16[512,1024]{1,0:T(8,128)(2,1)}, u32[]{:S(2)}, u32[]{:S(2)}) collective-permute-start(bf16[512,1024]{1,0:T(8,128)(2,1)} %pad_maximum_fusion.1), channel_id=1, source_target_pairs={{0,24},{4,28},{8,0},{12,4},{16,8},{20,12},{24,16},{28,20},{1,25},{... | collective-permute-start | bytes 3145736 | tf_op jit(solution)/shard_map/ppermute | solution.py:130
  9.6 4.6 %copy.23 = bf16[512,2752]{1,0:T(8,128)(2,1)} copy(bf16[512,2752]{0,1:T(8,128)(2,1)} %param.4) | data formatting | bytes 5636096 | tf_op args[1]
  16.2 14.6 %collective-permute-done.2 = bf16[512,1024]{1,0:T(8,128)(2,1)} collective-permute-done((bf16[512,1024]{1,0:T(8,128)(2,1)}, bf16[512,1024]{1,0:T(8,128)(2,1)}, u32[]{:S(2)}, u32[]{:S(2)}) %collective-permute-start.2) | collective-permute-done | bytes 1048608 | tf_op jit(solution)/shard_map/ppermute | solution.py:130
  30.8 2.2 %collective-permute-done.3 = bf16[512,1024]{1,0:T(8,128)(2,1)} collective-permute-done((bf16[512,1024]{1,0:T(8,128)(2,1)}, bf16[512,1024]{1,0:T(8,128)(2,1)}, u32[]{:S(2)}, u32[]{:S(2)}) %collective-permute-start.3) | collective-permute-done | bytes 1048608 | tf_op jit(solution)/shard_map/ppermute | solution.py:131
  34.8 14.6 %shard_map.39 = (f32[2,2048,128]{2,1,0:T(8,128)S(1)}, f32[2,2048,128]{2,1,0:T(8,128)}) custom-call(s32[5]{0:T(128)S(1)} %stack.23.refs_0_, bf16[128,1024]{1,0:T(8,128)(2,1)S(1)} %bitcast.109, bf16[128,1024]{1,0:T(8,128)(2,1)S(1)} %bitcast.106, bf16[128,1024]{1,0:T(8,128)(2,1)S(1)} %bitcast.103, bf16[128,1024]{1,0:T(8,128)(2,1)S(1)} %bitcast.100, ...), custom_call_target="tpu_custom_call" | custom-call | tf_op jit(solution)/shard_map/pallas_call | solution.py:69
  57.3 5.2 %shard_map.37 = (f32[2,512,128]{2,1,0:T(8,128)S(1)}, f32[2,512,128]{2,1,0:T(8,128)S(1)}) custom-call(s32[5]{0:T(128)S(1)} %stack.23.refs_0_, bf16[128,1024]{1,0:T(8,128)(2,1)S(1)} %bitcast.110, bf16[128,1024]{1,0:T(8,128)(2,1)S(1)} %bitcast.107, bf16[128,1024]{1,0:T(8,128)(2,1)S(1)} %bitcast.104, bf16[128,1024]{1,0:T(8,128)(2,1)S(1)} %bitcast.101), custom_call_target="tpu_custom_call" | custom-call | tf_op jit(solution)/shard_map/pallas_call | solution.py:69
  64.2 9.2 %shard_map.38 = (f32[2,512,128]{2,1,0:T(8,128)S(1)}, f32[2,512,128]{2,1,0:T(8,128)S(1)}) custom-call(s32[5]{0:T(128)S(1)} %stack.23.refs_0_, bf16[128,2752]{1,0:T(8,128)(2,1)S(1)} %bitcast.94, bf16[128,2752]{1,0:T(8,128)(2,1)S(1)} %bitcast.87, bf16[128,2752]{1,0:T(8,128)(2,1)S(1)} %bitcast.81, bf16[128,2752]{1,0:T(8,128)(2,1)S(1)} %bitcast.75), custom_call_target="tpu_custom_call" | custom-call | tf_op jit(solution)/shard_map/pallas_call | solution.py:69
  75.3 2.3 %pad_maximum_fusion = f32[2,1024,128]{2,1,0:T(8,128)} fusion(f32[2,512,128]{2,1,0:T(8,128)} %copy-done.30, f32[2,512,128]{2,1,0:T(8,128)} %copy-done.29), kind=kLoop, calls=%fused_computation.5 | loop fusion | flops 262144 | bytes 2097152 | tf_op jit(solution)/shard_map/concatenate | solution.py:153
  79.5 14.7 %collective-permute-done.12 = bf16[128,2752]{0,1:T(8,128)(2,1)S(1)} collective-permute-done((bf16[128,2752]{0,1:T(8,128)(2,1)}, bf16[128,2752]{0,1:T(8,128)(2,1)S(1)}, u32[]{:S(2)}, u32[]{:S(2)}) %collective-permute-start.12) | collective-permute-done | bytes 704544 | tf_op jit(solution)/shard_map/ppermute | solution.py:143
  101.4 4.3 %shard_map.40 = (f32[2,320,128]{2,1,0:T(8,128)S(1)}, f32[2,320,128]{2,1,0:T(8,128)}) custom-call(s32[5]{0:T(128)S(1)} %stack.23.refs_0_, bf16[128,2752]{1,0:T(8,128)(2,1)S(1)} %bitcast.95, bf16[128,2752]{1,0:T(8,128)(2,1)S(1)} %bitcast.89, bf16[128,2752]{1,0:T(8,128)(2,1)S(1)} %bitcast.83, bf16[128,2752]{1,0:T(8,128)(2,1)S(1)} %bitcast.76, ...), custom_call_target="tpu_custom_call" | custom-call | tf_op jit(solution)/shard_map/pallas_call | solution.py:69
  112.2 2.3 %copy.48.refs_7_ = bf16[128,2752]{1,0:T(8,128)(2,1)} copy(bf16[128,2752]{0,1:T(8,128)(2,1)} %collective-permute-done.18) | data formatting | bytes 1409024 | tf_op jit(solution)/shard_map/ppermute | solution.py:143
  114.5 2.2 %copy.52.refs_11_ = bf16[128,2752]{1,0:T(8,128)(2,1)} copy(bf16[128,2752]{0,1:T(8,128)(2,1)} %collective-permute-done.19) | data formatting | bytes 1409024 | tf_op jit(solution)/shard_map/ppermute | solution.py:144
  118.2 2.2 %copy.37.refs_6_ = bf16[128,2752]{1,0:T(8,128)(2,1)} copy(bf16[128,2752]{0,1:T(8,128)(2,1)} %copy-done.37) | data formatting | bytes 1409024 | tf_op jit(solution)/shard_map/optimization_barrier | solution.py:138
  120.4 2.2 %copy.41.refs_10_ = bf16[128,2752]{1,0:T(8,128)(2,1)} copy(bf16[128,2752]{0,1:T(8,128)(2,1)} %collective-permute-done.13) | data formatting | bytes 1409024 | tf_op jit(solution)/shard_map/optimization_barrier | solution.py:138
  127.1 5.6 %shard_map.41 = (f32[2,448,128]{2,1,0:T(8,128)S(1)}, f32[2,448,128]{2,1,0:T(8,128)}) custom-call(s32[5]{0:T(128)S(1)} %stack.23.refs_0_, bf16[128,2752]{1,0:T(8,128)(2,1)S(1)} %bitcast.96, bf16[128,2752]{1,0:T(8,128)(2,1)S(1)} %bitcast.90, bf16[128,2752]{1,0:T(8,128)(2,1)S(1)} %bitcast.84, bf16[128,2752]{1,0:T(8,128)(2,1)S(1)} %bitcast.78, ...), custom_call_target="tpu_custom_call" | custom-call | tf_op jit(solution)/shard_map/pallas_call | solution.py:69
  133.5 6.9 %shard_map.42 = (f32[2,576,128]{2,1,0:T(8,128)S(1)}, f32[2,576,128]{2,1,0:T(8,128)}) custom-call(s32[5]{0:T(128)S(1)} %stack.23.refs_0_, bf16[128,2752]{1,0:T(8,128)(2,1)S(1)} %bitcast.97, bf16[128,2752]{1,0:T(8,128)(2,1)S(1)} %bitcast.91, bf16[128,2752]{1,0:T(8,128)(2,1)S(1)} %bitcast.85, bf16[128,2752]{1,0:T(8,128)(2,1)S(1)} %bitcast.79, ...), custom_call_target="tpu_custom_call" | custom-call | tf_op jit(solution)/shard_map/pallas_call | solution.py:69
  140.4 2.4 %fusion = f32[2048,128]{1,0:T(8,128)} fusion(f32[2,2048,128]{2,1,0:T(8,128)} %collective-permute-done.4, f32[2,2048,128]{2,1,0:T(8,128)S(1)} %copy-done.25), kind=kLoop, calls=%fused_computation.1 | loop fusion | flops 262144 | bytes 3145728 | tf_op jit(solution)/shard_map/add | solution.py:80
  145.4 2.3 %copy.59.refs_8_ = bf16[128,2752]{1,0:T(8,128)(2,1)} copy(bf16[128,2752]{0,1:T(8,128)(2,1)} %collective-permute-done.24) | data formatting | bytes 1409024 | tf_op jit(solution)/shard_map/ppermute | solution.py:143
  149.1 2.3 %copy.63.refs_12_ = bf16[128,2752]{1,0:T(8,128)(2,1)} copy(bf16[128,2752]{0,1:T(8,128)(2,1)} %collective-permute-done.25) | data formatting | bytes 1409024 | tf_op jit(solution)/shard_map/ppermute | solution.py:144
  160.3 7.6 %shard_map.43 = (f32[2,704,128]{2,1,0:T(8,128)S(1)}, f32[2,704,128]{2,1,0:T(8,128)S(1)}) custom-call(s32[5]{0:T(128)S(1)} %stack.23.refs_0_, bf16[128,2752]{1,0:T(8,128)(2,1)S(1)} %bitcast.98, bf16[128,2752]{1,0:T(8,128)(2,1)S(1)} %bitcast.92, bf16[128,2752]{1,0:T(8,128)(2,1)S(1)} %bitcast.86, bf16[128,2752]{1,0:T(8,128)(2,1)S(1)} %bitcast.80, ...), custom_call_target="tpu_custom_call" | custom-call | tf_op jit(solution)/shard_map/pallas_call | solution.py:69
  180.7 11.8 %collective-permute-done.27 = f32[704,128]{1,0:T(8,128)S(1)} collective-permute-done((f32[704,128]{1,0:T(8,128)S(1)}, f32[704,128]{1,0:T(8,128)S(1)}, u32[]{:S(2)}, u32[]{:S(2)}) %collective-permute-start.27) | collective-permute-done | bytes 360480 | tf_op jit(solution)/shard_map/ppermute | solution.py:80
  199.1 2.6 %collective-permute-done.16.refs_7_ = f32[224,128]{1,0:T(8,128)S(1)} collective-permute-done((f32[224,128]{1,0:T(8,128)S(1)}, f32[224,128]{1,0:T(8,128)S(1)}, u32[]{:S(2)}, u32[]{:S(2)}) %collective-permute-start.16) | collective-permute-done | bytes 114720 | tf_op jit(solution)/shard_map/ppermute | solution.py:171
  201.7 3.2 %collective-permute-done.22.refs_10_ = f32[288,128]{1,0:T(8,128)S(1)} collective-permute-done((f32[288,128]{1,0:T(8,128)S(1)}, f32[288,128]{1,0:T(8,128)S(1)}, u32[]{:S(2)}, u32[]{:S(2)}) %collective-permute-start.22) | collective-permute-done | bytes 147488 | tf_op jit(solution)/shard_map/ppermute | solution.py:171
  204.8 2.4 %collective-permute-done.28.refs_13_ = f32[352,128]{1,0:T(8,128)S(1)} collective-permute-done((f32[352,128]{1,0:T(8,128)S(1)}, f32[352,128]{1,0:T(8,128)S(1)}, u32[]{:S(2)}, u32[]{:S(2)}) %collective-permute-start.28) | collective-permute-done | bytes 180256 | tf_op jit(solution)/shard_map/ppermute | solution.py:171
  (163 shorter events, 77.1 us)
Async XLA Ops:
  3.1 27.8 %collective-permute-start.2 = (bf16[512,1024]{1,0:T(8,128)(2,1)}, bf16[512,1024]{1,0:T(8,128)(2,1)}, u32[]{:S(2)}, u32[]{:S(2)}) collective-permute-start(bf16[512,1024]{1,0:T(8,128)(2,1)} %pad_maximum_fusion.1), channel_id=1, source_target_pairs={{0,24},{4,28},{8,0},{12,4},{16,8},{20,12},{24,16},{28,20},{1,25},{... | collective-permute-start | bytes 3145736 | tf_op jit(solution)/shard_map/ppermute | solution.py:130
  8.1 24.9 %collective-permute-start.3 = (bf16[512,1024]{1,0:T(8,128)(2,1)}, bf16[512,1024]{1,0:T(8,128)(2,1)}, u32[]{:S(2)}, u32[]{:S(2)}) collective-permute-start(bf16[512,1024]{1,0:T(8,128)(2,1)} %pad_maximum_fusion.1), channel_id=1, source_target_pairs={{0,4},{4,0},{8,12},{12,8},{16,20},{20,16},{24,28},{28,24},{1,5},{5... | collective-permute-start | bytes 3145736 | tf_op jit(solution)/shard_map/ppermute | solution.py:131
  50.7 89.7 %collective-permute-start.4 = (f32[2,2048,128]{2,1,0:T(8,128)}, f32[2,2048,128]{2,1,0:T(8,128)}, u32[]{:S(2)}, u32[]{:S(2)}) collective-permute-start(f32[2,2048,128]{2,1,0:T(8,128)} %get-tuple-element.35), channel_id=1, source_target_pairs={{0,1},{1,0},{2,3},{3,2},{4,5},{5,4},{6,7},{7,6},{8,9},{9,8},{10,11... | collective-permute-start | bytes 6291464 | tf_op jit(solution)/shard_map/ppermute | solution.py:79
  51.9 25.8 %collective-permute-start.6 = (bf16[128,2752]{0,1:T(8,128)(2,1)}, bf16[128,2752]{0,1:T(8,128)(2,1)}, u32[]{:S(2)}, u32[]{:S(2)}) collective-permute-start(bf16[128,2752]{0,1:T(8,128)(2,1)} %copy.24), channel_id=1, source_target_pairs={{0,24},{4,28},{8,0},{12,4},{16,8},{20,12},{24,16},{28,20},{1,25},{... | collective-permute-start | bytes 2113544 | tf_op jit(solution)/shard_map/ppermute | solution.py:143
  53.9 24.2 %collective-permute-start.7 = (bf16[128,2752]{0,1:T(8,128)(2,1)}, bf16[128,2752]{0,1:T(8,128)(2,1)}, u32[]{:S(2)}, u32[]{:S(2)}) collective-permute-start(bf16[128,2752]{0,1:T(8,128)(2,1)} %copy.24), channel_id=1, source_target_pairs={{0,4},{4,0},{8,12},{12,8},{16,20},{20,16},{24,28},{28,24},{1,5},{5... | collective-permute-start | bytes 2113544 | tf_op jit(solution)/shard_map/ppermute | solution.py:144
  75.3 18.9 %collective-permute-start.12 = (bf16[128,2752]{0,1:T(8,128)(2,1)}, bf16[128,2752]{0,1:T(8,128)(2,1)S(1)}, u32[]{:S(2)}, u32[]{:S(2)}) collective-permute-start(bf16[128,2752]{0,1:T(8,128)(2,1)} %copy.34), channel_id=1, source_target_pairs={{0,24},{4,28},{8,0},{12,4},{16,8},{20,12},{24,16},{28,20},{1,25},{... | collective-permute-start | bytes 2113544 | tf_op jit(solution)/shard_map/ppermute | solution.py:143
  77.6 29.2 %collective-permute-start = (f32[2,1024,128]{2,1,0:T(8,128)}, f32[2,1024,128]{2,1,0:T(8,128)}, u32[]{:S(2)}, u32[]{:S(2)}) collective-permute-start(f32[2,1024,128]{2,1,0:T(8,128)} %pad_maximum_fusion), channel_id=1, source_target_pairs={{0,1},{1,0},{2,3},{3,2},{4,5},{5,4},{6,7},{7,6},{8,9},{9,8},{10,11... | collective-permute-start | bytes 3145736 | tf_op jit(solution)/shard_map/ppermute | solution.py:79
  77.6 28.0 %collective-permute-start.13 = (bf16[128,2752]{0,1:T(8,128)(2,1)}, bf16[128,2752]{0,1:T(8,128)(2,1)}, u32[]{:S(2)}, u32[]{:S(2)}) collective-permute-start(bf16[128,2752]{0,1:T(8,128)(2,1)} %copy.34), channel_id=1, source_target_pairs={{0,4},{4,0},{8,12},{12,8},{16,20},{20,16},{24,28},{28,24},{1,5},{5... | collective-permute-start | bytes 2113544 | tf_op jit(solution)/shard_map/ppermute | solution.py:144
  79.3 31.3 %collective-permute-start.18 = (bf16[128,2752]{0,1:T(8,128)(2,1)}, bf16[128,2752]{0,1:T(8,128)(2,1)}, u32[]{:S(2)}, u32[]{:S(2)}) collective-permute-start(bf16[128,2752]{0,1:T(8,128)(2,1)} %copy.44), channel_id=1, source_target_pairs={{0,24},{4,28},{8,0},{12,4},{16,8},{20,12},{24,16},{28,20},{1,25},{... | collective-permute-start | bytes 2113544 | tf_op jit(solution)/shard_map/ppermute | solution.py:143
  94.2 20.3 %collective-permute-start.19 = (bf16[128,2752]{0,1:T(8,128)(2,1)}, bf16[128,2752]{0,1:T(8,128)(2,1)}, u32[]{:S(2)}, u32[]{:S(2)}) collective-permute-start(bf16[128,2752]{0,1:T(8,128)(2,1)} %copy.44), channel_id=1, source_target_pairs={{0,4},{4,0},{8,12},{12,8},{16,20},{20,16},{24,28},{28,24},{1,5},{5... | collective-permute-start | bytes 2113544 | tf_op jit(solution)/shard_map/ppermute | solution.py:144
  105.7 37.1 %collective-permute-start.8 = (f32[2,320,128]{2,1,0:T(8,128)}, f32[2,320,128]{2,1,0:T(8,128)}, u32[]{:S(2)}, u32[]{:S(2)}) collective-permute-start(f32[2,320,128]{2,1,0:T(8,128)} %get-tuple-element.39), channel_id=1, source_target_pairs={{0,1},{1,0},{2,3},{3,2},{4,5},{5,4},{6,7},{7,6},{8,9},{9,8},{10,11... | collective-permute-start | bytes 983048 | tf_op jit(solution)/shard_map/ppermute | solution.py:79
  106.8 36.4 %collective-permute-start.24 = (bf16[128,2752]{0,1:T(8,128)(2,1)}, bf16[128,2752]{0,1:T(8,128)(2,1)}, u32[]{:S(2)}, u32[]{:S(2)}) collective-permute-start(bf16[128,2752]{0,1:T(8,128)(2,1)} %copy.54), channel_id=1, source_target_pairs={{0,24},{4,28},{8,0},{12,4},{16,8},{20,12},{24,16},{28,20},{1,25},{... | collective-permute-start | bytes 2113544 | tf_op jit(solution)/shard_map/ppermute | solution.py:143
  110.6 57.2 %collective-permute-start.1 = (f32[1024,128]{1,0:T(8,128)}, f32[1024,128]{1,0:T(8,128)}, u32[]{:S(2)}, u32[]{:S(2)}) collective-permute-start(f32[1024,128]{1,0:T(8,128)} %fusion.3), channel_id=1, source_target_pairs={{0,2},{1,3},{2,0},{3,1},{4,6},{5,7},{6,4},{7,5},{8,10},{9,11},{10,... | collective-permute-start | bytes 1572872 | tf_op jit(solution)/shard_map/ppermute | solution.py:80
  116.7 30.9 %collective-permute-start.25 = (bf16[128,2752]{0,1:T(8,128)(2,1)}, bf16[128,2752]{0,1:T(8,128)(2,1)}, u32[]{:S(2)}, u32[]{:S(2)}) collective-permute-start(bf16[128,2752]{0,1:T(8,128)(2,1)} %copy.54), channel_id=1, source_target_pairs={{0,4},{4,0},{8,12},{12,8},{16,20},{20,16},{24,28},{28,24},{1,5},{5... | collective-permute-start | bytes 2113544 | tf_op jit(solution)/shard_map/ppermute | solution.py:144
  140.4 29.2 %collective-permute-start.14 = (f32[2,448,128]{2,1,0:T(8,128)}, f32[2,448,128]{2,1,0:T(8,128)}, u32[]{:S(2)}, u32[]{:S(2)}) collective-permute-start(f32[2,448,128]{2,1,0:T(8,128)} %get-tuple-element.44), channel_id=1, source_target_pairs={{0,1},{1,0},{2,3},{3,2},{4,5},{5,4},{6,7},{7,6},{8,9},{9,8},{10,11... | collective-permute-start | bytes 1376264 | tf_op jit(solution)/shard_map/ppermute | solution.py:79
  142.8 28.3 %collective-permute-start.20 = (f32[2,576,128]{2,1,0:T(8,128)}, f32[2,576,128]{2,1,0:T(8,128)}, u32[]{:S(2)}, u32[]{:S(2)}) collective-permute-start(f32[2,576,128]{2,1,0:T(8,128)} %get-tuple-element.47), channel_id=1, source_target_pairs={{0,1},{1,0},{2,3},{3,2},{4,5},{5,4},{6,7},{7,6},{8,9},{9,8},{10,11... | collective-permute-start | bytes 1769480 | tf_op jit(solution)/shard_map/ppermute | solution.py:79
  143.2 31.1 %collective-permute-start.5 = (f32[2048,128]{1,0:T(8,128)}, f32[2048,128]{1,0:T(8,128)}, u32[]{:S(2)}, u32[]{:S(2)}) collective-permute-start(f32[2048,128]{1,0:T(8,128)} %fusion), channel_id=1, source_target_pairs={{0,2},{1,3},{2,0},{3,1},{4,6},{5,7},{6,4},{7,5},{8,10},{9,11},{10,... | collective-permute-start | bytes 3145736 | tf_op jit(solution)/shard_map/ppermute | solution.py:80
  147.6 28.5 %collective-permute-start.9 = (f32[320,128]{1,0:T(8,128)}, f32[320,128]{1,0:T(8,128)}, u32[]{:S(2)}, u32[]{:S(2)}) collective-permute-start(f32[320,128]{1,0:T(8,128)} %fusion.22), channel_id=1, source_target_pairs={{0,2},{1,3},{2,0},{3,1},{4,6},{5,7},{6,4},{7,5},{8,10},{9,11},{10,... | collective-permute-start | bytes 491528 | tf_op jit(solution)/shard_map/ppermute | solution.py:80
  172.1 20.5 %collective-permute-start.21 = (f32[576,128]{1,0:T(8,128)S(1)}, f32[576,128]{1,0:T(8,128)S(1)}, u32[]{:S(2)}, u32[]{:S(2)}) collective-permute-start(f32[576,128]{1,0:T(8,128)S(1)} %fusion.11), channel_id=1, source_target_pairs={{0,2},{1,3},{2,0},{3,1},{4,6},{5,7},{6,4},{7,5},{8,10},{9,11},{10,... | collective-permute-start | bytes 884744 | tf_op jit(solution)/shard_map/ppermute | solution.py:80
  173.8 18.7 %collective-permute-start.27 = (f32[704,128]{1,0:T(8,128)S(1)}, f32[704,128]{1,0:T(8,128)S(1)}, u32[]{:S(2)}, u32[]{:S(2)}) collective-permute-start(f32[704,128]{1,0:T(8,128)S(1)} %fusion.6), channel_id=1, source_target_pairs={{0,2},{1,3},{2,0},{3,1},{4,6},{5,7},{6,4},{7,5},{8,10},{9,11},{10,... | collective-permute-start | bytes 1081352 | tf_op jit(solution)/shard_map/ppermute | solution.py:80
  177.2 18.2 %collective-permute-start.10 = (f32[160,128]{1,0:T(8,128)S(1)}, f32[160,128]{1,0:T(8,128)S(1)}, u32[]{:S(2)}, u32[]{:S(2)}) collective-permute-start(f32[160,128]{1,0:T(8,128)S(1)} %slice.235), channel_id=1, source_target_pairs={{0,8},{4,12},{8,16},{12,20},{16,24},{20,28},{24,0},{28,4},{1,9},{5... | collective-permute-start | bytes 245768 | tf_op jit(solution)/shard_map/ppermute | solution.py:171
  177.6 16.6 %collective-permute-start.11 = (f32[32,128]{1,0:T(8,128)S(1)}, f32[32,128]{1,0:T(8,128)S(1)}, u32[]{:S(2)}, u32[]{:S(2)}) collective-permute-start(f32[32,128]{1,0:T(8,128)S(1)} %slice.236), channel_id=1, source_target_pairs={{0,4},{4,0},{8,12},{12,8},{16,20},{20,16},{24,28},{28,24},{1,5},{5... | collective-permute-start | bytes 49160 | tf_op jit(solution)/shard_map/ppermute | solution.py:172
  180.0 14.6 %collective-permute-start.17 = (f32[96,128]{1,0:T(8,128)S(1)}, f32[96,128]{1,0:T(8,128)S(1)}, u32[]{:S(2)}, u32[]{:S(2)}) collective-permute-start(f32[96,128]{1,0:T(8,128)S(1)} %slice.241), channel_id=1, source_target_pairs={{0,4},{4,0},{8,12},{12,8},{16,20},{20,16},{24,28},{28,24},{1,5},{5... | collective-permute-start | bytes 147464 | tf_op jit(solution)/shard_map/ppermute | solution.py:172
  194.7 12.5 %collective-permute-start.28 = (f32[352,128]{1,0:T(8,128)S(1)}, f32[352,128]{1,0:T(8,128)S(1)}, u32[]{:S(2)}, u32[]{:S(2)}) collective-permute-start(f32[352,128]{1,0:T(8,128)S(1)} %slice.250), channel_id=1, source_target_pairs={{0,8},{4,12},{8,16},{12,20},{16,24},{20,28},{24,0},{28,4},{1,9},{5... | collective-permute-start | bytes 540680 | tf_op jit(solution)/shard_map/ppermute | solution.py:171
  (44 other events, 254.3 us)

commit v2 on v0

v2 whole, which is shorter than its diff:
```python
import jax
import jax.numpy as jnp
from jax import lax
from jax.experimental import pallas as pl
from jax.experimental.pallas import tpu as pltpu
from jax.sharding import PartitionSpec as P

D = 4096
FF = 11008
WID = 4
UNIT = 128
SUB = UNIT // WID
VMEM_LIMIT = 24 << 20
SMEM = pl.BlockSpec(memory_space=pltpu.SMEM)
VMEM = pl.BlockSpec(memory_space=pltpu.VMEM)


def call(kernel, outs, *args, scalars=0):
    return pl.pallas_call(
        kernel,
        out_shape=outs,
        in_specs=[SMEM] * scalars + [VMEM] * (len(args) - scalars),
        out_specs=jax.tree.map(lambda _: VMEM, outs),
        cost_estimate=pl.CostEstimate(flops=0, bytes_accessed=0, transcendentals=0),
        compiler_params=pltpu.CompilerParams(vmem_limit_bytes=VMEM_LIMIT),
    )(*args)


def dot(left, right, dims):
    return lax.dot_general(left, right, (dims, ((), ())), preferred_element_type=jnp.float32)


def row_dot(left, right):
    return dot(left, right, ((1,), (1,)))


def put(place_ref, keep, send, at, quarters):
    core = place_ref[1] == 0
    side = place_ref[2] == 0
    rows = pl.ds(at, quarters[0].shape[0])
    kept = [jnp.where(core, quarters[2 * s], quarters[2 * s + 1]) for s in range(2)]
    sent = [jnp.where(core, quarters[2 * s + 1], quarters[2 * s]) for s in range(2)]
    for ref, pair in ((keep, kept), (send, sent)):
        ref[0, rows, :] = jnp.where(side, pair[0], pair[1])
        ref[1, rows, :] = jnp.where(side, pair[1], pair[0])


def split_rows(block):
    n = block.shape[0] // WID
    return [block[q * n : (q + 1) * n] for q in range(WID)]


def lanes(block, b):
    return block[:, b * UNIT : (b + 1) * UNIT]


def step_layout(step, units):
    fresh = [(step, b) for b in range(step + 1)] + [(a, step) for a in range(step)]
    at, spot = UNIT, {("rt", step): 0}
    for a, b in fresh:
        spot[("tt", b, a)] = at
        at += SUB
    n_ring = at
    for a, b in fresh:
        spot[("tj", a, b)] = at
        at += SUB
    n_swap = at
    for b in range(WID):
        spot[("rj", step, b)] = at
        at += SUB
    return spot, n_ring, n_swap, at


def put_ring(place_ref, keep, send, spot, base, step, block):
    columns = [lanes(block, b) for b in range(WID)]
    put(place_ref, keep, send, base + spot[("rt", step)], [c.T for c in columns])
    for b in range(WID):
        put(place_ref, keep, send, base + spot[("rj", step, b)], split_rows(columns[b]))


def put_third(place_ref, keep, send, spot, base, a, b, block):
    put(place_ref, keep, send, base + spot[("tj", a, b)], split_rows(block))
    put(place_ref, keep, send, base + spot[("tt", b, a)], split_rows(block.T))


def reorder_kernel(g_ref, *outs):
    units = len(outs)
    tokens = g_ref.shape[1]
    source = lax.broadcasted_iota(jnp.int32, (tokens, UNIT), 0)
    lane = lax.broadcasted_iota(jnp.int32, (tokens, UNIT), 1)
    for c, out in enumerate(outs):
        wanted = (lane // SUB) * UNIT + c * SUB + lane % SUB
        pick = jnp.where(source == wanted, 1.0, 0.0).astype(jnp.bfloat16)
        out[...] = dot(g_ref[...], pick, ((1,), (0,))).astype(jnp.bfloat16)


def self_kernel(place_ref, a_ref, g_ref, keep, send):
    acts = a_ref[...]
    grads = g_ref[...]
    for i, block in enumerate((row_dot(acts, acts), dot(grads.T, grads, ((1,), (0,))))):
        for b in range(WID):
            put(place_ref, keep, send, (i * WID + b) * UNIT, split_rows(lanes(block, b)))


def acts_kernel(layouts, place_ref, own_ref, ring_ref, other_ref, keep, send):
    units = len(layouts)
    even = place_ref[0] == 0

    def arrival(x):
        return jnp.concatenate([x[q * UNIT + c * SUB : q * UNIT + (c + 1) * SUB] for c in range(units) for q in range(WID)], axis=0)

    own, ring, other = own_ref[...], ring_ref[...], other_ref[...]
    chosen = arrival(jnp.where(even, ring, own))
    ring = arrival(ring)
    other = arrival(other)
    base = 0
    for c, (spot, _, _, size) in enumerate(layouts):
        put_ring(place_ref, keep, send, spot, base, c, row_dot(ring[c * UNIT : (c + 1) * UNIT], own))
        base += size
    for a in range(units):
        block = row_dot(chosen[a * UNIT : (a + 1) * UNIT], other)
        for b in range(units):
            step = max(a, b)
            base = sum(layouts[s][3] for s in range(step))
            put_third(place_ref, keep, send, layouts[step][0], base, a, b, lanes(block, b))


def grads_kernel(step, spot, place_ref, own_ref, *refs):
    n = step + 1
    mine, ring, other, (keep, send) = refs[:n], refs[n : 2 * n], refs[2 * n : 3 * n], refs[3 * n :]
    even = place_ref[0] == 0
    chosen = [jnp.where(even, ring[a][...], mine[a][...]) for a in range(n)]
    put_ring(place_ref, keep, send, spot, 0, step, dot(ring[step][...].T, own_ref[...], ((1,), (0,))))
    block = dot(chosen[step].T, jnp.concatenate([o[...] for o in other], axis=1), ((1,), (0,)))
    for b in range(n):
        put_third(place_ref, keep, send, spot, 0, step, b, lanes(block, b))
    if step:
        block = dot(other[step][...].T, jnp.concatenate(chosen[:step], axis=1), ((1,), (0,))).T
        for a in range(step):
            put_third(place_ref, keep, send, spot, 0, a, step, block[a * UNIT : (a + 1) * UNIT])


def final_kernel(layouts, place_ref, lengths_ref, self_ref, *refs):
    out = refs[-1]
    units = len(layouts)
    local, ring, swap = refs[:units], refs[units : 2 * units], refs[2 * units : 3 * units]
    even = place_ref[0] == 0
    width = place_ref[3]
    token = place_ref[4]
    total = lengths_ref.shape[0]
    here = lengths_ref[token]
    columns = width * UNIT + lax.broadcasted_iota(jnp.int32, (UNIT, UNIT), 1)
    line = lax.broadcasted_iota(jnp.int32, (UNIT, UNIT), 0)

    def block(refs, name, step, shift=0):
        spot = layouts[step][0][name] - shift
        size = UNIT if name[0] == "rt" else SUB
        return refs[step][spot : spot + size, :]

    def natural(offset, b, tile, there):
        live = (b * UNIT + line < here) & (columns < there)
        out[offset, b * UNIT : (b + 1) * UNIT, :] = jnp.where(live, tile.T, 0.0)

    def arrival(offset, c, tile, there):
        token_at = (line // SUB) * UNIT + c * SUB + line % SUB
        tile = jnp.where((token_at < here) & (columns < there), tile.T, 0.0)
        for q in range(WID):
            first = q * UNIT + c * SUB
            out[offset, first : first + SUB, :] = tile[q * SUB : (q + 1) * SUB]

    there = [lengths_ref[lax.rem(token + offset + total - 2, total)] for offset in range(5)]
    for c in range(units):
        arrival(0, c, block(ring, ("rt", c), c), there[0])
        tt = [[block(r, ("tt", a, c), max(a, c)) for a in range(units)] for r in (ring, local)]
        arrival(1, c, jnp.where(even, jnp.concatenate(tt[0], axis=0), jnp.concatenate(tt[1], axis=0)), there[1])
        tj = [block(swap, ("tj", a, c), max(a, c), layouts[max(a, c)][1]) for a in range(units)]
        arrival(3, c, jnp.concatenate(tj, axis=0), there[3])
    for b in range(WID):
        natural(2, b, self_ref[b * UNIT : (b + 1) * UNIT, :], there[2])
        natural(4, b, jnp.concatenate([block(local, ("rj", c, b), c) for c in range(units)], axis=0), there[4])


def shards(acts, grads, lengths):
    rows = acts.shape[0]
    units = rows // UNIT
    length = lax.axis_size("tok")
    token = lax.axis_index("tok")
    width = lax.axis_index("wid")
    place = jnp.stack([token % 2, width % 2, width // 2, width, token]).astype(jnp.int32)
    swap = [(i, i ^ 1) for i in range(length)]
    down = [(i, (i - 2) % length) for i in range(length)]
    up = [(i, (i + 2) % length) for i in range(length)]
    layouts = [step_layout(c, units) for c in range(units)]

    def floats(n):
        return (jax.ShapeDtypeStruct((2, n, UNIT), jnp.float32),) * 2

    def wid_total(keep, send):
        arrived = lax.ppermute(send, "wid", [(w, w ^ 1) for w in range(WID)])
        across = lax.ppermute(keep[1] + arrived[1], "wid", [(w, w ^ 2) for w in range(WID)])
        return keep[0], arrived[0], across

    def total(parts, start, stop):
        return parts[0][start:stop] + parts[1][start:stop] + parts[2][start:stop]

    scale_a = 1.0 / jnp.sqrt(jnp.float32(D))
    scale_g = 1.0 / jnp.sqrt(jnp.float32(FF))

    ring_a = lax.ppermute(acts, "tok", down)
    other_a = lax.ppermute(acts, "tok", swap)
    own_g = grads.T
    mine = call(reorder_kernel, (jax.ShapeDtypeStruct((grads.shape[1], UNIT), jnp.bfloat16),) * units, own_g)
    ring_g, other_g = [], []
    for c in range(units):
        chunk = mine[c]
        if c == 1:
            chunk, ring_a, other_a = lax.optimization_barrier((chunk, ring_a, other_a))
        elif c > 1:
            chunk, ring_g[c - 2], other_g[c - 2] = lax.optimization_barrier((chunk, ring_g[c - 2], other_g[c - 2]))
        ring_g.append(lax.ppermute(chunk, "tok", down))
        other_g.append(lax.ppermute(chunk, "tok", swap))

    parts = wid_total(*call(self_kernel, floats(2 * WID * UNIT), place, acts, own_g, scalars=1))
    half = WID * UNIT
    self_tile = (total(parts, 0, half) * scale_a) * (total(parts, half, 2 * half) * scale_g)

    everything = sum(size for _, _, _, size in layouts)
    act_parts = wid_total(
        *call(lambda *refs: acts_kernel(layouts, *refs), floats(everything), place, acts, ring_a, other_a, scalars=1)
    )

    local, from_ring, from_swap = [], [], []
    base = 0
    for c, (spot, n_ring, n_swap, size) in enumerate(layouts):
        parts = wid_total(
            *call(
                lambda *refs, c=c, spot=spot: grads_kernel(c, spot, *refs),
                floats(size), place, own_g, *mine[: c + 1], *ring_g[: c + 1], *other_g[: c + 1], scalars=1,
            )
        )
        tile = (total(act_parts, base, base + size) * scale_a) * (total(parts, 0, size) * scale_g)
        base += size
        local.append(tile)
        from_ring.append(lax.ppermute(tile[:n_ring], "tok", up))
        from_swap.append(lax.ppermute(tile[n_ring:n_swap], "tok", swap))

    out = call(
        lambda *refs: final_kernel(layouts, *refs),
        jax.ShapeDtypeStruct((5, rows, UNIT), jnp.float32),
        place, lengths, self_tile, *local, *from_ring, *from_swap, scalars=2,
    )
    return out.transpose(1, 0, 2)


def solution(mesh):
    return jax.shard_map(
        shards,
        mesh=mesh,
        in_specs=(P("tok", "wid"), P("tok", "wid"), P()),
        out_specs=P("tok", None, "wid"),
        check_vma=False,
    )
```

time: 335 us -> 175 us (0.52)
  waiting for transfers between devices: 271 us -> 109 us
  matrix products: 22.1 us -> 0 us
  Pallas kernels: 0 us -> 20.4 us
  starting transfers between devices: 19.9 us -> 38.8 us
  between operations: 13.4 us -> 0.32 us
  other arithmetic: 5.13 us -> 0.7 us
    ppermute x8 -> x30, waiting for transfers between devices: 221 us -> 109 us  [the longest x6 40.5 us: wid_total(): lax.ppermute(keep[1] + arrived[1], 'wid', [(w, w ^ 2) for w in range(WID)])]
    reduce_scatter x2 -> x0, waiting for transfers between devices: 50.3 us -> none  [the longest x1 50.3 us: width_total(): lax.psum_scatter(grad_gram, 'wid', scatter_dimension=2, tiled=True)]
    dot_general x10 -> x0, matrix products: 22.1 us -> none  [the longest x5 13.4 us: gram_tiles(): jnp.dot(masked_grads, other_grads.T, preferred_element_type=jnp.float32)]
    pallas_call x0 -> x8, Pallas kernels: none -> 20.4 us  [call(): pl.pallas_call(kernel, out_shape=outs, in_specs=[SMEM] * scalars + [VMEM]...]
    ppermute x8 -> x30, starting transfers between devices: 19.9 us -> 38.8 us  [the longest x4 9.85 us: shards(): ring_g.append(lax.ppermute(chunk, 'tok', down))]
    mul x3 -> x5, other arithmetic: 4.49 us -> 0.42 us  [the longest x4 0.34 us: shards(): total(act_parts, base, base + size) * scale_a * (total(parts, 0, size) *...]
    unnamed x2 -> x20, local copies, waits for them, and re-layouts: 1.72 us -> 5.61 us
  transfers between devices with their start and end apart: 10 -> 30, of which waited for: 7 -> 18; matrix products, arithmetic and copies ran while one was open for 6% -> 0% of each run, Pallas kernels for 0% -> 8%
where the time goes in v2:
time: 175 us
  waiting for transfers between devices  109 us (62%)
  starting transfers between devices  38.8 us (22%)
  Pallas kernels  20.4 us (12%)
  local copies, waits for them, and re-layouts  5.76 us (3%)
    ppermute x6, waiting for transfers between devices, wid_total(): lax.ppermute(keep[1] + arrived[1], 'wid', [(w, w ^ 2) for w in range(WID)])  40.5 us
    ppermute x4, waiting for transfers between devices, shards(): other_g.append(lax.ppermute(chunk, 'tok', swap))  37.5 us
    pallas_call x8, Pallas kernels, call(): pl.pallas_call(kernel, out_shape=outs, in_specs=[SMEM] * scalars + [VMEM]...  20.4 us
    ppermute x1, waiting for transfers between devices, shards(): ring_a = lax.ppermute(acts, 'tok', down)  13.7 us
    ppermute x4, starting transfers between devices, shards(): ring_g.append(lax.ppermute(chunk, 'tok', down))  9.85 us
    ppermute x4, waiting for transfers between devices, shards(): from_ring.append(lax.ppermute(tile[:n_ring], 'tok', up))  8.28 us
    ppermute x6, starting transfers between devices, wid_total(): lax.ppermute(keep[1] + arrived[1], 'wid', [(w, w ^ 2) for w in range(WID)])  7.3 us
    ppermute x4, waiting for transfers between devices, shards(): ring_g.append(lax.ppermute(chunk, 'tok', down))  6.84 us
  transfers between devices with their start and end apart: 30, of which 18 were waited for; matrix products, arithmetic and copies ran while one was open for 0% of the time, Pallas kernels for 8%

profile of v2, /device:TPU:0, one launch (start us, length us, event | category | flops | bytes accessed | tf_op | source)
XLA Modules:
  0.0 174.9 jit_solution(11945306510586475440)
XLA Ops:
  0.0 5.0 %collective-permute-start.2 = (bf16[512,1024]{1,0:T(8,128)(2,1)}, bf16[512,1024]{1,0:T(8,128)(2,1)}, u32[]{:S(2)}, u32[]{:S(2)}) collective-permute-start(bf16[512,1024]{1,0:T(8,128)(2,1)} %refs_1_.2), channel_id=1, source_target_pairs={{0,24},{4,28},{8,0},{12,4},{16,8},{20,12},{24,16},{28,20},{1,25},{... | collective-permute-start | bytes 3145736 | tf_op jit(solution)/shard_map/ppermute | solution.py:209
  8.3 3.1 %shard_map.38 = (bf16[2752,128]{1,0:T(8,128)(2,1)S(1)}, bf16[2752,128]{1,0:T(8,128)(2,1)S(1)}, bf16[2752,128]{1,0:T(8,128)(2,1)S(1)}, bf16[2752,128]{1,0:T(8,128)(2,1)S(1)}) custom-call(bf16[2752,512]{1,0:T(8,128)(2,1)S(1)} %bitcast.75), custom_call_target="tpu_custom_call" | custom-call | tf_op jit(solution)/shard_map/pallas_call | solution.py:19
  14.1 13.7 %collective-permute-done.2.refs_2_ = bf16[512,1024]{1,0:T(8,128)(2,1)} collective-permute-done((bf16[512,1024]{1,0:T(8,128)(2,1)}, bf16[512,1024]{1,0:T(8,128)(2,1)}, u32[]{:S(2)}, u32[]{:S(2)}) %collective-permute-start.2) | collective-permute-done | bytes 1048608 | tf_op jit(solution)/shard_map/ppermute | solution.py:209
  27.8 2.2 %collective-permute-done.3.refs_3_ = bf16[512,1024]{1,0:T(8,128)(2,1)} collective-permute-done((bf16[512,1024]{1,0:T(8,128)(2,1)}, bf16[512,1024]{1,0:T(8,128)(2,1)}, u32[]{:S(2)}, u32[]{:S(2)}) %collective-permute-start.3) | collective-permute-done | bytes 1048608 | tf_op jit(solution)/shard_map/ppermute | solution.py:210
  31.2 4.6 %shard_map.39 = (f32[2,2048,128]{2,1,0:T(8,128)S(1)}, f32[2,2048,128]{2,1,0:T(8,128)S(1)}) custom-call(s32[5]{0:T(128)S(1)} %stack.23.place_ref.refs_0_, bf16[512,1024]{1,0:T(8,128)(2,1)S(1)} %copy-done.4, bf16[512,1024]{1,0:T(8,128)(2,1)} %collective-permute-done.2.refs_2_, bf16[512,1024]{1,0:T(8,128)(2,1)} %collective-permute-done.3.refs_3_), custom_call_target="tpu_custom_call" | custom-call | tf_op jit(solution)/shard_map/pallas_call | solution.py:19
  37.4 2.1 %collective-permute-start.6 = (bf16[2752,128]{1,0:T(8,128)(2,1)S(1)}, bf16[2752,128]{1,0:T(8,128)(2,1)S(1)}, u32[]{:S(2)}, u32[]{:S(2)}) collective-permute-start(bf16[2752,128]{1,0:T(8,128)(2,1)S(1)} %get-tuple-element.37.refs_2_), channel_id=1, source_target_pairs={{0,24},{4,28},{8,0},{12,4},{16,8},{20,12},{24,16},{28,20},{1,25},{... | collective-permute-start | bytes 2113544 | tf_op jit(solution)/shard_map/ppermute | solution.py:220
  40.1 14.5 %collective-permute-done.7.refs_4_.refs_6_.refs_8_.refs_10_ = bf16[2752,128]{1,0:T(8,128)(2,1)S(1)} collective-permute-done((bf16[2752,128]{1,0:T(8,128)(2,1)S(1)}, bf16[2752,128]{1,0:T(8,128)(2,1)S(1)}, u32[]{:S(2)}, u32[]{:S(2)}) %collective-permute-start.7) | collective-permute-done | bytes 704544 | tf_op jit(solution)/shard_map/ppermute | solution.py:221
  56.6 3.9 %collective-permute-start.14 = (bf16[2752,128]{1,0:T(8,128)(2,1)}, bf16[2752,128]{1,0:T(8,128)(2,1)S(1)}, u32[]{:S(2)}, u32[]{:S(2)}) collective-permute-start(bf16[2752,128]{1,0:T(8,128)(2,1)} %copy-done.5), channel_id=1, source_target_pairs={{0,24},{4,28},{8,0},{12,4},{16,8},{20,12},{24,16},{28,20},{1,25},{... | collective-permute-start | bytes 2113544 | tf_op jit(solution)/shard_map/ppermute | solution.py:220
  60.5 2.9 %shard_map.37 = (f32[2,1024,128]{2,1,0:T(8,128)S(1)}, f32[2,1024,128]{2,1,0:T(8,128)S(1)}) custom-call(s32[5]{0:T(128)S(1)} %stack.23.place_ref.refs_0_, bf16[512,1024]{1,0:T(8,128)(2,1)S(1)} %copy-done.4, bf16[2752,512]{1,0:T(8,128)(2,1)S(1)} %bitcast.76), custom_call_target="tpu_custom_call" | custom-call | tf_op jit(solution)/shard_map/pallas_call | solution.py:19
  63.4 6.2 %collective-permute-done.11.refs_7_.refs_9_.refs_11_ = bf16[2752,128]{1,0:T(8,128)(2,1)S(1)} collective-permute-done((bf16[2752,128]{1,0:T(8,128)(2,1)}, bf16[2752,128]{1,0:T(8,128)(2,1)S(1)}, u32[]{:S(2)}, u32[]{:S(2)}) %collective-permute-start.11) | collective-permute-done | bytes 704544 | tf_op jit(solution)/shard_map/ppermute | solution.py:221
  75.0 9.7 %collective-permute-done.15.refs_10_.refs_12_ = bf16[2752,128]{1,0:T(8,128)(2,1)S(1)} collective-permute-done((bf16[2752,128]{1,0:T(8,128)(2,1)}, bf16[2752,128]{1,0:T(8,128)(2,1)S(1)}, u32[]{:S(2)}, u32[]{:S(2)}) %collective-permute-start.15) | collective-permute-done | bytes 704544 | tf_op jit(solution)/shard_map/ppermute | solution.py:221
  85.5 3.9 %collective-permute-start.18 = (bf16[2752,128]{1,0:T(8,128)(2,1)S(1)}, bf16[2752,128]{1,0:T(8,128)(2,1)S(1)}, u32[]{:S(2)}, u32[]{:S(2)}) collective-permute-start(bf16[2752,128]{1,0:T(8,128)(2,1)S(1)} %copy-done.8), channel_id=1, source_target_pairs={{0,24},{4,28},{8,0},{12,4},{16,8},{20,12},{24,16},{28,20},{1,25},{... | collective-permute-start | bytes 2113544 | tf_op jit(solution)/shard_map/ppermute | solution.py:220
  89.4 2.1 %shard_map.42 = (f32[2,576,128]{2,1,0:T(8,128)S(1)}, f32[2,576,128]{2,1,0:T(8,128)S(1)}) custom-call(s32[5]{0:T(128)S(1)} %stack.23.place_ref.refs_0_, bf16[2752,512]{1,0:T(8,128)(2,1)S(1)} %bitcast.79, bf16[2752,128]{1,0:T(8,128)(2,1)S(1)} %get-tuple-element.37.refs_2_, bf16[2752,128]{1,0:T(8,128)(2,1)S(1)} %copy-done.3, bf16[2752,128]{1,0:T(8,128)(2,1)S(1)} %copy-done.6, ...), custom_call_target="tpu_custom_call" | custom-call | tf_op jit(solution)/shard_map/pallas_call | solution.py:19
  92.3 7.1 %collective-permute-done.19.refs_13_ = bf16[2752,128]{1,0:T(8,128)(2,1)S(1)} collective-permute-done((bf16[2752,128]{1,0:T(8,128)(2,1)S(1)}, bf16[2752,128]{1,0:T(8,128)(2,1)S(1)}, u32[]{:S(2)}, u32[]{:S(2)}) %collective-permute-start.19) | collective-permute-done | bytes 704544 | tf_op jit(solution)/shard_map/ppermute | solution.py:221
  100.9 3.0 %collective-permute-done.18.refs_9_ = bf16[2752,128]{1,0:T(8,128)(2,1)S(1)} collective-permute-done((bf16[2752,128]{1,0:T(8,128)(2,1)S(1)}, bf16[2752,128]{1,0:T(8,128)(2,1)S(1)}, u32[]{:S(2)}, u32[]{:S(2)}) %collective-permute-start.18) | collective-permute-done | bytes 704544 | tf_op jit(solution)/shard_map/ppermute | solution.py:220
  105.4 2.4 %shard_map.43 = (f32[2,704,128]{2,1,0:T(8,128)S(1)}, f32[2,704,128]{2,1,0:T(8,128)S(1)}) custom-call(s32[5]{0:T(128)S(1)} %stack.23.place_ref.refs_0_, bf16[2752,512]{1,0:T(8,128)(2,1)S(1)} %bitcast.80, bf16[2752,128]{1,0:T(8,128)(2,1)S(1)} %get-tuple-element.37.refs_2_, bf16[2752,128]{1,0:T(8,128)(2,1)S(1)} %copy-done.3, bf16[2752,128]{1,0:T(8,128)(2,1)S(1)} %copy-done.6, ...), custom_call_target="tpu_custom_call" | custom-call | tf_op jit(solution)/shard_map/pallas_call | solution.py:19
  110.9 18.1 %collective-permute-done.9 = f32[320,128]{1,0:T(8,128)S(1)} collective-permute-done((f32[320,128]{1,0:T(8,128)S(1)}, f32[320,128]{1,0:T(8,128)S(1)}, u32[]{:S(2)}, u32[]{:S(2)}) %collective-permute-start.9) | collective-permute-done | bytes 163872 | tf_op jit(solution)/shard_map/ppermute | solution.py:200
  132.1 13.0 %collective-permute-done.13 = f32[448,128]{1,0:T(8,128)S(1)} collective-permute-done((f32[448,128]{1,0:T(8,128)S(1)}, f32[448,128]{1,0:T(8,128)S(1)}, u32[]{:S(2)}, u32[]{:S(2)}) %collective-permute-start.13) | collective-permute-done | bytes 229408 | tf_op jit(solution)/shard_map/ppermute | solution.py:200
  146.8 4.7 %collective-permute-done.17 = f32[576,128]{1,0:T(8,128)S(1)} collective-permute-done((f32[576,128]{1,0:T(8,128)S(1)}, f32[576,128]{1,0:T(8,128)S(1)}, u32[]{:S(2)}, u32[]{:S(2)}) %collective-permute-start.17) | collective-permute-done | bytes 294944 | tf_op jit(solution)/shard_map/ppermute | solution.py:200
  153.1 4.7 %collective-permute-done.21 = f32[704,128]{1,0:T(8,128)S(1)} collective-permute-done((f32[704,128]{1,0:T(8,128)S(1)}, f32[704,128]{1,0:T(8,128)S(1)}, u32[]{:S(2)}, u32[]{:S(2)}) %collective-permute-start.21) | collective-permute-done | bytes 360480 | tf_op jit(solution)/shard_map/ppermute | solution.py:200
  159.7 3.1 %collective-permute-start.24 = (f32[288,128]{1,0:T(8,128)S(1)}, f32[288,128]{1,0:T(8,128)S(1)}, u32[]{:S(2)}, u32[]{:S(2)}) collective-permute-start(f32[288,128]{1,0:T(8,128)S(1)} %slice.236), channel_id=1, source_target_pairs={{0,8},{4,12},{8,16},{12,20},{16,24},{20,28},{24,0},{28,4},{1,9},{5... | collective-permute-start | bytes 442376 | tf_op jit(solution)/shard_map/ppermute | solution.py:244
  165.2 2.5 %collective-permute-done.23.refs_8_ = f32[224,128]{1,0:T(8,128)S(1)} collective-permute-done((f32[224,128]{1,0:T(8,128)S(1)}, f32[224,128]{1,0:T(8,128)S(1)}, u32[]{:S(2)}, u32[]{:S(2)}) %collective-permute-start.23) | collective-permute-done | bytes 114720 | tf_op jit(solution)/shard_map/ppermute | solution.py:244
  167.7 3.2 %collective-permute-done.24.refs_9_ = f32[288,128]{1,0:T(8,128)S(1)} collective-permute-done((f32[288,128]{1,0:T(8,128)S(1)}, f32[288,128]{1,0:T(8,128)S(1)}, u32[]{:S(2)}, u32[]{:S(2)}) %collective-permute-start.24) | collective-permute-done | bytes 147488 | tf_op jit(solution)/shard_map/ppermute | solution.py:244
  170.8 2.1 %collective-permute-done.25.refs_10_ = f32[352,128]{1,0:T(8,128)S(1)} collective-permute-done((f32[352,128]{1,0:T(8,128)S(1)}, f32[352,128]{1,0:T(8,128)S(1)}, u32[]{:S(2)}, u32[]{:S(2)}) %collective-permute-start.25) | collective-permute-done | bytes 180256 | tf_op jit(solution)/shard_map/ppermute | solution.py:244
  (84 shorter events, 37.0 us)
Async XLA Ops:
  0.0 27.8 %collective-permute-start.2 = (bf16[512,1024]{1,0:T(8,128)(2,1)}, bf16[512,1024]{1,0:T(8,128)(2,1)}, u32[]{:S(2)}, u32[]{:S(2)}) collective-permute-start(bf16[512,1024]{1,0:T(8,128)(2,1)} %refs_1_.2), channel_id=1, source_target_pairs={{0,24},{4,28},{8,0},{12,4},{16,8},{20,12},{24,16},{28,20},{1,25},{... | collective-permute-start | bytes 3145736 | tf_op jit(solution)/shard_map/ppermute | solution.py:209
  5.0 24.9 %collective-permute-start.3 = (bf16[512,1024]{1,0:T(8,128)(2,1)}, bf16[512,1024]{1,0:T(8,128)(2,1)}, u32[]{:S(2)}, u32[]{:S(2)}) collective-permute-start(bf16[512,1024]{1,0:T(8,128)(2,1)} %refs_1_.2), channel_id=1, source_target_pairs={{0,4},{4,0},{8,12},{12,8},{16,20},{20,16},{24,28},{28,24},{1,5},{5... | collective-permute-start | bytes 3145736 | tf_op jit(solution)/shard_map/ppermute | solution.py:210
  35.8 55.7 %collective-permute-start.4 = (f32[2,2048,128]{2,1,0:T(8,128)S(1)}, f32[2,2048,128]{2,1,0:T(8,128)S(1)}, u32[]{:S(2)}, u32[]{:S(2)}) collective-permute-start(f32[2,2048,128]{2,1,0:T(8,128)S(1)} %get-tuple-element.36), channel_id=1, source_target_pairs={{0,1},{1,0},{2,3},{3,2},{4,5},{5,4},{6,7},{7,6},{8,9},{9,8},{10,11... | collective-permute-start | bytes 6291464 | tf_op jit(solution)/shard_map/ppermute | solution.py:199
  35.9 18.7 %collective-permute-start.7 = (bf16[2752,128]{1,0:T(8,128)(2,1)S(1)}, bf16[2752,128]{1,0:T(8,128)(2,1)S(1)}, u32[]{:S(2)}, u32[]{:S(2)}) collective-permute-start(bf16[2752,128]{1,0:T(8,128)(2,1)S(1)} %get-tuple-element.37.refs_2_), channel_id=1, source_target_pairs={{0,4},{4,0},{8,12},{12,8},{16,20},{20,16},{24,28},{28,24},{1,5},{5... | collective-permute-start | bytes 2113544 | tf_op jit(solution)/shard_map/ppermute | solution.py:221
  37.4 18.6 %collective-permute-start.6 = (bf16[2752,128]{1,0:T(8,128)(2,1)S(1)}, bf16[2752,128]{1,0:T(8,128)(2,1)S(1)}, u32[]{:S(2)}, u32[]{:S(2)}) collective-permute-start(bf16[2752,128]{1,0:T(8,128)(2,1)S(1)} %get-tuple-element.37.refs_2_), channel_id=1, source_target_pairs={{0,24},{4,28},{8,0},{12,4},{16,8},{20,12},{24,16},{28,20},{1,25},{... | collective-permute-start | bytes 2113544 | tf_op jit(solution)/shard_map/ppermute | solution.py:220
  39.5 30.1 %collective-permute-start.11 = (bf16[2752,128]{1,0:T(8,128)(2,1)}, bf16[2752,128]{1,0:T(8,128)(2,1)S(1)}, u32[]{:S(2)}, u32[]{:S(2)}) collective-permute-start(bf16[2752,128]{1,0:T(8,128)(2,1)} %copy-done.2), channel_id=1, source_target_pairs={{0,4},{4,0},{8,12},{12,8},{16,20},{20,16},{24,28},{28,24},{1,5},{5... | collective-permute-start | bytes 2113544 | tf_op jit(solution)/shard_map/ppermute | solution.py:221
  40.1 31.1 %collective-permute-start.10 = (bf16[2752,128]{1,0:T(8,128)(2,1)}, bf16[2752,128]{1,0:T(8,128)(2,1)S(1)}, u32[]{:S(2)}, u32[]{:S(2)}) collective-permute-start(bf16[2752,128]{1,0:T(8,128)(2,1)} %copy-done.2), channel_id=1, source_target_pairs={{0,24},{4,28},{8,0},{12,4},{16,8},{20,12},{24,16},{28,20},{1,25},{... | collective-permute-start | bytes 2113544 | tf_op jit(solution)/shard_map/ppermute | solution.py:220
  56.1 28.7 %collective-permute-start.15 = (bf16[2752,128]{1,0:T(8,128)(2,1)}, bf16[2752,128]{1,0:T(8,128)(2,1)S(1)}, u32[]{:S(2)}, u32[]{:S(2)}) collective-permute-start(bf16[2752,128]{1,0:T(8,128)(2,1)} %copy-done.5), channel_id=1, source_target_pairs={{0,4},{4,0},{8,12},{12,8},{16,20},{20,16},{24,28},{28,24},{1,5},{5... | collective-permute-start | bytes 2113544 | tf_op jit(solution)/shard_map/ppermute | solution.py:221
  56.6 28.9 %collective-permute-start.14 = (bf16[2752,128]{1,0:T(8,128)(2,1)}, bf16[2752,128]{1,0:T(8,128)(2,1)S(1)}, u32[]{:S(2)}, u32[]{:S(2)}) collective-permute-start(bf16[2752,128]{1,0:T(8,128)(2,1)} %copy-done.5), channel_id=1, source_target_pairs={{0,24},{4,28},{8,0},{12,4},{16,8},{20,12},{24,16},{28,20},{1,25},{... | collective-permute-start | bytes 2113544 | tf_op jit(solution)/shard_map/ppermute | solution.py:220
  69.6 38.2 %collective-permute-start = (f32[2,1024,128]{2,1,0:T(8,128)S(1)}, f32[2,1024,128]{2,1,0:T(8,128)S(1)}, u32[]{:S(2)}, u32[]{:S(2)}) collective-permute-start(f32[2,1024,128]{2,1,0:T(8,128)S(1)} %get-tuple-element.31), channel_id=1, source_target_pairs={{0,1},{1,0},{2,3},{3,2},{4,5},{5,4},{6,7},{7,6},{8,9},{9,8},{10,11... | collective-permute-start | bytes 3145736 | tf_op jit(solution)/shard_map/ppermute | solution.py:199
  71.2 28.2 %collective-permute-start.19 = (bf16[2752,128]{1,0:T(8,128)(2,1)S(1)}, bf16[2752,128]{1,0:T(8,128)(2,1)S(1)}, u32[]{:S(2)}, u32[]{:S(2)}) collective-permute-start(bf16[2752,128]{1,0:T(8,128)(2,1)S(1)} %copy-done.8), channel_id=1, source_target_pairs={{0,4},{4,0},{8,12},{12,8},{16,20},{20,16},{24,28},{28,24},{1,5},{5... | collective-permute-start | bytes 2113544 | tf_op jit(solution)/shard_map/ppermute | solution.py:221
  85.5 18.4 %collective-permute-start.18 = (bf16[2752,128]{1,0:T(8,128)(2,1)S(1)}, bf16[2752,128]{1,0:T(8,128)(2,1)S(1)}, u32[]{:S(2)}, u32[]{:S(2)}) collective-permute-start(bf16[2752,128]{1,0:T(8,128)(2,1)S(1)} %copy-done.8), channel_id=1, source_target_pairs={{0,24},{4,28},{8,0},{12,4},{16,8},{20,12},{24,16},{28,20},{1,25},{... | collective-permute-start | bytes 2113544 | tf_op jit(solution)/shard_map/ppermute | solution.py:220
  91.5 16.5 %collective-permute-start.12 = (f32[2,448,128]{2,1,0:T(8,128)S(1)}, f32[2,448,128]{2,1,0:T(8,128)S(1)}, u32[]{:S(2)}, u32[]{:S(2)}) collective-permute-start(f32[2,448,128]{2,1,0:T(8,128)S(1)} %get-tuple-element.48), channel_id=1, source_target_pairs={{0,1},{1,0},{2,3},{3,2},{4,5},{5,4},{6,7},{7,6},{8,9},{9,8},{10,11... | collective-permute-start | bytes 1376264 | tf_op jit(solution)/shard_map/ppermute | solution.py:199
  91.7 16.9 %collective-permute-start.16 = (f32[2,576,128]{2,1,0:T(8,128)S(1)}, f32[2,576,128]{2,1,0:T(8,128)S(1)}, u32[]{:S(2)}, u32[]{:S(2)}) collective-permute-start(f32[2,576,128]{2,1,0:T(8,128)S(1)} %get-tuple-element.51), channel_id=1, source_target_pairs={{0,1},{1,0},{2,3},{3,2},{4,5},{5,4},{6,7},{7,6},{8,9},{9,8},{10,11... | collective-permute-start | bytes 1769480 | tf_op jit(solution)/shard_map/ppermute | solution.py:199
  99.4 31.1 %collective-permute-start.5 = (f32[2048,128]{1,0:T(8,128)S(1)}, f32[2048,128]{1,0:T(8,128)S(1)}, u32[]{:S(2)}, u32[]{:S(2)}) collective-permute-start(f32[2048,128]{1,0:T(8,128)S(1)} %fusion), channel_id=1, source_target_pairs={{0,2},{1,3},{2,0},{3,1},{4,6},{5,7},{6,4},{7,5},{8,10},{9,11},{10,... | collective-permute-start | bytes 3145736 | tf_op jit(solution)/shard_map/ppermute | solution.py:200
  103.9 25.0 %collective-permute-start.9 = (f32[320,128]{1,0:T(8,128)S(1)}, f32[320,128]{1,0:T(8,128)S(1)}, u32[]{:S(2)}, u32[]{:S(2)}) collective-permute-start(f32[320,128]{1,0:T(8,128)S(1)} %fusion.28), channel_id=1, source_target_pairs={{0,2},{1,3},{2,0},{3,1},{4,6},{5,7},{6,4},{7,5},{8,10},{9,11},{10,... | collective-permute-start | bytes 491528 | tf_op jit(solution)/shard_map/ppermute | solution.py:200
  108.0 50.1 %collective-permute-start.1 = (f32[1024,128]{1,0:T(8,128)S(1)}, f32[1024,128]{1,0:T(8,128)S(1)}, u32[]{:S(2)}, u32[]{:S(2)}) collective-permute-start(f32[1024,128]{1,0:T(8,128)S(1)} %fusion.1), channel_id=1, source_target_pairs={{0,2},{1,3},{2,0},{3,1},{4,6},{5,7},{6,4},{7,5},{8,10},{9,11},{10,... | collective-permute-start | bytes 1572872 | tf_op jit(solution)/shard_map/ppermute | solution.py:200
  108.6 36.5 %collective-permute-start.13 = (f32[448,128]{1,0:T(8,128)S(1)}, f32[448,128]{1,0:T(8,128)S(1)}, u32[]{:S(2)}, u32[]{:S(2)}) collective-permute-start(f32[448,128]{1,0:T(8,128)S(1)} %fusion.21), channel_id=1, source_target_pairs={{0,2},{1,3},{2,0},{3,1},{4,6},{5,7},{6,4},{7,5},{8,10},{9,11},{10,... | collective-permute-start | bytes 688136 | tf_op jit(solution)/shard_map/ppermute | solution.py:200
  110.2 41.2 %collective-permute-start.17 = (f32[576,128]{1,0:T(8,128)S(1)}, f32[576,128]{1,0:T(8,128)S(1)}, u32[]{:S(2)}, u32[]{:S(2)}) collective-permute-start(f32[576,128]{1,0:T(8,128)S(1)} %fusion.9), channel_id=1, source_target_pairs={{0,2},{1,3},{2,0},{3,1},{4,6},{5,7},{6,4},{7,5},{8,10},{9,11},{10,... | collective-permute-start | bytes 884744 | tf_op jit(solution)/shard_map/ppermute | solution.py:200
  129.0 28.9 %collective-permute-start.21 = (f32[704,128]{1,0:T(8,128)S(1)}, f32[704,128]{1,0:T(8,128)S(1)}, u32[]{:S(2)}, u32[]{:S(2)}) collective-permute-start(f32[704,128]{1,0:T(8,128)S(1)} %fusion.2), channel_id=1, source_target_pairs={{0,2},{1,3},{2,0},{3,1},{4,6},{5,7},{6,4},{7,5},{8,10},{9,11},{10,... | collective-permute-start | bytes 1081352 | tf_op jit(solution)/shard_map/ppermute | solution.py:200
  130.6 29.1 %collective-permute-start.26 = (f32[32,128]{1,0:T(8,128)S(1)}, f32[32,128]{1,0:T(8,128)S(1)}, u32[]{:S(2)}, u32[]{:S(2)}) collective-permute-start(f32[32,128]{1,0:T(8,128)S(1)} %slice.238), channel_id=1, source_target_pairs={{0,4},{4,0},{8,12},{12,8},{16,20},{20,16},{24,28},{28,24},{1,5},{5... | collective-permute-start | bytes 49160 | tf_op jit(solution)/shard_map/ppermute | solution.py:245
  145.2 14.5 %collective-permute-start.27 = (f32[96,128]{1,0:T(8,128)S(1)}, f32[96,128]{1,0:T(8,128)S(1)}, u32[]{:S(2)}, u32[]{:S(2)}) collective-permute-start(f32[96,128]{1,0:T(8,128)S(1)} %slice.239), channel_id=1, source_target_pairs={{0,4},{4,0},{8,12},{12,8},{16,20},{20,16},{24,28},{28,24},{1,5},{5... | collective-permute-start | bytes 147464 | tf_op jit(solution)/shard_map/ppermute | solution.py:245
  151.5 11.3 %collective-permute-start.28 = (f32[160,128]{1,0:T(8,128)S(1)}, f32[160,128]{1,0:T(8,128)S(1)}, u32[]{:S(2)}, u32[]{:S(2)}) collective-permute-start(f32[160,128]{1,0:T(8,128)S(1)} %slice.240), channel_id=1, source_target_pairs={{0,4},{4,0},{8,12},{12,8},{16,20},{20,16},{24,28},{28,24},{1,5},{5... | collective-permute-start | bytes 245768 | tf_op jit(solution)/shard_map/ppermute | solution.py:245
  159.7 11.1 %collective-permute-start.24 = (f32[288,128]{1,0:T(8,128)S(1)}, f32[288,128]{1,0:T(8,128)S(1)}, u32[]{:S(2)}, u32[]{:S(2)}) collective-permute-start(f32[288,128]{1,0:T(8,128)S(1)} %slice.236), channel_id=1, source_target_pairs={{0,8},{4,12},{8,16},{12,20},{16,24},{20,28},{24,0},{28,4},{1,9},{5... | collective-permute-start | bytes 442376 | tf_op jit(solution)/shard_map/ppermute | solution.py:244
  (16 other events, 162.3 us)

commit v3 on v2

--- a/solution.py
+++ b/solution.py
@@ -195,54 +195,82 @@
     def floats(n):
         return (jax.ShapeDtypeStruct((2, n, UNIT), jnp.float32),) * 2
 
-    def wid_total(keep, send):
-        arrived = lax.ppermute(send, "wid", [(w, w ^ 1) for w in range(WID)])
-        across = lax.ppermute(keep[1] + arrived[1], "wid", [(w, w ^ 2) for w in range(WID)])
-        return keep[0], arrived[0], across
-
-    def total(parts, start, stop):
-        return parts[0][start:stop] + parts[1][start:stop] + parts[2][start:stop]
-
     scale_a = 1.0 / jnp.sqrt(jnp.float32(D))
     scale_g = 1.0 / jnp.sqrt(jnp.float32(FF))
+
+    def tie(*arrays):
+        return lax.optimization_barrier(arrays)
+
+    def over_core(send):
+        return lax.ppermute(send, "wid", [(w, w ^ 1) for w in range(WID)])
+
+    def over_side(keep, arrived):
+        return lax.ppermute(keep[1] + arrived[1], "wid", [(w, w ^ 2) for w in range(WID)])
 
     ring_a = lax.ppermute(acts, "tok", down)
     other_a = lax.ppermute(acts, "tok", swap)
     own_g = grads.T
-    mine = call(reorder_kernel, (jax.ShapeDtypeStruct((grads.shape[1], UNIT), jnp.bfloat16),) * units, own_g)
-    ring_g, other_g = [], []
-    for c in range(units):
-        chunk = mine[c]
-        if c == 1:
-            chunk, ring_a, other_a = lax.optimization_barrier((chunk, ring_a, other_a))
-        elif c > 1:
-            chunk, ring_g[c - 2], other_g[c - 2] = lax.optimization_barrier((chunk, ring_g[c - 2], other_g[c - 2]))
-        ring_g.append(lax.ppermute(chunk, "tok", down))
-        other_g.append(lax.ppermute(chunk, "tok", swap))
-
-    parts = wid_total(*call(self_kernel, floats(2 * WID * UNIT), place, acts, own_g, scalars=1))
+    mine = list(call(reorder_kernel, (jax.ShapeDtypeStruct((grads.shape[1], UNIT), jnp.bfloat16),) * units, own_g))
+    ring_g, other_g = [None] * units, [None] * units
+
+    def start(chunk, *held):
+        if held:
+            chunk, *held = tie(chunk, *held)
+        return lax.ppermute(chunk, "tok", down), lax.ppermute(chunk, "tok", swap), held
+
+    ring_g[0], other_g[0], _ = start(mine[0])
+    ring_g[1], other_g[1], (ring_a, other_a) = start(mine[1], ring_a, other_a)
+    ring_g[2], other_g[2], (ring_g[0], other_g[0]) = start(mine[2], ring_g[0], other_g[0])
+
+    alive = jnp.max(lengths) > 0
+
+    def exchange(kernel, n, *args):
+        def summed(*args):
+            keep, send = call(kernel, floats(n), *args, scalars=1)
+            arrived = over_core(send)
+            return keep[0] + arrived[0] + over_side(keep, arrived)
+
+        return lax.cond(alive, summed, lambda *args: jnp.zeros((n, UNIT), jnp.float32), *args)
+
+    self_sum = exchange(self_kernel, 2 * WID * UNIT, place, acts, own_g)
+
+    everything = sum(size for _, _, _, size in layouts)
+    act_sum = exchange(lambda *refs: acts_kernel(layouts, *refs), everything, place, acts, ring_a, other_a)
     half = WID * UNIT
-    self_tile = (total(parts, 0, half) * scale_a) * (total(parts, half, 2 * half) * scale_g)
-
-    everything = sum(size for _, _, _, size in layouts)
-    act_parts = wid_total(
-        *call(lambda *refs: acts_kernel(layouts, *refs), floats(everything), place, acts, ring_a, other_a, scalars=1)
-    )
-
-    local, from_ring, from_swap = [], [], []
+    self_tile = (self_sum[:half] * scale_a) * (self_sum[half:] * scale_g)
+
+    last = units - 1
+    cut = mine[last].shape[0] // 2
+    piece = [mine[last][:cut], mine[last][cut:]]
+    first_ring, first_other, (ring_g[1], other_g[1]) = start(piece[0], ring_g[1], other_g[1])
+    second_ring, second_other, (ring_g[2], other_g[2]) = start(piece[1], ring_g[2], other_g[2])
+    local = []
     base = 0
     for c, (spot, n_ring, n_swap, size) in enumerate(layouts):
-        parts = wid_total(
-            *call(
-                lambda *refs, c=c, spot=spot: grads_kernel(c, spot, *refs),
-                floats(size), place, own_g, *mine[: c + 1], *ring_g[: c + 1], *other_g[: c + 1], scalars=1,
-            )
+        if c == last:
+            ring_g[c] = jnp.concatenate([first_ring, second_ring], axis=0)
+            other_g[c] = jnp.concatenate([first_other, second_other], axis=0)
+        grad_sum = exchange(
+            lambda *refs, c=c, spot=spot: grads_kernel(c, spot, *refs),
+            size, place, own_g, *mine[: c + 1], *ring_g[: c + 1], *other_g[: c + 1],
         )
-        tile = (total(act_parts, base, base + size) * scale_a) * (total(parts, 0, size) * scale_g)
+        local.append((act_sum[base : base + size] * scale_a) * (grad_sum * scale_g))
         base += size
-        local.append(tile)
-        from_ring.append(lax.ppermute(tile[:n_ring], "tok", up))
-        from_swap.append(lax.ppermute(tile[n_ring:n_swap], "tok", swap))
+
+    def back(tiles, steps):
+        ring = jnp.concatenate([tiles[c][: layouts[c][1]] for c in steps], axis=0)
+        swapped = jnp.concatenate([tiles[c][layouts[c][1] : layouts[c][2]] for c in steps], axis=0)
+        return lax.ppermute(ring, "tok", up), lax.ppermute(swapped, "tok", swap)
+
+    early = back(local, range(units - 1))
+    late = back(local, [units - 1])
+
+    def apart(joined, widths):
+        ends = [sum(widths[:i]) for i in range(len(widths) + 1)]
+        return [joined[a:b] for a, b in zip(ends, ends[1:])]
+
+    from_ring = apart(early[0], [n for _, n, _, _ in layouts[:-1]]) + [late[0]]
+    from_swap = apart(early[1], [m - n for _, n, m, _ in layouts[:-1]]) + [late[1]]
 
     out = call(
         lambda *refs: final_kernel(layouts, *refs),

time: 175 us -> 174 us (level)
  waiting for transfers between devices: 109 us -> 87.5 us
  other arithmetic: 0.7 us -> 13.2 us
  Pallas kernels: 20.4 us -> 31.8 us
  starting transfers between devices: 38.8 us -> 29.8 us
  local copies, waits for them, and re-layouts: 5.76 us -> 9.39 us
    ppermute x1, waiting for transfers between devices: 13.7 us -> 0.01 us  [shards(): ring_a = lax.ppermute(acts, 'tok', down)]
    pallas_call x8, Pallas kernels: 20.4 us -> 31.8 us  [call(): pl.pallas_call(kernel, out_shape=outs, in_specs=[SMEM] * scalars + [VMEM]...]
    ppermute x28 -> x26, starting transfers between devices: 32.2 us -> 23.3 us  [the longest x6 9.51 us: over_side(): lax.ppermute(keep[1] + arrived[1], 'wid', [(w, w ^ 2) for w in range(WID)])]
    slice x8 -> x17, local copies, waits for them, and re-layouts: 0.07 us -> 7.21 us  [the longest x6 5.13 us: apart(): return [joined[a:b] for a, b in zip(ends, ends[1:])]]
    ppermute x28 -> x26, waiting for transfers between devices: 93.2 us -> 87.5 us  [the longest x6 63.4 us: over_side(): lax.ppermute(keep[1] + arrived[1], 'wid', [(w, w ^ 2) for w in range(WID)])]
    concatenate x0 -> x4, other arithmetic: none -> 5.43 us  [the longest x1 2.01 us: shards(): other_g[c] = jnp.concatenate([first_other, second_other], axis=0)]
    mul x5, other arithmetic: 0.42 us -> 5.38 us  [the longest x4 4.32 us: shards(): local.append(act_sum[base:base + size] * scale_a * (grad_sum * scale_g))]
    unnamed x20 -> x16, local copies, waits for them, and re-layouts: 5.61 us -> 2.1 us
  transfers between devices with their start and end apart: 30 -> 28, of which waited for: 18 -> 14; matrix products, arithmetic and copies ran while one was open for 0% -> 12% of each run, Pallas kernels for 8% -> 17%
where the time goes in v3:
time: 174 us; the launch traced here: 173 us
  waiting for transfers between devices  87.5 us (50%)
  Pallas kernels  31.8 us (18%)
  starting transfers between devices  29.8 us (17%)
  other arithmetic  13.2 us (8%)
  local copies, waits for them, and re-layouts  9.39 us (5%)
    ppermute x6, waiting for transfers between devices, over_side(): lax.ppermute(keep[1] + arrived[1], 'wid', [(w, w ^ 2) for w in range(WID)])  63.4 us
    pallas_call x8, Pallas kernels, call(): pl.pallas_call(kernel, out_shape=outs, in_specs=[SMEM] * scalars + [VMEM]...  31.8 us
    ppermute x6, waiting for transfers between devices, over_core(): return lax.ppermute(send, 'wid', [(w, w ^ 1) for w in range(WID)])  14.4 us
    ppermute x6, starting transfers between devices, over_side(): lax.ppermute(keep[1] + arrived[1], 'wid', [(w, w ^ 2) for w in range(WID)])  9.51 us
    ppermute x5, waiting for transfers between devices, start(): lax.ppermute(chunk, 'tok', down)  7.43 us
    ppermute x5, starting transfers between devices, start(): lax.ppermute(chunk, 'tok', down)  5.3 us
    slice x6, local copies, waits for them, and re-layouts, apart(): return [joined[a:b] for a, b in zip(ends, ends[1:])]  5.13 us
    ppermute x1, starting transfers between devices, shards(): ring_a = lax.ppermute(acts, 'tok', down)  5.05 us
  transfers between devices with their start and end apart: 28, of which 14 were waited for; matrix products, arithmetic and copies ran while one was open for 12% of the time, Pallas kernels for 17%

profile of v3, /device:TPU:0, one launch (start us, length us, event | category | flops | bytes accessed | tf_op | source)
XLA Modules:
  0.0 172.9 jit_solution(16303444807662099967)
XLA Ops:
  0.0 5.0 %collective-permute-start.12 = (bf16[512,1024]{1,0:T(8,128)(2,1)}, bf16[512,1024]{1,0:T(8,128)(2,1)}, u32[]{:S(2)}, u32[]{:S(2)}) collective-permute-start(bf16[512,1024]{1,0:T(8,128)(2,1)} %param.15), channel_id=1, source_target_pairs={{0,24},{4,28},{8,0},{12,4},{16,8},{20,12},{24,16},{28,20},{1,25},{... | collective-permute-start | bytes 3145736 | tf_op jit(solution)/shard_map/ppermute | solution.py:210
  6.5 6.0 %shard_map.37 = (bf16[2752,128]{1,0:T(8,128)(2,1)}, bf16[2752,128]{1,0:T(8,128)(2,1)}, bf16[2752,128]{1,0:T(8,128)(2,1)}, bf16[2752,128]{1,0:T(8,128)(2,1)}) custom-call(bf16[2752,512]{1,0:T(8,128)(2,1)} %bitcast.43), custom_call_target="tpu_custom_call" | custom-call | tf_op jit(solution)/shard_map/pallas_call | solution.py:19
  15.0 20.5 %conditional.6 = (f32[1024,128]{1,0:T(8,128)S(1)}) conditional(s32[]{:T(128)} %convert_element_type.2, () %tuple.45, (s32[5]{0:T(128)S(1)}, bf16[512,1024]{1,0:T(8,128)(2,1)}, bf16[2752,512]{1,0:T(8,128)(2,1)S(1)}) %tuple.74), branch_computations={%region_1.2_spmd, %region_2.3_spmd} | conditional | flops 393216 | bytes 9961560 | solution.py:233
  15.0 3.6 %branch_1_fun.6 = (f32[2,1024,128]{2,1,0:T(8,128)S(1)}, f32[2,1024,128]{2,1,0:T(8,128)S(1)}) custom-call(s32[5]{0:T(128)S(1)} %get-tuple-element.96.place_ref, bf16[512,1024]{1,0:T(8,128)(2,1)} %get-tuple-element.97.a_ref, bf16[2752,512]{1,0:T(8,128)(2,1)S(1)} %get-tuple-element.98.g_ref), custom_call_target="tpu_custom_call" | custom-call | tf_op jit(solution)/shard_map/cond/branch_1_fun/pallas_call | solution.py:19
  18.6 2.6 %collective-permute-done = f32[2,1024,128]{2,1,0:T(8,128)S(1)} collective-permute-done((f32[2,1024,128]{2,1,0:T(8,128)S(1)}, f32[2,1024,128]{2,1,0:T(8,128)S(1)}, u32[]{:S(2)}, u32[]{:S(2)}) %collective-permute-start) | collective-permute-done | bytes 1048608 | tf_op jit(solution)/shard_map/cond/branch_1_fun/ppermute | solution.py:205
  22.9 12.4 %collective-permute-done.1 = f32[1024,128]{1,0:T(8,128)S(1)} collective-permute-done((f32[1024,128]{1,0:T(8,128)S(1)}, f32[1024,128]{1,0:T(8,128)S(1)}, u32[]{:S(2)}, u32[]{:S(2)}) %collective-permute-start.1) | collective-permute-done | bytes 524320 | tf_op jit(solution)/shard_map/cond/branch_1_fun/ppermute | solution.py:208
  35.5 7.4 %collective-permute-done.14 = bf16[2752,128]{1,0:T(8,128)(2,1)} collective-permute-done((bf16[2752,128]{1,0:T(8,128)(2,1)}, bf16[2752,128]{1,0:T(8,128)(2,1)}, u32[]{:S(2)}, u32[]{:S(2)}) %collective-permute-start.14) | collective-permute-done | bytes 704544 | tf_op jit(solution)/shard_map/ppermute | solution.py:219
  51.3 10.5 %conditional.8 = (f32[320,128]{1,0:T(8,128)S(1)}) conditional(s32[]{:T(128)} %convert_element_type.2, () %tuple.50, (s32[5]{0:T(128)S(1)}, bf16[2752,512]{1,0:T(8,128)(2,1)S(1)}, bf16[2752,128]{1,0:T(8,128)(2,1)}, bf16[2752,128]{1,0:T(8,128)(2,1)}, bf16[2752,128]{1,0:T(8,128)(2,1)}) %tuple.75), branch_computations={%region_5.6_spmd, %region_6.7_spmd} | conditional | flops 122880 | bytes 3113048 | solution.py:233
  51.3 2.4 %branch_1_fun.8 = (f32[2,320,128]{2,1,0:T(8,128)S(1)}, f32[2,320,128]{2,1,0:T(8,128)S(1)}) custom-call(s32[5]{0:T(128)S(1)} %get-tuple-element.124.refs_0_, bf16[2752,512]{1,0:T(8,128)(2,1)S(1)} %get-tuple-element.125.refs_1_, bf16[2752,128]{1,0:T(8,128)(2,1)} %get-tuple-element.126.refs_2_, bf16[2752,128]{1,0:T(8,128)(2,1)} %get-tuple-element.127.refs_3_, ...), custom_call_target="tpu_custom_call" | custom-call | tf_op jit(solution)/shard_map/cond/branch_1_fun/pallas_call | solution.py:19
  57.0 4.7 %collective-permute-done.5 = f32[320,128]{1,0:T(8,128)S(1)} collective-permute-done((f32[320,128]{1,0:T(8,128)S(1)}, f32[320,128]{1,0:T(8,128)S(1)}, u32[]{:S(2)}, u32[]{:S(2)}) %collective-permute-start.5) | collective-permute-done | bytes 163872 | tf_op jit(solution)/shard_map/cond/branch_1_fun/ppermute | solution.py:208
  62.5 35.6 %conditional.7 = (f32[2048,128]{1,0:T(8,128)}) conditional(s32[]{:T(128)} %convert_element_type.2, () %tuple.47, (s32[5]{0:T(128)S(1)}, bf16[512,1024]{1,0:T(8,128)(2,1)}, bf16[512,1024]{1,0:T(8,128)(2,1)}, bf16[512,1024]{1,0:T(8,128)(2,1)}) %tuple.49), branch_computations={%region_3.4_spmd, %region_4.5_spmd} | conditional | flops 786432 | bytes 19923032 | solution.py:233
  62.5 4.9 %branch_1_fun.7 = (f32[2,2048,128]{2,1,0:T(8,128)S(1)}, f32[2,2048,128]{2,1,0:T(8,128)S(1)}) custom-call(s32[5]{0:T(128)S(1)} %get-tuple-element.118.refs_0_, bf16[512,1024]{1,0:T(8,128)(2,1)} %get-tuple-element.119.refs_1_, bf16[512,1024]{1,0:T(8,128)(2,1)} %get-tuple-element.120.refs_2_, bf16[512,1024]{1,0:T(8,128)(2,1)} %get-tuple-element.121.refs_3_), custom_call_target="tpu_custom_call" | custom-call | tf_op jit(solution)/shard_map/cond/branch_1_fun/pallas_call | solution.py:19
  67.4 4.1 %collective-permute-done.2 = f32[2,2048,128]{2,1,0:T(8,128)S(1)} collective-permute-done((f32[2,2048,128]{2,1,0:T(8,128)S(1)}, f32[2,2048,128]{2,1,0:T(8,128)S(1)}, u32[]{:S(2)}, u32[]{:S(2)}) %collective-permute-start.2) | collective-permute-done | bytes 2097184 | tf_op jit(solution)/shard_map/cond/branch_1_fun/ppermute | solution.py:205
  73.3 23.7 %collective-permute-done.3 = f32[2048,128]{1,0:T(8,128)S(1)} collective-permute-done((f32[2048,128]{1,0:T(8,128)S(1)}, f32[2048,128]{1,0:T(8,128)S(1)}, u32[]{:S(2)}, u32[]{:S(2)}) %collective-permute-start.3) | collective-permute-done | bytes 1048608 | tf_op jit(solution)/shard_map/cond/branch_1_fun/ppermute | solution.py:208
  100.8 2.7 %collective-permute-start.20 = (bf16[1376,128]{1,0:T(8,128)(2,1)}, bf16[1376,128]{1,0:T(8,128)(2,1)}, u32[]{:S(2)}, u32[]{:S(2)}) collective-permute-start(bf16[1376,128]{1,0:T(8,128)(2,1)} %get-tuple-element.200), channel_id=1, source_target_pairs={{0,24},{4,28},{8,0},{12,4},{16,8},{20,12},{24,16},{28,20},{1,25},{... | collective-permute-start | bytes 1056776 | tf_op jit(solution)/shard_map/ppermute | solution.py:219
  104.0 15.6 %conditional.10 = (f32[576,128]{1,0:T(8,128)S(1)}) conditional(s32[]{:T(128)} %convert_element_type.2, () %tuple.56, (s32[5]{0:T(128)S(1)}, bf16[2752,512]{1,0:T(8,128)(2,1)S(1)}, bf16[2752,128]{1,0:T(8,128)(2,1)}, bf16[2752,128]{1,0:T(8,128)(2,1)}, bf16[2752,128]{1,0:T(8,128)(2,1)}, /*index=5*/bf16[2752,128]{1,0:T(8,128)(2,1)}, ...), branch_computations={%region_9.10_spmd, %region_10.11_spmd} | conditional | flops 221184 | bytes 5603416 | solution.py:233
  104.0 4.3 %branch_1_fun.10 = (f32[2,576,128]{2,1,0:T(8,128)S(1)}, f32[2,576,128]{2,1,0:T(8,128)S(1)}) custom-call(s32[5]{0:T(128)S(1)} %get-tuple-element.141.refs_0_, bf16[2752,512]{1,0:T(8,128)(2,1)S(1)} %get-tuple-element.142.refs_1_, bf16[2752,128]{1,0:T(8,128)(2,1)} %get-tuple-element.143.refs_2_, bf16[2752,128]{1,0:T(8,128)(2,1)} %get-tuple-element.144.refs_3_, ...), custom_call_target="tpu_custom_call" | custom-call | tf_op jit(solution)/shard_map/cond/branch_1_fun/pallas_call | solution.py:19
  112.0 7.5 %collective-permute-done.9 = f32[576,128]{1,0:T(8,128)S(1)} collective-permute-done((f32[576,128]{1,0:T(8,128)S(1)}, f32[576,128]{1,0:T(8,128)S(1)}, u32[]{:S(2)}, u32[]{:S(2)}) %collective-permute-start.9) | collective-permute-done | bytes 294944 | tf_op jit(solution)/shard_map/cond/branch_1_fun/ppermute | solution.py:208
  121.4 13.3 %conditional.9 = (f32[448,128]{1,0:T(8,128)S(1)}) conditional(s32[]{:T(128)} %convert_element_type.2, () %tuple.53, (s32[5]{0:T(128)S(1)}, bf16[2752,512]{1,0:T(8,128)(2,1)S(1)}, bf16[2752,128]{1,0:T(8,128)(2,1)}, bf16[2752,128]{1,0:T(8,128)(2,1)}, bf16[2752,128]{1,0:T(8,128)(2,1)}, /*index=5*/bf16[2752,128]{1,0:T(8,128)(2,1)}, ...), branch_computations={%region_7.8_spmd, %region_8.9_spmd} | conditional | flops 172032 | bytes 4358232 | solution.py:233
  121.6 3.4 %branch_1_fun.9 = (f32[2,448,128]{2,1,0:T(8,128)S(1)}, f32[2,448,128]{2,1,0:T(8,128)S(1)}) custom-call(s32[5]{0:T(128)S(1)} %get-tuple-element.131.refs_0_, bf16[2752,512]{1,0:T(8,128)(2,1)S(1)} %get-tuple-element.132.refs_1_, bf16[2752,128]{1,0:T(8,128)(2,1)} %get-tuple-element.133.refs_2_, bf16[2752,128]{1,0:T(8,128)(2,1)} %get-tuple-element.134.refs_3_, ...), custom_call_target="tpu_custom_call" | custom-call | tf_op jit(solution)/shard_map/cond/branch_1_fun/pallas_call | solution.py:19
  128.5 6.1 %collective-permute-done.7 = f32[448,128]{1,0:T(8,128)S(1)} collective-permute-done((f32[448,128]{1,0:T(8,128)S(1)}, f32[448,128]{1,0:T(8,128)S(1)}, u32[]{:S(2)}, u32[]{:S(2)}) %collective-permute-start.7) | collective-permute-done | bytes 229408 | tf_op jit(solution)/shard_map/cond/branch_1_fun/ppermute | solution.py:208
  143.5 18.1 %conditional.11 = (f32[704,128]{1,0:T(8,128)S(1)}) conditional(s32[]{:T(128)} %convert_element_type.2, () %tuple.59, (s32[5]{0:T(128)S(1)}, bf16[2752,512]{1,0:T(8,128)(2,1)S(1)}, bf16[2752,128]{1,0:T(8,128)(2,1)}, bf16[2752,128]{1,0:T(8,128)(2,1)}, bf16[2752,128]{1,0:T(8,128)(2,1)}, /*index=5*/bf16[2752,128]{1,0:T(8,128)(2,1)}, ...), branch_computations={%region_11.12_spmd, %region_12.13_spmd} | conditional | flops 270336 | bytes 6848600 | solution.py:233
  143.5 5.2 %branch_1_fun.11 = (f32[2,704,128]{2,1,0:T(8,128)S(1)}, f32[2,704,128]{2,1,0:T(8,128)S(1)}) custom-call(s32[5]{0:T(128)S(1)} %get-tuple-element.154.refs_0_, bf16[2752,512]{1,0:T(8,128)(2,1)S(1)} %get-tuple-element.155.refs_1_, bf16[2752,128]{1,0:T(8,128)(2,1)} %get-tuple-element.156.refs_2_, bf16[2752,128]{1,0:T(8,128)(2,1)} %get-tuple-element.157.refs_3_, ...), custom_call_target="tpu_custom_call" | custom-call | tf_op jit(solution)/shard_map/cond/branch_1_fun/pallas_call | solution.py:19
  152.6 8.9 %collective-permute-done.11 = f32[704,128]{1,0:T(8,128)S(1)} collective-permute-done((f32[704,128]{1,0:T(8,128)S(1)}, f32[704,128]{1,0:T(8,128)S(1)}, u32[]{:S(2)}, u32[]{:S(2)}) %collective-permute-start.11) | collective-permute-done | bytes 360480 | tf_op jit(solution)/shard_map/cond/branch_1_fun/ppermute | solution.py:208
  (102 shorter events, 56.5 us)
Async XLA Ops:
  0.0 48.7 %collective-permute-start.12 = (bf16[512,1024]{1,0:T(8,128)(2,1)}, bf16[512,1024]{1,0:T(8,128)(2,1)}, u32[]{:S(2)}, u32[]{:S(2)}) collective-permute-start(bf16[512,1024]{1,0:T(8,128)(2,1)} %param.15), channel_id=1, source_target_pairs={{0,24},{4,28},{8,0},{12,4},{16,8},{20,12},{24,16},{28,20},{1,25},{... | collective-permute-start | bytes 3145736 | tf_op jit(solution)/shard_map/ppermute | solution.py:210
  5.1 43.6 %collective-permute-start.13 = (bf16[512,1024]{1,0:T(8,128)(2,1)}, bf16[512,1024]{1,0:T(8,128)(2,1)}, u32[]{:S(2)}, u32[]{:S(2)}) collective-permute-start(bf16[512,1024]{1,0:T(8,128)(2,1)} %param.15), channel_id=1, source_target_pairs={{0,4},{4,0},{8,12},{12,8},{16,20},{20,16},{24,28},{28,24},{1,5},{5... | collective-permute-start | bytes 3145736 | tf_op jit(solution)/shard_map/ppermute | solution.py:211
  12.6 30.3 %collective-permute-start.14 = (bf16[2752,128]{1,0:T(8,128)(2,1)}, bf16[2752,128]{1,0:T(8,128)(2,1)}, u32[]{:S(2)}, u32[]{:S(2)}) collective-permute-start(bf16[2752,128]{1,0:T(8,128)(2,1)} %get-tuple-element.189), channel_id=1, source_target_pairs={{0,24},{4,28},{8,0},{12,4},{16,8},{20,12},{24,16},{28,20},{1,25},{... | collective-permute-start | bytes 2113544 | tf_op jit(solution)/shard_map/ppermute | solution.py:219
  13.0 32.1 %collective-permute-start.15 = (bf16[2752,128]{1,0:T(8,128)(2,1)}, bf16[2752,128]{1,0:T(8,128)(2,1)}, u32[]{:S(2)}, u32[]{:S(2)}) collective-permute-start(bf16[2752,128]{1,0:T(8,128)(2,1)} %get-tuple-element.189), channel_id=1, source_target_pairs={{0,4},{4,0},{8,12},{12,8},{16,20},{20,16},{24,28},{28,24},{1,5},{5... | collective-permute-start | bytes 2113544 | tf_op jit(solution)/shard_map/ppermute | solution.py:219
  18.6 2.7 %collective-permute-start = (f32[2,1024,128]{2,1,0:T(8,128)S(1)}, f32[2,1024,128]{2,1,0:T(8,128)S(1)}, u32[]{:S(2)}, u32[]{:S(2)}) collective-permute-start(f32[2,1024,128]{2,1,0:T(8,128)S(1)} %get-tuple-element.116), channel_id=1, source_target_pairs={{0,1},{1,0},{2,3},{3,2},{4,5},{5,4},{6,7},{7,6},{8,9},{9,8},{10,11... | collective-permute-start | bytes 3145736 | tf_op jit(solution)/shard_map/cond/branch_1_fun/ppermute | solution.py:205
  21.3 14.0 %collective-permute-start.1 = (f32[1024,128]{1,0:T(8,128)S(1)}, f32[1024,128]{1,0:T(8,128)S(1)}, u32[]{:S(2)}, u32[]{:S(2)}) collective-permute-start(f32[1024,128]{1,0:T(8,128)S(1)} %fusion), channel_id=1, source_target_pairs={{0,2},{1,3},{2,0},{3,1},{4,6},{5,7},{6,4},{7,5},{8,10},{9,11},{10,... | collective-permute-start | bytes 1572872 | tf_op jit(solution)/shard_map/cond/branch_1_fun/ppermute | solution.py:208
  45.1 54.0 %collective-permute-start.18 = (bf16[2752,128]{1,0:T(8,128)(2,1)}, bf16[2752,128]{1,0:T(8,128)(2,1)}, u32[]{:S(2)}, u32[]{:S(2)}) collective-permute-start(bf16[2752,128]{1,0:T(8,128)(2,1)} %get-tuple-element.197), channel_id=1, source_target_pairs={{0,24},{4,28},{8,0},{12,4},{16,8},{20,12},{24,16},{28,20},{1,25},{... | collective-permute-start | bytes 2113544 | tf_op jit(solution)/shard_map/ppermute | solution.py:219
  47.2 52.0 %collective-permute-start.19 = (bf16[2752,128]{1,0:T(8,128)(2,1)}, bf16[2752,128]{1,0:T(8,128)(2,1)}, u32[]{:S(2)}, u32[]{:S(2)}) collective-permute-start(bf16[2752,128]{1,0:T(8,128)(2,1)} %get-tuple-element.197), channel_id=1, source_target_pairs={{0,4},{4,0},{8,12},{12,8},{16,20},{20,16},{24,28},{28,24},{1,5},{5... | collective-permute-start | bytes 2113544 | tf_op jit(solution)/shard_map/ppermute | solution.py:219
  48.7 52.1 %collective-permute-start.16 = (bf16[2752,128]{1,0:T(8,128)(2,1)}, bf16[2752,128]{1,0:T(8,128)(2,1)}, u32[]{:S(2)}, u32[]{:S(2)}) collective-permute-start(bf16[2752,128]{1,0:T(8,128)(2,1)} %get-tuple-element.194), channel_id=1, source_target_pairs={{0,24},{4,28},{8,0},{12,4},{16,8},{20,12},{24,16},{28,20},{1,25},{... | collective-permute-start | bytes 2113544 | tf_op jit(solution)/shard_map/ppermute | solution.py:219
  48.7 52.1 %collective-permute-start.17 = (bf16[2752,128]{1,0:T(8,128)(2,1)}, bf16[2752,128]{1,0:T(8,128)(2,1)}, u32[]{:S(2)}, u32[]{:S(2)}) collective-permute-start(bf16[2752,128]{1,0:T(8,128)(2,1)} %get-tuple-element.194), channel_id=1, source_target_pairs={{0,4},{4,0},{8,12},{12,8},{16,20},{20,16},{24,28},{28,24},{1,5},{5... | collective-permute-start | bytes 2113544 | tf_op jit(solution)/shard_map/ppermute | solution.py:219
  55.4 6.3 %collective-permute-start.5 = (f32[320,128]{1,0:T(8,128)S(1)}, f32[320,128]{1,0:T(8,128)S(1)}, u32[]{:S(2)}, u32[]{:S(2)}) collective-permute-start(f32[320,128]{1,0:T(8,128)S(1)} %fusion.6), channel_id=1, source_target_pairs={{0,2},{1,3},{2,0},{3,1},{4,6},{5,7},{6,4},{7,5},{8,10},{9,11},{10,... | collective-permute-start | bytes 491528 | tf_op jit(solution)/shard_map/cond/branch_1_fun/ppermute | solution.py:208
  67.3 4.2 %collective-permute-start.2 = (f32[2,2048,128]{2,1,0:T(8,128)S(1)}, f32[2,2048,128]{2,1,0:T(8,128)S(1)}, u32[]{:S(2)}, u32[]{:S(2)}) collective-permute-start(f32[2,2048,128]{2,1,0:T(8,128)S(1)} %get-tuple-element.123), channel_id=1, source_target_pairs={{0,1},{1,0},{2,3},{3,2},{4,5},{5,4},{6,7},{7,6},{8,9},{9,8},{10,11... | collective-permute-start | bytes 6291464 | tf_op jit(solution)/shard_map/cond/branch_1_fun/ppermute | solution.py:205
  71.7 25.3 %collective-permute-start.3 = (f32[2048,128]{1,0:T(8,128)S(1)}, f32[2048,128]{1,0:T(8,128)S(1)}, u32[]{:S(2)}, u32[]{:S(2)}) collective-permute-start(f32[2048,128]{1,0:T(8,128)S(1)} %fusion.3), channel_id=1, source_target_pairs={{0,2},{1,3},{2,0},{3,1},{4,6},{5,7},{6,4},{7,5},{8,10},{9,11},{10,... | collective-permute-start | bytes 3145736 | tf_op jit(solution)/shard_map/cond/branch_1_fun/ppermute | solution.py:208
  99.1 38.9 %collective-permute-start.21 = (bf16[1376,128]{1,0:T(8,128)(2,1)}, bf16[1376,128]{1,0:T(8,128)(2,1)}, u32[]{:S(2)}, u32[]{:S(2)}) collective-permute-start(bf16[1376,128]{1,0:T(8,128)(2,1)} %get-tuple-element.201), channel_id=1, source_target_pairs={{0,24},{4,28},{8,0},{12,4},{16,8},{20,12},{24,16},{28,20},{1,25},{... | collective-permute-start | bytes 1056776 | tf_op jit(solution)/shard_map/ppermute | solution.py:219
  99.2 42.3 %collective-permute-start.23 = (bf16[1376,128]{1,0:T(8,128)(2,1)}, bf16[1376,128]{1,0:T(8,128)(2,1)}, u32[]{:S(2)}, u32[]{:S(2)}) collective-permute-start(bf16[1376,128]{1,0:T(8,128)(2,1)} %get-tuple-element.201), channel_id=1, source_target_pairs={{0,4},{4,0},{8,12},{12,8},{16,20},{20,16},{24,28},{28,24},{1,5},{5... | collective-permute-start | bytes 1056776 | tf_op jit(solution)/shard_map/ppermute | solution.py:219
  100.8 38.7 %collective-permute-start.20 = (bf16[1376,128]{1,0:T(8,128)(2,1)}, bf16[1376,128]{1,0:T(8,128)(2,1)}, u32[]{:S(2)}, u32[]{:S(2)}) collective-permute-start(bf16[1376,128]{1,0:T(8,128)(2,1)} %get-tuple-element.200), channel_id=1, source_target_pairs={{0,24},{4,28},{8,0},{12,4},{16,8},{20,12},{24,16},{28,20},{1,25},{... | collective-permute-start | bytes 1056776 | tf_op jit(solution)/shard_map/ppermute | solution.py:219
  103.5 38.0 %collective-permute-start.22 = (bf16[1376,128]{1,0:T(8,128)(2,1)}, bf16[1376,128]{1,0:T(8,128)(2,1)}, u32[]{:S(2)}, u32[]{:S(2)}) collective-permute-start(bf16[1376,128]{1,0:T(8,128)(2,1)} %get-tuple-element.200), channel_id=1, source_target_pairs={{0,4},{4,0},{8,12},{12,8},{16,20},{20,16},{24,28},{28,24},{1,5},{5... | collective-permute-start | bytes 1056776 | tf_op jit(solution)/shard_map/ppermute | solution.py:219
  110.4 9.1 %collective-permute-start.9 = (f32[576,128]{1,0:T(8,128)S(1)}, f32[576,128]{1,0:T(8,128)S(1)}, u32[]{:S(2)}, u32[]{:S(2)}) collective-permute-start(f32[576,128]{1,0:T(8,128)S(1)} %fusion.12), channel_id=1, source_target_pairs={{0,2},{1,3},{2,0},{3,1},{4,6},{5,7},{6,4},{7,5},{8,10},{9,11},{10,... | collective-permute-start | bytes 884744 | tf_op jit(solution)/shard_map/cond/branch_1_fun/ppermute | solution.py:208
  127.0 7.7 %collective-permute-start.7 = (f32[448,128]{1,0:T(8,128)S(1)}, f32[448,128]{1,0:T(8,128)S(1)}, u32[]{:S(2)}, u32[]{:S(2)}) collective-permute-start(f32[448,128]{1,0:T(8,128)S(1)} %fusion.9), channel_id=1, source_target_pairs={{0,2},{1,3},{2,0},{3,1},{4,6},{5,7},{6,4},{7,5},{8,10},{9,11},{10,... | collective-permute-start | bytes 688136 | tf_op jit(solution)/shard_map/cond/branch_1_fun/ppermute | solution.py:208
  137.4 30.8 %collective-permute-start.24 = (f32[672,128]{1,0:T(8,128)}, f32[672,128]{1,0:T(8,128)}, u32[]{:S(2)}, u32[]{:S(2)}) collective-permute-start(f32[672,128]{1,0:T(8,128)} %pad_maximum_fusion.2), channel_id=1, source_target_pairs={{0,8},{4,12},{8,16},{12,20},{16,24},{20,28},{24,0},{28,4},{1,9},{5... | collective-permute-start | bytes 1032200 | tf_op jit(solution)/shard_map/ppermute | solution.py:263
  138.0 27.7 %collective-permute-start.26 = (f32[288,128]{1,0:T(8,128)}, f32[288,128]{1,0:T(8,128)}, u32[]{:S(2)}, u32[]{:S(2)}) collective-permute-start(f32[288,128]{1,0:T(8,128)} %pad_maximum_fusion.3), channel_id=1, source_target_pairs={{0,4},{4,0},{8,12},{12,8},{16,20},{20,16},{24,28},{28,24},{1,5},{5... | collective-permute-start | bytes 442376 | tf_op jit(solution)/shard_map/ppermute | solution.py:263
  151.0 10.5 %collective-permute-start.11 = (f32[704,128]{1,0:T(8,128)S(1)}, f32[704,128]{1,0:T(8,128)S(1)}, u32[]{:S(2)}, u32[]{:S(2)}) collective-permute-start(f32[704,128]{1,0:T(8,128)S(1)} %fusion.15), channel_id=1, source_target_pairs={{0,2},{1,3},{2,0},{3,1},{4,6},{5,7},{6,4},{7,5},{8,10},{9,11},{10,... | collective-permute-start | bytes 1081352 | tf_op jit(solution)/shard_map/cond/branch_1_fun/ppermute | solution.py:208
  162.8 8.1 %collective-permute-start.25 = (f32[352,128]{1,0:T(8,128)S(1)}, f32[352,128]{1,0:T(8,128)S(1)}, u32[]{:S(2)}, u32[]{:S(2)}) collective-permute-start(f32[352,128]{1,0:T(8,128)S(1)} %slice.184), channel_id=1, source_target_pairs={{0,8},{4,12},{8,16},{12,20},{16,24},{20,28},{24,0},{28,4},{1,9},{5... | collective-permute-start | bytes 540680 | tf_op jit(solution)/shard_map/ppermute | solution.py:263
  164.1 6.8 %collective-permute-start.27 = (f32[224,128]{1,0:T(8,128)S(1)}, f32[224,128]{1,0:T(8,128)S(1)}, u32[]{:S(2)}, u32[]{:S(2)}) collective-permute-start(f32[224,128]{1,0:T(8,128)S(1)} %slice.191), channel_id=1, source_target_pairs={{0,4},{4,0},{8,12},{12,8},{16,20},{20,16},{24,28},{28,24},{1,5},{5... | collective-permute-start | bytes 344072 | tf_op jit(solution)/shard_map/ppermute | solution.py:263
  (14 other events, 85.6 us)

commit v4 on v2

--- a/solution.py
+++ b/solution.py
@@ -1,3 +1,5 @@
+import math
+
 import jax
 import jax.numpy as jnp
 from jax import lax
@@ -11,6 +13,10 @@
 UNIT = 128
 SUB = UNIT // WID
 VMEM_LIMIT = 24 << 20
+PIECES = ['A', '0', 'kS', '1', 'kA', '2', '3', 'k0', 'k1', 'k2', 'k3']
+GATES = {'R1': ['RA'], 'O1': ['OA'], 'R2': ['RA'], 'O2': ['OA'], 'R3': ['R0'], 'O3': ['O0'], 'KA': ['SS'], 'K0': ['SA', 'R1', 'O1'], 'K1': ['SA'], 'K2': ['S1'], 'K3': ['S0', 'S1'], 'SA': [], 'S0': ['SA'], 'S1': [], 'S2': [], 'S3': ['S0', 'S1'], 'G0': [], 'G1': []}
+PLAIN = []
+GROUPS = [[0, 1, 2], [3]]
 SMEM = pl.BlockSpec(memory_space=pltpu.SMEM)
 VMEM = pl.BlockSpec(memory_space=pltpu.VMEM)
 
@@ -21,7 +27,7 @@
         out_shape=outs,
         in_specs=[SMEM] * scalars + [VMEM] * (len(args) - scalars),
         out_specs=jax.tree.map(lambda _: VMEM, outs),
-        cost_estimate=pl.CostEstimate(flops=0, bytes_accessed=0, transcendentals=0),
+        cost_estimate=pl.CostEstimate(flops=2000000000, bytes_accessed=2000000, transcendentals=0),
         compiler_params=pltpu.CompilerParams(vmem_limit_bytes=VMEM_LIMIT),
     )(*args)
 
@@ -140,10 +146,38 @@
             put_third(place_ref, keep, send, spot, 0, a, step, block[a * UNIT : (a + 1) * UNIT])
 
 
-def final_kernel(layouts, place_ref, lengths_ref, self_ref, *refs):
-    out = refs[-1]
+def product(acts, grads, act_at, grad_at, rows):
+    act_sum = acts[0][act_at : act_at + rows, :] + acts[1][act_at : act_at + rows, :]
+    grad_sum = grads[0][grad_at : grad_at + rows, :] + grads[1][grad_at : grad_at + rows, :]
+    return (act_sum * (1.0 / math.sqrt(D))) * (grad_sum * (1.0 / math.sqrt(FF)))
+
+
+def return_kernel(layouts, steps, *refs):
+    acts, (ring, swap) = refs[:2], refs[-2:]
+    ring_at = swap_at = 0
+    for i, c in enumerate(steps):
+        grads = refs[2 + 2 * i : 4 + 2 * i]
+        _, n_ring, n_swap, _ = layouts[c]
+        base = sum(layouts[s][3] for s in range(c))
+        ring[ring_at : ring_at + n_ring, :] = product(acts, grads, base, 0, n_ring)
+        swap[swap_at : swap_at + n_swap - n_ring, :] = product(acts, grads, base + n_ring, n_ring, n_swap - n_ring)
+        ring_at += n_ring
+        swap_at += n_swap - n_ring
+
+
+def final_kernel(layouts, groups, place_ref, lengths_ref, *refs):
     units = len(layouts)
-    local, ring, swap = refs[:units], refs[units : 2 * units], refs[2 * units : 3 * units]
+    selves, acts, out = refs[:2], refs[2:4], refs[-1]
+    grads = [refs[4 + 2 * c : 6 + 2 * c] for c in range(units)]
+    returned = {}
+    for i, steps in enumerate(groups):
+        ring, swap = refs[4 + 2 * units + 2 * i : 6 + 2 * units + 2 * i]
+        ring_at = swap_at = 0
+        for c in steps:
+            _, n_ring, n_swap, _ = layouts[c]
+            returned[c] = ring, ring_at, swap, swap_at - n_ring
+            ring_at += n_ring
+            swap_at += n_swap - n_ring
     even = place_ref[0] == 0
     width = place_ref[3]
     token = place_ref[4]
@@ -152,10 +186,15 @@
     columns = width * UNIT + lax.broadcasted_iota(jnp.int32, (UNIT, UNIT), 1)
     line = lax.broadcasted_iota(jnp.int32, (UNIT, UNIT), 0)
 
-    def block(refs, name, step, shift=0):
-        spot = layouts[step][0][name] - shift
+    def block(where, name, step):
+        spot = layouts[step][0][name]
         size = UNIT if name[0] == "rt" else SUB
-        return refs[step][spot : spot + size, :]
+        if where == "local":
+            base = sum(layouts[s][3] for s in range(step))
+            return product(acts, grads[step], base + spot, spot, size)
+        ring, ring_at, swap, swap_at = returned[step]
+        ref, at = (ring, ring_at + spot) if where == "ring" else (swap, swap_at + spot)
+        return ref[at : at + size, :]
 
     def natural(offset, b, tile, there):
         live = (b * UNIT + line < here) & (columns < there)
@@ -170,14 +209,13 @@
 
     there = [lengths_ref[lax.rem(token + offset + total - 2, total)] for offset in range(5)]
     for c in range(units):
-        arrival(0, c, block(ring, ("rt", c), c), there[0])
-        tt = [[block(r, ("tt", a, c), max(a, c)) for a in range(units)] for r in (ring, local)]
-        arrival(1, c, jnp.where(even, jnp.concatenate(tt[0], axis=0), jnp.concatenate(tt[1], axis=0)), there[1])
-        tj = [block(swap, ("tj", a, c), max(a, c), layouts[max(a, c)][1]) for a in range(units)]
-        arrival(3, c, jnp.concatenate(tj, axis=0), there[3])
+        arrival(0, c, block("ring", ("rt", c), c), there[0])
+        tt = [jnp.concatenate([block(r, ("tt", a, c), max(a, c)) for a in range(units)], axis=0) for r in ("ring", "local")]
+        arrival(1, c, jnp.where(even, tt[0], tt[1]), there[1])
+        arrival(3, c, jnp.concatenate([block("swap", ("tj", a, c), max(a, c)) for a in range(units)], axis=0), there[3])
     for b in range(WID):
-        natural(2, b, self_ref[b * UNIT : (b + 1) * UNIT, :], there[2])
-        natural(4, b, jnp.concatenate([block(local, ("rj", c, b), c) for c in range(units)], axis=0), there[4])
+        natural(2, b, product(selves, selves, b * UNIT, (WID + b) * UNIT, UNIT), there[2])
+        natural(4, b, jnp.concatenate([block("local", ("rj", c, b), c) for c in range(units)], axis=0), there[4])
 
 
 def shards(acts, grads, lengths):
@@ -195,59 +233,86 @@
     def floats(n):
         return (jax.ShapeDtypeStruct((2, n, UNIT), jnp.float32),) * 2
 
-    def wid_total(keep, send):
-        arrived = lax.ppermute(send, "wid", [(w, w ^ 1) for w in range(WID)])
-        across = lax.ppermute(keep[1] + arrived[1], "wid", [(w, w ^ 2) for w in range(WID)])
-        return keep[0], arrived[0], across
-
-    def total(parts, start, stop):
-        return parts[0][start:stop] + parts[1][start:stop] + parts[2][start:stop]
-
-    scale_a = 1.0 / jnp.sqrt(jnp.float32(D))
-    scale_g = 1.0 / jnp.sqrt(jnp.float32(FF))
-
-    ring_a = lax.ppermute(acts, "tok", down)
-    other_a = lax.ppermute(acts, "tok", swap)
+    def over_core(send):
+        return lax.ppermute(send, "wid", [(w, w ^ 1) for w in range(WID)])
+
     own_g = grads.T
-    mine = call(reorder_kernel, (jax.ShapeDtypeStruct((grads.shape[1], UNIT), jnp.bfloat16),) * units, own_g)
-    ring_g, other_g = [], []
-    for c in range(units):
-        chunk = mine[c]
-        if c == 1:
-            chunk, ring_a, other_a = lax.optimization_barrier((chunk, ring_a, other_a))
-        elif c > 1:
-            chunk, ring_g[c - 2], other_g[c - 2] = lax.optimization_barrier((chunk, ring_g[c - 2], other_g[c - 2]))
-        ring_g.append(lax.ppermute(chunk, "tok", down))
-        other_g.append(lax.ppermute(chunk, "tok", swap))
-
-    parts = wid_total(*call(self_kernel, floats(2 * WID * UNIT), place, acts, own_g, scalars=1))
-    half = WID * UNIT
-    self_tile = (total(parts, 0, half) * scale_a) * (total(parts, half, 2 * half) * scale_g)
-
-    everything = sum(size for _, _, _, size in layouts)
-    act_parts = wid_total(
-        *call(lambda *refs: acts_kernel(layouts, *refs), floats(everything), place, acts, ring_a, other_a, scalars=1)
-    )
-
-    local, from_ring, from_swap = [], [], []
-    base = 0
-    for c, (spot, n_ring, n_swap, size) in enumerate(layouts):
-        parts = wid_total(
-            *call(
-                lambda *refs, c=c, spot=spot: grads_kernel(c, spot, *refs),
-                floats(size), place, own_g, *mine[: c + 1], *ring_g[: c + 1], *other_g[: c + 1], scalars=1,
+    mine = list(call(reorder_kernel, (jax.ShapeDtypeStruct((grads.shape[1], UNIT), jnp.bfloat16),) * units, own_g))
+    alive = jnp.max(lengths) > 0
+    seen = {}
+
+    def after(x, names):
+        if not names:
+            return x
+        x, *held = lax.optimization_barrier((x, *[seen[name] for name in names]))
+        seen.update(zip(names, held))
+        return x
+
+    def start(name, chunk):
+        seen["R" + name] = lax.ppermute(after(chunk, GATES.get("R" + name)), "tok", down)
+        seen["O" + name] = lax.ppermute(after(chunk, GATES.get("O" + name)), "tok", swap)
+
+    def exchange(name, kernel, n, first, *rest):
+        def summed(*args):
+            keep, send = call(kernel, floats(n), place, *args, scalars=1)
+            arrived = over_core(send)
+            return keep[0] + arrived[0], keep[1] + arrived[1]
+
+        def nothing(*args):
+            return (jnp.zeros((n, UNIT), jnp.float32),) * 2
+
+        first = after(first, GATES.get("K" + name))
+        if name in PLAIN:
+            near, far = summed(first, *rest)
+        else:
+            near, far = lax.cond(alive, summed, nothing, first, *rest)
+        seen["S" + name] = lax.ppermute(after(far, GATES.get("S" + name)), "wid", [(w, w ^ 2) for w in range(WID)])
+        return near
+
+    def pair(c):
+        if str(c) in PIECES:
+            return seen["R%d" % c], seen["O%d" % c]
+        return tuple(jnp.concatenate([seen["%s%d%s" % (side, c, half)] for half in "ab"], axis=0) for side in "RO")
+
+    near = {}
+    for piece in PIECES:
+        if piece == "A":
+            start(piece, acts)
+        elif piece[0] in "0123":
+            chunk = mine[int(piece[0])]
+            cut = chunk.shape[0] // 2
+            start(piece, {"": chunk, "a": chunk[:cut], "b": chunk[cut:]}[piece[1:]])
+        elif piece == "kS":
+            near["S"] = exchange("S", self_kernel, 2 * WID * UNIT, acts, own_g)
+        elif piece == "kA":
+            everything = sum(size for _, _, _, size in layouts)
+            near["A"] = exchange("A", lambda *refs: acts_kernel(layouts, *refs), everything, acts, seen["RA"], seen["OA"])
+        else:
+            c = int(piece[1])
+            spot, size = layouts[c][0], layouts[c][3]
+            pairs = [pair(a) for a in range(c + 1)]
+            near[c] = seen["N%d" % c] = exchange(
+                piece[1], lambda *refs, c=c, spot=spot: grads_kernel(c, spot, *refs),
+                size, own_g, *mine[: c + 1], *[p[0] for p in pairs], *[p[1] for p in pairs],
             )
+
+    returned = []
+    for i, steps in enumerate(GROUPS):
+        sizes = [sum(layouts[c][1] for c in steps), sum(layouts[c][2] - layouts[c][1] for c in steps)]
+        first = after(near[steps[0]], GATES.get("G%d" % i))
+        grams = sum([[first if c == steps[0] else near[c], seen["S%d" % c]] for c in steps], [])
+        ring, swapped = call(
+            lambda *refs, steps=steps: return_kernel(layouts, steps, *refs),
+            tuple(jax.ShapeDtypeStruct((n, UNIT), jnp.float32) for n in sizes),
+            near["A"], seen["SA"], *grams,
         )
-        tile = (total(act_parts, base, base + size) * scale_a) * (total(parts, 0, size) * scale_g)
-        base += size
-        local.append(tile)
-        from_ring.append(lax.ppermute(tile[:n_ring], "tok", up))
-        from_swap.append(lax.ppermute(tile[n_ring:n_swap], "tok", swap))
-
+        returned += [lax.ppermute(ring, "tok", up), lax.ppermute(swapped, "tok", swap)]
+
+    grams = sum([[near[c], seen["S%d" % c]] for c in range(units)], [])
     out = call(
-        lambda *refs: final_kernel(layouts, *refs),
+        lambda *refs: final_kernel(layouts, GROUPS, *refs),
         jax.ShapeDtypeStruct((5, rows, UNIT), jnp.float32),
-        place, lengths, self_tile, *local, *from_ring, *from_swap, scalars=2,
+        place, lengths, near["S"], seen["SS"], near["A"], seen["SA"], *grams, *returned, scalars=2,
     )
     return out.transpose(1, 0, 2)
 

time: 175 us -> 126 us (0.72)
  waiting for transfers between devices: 109 us -> 57.1 us
  Pallas kernels: 20.4 us -> 35.8 us
  starting transfers between devices: 38.8 us -> 25.8 us
  local copies, waits for them, and re-layouts: 5.76 us -> 3.37 us
  other arithmetic: 0.7 us -> 2.69 us
    ppermute x30 -> x26, waiting for transfers between devices: 109 us -> 57.1 us  [the longest x6 20.8 us: exchange(): lax.ppermute(after(far, GATES.get('S' + name)), 'wid', [(w, w ^ 2) for w...]
    pallas_call x8 -> x10, Pallas kernels: 20.4 us -> 35.8 us  [call(): pl.pallas_call(kernel, out_shape=outs, in_specs=[SMEM] * scalars + [VMEM]...]
    ppermute x30 -> x26, starting transfers between devices: 38.8 us -> 25.8 us  [the longest x5 10.6 us: start(): lax.ppermute(after(chunk, GATES.get('R' + name)), 'tok', down)]
    unnamed x20 -> x40, local copies, waits for them, and re-layouts: 5.61 us -> 3.28 us
  transfers between devices with their start and end apart: 30 -> 26, of which waited for: 18 -> 14; matrix products, arithmetic and copies ran while one was open for 0% -> 2% of each run, Pallas kernels for 8% -> 27%
where the time goes in v4:
time: 126 us
  waiting for transfers between devices  57.1 us (45%)
  Pallas kernels  35.8 us (28%)
  starting transfers between devices  25.8 us (20%)
  local copies, waits for them, and re-layouts  3.37 us (3%)
  other arithmetic  2.69 us (2%)
    pallas_call x10, Pallas kernels, call(): pl.pallas_call(kernel, out_shape=outs, in_specs=[SMEM] * scalars + [VMEM]...  35.8 us
    ppermute x6, waiting for transfers between devices, exchange(): lax.ppermute(after(far, GATES.get('S' + name)), 'wid', [(w, w ^ 2) for w...  20.8 us
    ppermute x5, waiting for transfers between devices, start(): lax.ppermute(after(chunk, GATES.get('R' + name)), 'tok', down)  14.5 us
    ppermute x6, waiting for transfers between devices, over_core(): return lax.ppermute(send, 'wid', [(w, w ^ 1) for w in range(WID)])  14.3 us
    ppermute x5, starting transfers between devices, start(): lax.ppermute(after(chunk, GATES.get('R' + name)), 'tok', down)  10.6 us
    ppermute x6, starting transfers between devices, exchange(): lax.ppermute(after(far, GATES.get('S' + name)), 'wid', [(w, w ^ 2) for w...  6.27 us
    ppermute x5, starting transfers between devices, start(): lax.ppermute(after(chunk, GATES.get('O' + name)), 'tok', swap)  6.1 us
    ppermute x2, waiting for transfers between devices, shards(): lax.ppermute(swapped, 'tok', swap)  5.49 us
  transfers between devices with their start and end apart: 26, of which 14 were waited for; matrix products, arithmetic and copies ran while one was open for 2% of the time, Pallas kernels for 27%

profile of v4, /device:TPU:0, one launch (start us, length us, event | category | flops | bytes accessed | tf_op | source)
XLA Modules:
  0.0 125.9 jit_solution(8370031174018559280)
XLA Ops:
  0.0 2.9 %collective-permute-start.8 = (bf16[512,1024]{1,0:T(8,128)(2,1)}, bf16[512,1024]{1,0:T(8,128)(2,1)}, u32[]{:S(2)}, u32[]{:S(2)}) collective-permute-start(bf16[512,1024]{1,0:T(8,128)(2,1)} %param.15), channel_id=1, source_target_pairs={{0,4},{4,0},{8,12},{12,8},{16,20},{20,16},{24,28},{28,24},{1,5},{5... | collective-permute-start | bytes 3145736 | tf_op jit(solution)/shard_map/ppermute | solution.py:253
  2.9 3.6 %collective-permute-start.7 = (bf16[512,1024]{1,0:T(8,128)(2,1)}, bf16[512,1024]{1,0:T(8,128)(2,1)}, u32[]{:S(2)}, u32[]{:S(2)}) collective-permute-start(bf16[512,1024]{1,0:T(8,128)(2,1)} %param.15), channel_id=1, source_target_pairs={{0,24},{4,28},{8,0},{12,4},{16,8},{20,12},{24,16},{28,20},{1,25},{... | collective-permute-start | bytes 3145736 | tf_op jit(solution)/shard_map/ppermute | solution.py:252
  8.6 7.3 %conditional.6 = (f32[1024,128]{1,0:T(8,128)S(1)}, f32[1024,128]{1,0:T(8,128)S(1)}) conditional(s32[]{:T(128)} %convert_element_type.2, () %tuple.66, (s32[5]{0:T(128)S(1)}, bf16[512,1024]{1,0:T(8,128)(2,1)}, bf16[2752,512]{1,0:T(8,128)(2,1)}) %tuple.109), branch_computations={%region_1.2_spmd, %region_2.3_spmd} | conditional | flops 2000262144 | bytes 9340088 | solution.py:268
  8.6 4.5 %branch_1_fun.6 = (f32[2,1024,128]{2,1,0:T(8,128)S(1)}, f32[2,1024,128]{2,1,0:T(8,128)S(1)}) custom-call(s32[5]{0:T(128)S(1)} %get-tuple-element.95.place_ref, bf16[512,1024]{1,0:T(8,128)(2,1)} %get-tuple-element.96.a_ref, bf16[2752,512]{1,0:T(8,128)(2,1)} %get-tuple-element.97.g_ref), custom_call_target="tpu_custom_call" | custom-call | flops 2000000000 | bytes 2000000 | tf_op jit(solution)/shard_map/cond/branch_1_fun/pallas_call | solution.py:25
  13.2 2.6 %collective-permute-done = f32[2,1024,128]{2,1,0:T(8,128)S(1)} collective-permute-done((f32[2,1024,128]{2,1,0:T(8,128)S(1)}, f32[2,1024,128]{2,1,0:T(8,128)S(1)}, u32[]{:S(2)}, u32[]{:S(2)}) %collective-permute-start) | collective-permute-done | bytes 1048608 | tf_op jit(solution)/shard_map/cond/branch_1_fun/ppermute | solution.py:237
  17.6 6.0 %shard_map.37 = (bf16[2752,128]{1,0:T(8,128)(2,1)S(1)}, bf16[2752,128]{1,0:T(8,128)(2,1)S(1)}, bf16[2752,128]{1,0:T(8,128)(2,1)}, bf16[2752,128]{1,0:T(8,128)(2,1)}) custom-call(bf16[2752,512]{1,0:T(8,128)(2,1)} %bitcast.32), custom_call_target="tpu_custom_call" | custom-call | flops 2000000000 | bytes 2000000 | tf_op jit(solution)/shard_map/pallas_call | solution.py:25
  24.6 5.5 %collective-permute-done.6.refs_3_ = f32[1024,128]{1,0:T(8,128)S(1)} collective-permute-done((f32[1024,128]{1,0:T(8,128)S(1)}, f32[1024,128]{1,0:T(8,128)S(1)}, u32[]{:S(2)}, u32[]{:S(2)}) %collective-permute-start.6) | collective-permute-done | bytes 524320 | tf_op jit(solution)/shard_map/ppermute | solution.py:269
  30.5 9.1 %conditional.7 = (f32[2048,128]{1,0:T(8,128)S(1)}, f32[2048,128]{1,0:T(8,128)S(1)}) conditional(s32[]{:T(128)} %convert_element_type.2, () %tuple.69, (s32[5]{0:T(128)S(1)}, bf16[512,1024]{1,0:T(8,128)(2,1)S(1)}, bf16[512,1024]{1,0:T(8,128)(2,1)}, bf16[512,1024]{1,0:T(8,128)(2,1)}) %tuple.121), branch_computations={%region_3.4_spmd, %region_4.5_spmd} | conditional | flops 2000524288 | bytes 16680120 | solution.py:268
  30.5 4.6 %branch_1_fun.7 = (f32[2,2048,128]{2,1,0:T(8,128)S(1)}, f32[2,2048,128]{2,1,0:T(8,128)S(1)}) custom-call(s32[5]{0:T(128)S(1)} %get-tuple-element.100.refs_0_, bf16[512,1024]{1,0:T(8,128)(2,1)S(1)} %get-tuple-element.101.refs_1_, bf16[512,1024]{1,0:T(8,128)(2,1)} %get-tuple-element.102.refs_2_, bf16[512,1024]{1,0:T(8,128)(2,1)} %get-tuple-element.103.refs_3_), custom_call_target="tpu_custom_call" | custom-call | flops 2000000000 | bytes 2000000 | tf_op jit(solution)/shard_map/cond/branch_1_fun/pallas_call | solution.py:25
  35.1 4.1 %collective-permute-done.1 = f32[2,2048,128]{2,1,0:T(8,128)S(1)} collective-permute-done((f32[2,2048,128]{2,1,0:T(8,128)S(1)}, f32[2,2048,128]{2,1,0:T(8,128)S(1)}, u32[]{:S(2)}, u32[]{:S(2)}) %collective-permute-start.1) | collective-permute-done | bytes 2097184 | tf_op jit(solution)/shard_map/cond/branch_1_fun/ppermute | solution.py:237
  42.0 4.3 %collective-permute-start.10 = (bf16[2752,128]{1,0:T(8,128)(2,1)S(1)}, bf16[2752,128]{1,0:T(8,128)(2,1)S(1)}, u32[]{:S(2)}, u32[]{:S(2)}) collective-permute-start(bf16[2752,128]{1,0:T(8,128)(2,1)S(1)} %get-tuple-element.210), channel_id=1, source_target_pairs={{0,24},{4,28},{8,0},{12,4},{16,8},{20,12},{24,16},{28,20},{1,25},{... | collective-permute-start | bytes 2113544 | tf_op jit(solution)/shard_map/ppermute | solution.py:252
  48.4 14.1 %collective-permute-done.10 = bf16[2752,128]{1,0:T(8,128)(2,1)S(1)} collective-permute-done((bf16[2752,128]{1,0:T(8,128)(2,1)S(1)}, bf16[2752,128]{1,0:T(8,128)(2,1)S(1)}, u32[]{:S(2)}, u32[]{:S(2)}) %collective-permute-start.10) | collective-permute-done | bytes 704544 | tf_op jit(solution)/shard_map/ppermute | solution.py:252
  65.0 2.3 %collective-permute-start.17 = (bf16[2752,128]{1,0:T(8,128)(2,1)}, bf16[2752,128]{1,0:T(8,128)(2,1)}, u32[]{:S(2)}, u32[]{:S(2)}) collective-permute-start(bf16[2752,128]{1,0:T(8,128)(2,1)} %get-tuple-element.232), channel_id=1, source_target_pairs={{0,24},{4,28},{8,0},{12,4},{16,8},{20,12},{24,16},{28,20},{1,25},{... | collective-permute-start | bytes 2113544 | tf_op jit(solution)/shard_map/ppermute | solution.py:252
  67.4 4.8 %conditional.8 = (f32[320,128]{1,0:T(8,128)S(1)}, f32[320,128]{1,0:T(8,128)S(1)}) conditional(s32[]{:T(128)} %convert_element_type.2, () %tuple.73, (s32[5]{0:T(128)S(1)}, bf16[2752,512]{1,0:T(8,128)(2,1)}, bf16[2752,128]{1,0:T(8,128)(2,1)S(1)}, bf16[2752,128]{1,0:T(8,128)(2,1)}, bf16[2752,128]{1,0:T(8,128)(2,1)}) %tuple.110), branch_computations={%region_5.6_spmd, %region_6.7_spmd} | conditional | flops 2000081920 | bytes 4293816 | solution.py:268
  67.4 3.0 %branch_1_fun.8 = (f32[2,320,128]{2,1,0:T(8,128)S(1)}, f32[2,320,128]{2,1,0:T(8,128)S(1)}) custom-call(s32[5]{0:T(128)S(1)} %get-tuple-element.106.refs_0_, bf16[2752,512]{1,0:T(8,128)(2,1)} %get-tuple-element.107.refs_1_, bf16[2752,128]{1,0:T(8,128)(2,1)S(1)} %get-tuple-element.108.refs_2_, bf16[2752,128]{1,0:T(8,128)(2,1)} %get-tuple-element.109.refs_3_, ...), custom_call_target="tpu_custom_call" | custom-call | flops 2000000000 | bytes 2000000 | tf_op jit(solution)/shard_map/cond/branch_1_fun/pallas_call | solution.py:25
  72.9 5.7 %conditional.9 = (f32[448,128]{1,0:T(8,128)S(1)}, f32[448,128]{1,0:T(8,128)S(1)}) conditional(s32[]{:T(128)} %convert_element_type.2, () %tuple.81, (s32[5]{0:T(128)S(1)}, bf16[2752,512]{1,0:T(8,128)(2,1)}, bf16[2752,128]{1,0:T(8,128)(2,1)S(1)}, bf16[2752,128]{1,0:T(8,128)(2,1)S(1)}, bf16[2752,128]{1,0:T(8,128)(2,1)}, ...), branch_computations={%region_7.8_spmd, %region_8.9_spmd} | conditional | flops 2000114688 | bytes 5211320 | solution.py:268
  72.9 3.7 %branch_1_fun.9 = (f32[2,448,128]{2,1,0:T(8,128)S(1)}, f32[2,448,128]{2,1,0:T(8,128)S(1)}) custom-call(s32[5]{0:T(128)S(1)} %get-tuple-element.113.refs_0_, bf16[2752,512]{1,0:T(8,128)(2,1)} %get-tuple-element.114.refs_1_, bf16[2752,128]{1,0:T(8,128)(2,1)S(1)} %get-tuple-element.115.refs_2_, bf16[2752,128]{1,0:T(8,128)(2,1)S(1)} %get-tuple-element.116.refs_3_, ...), custom_call_target="tpu_custom_call" | custom-call | flops 2000000000 | bytes 2000000 | tf_op jit(solution)/shard_map/cond/branch_1_fun/pallas_call | solution.py:25
  79.8 7.1 %collective-permute-done.15.refs_5_.refs_9_ = f32[448,128]{1,0:T(8,128)S(1)} collective-permute-done((f32[448,128]{1,0:T(8,128)S(1)}, f32[448,128]{1,0:T(8,128)S(1)}, u32[]{:S(2)}, u32[]{:S(2)}) %collective-permute-start.15) | collective-permute-done | bytes 229408 | tf_op jit(solution)/shard_map/ppermute | solution.py:269
  87.4 7.6 %conditional.11 = (f32[576,128]{1,0:T(8,128)S(1)}, f32[576,128]{1,0:T(8,128)}) conditional(s32[]{:T(128)} %convert_element_type.2, () %tuple.89, (s32[5]{0:T(128)S(1)}, bf16[2752,512]{1,0:T(8,128)(2,1)}, bf16[2752,128]{1,0:T(8,128)(2,1)S(1)}, bf16[2752,128]{1,0:T(8,128)(2,1)S(1)}, bf16[2752,128]{1,0:T(8,128)(2,1)}, ...), branch_computations={%region_11.12_spmd, %region_12.13_spmd} | conditional | flops 2000147456 | bytes 6128824 | solution.py:268
  87.6 4.6 %branch_1_fun.11 = (f32[2,576,128]{2,1,0:T(8,128)S(1)}, f32[2,576,128]{2,1,0:T(8,128)S(1)}) custom-call(s32[5]{0:T(128)S(1)} %get-tuple-element.139.refs_0_, bf16[2752,512]{1,0:T(8,128)(2,1)} %get-tuple-element.140.refs_1_, bf16[2752,128]{1,0:T(8,128)(2,1)S(1)} %get-tuple-element.141.refs_2_, bf16[2752,128]{1,0:T(8,128)(2,1)S(1)} %get-tuple-element.142.refs_3_, ...), custom_call_target="tpu_custom_call" | custom-call | flops 2000000000 | bytes 2000000 | tf_op jit(solution)/shard_map/cond/branch_1_fun/pallas_call | solution.py:25
  96.6 8.1 %conditional.10 = (f32[704,128]{1,0:T(8,128)S(1)}, f32[704,128]{1,0:T(8,128)S(1)}) conditional(s32[]{:T(128)} %convert_element_type.2, () %tuple.80, (s32[5]{0:T(128)S(1)}, bf16[2752,512]{1,0:T(8,128)(2,1)}, bf16[2752,128]{1,0:T(8,128)(2,1)S(1)}, bf16[2752,128]{1,0:T(8,128)(2,1)}, bf16[2752,128]{1,0:T(8,128)(2,1)}, ...), branch_computations={%region_9.10_spmd, %region_10.11_spmd} | conditional | flops 2000180224 | bytes 7046328 | solution.py:268
  96.6 5.7 %branch_1_fun.10 = (f32[2,704,128]{2,1,0:T(8,128)S(1)}, f32[2,704,128]{2,1,0:T(8,128)S(1)}) custom-call(s32[5]{0:T(128)S(1)} %get-tuple-element.123.refs_0_, bf16[2752,512]{1,0:T(8,128)(2,1)} %get-tuple-element.124.refs_1_, bf16[2752,128]{1,0:T(8,128)(2,1)S(1)} %get-tuple-element.125.refs_2_, bf16[2752,128]{1,0:T(8,128)(2,1)} %get-tuple-element.126.refs_3_, ...), custom_call_target="tpu_custom_call" | custom-call | flops 2000000000 | bytes 2000000 | tf_op jit(solution)/shard_map/cond/branch_1_fun/pallas_call | solution.py:25
  107.8 8.2 %collective-permute-done.21.refs_3_.refs_13_ = f32[704,128]{1,0:T(8,128)S(1)} collective-permute-done((f32[704,128]{1,0:T(8,128)}, f32[704,128]{1,0:T(8,128)S(1)}, u32[]{:S(2)}, u32[]{:S(2)}) %collective-permute-start.21) | collective-permute-done | bytes 360480 | tf_op jit(solution)/shard_map/ppermute | solution.py:269
  118.3 4.3 %collective-permute-done.23.refs_15_ = f32[288,128]{1,0:T(8,128)S(1)} collective-permute-done((f32[288,128]{1,0:T(8,128)S(1)}, f32[288,128]{1,0:T(8,128)S(1)}, u32[]{:S(2)}, u32[]{:S(2)}) %collective-permute-start.23) | collective-permute-done | bytes 147488 | tf_op jit(solution)/shard_map/ppermute | solution.py:309
  (92 shorter events, 33.5 us)
Async XLA Ops:
  0.0 30.0 %collective-permute-start.8 = (bf16[512,1024]{1,0:T(8,128)(2,1)}, bf16[512,1024]{1,0:T(8,128)(2,1)}, u32[]{:S(2)}, u32[]{:S(2)}) collective-permute-start(bf16[512,1024]{1,0:T(8,128)(2,1)} %param.15), channel_id=1, source_target_pairs={{0,4},{4,0},{8,12},{12,8},{16,20},{20,16},{24,28},{28,24},{1,5},{5... | collective-permute-start | bytes 3145736 | tf_op jit(solution)/shard_map/ppermute | solution.py:253
  2.9 27.5 %collective-permute-start.7 = (bf16[512,1024]{1,0:T(8,128)(2,1)}, bf16[512,1024]{1,0:T(8,128)(2,1)}, u32[]{:S(2)}, u32[]{:S(2)}) collective-permute-start(bf16[512,1024]{1,0:T(8,128)(2,1)} %param.15), channel_id=1, source_target_pairs={{0,24},{4,28},{8,0},{12,4},{16,8},{20,12},{24,16},{28,20},{1,25},{... | collective-permute-start | bytes 3145736 | tf_op jit(solution)/shard_map/ppermute | solution.py:252
  13.1 2.7 %collective-permute-start = (f32[2,1024,128]{2,1,0:T(8,128)S(1)}, f32[2,1024,128]{2,1,0:T(8,128)S(1)}, u32[]{:S(2)}, u32[]{:S(2)}) collective-permute-start(f32[2,1024,128]{2,1,0:T(8,128)S(1)} %get-tuple-element.99), channel_id=1, source_target_pairs={{0,1},{1,0},{2,3},{3,2},{4,5},{5,4},{6,7},{7,6},{8,9},{9,8},{10,11... | collective-permute-start | bytes 3145736 | tf_op jit(solution)/shard_map/cond/branch_1_fun/ppermute | solution.py:237
  16.0 14.0 %collective-permute-start.6 = (f32[1024,128]{1,0:T(8,128)S(1)}, f32[1024,128]{1,0:T(8,128)S(1)}, u32[]{:S(2)}, u32[]{:S(2)}) collective-permute-start(f32[1024,128]{1,0:T(8,128)S(1)} %get-tuple-element.201), channel_id=1, source_target_pairs={{0,2},{1,3},{2,0},{3,1},{4,6},{5,7},{6,4},{7,5},{8,10},{9,11},{10,... | collective-permute-start | bytes 1572872 | tf_op jit(solution)/shard_map/ppermute | solution.py:269
  23.6 23.3 %collective-permute-start.13 = (bf16[2752,128]{1,0:T(8,128)(2,1)S(1)}, bf16[2752,128]{1,0:T(8,128)(2,1)}, u32[]{:S(2)}, u32[]{:S(2)}) collective-permute-start(bf16[2752,128]{1,0:T(8,128)(2,1)S(1)} %get-tuple-element.212), channel_id=1, source_target_pairs={{0,4},{4,0},{8,12},{12,8},{16,20},{20,16},{24,28},{28,24},{1,5},{5... | collective-permute-start | bytes 2113544 | tf_op jit(solution)/shard_map/ppermute | solution.py:253
  24.1 22.8 %collective-permute-start.12 = (bf16[2752,128]{1,0:T(8,128)(2,1)S(1)}, bf16[2752,128]{1,0:T(8,128)(2,1)}, u32[]{:S(2)}, u32[]{:S(2)}) collective-permute-start(bf16[2752,128]{1,0:T(8,128)(2,1)S(1)} %get-tuple-element.212), channel_id=1, source_target_pairs={{0,24},{4,28},{8,0},{12,4},{16,8},{20,12},{24,16},{28,20},{1,25},{... | collective-permute-start | bytes 2113544 | tf_op jit(solution)/shard_map/ppermute | solution.py:252
  35.0 4.2 %collective-permute-start.1 = (f32[2,2048,128]{2,1,0:T(8,128)S(1)}, f32[2,2048,128]{2,1,0:T(8,128)S(1)}, u32[]{:S(2)}, u32[]{:S(2)}) collective-permute-start(f32[2,2048,128]{2,1,0:T(8,128)S(1)} %get-tuple-element.105), channel_id=1, source_target_pairs={{0,1},{1,0},{2,3},{3,2},{4,5},{5,4},{6,7},{7,6},{8,9},{9,8},{10,11... | collective-permute-start | bytes 6291464 | tf_op jit(solution)/shard_map/cond/branch_1_fun/ppermute | solution.py:237
  40.5 26.8 %collective-permute-start.9 = (f32[2048,128]{1,0:T(8,128)}, f32[2048,128]{1,0:T(8,128)S(1)}, u32[]{:S(2)}, u32[]{:S(2)}) collective-permute-start(f32[2048,128]{1,0:T(8,128)} %copy-done.4), channel_id=1, source_target_pairs={{0,2},{1,3},{2,0},{3,1},{4,6},{5,7},{6,4},{7,5},{8,10},{9,11},{10,... | collective-permute-start | bytes 3145736 | tf_op jit(solution)/shard_map/ppermute | solution.py:269
  42.0 20.5 %collective-permute-start.10 = (bf16[2752,128]{1,0:T(8,128)(2,1)S(1)}, bf16[2752,128]{1,0:T(8,128)(2,1)S(1)}, u32[]{:S(2)}, u32[]{:S(2)}) collective-permute-start(bf16[2752,128]{1,0:T(8,128)(2,1)S(1)} %get-tuple-element.210), channel_id=1, source_target_pairs={{0,24},{4,28},{8,0},{12,4},{16,8},{20,12},{24,16},{28,20},{1,25},{... | collective-permute-start | bytes 2113544 | tf_op jit(solution)/shard_map/ppermute | solution.py:252
  46.3 18.7 %collective-permute-start.11 = (bf16[2752,128]{1,0:T(8,128)(2,1)S(1)}, bf16[2752,128]{1,0:T(8,128)(2,1)S(1)}, u32[]{:S(2)}, u32[]{:S(2)}) collective-permute-start(bf16[2752,128]{1,0:T(8,128)(2,1)S(1)} %get-tuple-element.210), channel_id=1, source_target_pairs={{0,4},{4,0},{8,12},{12,8},{16,20},{20,16},{24,28},{28,24},{1,5},{5... | collective-permute-start | bytes 2113544 | tf_op jit(solution)/shard_map/ppermute | solution.py:253
  46.9 40.6 %collective-permute-start.16 = (bf16[2752,128]{1,0:T(8,128)(2,1)}, bf16[2752,128]{1,0:T(8,128)(2,1)}, u32[]{:S(2)}, u32[]{:S(2)}) collective-permute-start(bf16[2752,128]{1,0:T(8,128)(2,1)} %get-tuple-element.231), channel_id=1, source_target_pairs={{0,24},{4,28},{8,0},{12,4},{16,8},{20,12},{24,16},{28,20},{1,25},{... | collective-permute-start | bytes 2113544 | tf_op jit(solution)/shard_map/ppermute | solution.py:252
  46.9 40.5 %collective-permute-start.18 = (bf16[2752,128]{1,0:T(8,128)(2,1)}, bf16[2752,128]{1,0:T(8,128)(2,1)}, u32[]{:S(2)}, u32[]{:S(2)}) collective-permute-start(bf16[2752,128]{1,0:T(8,128)(2,1)} %get-tuple-element.231), channel_id=1, source_target_pairs={{0,4},{4,0},{8,12},{12,8},{16,20},{20,16},{24,28},{28,24},{1,5},{5... | collective-permute-start | bytes 2113544 | tf_op jit(solution)/shard_map/ppermute | solution.py:253
  62.5 34.1 %collective-permute-start.19 = (bf16[2752,128]{1,0:T(8,128)(2,1)}, bf16[2752,128]{1,0:T(8,128)(2,1)}, u32[]{:S(2)}, u32[]{:S(2)}) collective-permute-start(bf16[2752,128]{1,0:T(8,128)(2,1)} %get-tuple-element.232), channel_id=1, source_target_pairs={{0,4},{4,0},{8,12},{12,8},{16,20},{20,16},{24,28},{28,24},{1,5},{5... | collective-permute-start | bytes 2113544 | tf_op jit(solution)/shard_map/ppermute | solution.py:253
  65.0 31.6 %collective-permute-start.17 = (bf16[2752,128]{1,0:T(8,128)(2,1)}, bf16[2752,128]{1,0:T(8,128)(2,1)}, u32[]{:S(2)}, u32[]{:S(2)}) collective-permute-start(bf16[2752,128]{1,0:T(8,128)(2,1)} %get-tuple-element.232), channel_id=1, source_target_pairs={{0,24},{4,28},{8,0},{12,4},{16,8},{20,12},{24,16},{28,20},{1,25},{... | collective-permute-start | bytes 2113544 | tf_op jit(solution)/shard_map/ppermute | solution.py:252
  79.3 7.6 %collective-permute-start.15 = (f32[448,128]{1,0:T(8,128)S(1)}, f32[448,128]{1,0:T(8,128)S(1)}, u32[]{:S(2)}, u32[]{:S(2)}) collective-permute-start(f32[448,128]{1,0:T(8,128)S(1)} %get-tuple-element.225), channel_id=1, source_target_pairs={{0,2},{1,3},{2,0},{3,1},{4,6},{5,7},{6,4},{7,5},{8,10},{9,11},{10,... | collective-permute-start | bytes 688136 | tf_op jit(solution)/shard_map/ppermute | solution.py:269
  86.9 9.7 %collective-permute-start.14 = (f32[320,128]{1,0:T(8,128)}, f32[320,128]{1,0:T(8,128)S(1)}, u32[]{:S(2)}, u32[]{:S(2)}) collective-permute-start(f32[320,128]{1,0:T(8,128)} %copy-done.16), channel_id=1, source_target_pairs={{0,2},{1,3},{2,0},{3,1},{4,6},{5,7},{6,4},{7,5},{8,10},{9,11},{10,... | collective-permute-start | bytes 491528 | tf_op jit(solution)/shard_map/ppermute | solution.py:269
  92.2 2.1 %collective-permute-start.5 = (f32[2,576,128]{2,1,0:T(8,128)S(1)}, f32[2,576,128]{2,1,0:T(8,128)S(1)}, u32[]{:S(2)}, u32[]{:S(2)}) collective-permute-start(f32[2,576,128]{2,1,0:T(8,128)S(1)} %get-tuple-element.151), channel_id=1, source_target_pairs={{0,1},{1,0},{2,3},{3,2},{4,5},{5,4},{6,7},{7,6},{8,9},{9,8},{10,11... | collective-permute-start | bytes 1769480 | tf_op jit(solution)/shard_map/cond/branch_1_fun/ppermute | solution.py:237
  95.1 11.0 %collective-permute-start.20 = (f32[576,128]{1,0:T(8,128)}, f32[576,128]{1,0:T(8,128)S(1)}, u32[]{:S(2)}, u32[]{:S(2)}) collective-permute-start(f32[576,128]{1,0:T(8,128)} %get-tuple-element.241), channel_id=1, source_target_pairs={{0,2},{1,3},{2,0},{3,1},{4,6},{5,7},{6,4},{7,5},{8,10},{9,11},{10,... | collective-permute-start | bytes 884744 | tf_op jit(solution)/shard_map/ppermute | solution.py:269
  102.3 2.3 %collective-permute-start.4 = (f32[2,704,128]{2,1,0:T(8,128)S(1)}, f32[2,704,128]{2,1,0:T(8,128)S(1)}, u32[]{:S(2)}, u32[]{:S(2)}) collective-permute-start(f32[2,704,128]{2,1,0:T(8,128)S(1)} %get-tuple-element.138), channel_id=1, source_target_pairs={{0,1},{1,0},{2,3},{3,2},{4,5},{5,4},{6,7},{7,6},{8,9},{9,8},{10,11... | collective-permute-start | bytes 2162696 | tf_op jit(solution)/shard_map/cond/branch_1_fun/ppermute | solution.py:237
  105.4 10.7 %collective-permute-start.21 = (f32[704,128]{1,0:T(8,128)}, f32[704,128]{1,0:T(8,128)S(1)}, u32[]{:S(2)}, u32[]{:S(2)}) collective-permute-start(f32[704,128]{1,0:T(8,128)} %copy-done.9), channel_id=1, source_target_pairs={{0,2},{1,3},{2,0},{3,1},{4,6},{5,7},{6,4},{7,5},{8,10},{9,11},{10,... | collective-permute-start | bytes 1081352 | tf_op jit(solution)/shard_map/ppermute | solution.py:269
  107.8 16.1 %collective-permute-start.22 = (f32[672,128]{1,0:T(8,128)S(1)}, f32[672,128]{1,0:T(8,128)S(1)}, u32[]{:S(2)}, u32[]{:S(2)}) collective-permute-start(f32[672,128]{1,0:T(8,128)S(1)} %get-tuple-element.244), channel_id=1, source_target_pairs={{0,8},{4,12},{8,16},{12,20},{16,24},{20,28},{24,0},{28,4},{1,9},{5... | collective-permute-start | bytes 1032200 | tf_op jit(solution)/shard_map/ppermute | solution.py:309
  116.2 7.7 %collective-permute-start.24 = (f32[352,128]{1,0:T(8,128)S(1)}, f32[352,128]{1,0:T(8,128)S(1)}, u32[]{:S(2)}, u32[]{:S(2)}) collective-permute-start(f32[352,128]{1,0:T(8,128)S(1)} %get-tuple-element.246), channel_id=1, source_target_pairs={{0,8},{4,12},{8,16},{12,20},{16,24},{20,28},{24,0},{28,4},{1,9},{5... | collective-permute-start | bytes 540680 | tf_op jit(solution)/shard_map/ppermute | solution.py:309
  116.3 6.4 %collective-permute-start.23 = (f32[288,128]{1,0:T(8,128)S(1)}, f32[288,128]{1,0:T(8,128)S(1)}, u32[]{:S(2)}, u32[]{:S(2)}) collective-permute-start(f32[288,128]{1,0:T(8,128)S(1)} %get-tuple-element.245), channel_id=1, source_target_pairs={{0,4},{4,0},{8,12},{12,8},{16,20},{20,16},{24,28},{28,24},{1,5},{5... | collective-permute-start | bytes 442376 | tf_op jit(solution)/shard_map/ppermute | solution.py:309
  117.8 6.0 %collective-permute-start.25 = (f32[224,128]{1,0:T(8,128)S(1)}, f32[224,128]{1,0:T(8,128)S(1)}, u32[]{:S(2)}, u32[]{:S(2)}) collective-permute-start(f32[224,128]{1,0:T(8,128)S(1)} %get-tuple-element.247), channel_id=1, source_target_pairs={{0,4},{4,0},{8,12},{12,8},{16,20},{20,16},{24,28},{28,24},{1,5},{5... | collective-permute-start | bytes 344072 | tf_op jit(solution)/shard_map/ppermute | solution.py:309
  (22 other events, 190.0 us)

commit v5 on v4

--- a/solution.py
+++ b/solution.py
@@ -14,19 +14,20 @@
 SUB = UNIT // WID
 VMEM_LIMIT = 24 << 20
 PIECES = ['A', '0', 'kS', '1', 'kA', '2', '3', 'k0', 'k1', 'k2', 'k3']
-GATES = {'R1': ['RA'], 'O1': ['OA'], 'R2': ['RA'], 'O2': ['OA'], 'R3': ['R0'], 'O3': ['O0'], 'KA': ['SS'], 'K0': ['SA', 'R1', 'O1'], 'K1': ['SA'], 'K2': ['S1'], 'K3': ['S0', 'S1'], 'SA': [], 'S0': ['SA'], 'S1': [], 'S2': [], 'S3': ['S0', 'S1'], 'G0': [], 'G1': []}
+GATES = {'R1': ['RA'], 'O1': ['OA'], 'R2': ['RA'], 'O2': ['OA'], 'R3': ['R1'], 'O3': ['O1'], 'KA': ['SS'], 'K0': ['SS'], 'K1': ['SA'], 'K2': ['S0'], 'K3': ['S0', 'S1'], 'SA': [], 'S0': ['SA'], 'S1': [], 'S2': [], 'S3': ['S0', 'S1'], 'G0': [], 'G1': []}
 PLAIN = []
 GROUPS = [[0, 1, 2], [3]]
 SMEM = pl.BlockSpec(memory_space=pltpu.SMEM)
 VMEM = pl.BlockSpec(memory_space=pltpu.VMEM)
 
 
-def call(kernel, outs, *args, scalars=0):
+def call(kernel, outs, *args, scalars=0, memory=VMEM, scratch=()):
     return pl.pallas_call(
         kernel,
         out_shape=outs,
-        in_specs=[SMEM] * scalars + [VMEM] * (len(args) - scalars),
+        in_specs=[SMEM] * scalars + [memory] * (len(args) - scalars),
         out_specs=jax.tree.map(lambda _: VMEM, outs),
+        scratch_shapes=scratch,
         cost_estimate=pl.CostEstimate(flops=2000000000, bytes_accessed=2000000, transcendentals=0),
         compiler_params=pltpu.CompilerParams(vmem_limit_bytes=VMEM_LIMIT),
     )(*args)
@@ -131,19 +132,56 @@
             put_third(place_ref, keep, send, layouts[step][0], base, a, b, lanes(block, b))
 
 
-def grads_kernel(step, spot, place_ref, own_ref, *refs):
+def grads_kernel(step, spot, place_ref, own_hbm, *refs):
     n = step + 1
-    mine, ring, other, (keep, send) = refs[:n], refs[n : 2 * n], refs[2 * n : 3 * n], refs[3 * n :]
+    mine, ring, other, (keep, send, own, fresh, chosen, others, sems) = refs[:n], refs[n : 2 * n], refs[2 * n : 3 * n], refs[3 * n :]
     even = place_ref[0] == 0
-    chosen = [jnp.where(even, ring[a][...], mine[a][...]) for a in range(n)]
-    put_ring(place_ref, keep, send, spot, 0, step, dot(ring[step][...].T, own_ref[...], ((1,), (0,))))
-    block = dot(chosen[step].T, jnp.concatenate([o[...] for o in other], axis=1), ((1,), (0,)))
+    half = own.shape[0] // 2
+
+    def column(ref, a):
+        return ref.at[:, a * UNIT : (a + 1) * UNIT]
+
+    copies = [
+        pltpu.make_async_copy(ring[step], fresh, sems.at[0]),
+        pltpu.make_async_copy(own_hbm.at[:half], own.at[:half], sems.at[1]),
+        pltpu.make_async_copy(own_hbm.at[half:], own.at[half:], sems.at[2]),
+    ]
+    third = [pltpu.make_async_copy(other[a], column(others, a), sems.at[3 + a]) for a in range(n)]
+    from_ring = [pltpu.make_async_copy(ring[a], column(chosen, a), sems.at[3 + n + a]) for a in range(n)]
+    from_mine = [pltpu.make_async_copy(mine[a], column(chosen, a), sems.at[3 + n + a]) for a in range(n)]
+    for copy in copies:
+        copy.start()
+
+    @pl.when(even)
+    def _():
+        for copy in from_ring:
+            copy.start()
+
+    @pl.when(jnp.logical_not(even))
+    def _():
+        for copy in from_mine:
+            copy.start()
+
+    for copy in third:
+        copy.start()
+    for copy in copies:
+        copy.wait()
+    put_ring(place_ref, keep, send, spot, 0, step, dot(fresh[...].T, own[...], ((1,), (0,))))
+    for copy in from_ring + third:
+        copy.wait()
+    block = dot(column(chosen, step)[...].T, others[...], ((1,), (0,)))
     for b in range(n):
         put_third(place_ref, keep, send, spot, 0, step, b, lanes(block, b))
     if step:
-        block = dot(other[step][...].T, jnp.concatenate(chosen[:step], axis=1), ((1,), (0,))).T
+        block = dot(column(others, step)[...].T, chosen[:, : step * UNIT], ((1,), (0,))).T
         for a in range(step):
             put_third(place_ref, keep, send, spot, 0, a, step, block[a * UNIT : (a + 1) * UNIT])
+
+
+def grads_scratch(own, n):
+    deep = own.shape[0]
+    arrays = [pltpu.VMEM((deep, width), jnp.bfloat16) for width in (own.shape[1], UNIT, n * UNIT, n * UNIT)]
+    return (*arrays, pltpu.SemaphoreType.DMA((3 + 2 * n,)))
 
 
 def product(acts, grads, act_at, grad_at, rows):
@@ -252,9 +290,9 @@
         seen["R" + name] = lax.ppermute(after(chunk, GATES.get("R" + name)), "tok", down)
         seen["O" + name] = lax.ppermute(after(chunk, GATES.get("O" + name)), "tok", swap)
 
-    def exchange(name, kernel, n, first, *rest):
+    def exchange(name, kernel, n, first, *rest, **options):
         def summed(*args):
-            keep, send = call(kernel, floats(n), place, *args, scalars=1)
+            keep, send = call(kernel, floats(n), place, *args, scalars=1, **options)
             arrived = over_core(send)
             return keep[0] + arrived[0], keep[1] + arrived[1]
 
@@ -294,6 +332,7 @@
             near[c] = seen["N%d" % c] = exchange(
                 piece[1], lambda *refs, c=c, spot=spot: grads_kernel(c, spot, *refs),
                 size, own_g, *mine[: c + 1], *[p[0] for p in pairs], *[p[1] for p in pairs],
+                memory=pl.BlockSpec(memory_space=pl.ANY), scratch=grads_scratch(own_g, c + 1),
             )
 
     returned = []

time: 126 us -> 123 us (0.976)
  waiting for transfers between devices: 57.1 us -> 51.4 us
  starting transfers between devices: 25.8 us -> 28.1 us
  local copies, waits for them, and re-layouts: 3.37 us -> 2.07 us
    ppermute x5, waiting for transfers between devices: 14.5 us -> 9.87 us  [start(): lax.ppermute(after(chunk, GATES.get('R' + name)), 'tok', down)]
    ppermute x5, starting transfers between devices: 10.6 us -> 14.3 us  [start(): lax.ppermute(after(chunk, GATES.get('R' + name)), 'tok', down)]
    ppermute x6, waiting for transfers between devices: 20.8 us -> 19.5 us  [exchange(): lax.ppermute(after(far, GATES.get('S' + name)), 'wid', [(w, w ^ 2) for w...]
    unnamed x40 -> x30, local copies, waits for them, and re-layouts: 3.28 us -> 1.98 us
  transfers between devices with their start and end apart: 26 -> 26, of which waited for: 14 -> 15; matrix products, arithmetic and copies ran while one was open for 2% -> 3% of each run, Pallas kernels for 27% -> 28%
where the time goes in v5:
time: 123 us
  waiting for transfers between devices  51.4 us (42%)
  Pallas kernels  36.9 us (30%)
  starting transfers between devices  28.1 us (23%)
  other arithmetic  3.38 us (3%)
  local copies, waits for them, and re-layouts  2.07 us (2%)
    pallas_call x10, Pallas kernels, call(): pl.pallas_call(kernel, out_shape=outs, in_specs=[SMEM] * scalars + [memor...  36.9 us
    ppermute x6, waiting for transfers between devices, exchange(): lax.ppermute(after(far, GATES.get('S' + name)), 'wid', [(w, w ^ 2) for w...  19.5 us
    ppermute x6, waiting for transfers between devices, over_core(): return lax.ppermute(send, 'wid', [(w, w ^ 1) for w in range(WID)])  14.4 us
    ppermute x5, starting transfers between devices, start(): lax.ppermute(after(chunk, GATES.get('R' + name)), 'tok', down)  14.3 us
    ppermute x5, waiting for transfers between devices, start(): lax.ppermute(after(chunk, GATES.get('R' + name)), 'tok', down)  9.87 us
    ppermute x6, starting transfers between devices, exchange(): lax.ppermute(after(far, GATES.get('S' + name)), 'wid', [(w, w ^ 2) for w...  6.12 us
    ppermute x2, waiting for transfers between devices, shards(): lax.ppermute(swapped, 'tok', swap)  5.49 us
    ppermute x5, starting transfers between devices, start(): lax.ppermute(after(chunk, GATES.get('O' + name)), 'tok', swap)  5.08 us
  transfers between devices with their start and end apart: 26, of which 15 were waited for; matrix products, arithmetic and copies ran while one was open for 3% of the time, Pallas kernels for 28%

profile of v5, /device:TPU:0, one launch (start us, length us, event | category | flops | bytes accessed | tf_op | source)
XLA Modules:
  0.0 122.8 jit_solution(2468789773378729146)
XLA Ops:
  0.0 2.9 %collective-permute-start.8 = (bf16[512,1024]{1,0:T(8,128)(2,1)}, bf16[512,1024]{1,0:T(8,128)(2,1)}, u32[]{:S(2)}, u32[]{:S(2)}) collective-permute-start(bf16[512,1024]{1,0:T(8,128)(2,1)} %param.15), channel_id=1, source_target_pairs={{0,4},{4,0},{8,12},{12,8},{16,20},{20,16},{24,28},{28,24},{1,5},{5... | collective-permute-start | bytes 3145736 | tf_op jit(solution)/shard_map/ppermute | solution.py:291
  2.9 3.6 %collective-permute-start.7 = (bf16[512,1024]{1,0:T(8,128)(2,1)}, bf16[512,1024]{1,0:T(8,128)(2,1)}, u32[]{:S(2)}, u32[]{:S(2)}) collective-permute-start(bf16[512,1024]{1,0:T(8,128)(2,1)} %param.15), channel_id=1, source_target_pairs={{0,24},{4,28},{8,0},{12,4},{16,8},{20,12},{24,16},{28,20},{1,25},{... | collective-permute-start | bytes 3145736 | tf_op jit(solution)/shard_map/ppermute | solution.py:290
  8.6 7.3 %conditional.6 = (f32[1024,128]{1,0:T(8,128)S(1)}, f32[1024,128]{1,0:T(8,128)S(1)}) conditional(s32[]{:T(128)} %convert_element_type.2, () %tuple.66, (s32[5]{0:T(128)S(1)}, bf16[512,1024]{1,0:T(8,128)(2,1)}, bf16[2752,512]{1,0:T(8,128)(2,1)}) %tuple.109), branch_computations={%region_1.2_spmd, %region_2.3_spmd} | conditional | flops 2000262144 | bytes 9340088 | solution.py:306
  8.6 4.5 %branch_1_fun.6 = (f32[2,1024,128]{2,1,0:T(8,128)S(1)}, f32[2,1024,128]{2,1,0:T(8,128)S(1)}) custom-call(s32[5]{0:T(128)S(1)} %get-tuple-element.95.place_ref, bf16[512,1024]{1,0:T(8,128)(2,1)} %get-tuple-element.96.a_ref, bf16[2752,512]{1,0:T(8,128)(2,1)} %get-tuple-element.97.g_ref), custom_call_target="tpu_custom_call" | custom-call | flops 2000000000 | bytes 2000000 | tf_op jit(solution)/shard_map/cond/branch_1_fun/pallas_call | solution.py:25
  13.2 2.6 %collective-permute-done = f32[2,1024,128]{2,1,0:T(8,128)S(1)} collective-permute-done((f32[2,1024,128]{2,1,0:T(8,128)S(1)}, f32[2,1024,128]{2,1,0:T(8,128)S(1)}, u32[]{:S(2)}, u32[]{:S(2)}) %collective-permute-start) | collective-permute-done | bytes 1048608 | tf_op jit(solution)/shard_map/cond/branch_1_fun/ppermute | solution.py:275
  17.6 6.0 %shard_map.37 = (bf16[2752,128]{1,0:T(8,128)(2,1)S(1)}, bf16[2752,128]{1,0:T(8,128)(2,1)S(1)}, bf16[2752,128]{1,0:T(8,128)(2,1)}, bf16[2752,128]{1,0:T(8,128)(2,1)}) custom-call(bf16[2752,512]{1,0:T(8,128)(2,1)} %bitcast.32), custom_call_target="tpu_custom_call" | custom-call | flops 2000000000 | bytes 2000000 | tf_op jit(solution)/shard_map/pallas_call | solution.py:25
  24.6 5.5 %collective-permute-done.6.refs_3_ = f32[1024,128]{1,0:T(8,128)S(1)} collective-permute-done((f32[1024,128]{1,0:T(8,128)S(1)}, f32[1024,128]{1,0:T(8,128)S(1)}, u32[]{:S(2)}, u32[]{:S(2)}) %collective-permute-start.6) | collective-permute-done | bytes 524320 | tf_op jit(solution)/shard_map/ppermute | solution.py:307
  30.5 9.1 %conditional.7 = (f32[2048,128]{1,0:T(8,128)S(1)}, f32[2048,128]{1,0:T(8,128)S(1)}) conditional(s32[]{:T(128)} %convert_element_type.2, () %tuple.70, (s32[5]{0:T(128)S(1)}, bf16[512,1024]{1,0:T(8,128)(2,1)S(1)}, bf16[512,1024]{1,0:T(8,128)(2,1)}, bf16[512,1024]{1,0:T(8,128)(2,1)}) %tuple.115), branch_computations={%region_3.4_spmd, %region_4.5_spmd} | conditional | flops 2000524288 | bytes 16680120 | solution.py:306
  30.5 4.6 %branch_1_fun.7 = (f32[2,2048,128]{2,1,0:T(8,128)S(1)}, f32[2,2048,128]{2,1,0:T(8,128)S(1)}) custom-call(s32[5]{0:T(128)S(1)} %get-tuple-element.100.refs_0_, bf16[512,1024]{1,0:T(8,128)(2,1)S(1)} %get-tuple-element.101.refs_1_, bf16[512,1024]{1,0:T(8,128)(2,1)} %get-tuple-element.102.refs_2_, bf16[512,1024]{1,0:T(8,128)(2,1)} %get-tuple-element.103.refs_3_), custom_call_target="tpu_custom_call" | custom-call | flops 2000000000 | bytes 2000000 | tf_op jit(solution)/shard_map/cond/branch_1_fun/pallas_call | solution.py:25
  35.1 4.1 %collective-permute-done.1 = f32[2,2048,128]{2,1,0:T(8,128)S(1)} collective-permute-done((f32[2,2048,128]{2,1,0:T(8,128)S(1)}, f32[2,2048,128]{2,1,0:T(8,128)S(1)}, u32[]{:S(2)}, u32[]{:S(2)}) %collective-permute-start.1) | collective-permute-done | bytes 2097184 | tf_op jit(solution)/shard_map/cond/branch_1_fun/ppermute | solution.py:275
  42.0 4.3 %collective-permute-start.13 = (bf16[2752,128]{1,0:T(8,128)(2,1)S(1)}, bf16[2752,128]{1,0:T(8,128)(2,1)}, u32[]{:S(2)}, u32[]{:S(2)}) collective-permute-start(bf16[2752,128]{1,0:T(8,128)(2,1)S(1)} %get-tuple-element.220), channel_id=1, source_target_pairs={{0,24},{4,28},{8,0},{12,4},{16,8},{20,12},{24,16},{28,20},{1,25},{... | collective-permute-start | bytes 2113544 | tf_op jit(solution)/shard_map/ppermute | solution.py:290
  46.8 5.5 %conditional.8 = (f32[320,128]{1,0:T(8,128)S(1)}, f32[320,128]{1,0:T(8,128)S(1)}) conditional(s32[]{:T(128)} %convert_element_type.2, () %tuple.74, (s32[5]{0:T(128)S(1)}, bf16[2752,512]{1,0:T(8,128)(2,1)}, bf16[2752,128]{1,0:T(8,128)(2,1)S(1)}, bf16[2752,128]{1,0:T(8,128)(2,1)}, bf16[2752,128]{1,0:T(8,128)(2,1)}) %tuple.110), branch_computations={%region_5.6_spmd, %region_6.7_spmd} | conditional | flops 2000081920 | bytes 4293816 | solution.py:306
  46.9 3.7 %branch_1_fun.8 = (f32[2,320,128]{2,1,0:T(8,128)S(1)}, f32[2,320,128]{2,1,0:T(8,128)S(1)}) custom-call(s32[5]{0:T(128)S(1)} %get-tuple-element.106.refs_0_, bf16[2752,512]{1,0:T(8,128)(2,1)} %get-tuple-element.107.refs_1_, bf16[2752,128]{1,0:T(8,128)(2,1)S(1)} %get-tuple-element.108.refs_2_, bf16[2752,128]{1,0:T(8,128)(2,1)} %get-tuple-element.109.refs_3_, ...), custom_call_target="tpu_custom_call" | custom-call | flops 2000000000 | bytes 2000000 | tf_op jit(solution)/shard_map/cond/branch_1_fun/pallas_call | solution.py:25
  54.4 8.0 %collective-permute-done.13 = bf16[2752,128]{1,0:T(8,128)(2,1)} collective-permute-done((bf16[2752,128]{1,0:T(8,128)(2,1)S(1)}, bf16[2752,128]{1,0:T(8,128)(2,1)}, u32[]{:S(2)}, u32[]{:S(2)}) %collective-permute-start.13) | collective-permute-done | bytes 704544 | tf_op jit(solution)/shard_map/ppermute | solution.py:290
  62.5 4.4 %collective-permute-start.17 = (bf16[2752,128]{1,0:T(8,128)(2,1)}, bf16[2752,128]{1,0:T(8,128)(2,1)}, u32[]{:S(2)}, u32[]{:S(2)}) collective-permute-start(bf16[2752,128]{1,0:T(8,128)(2,1)} %get-tuple-element.228), channel_id=1, source_target_pairs={{0,24},{4,28},{8,0},{12,4},{16,8},{20,12},{24,16},{28,20},{1,25},{... | collective-permute-start | bytes 2113544 | tf_op jit(solution)/shard_map/ppermute | solution.py:290
  67.4 6.8 %conditional.9 = (f32[448,128]{1,0:T(8,128)S(1)}, f32[448,128]{1,0:T(8,128)}) conditional(s32[]{:T(128)} %convert_element_type.2, () %tuple.80, (s32[5]{0:T(128)S(1)}, bf16[2752,512]{1,0:T(8,128)(2,1)}, bf16[2752,128]{1,0:T(8,128)(2,1)S(1)}, bf16[2752,128]{1,0:T(8,128)(2,1)S(1)}, bf16[2752,128]{1,0:T(8,128)(2,1)}, ...), branch_computations={%region_7.8_spmd, %region_8.9_spmd} | conditional | flops 2000114688 | bytes 5211320 | solution.py:306
  67.4 4.1 %branch_1_fun.9 = (f32[2,448,128]{2,1,0:T(8,128)S(1)}, f32[2,448,128]{2,1,0:T(8,128)S(1)}) custom-call(s32[5]{0:T(128)S(1)} %get-tuple-element.113.refs_0_, bf16[2752,512]{1,0:T(8,128)(2,1)} %get-tuple-element.114.refs_1_, bf16[2752,128]{1,0:T(8,128)(2,1)S(1)} %get-tuple-element.115.refs_2_, bf16[2752,128]{1,0:T(8,128)(2,1)S(1)} %get-tuple-element.116.refs_3_, ...), custom_call_target="tpu_custom_call" | custom-call | flops 2000000000 | bytes 2000000 | tf_op jit(solution)/shard_map/cond/branch_1_fun/pallas_call | solution.py:25
  74.7 5.7 %collective-permute-done.12.refs_3_.refs_7_ = f32[320,128]{1,0:T(8,128)S(1)} collective-permute-done((f32[320,128]{1,0:T(8,128)S(1)}, f32[320,128]{1,0:T(8,128)S(1)}, u32[]{:S(2)}, u32[]{:S(2)}) %collective-permute-start.12) | collective-permute-done | bytes 163872 | tf_op jit(solution)/shard_map/ppermute | solution.py:307
  80.9 7.8 %conditional.11 = (f32[576,128]{1,0:T(8,128)S(1)}, f32[576,128]{1,0:T(8,128)}) conditional(s32[]{:T(128)} %convert_element_type.2, () %tuple.89, (s32[5]{0:T(128)S(1)}, bf16[2752,512]{1,0:T(8,128)(2,1)}, bf16[2752,128]{1,0:T(8,128)(2,1)S(1)}, bf16[2752,128]{1,0:T(8,128)(2,1)S(1)}, bf16[2752,128]{1,0:T(8,128)(2,1)}, ...), branch_computations={%region_11.12_spmd, %region_12.13_spmd} | conditional | flops 2000147456 | bytes 6128824 | solution.py:306
  81.0 4.9 %branch_1_fun.11 = (f32[2,576,128]{2,1,0:T(8,128)S(1)}, f32[2,576,128]{2,1,0:T(8,128)S(1)}) custom-call(s32[5]{0:T(128)S(1)} %get-tuple-element.139.refs_0_, bf16[2752,512]{1,0:T(8,128)(2,1)} %get-tuple-element.140.refs_1_, bf16[2752,128]{1,0:T(8,128)(2,1)S(1)} %get-tuple-element.141.refs_2_, bf16[2752,128]{1,0:T(8,128)(2,1)S(1)} %get-tuple-element.142.refs_3_, ...), custom_call_target="tpu_custom_call" | custom-call | flops 2000000000 | bytes 2000000 | tf_op jit(solution)/shard_map/cond/branch_1_fun/pallas_call | solution.py:25
  93.9 7.7 %conditional.10 = (f32[704,128]{1,0:T(8,128)S(1)}, f32[704,128]{1,0:T(8,128)S(1)}) conditional(s32[]{:T(128)} %convert_element_type.2, () %tuple.78, (s32[5]{0:T(128)S(1)}, bf16[2752,512]{1,0:T(8,128)(2,1)}, bf16[2752,128]{1,0:T(8,128)(2,1)S(1)}, bf16[2752,128]{1,0:T(8,128)(2,1)}, bf16[2752,128]{1,0:T(8,128)(2,1)}, ...), branch_computations={%region_9.10_spmd, %region_10.11_spmd} | conditional | flops 2000180224 | bytes 7046328 | solution.py:306
  93.9 5.4 %branch_1_fun.10 = (f32[2,704,128]{2,1,0:T(8,128)S(1)}, f32[2,704,128]{2,1,0:T(8,128)S(1)}) custom-call(s32[5]{0:T(128)S(1)} %get-tuple-element.123.refs_0_, bf16[2752,512]{1,0:T(8,128)(2,1)} %get-tuple-element.124.refs_1_, bf16[2752,128]{1,0:T(8,128)(2,1)S(1)} %get-tuple-element.125.refs_2_, bf16[2752,128]{1,0:T(8,128)(2,1)} %get-tuple-element.126.refs_3_, ...), custom_call_target="tpu_custom_call" | custom-call | flops 2000000000 | bytes 2000000 | tf_op jit(solution)/shard_map/cond/branch_1_fun/pallas_call | solution.py:25
  104.7 8.3 %collective-permute-done.21.refs_3_.refs_13_ = f32[704,128]{1,0:T(8,128)S(1)} collective-permute-done((f32[704,128]{1,0:T(8,128)}, f32[704,128]{1,0:T(8,128)S(1)}, u32[]{:S(2)}, u32[]{:S(2)}) %collective-permute-start.21) | collective-permute-done | bytes 360480 | tf_op jit(solution)/shard_map/ppermute | solution.py:307
  115.3 4.3 %collective-permute-done.23.refs_15_ = f32[288,128]{1,0:T(8,128)S(1)} collective-permute-done((f32[288,128]{1,0:T(8,128)S(1)}, f32[288,128]{1,0:T(8,128)S(1)}, u32[]{:S(2)}, u32[]{:S(2)}) %collective-permute-start.23) | collective-permute-done | bytes 147488 | tf_op jit(solution)/shard_map/ppermute | solution.py:348
  (82 shorter events, 34.9 us)
Async XLA Ops:
  0.0 30.0 %collective-permute-start.8 = (bf16[512,1024]{1,0:T(8,128)(2,1)}, bf16[512,1024]{1,0:T(8,128)(2,1)}, u32[]{:S(2)}, u32[]{:S(2)}) collective-permute-start(bf16[512,1024]{1,0:T(8,128)(2,1)} %param.15), channel_id=1, source_target_pairs={{0,4},{4,0},{8,12},{12,8},{16,20},{20,16},{24,28},{28,24},{1,5},{5... | collective-permute-start | bytes 3145736 | tf_op jit(solution)/shard_map/ppermute | solution.py:291
  2.9 27.5 %collective-permute-start.7 = (bf16[512,1024]{1,0:T(8,128)(2,1)}, bf16[512,1024]{1,0:T(8,128)(2,1)}, u32[]{:S(2)}, u32[]{:S(2)}) collective-permute-start(bf16[512,1024]{1,0:T(8,128)(2,1)} %param.15), channel_id=1, source_target_pairs={{0,24},{4,28},{8,0},{12,4},{16,8},{20,12},{24,16},{28,20},{1,25},{... | collective-permute-start | bytes 3145736 | tf_op jit(solution)/shard_map/ppermute | solution.py:290
  13.1 2.7 %collective-permute-start = (f32[2,1024,128]{2,1,0:T(8,128)S(1)}, f32[2,1024,128]{2,1,0:T(8,128)S(1)}, u32[]{:S(2)}, u32[]{:S(2)}) collective-permute-start(f32[2,1024,128]{2,1,0:T(8,128)S(1)} %get-tuple-element.99), channel_id=1, source_target_pairs={{0,1},{1,0},{2,3},{3,2},{4,5},{5,4},{6,7},{7,6},{8,9},{9,8},{10,11... | collective-permute-start | bytes 3145736 | tf_op jit(solution)/shard_map/cond/branch_1_fun/ppermute | solution.py:275
  16.0 14.0 %collective-permute-start.6 = (f32[1024,128]{1,0:T(8,128)S(1)}, f32[1024,128]{1,0:T(8,128)S(1)}, u32[]{:S(2)}, u32[]{:S(2)}) collective-permute-start(f32[1024,128]{1,0:T(8,128)S(1)} %get-tuple-element.199), channel_id=1, source_target_pairs={{0,2},{1,3},{2,0},{3,1},{4,6},{5,7},{6,4},{7,5},{8,10},{9,11},{10,... | collective-permute-start | bytes 1572872 | tf_op jit(solution)/shard_map/ppermute | solution.py:307
  23.6 23.2 %collective-permute-start.10 = (bf16[2752,128]{1,0:T(8,128)(2,1)S(1)}, bf16[2752,128]{1,0:T(8,128)(2,1)}, u32[]{:S(2)}, u32[]{:S(2)}) collective-permute-start(bf16[2752,128]{1,0:T(8,128)(2,1)S(1)} %get-tuple-element.208), channel_id=1, source_target_pairs={{0,4},{4,0},{8,12},{12,8},{16,20},{20,16},{24,28},{28,24},{1,5},{5... | collective-permute-start | bytes 2113544 | tf_op jit(solution)/shard_map/ppermute | solution.py:291
  24.1 22.7 %collective-permute-start.9 = (bf16[2752,128]{1,0:T(8,128)(2,1)S(1)}, bf16[2752,128]{1,0:T(8,128)(2,1)}, u32[]{:S(2)}, u32[]{:S(2)}) collective-permute-start(bf16[2752,128]{1,0:T(8,128)(2,1)S(1)} %get-tuple-element.208), channel_id=1, source_target_pairs={{0,24},{4,28},{8,0},{12,4},{16,8},{20,12},{24,16},{28,20},{1,25},{... | collective-permute-start | bytes 2113544 | tf_op jit(solution)/shard_map/ppermute | solution.py:290
  35.0 4.2 %collective-permute-start.1 = (f32[2,2048,128]{2,1,0:T(8,128)S(1)}, f32[2,2048,128]{2,1,0:T(8,128)S(1)}, u32[]{:S(2)}, u32[]{:S(2)}) collective-permute-start(f32[2,2048,128]{2,1,0:T(8,128)S(1)} %get-tuple-element.105), channel_id=1, source_target_pairs={{0,1},{1,0},{2,3},{3,2},{4,5},{5,4},{6,7},{7,6},{8,9},{9,8},{10,11... | collective-permute-start | bytes 6291464 | tf_op jit(solution)/shard_map/cond/branch_1_fun/ppermute | solution.py:275
  40.5 26.9 %collective-permute-start.11 = (f32[2048,128]{1,0:T(8,128)}, f32[2048,128]{1,0:T(8,128)S(1)}, u32[]{:S(2)}, u32[]{:S(2)}) collective-permute-start(f32[2048,128]{1,0:T(8,128)} %copy-done.2), channel_id=1, source_target_pairs={{0,2},{1,3},{2,0},{3,1},{4,6},{5,7},{6,4},{7,5},{8,10},{9,11},{10,... | collective-permute-start | bytes 3145736 | tf_op jit(solution)/shard_map/ppermute | solution.py:307
  42.0 20.5 %collective-permute-start.13 = (bf16[2752,128]{1,0:T(8,128)(2,1)S(1)}, bf16[2752,128]{1,0:T(8,128)(2,1)}, u32[]{:S(2)}, u32[]{:S(2)}) collective-permute-start(bf16[2752,128]{1,0:T(8,128)(2,1)S(1)} %get-tuple-element.220), channel_id=1, source_target_pairs={{0,24},{4,28},{8,0},{12,4},{16,8},{20,12},{24,16},{28,20},{1,25},{... | collective-permute-start | bytes 2113544 | tf_op jit(solution)/shard_map/ppermute | solution.py:290
  46.3 20.6 %collective-permute-start.14 = (bf16[2752,128]{1,0:T(8,128)(2,1)S(1)}, bf16[2752,128]{1,0:T(8,128)(2,1)}, u32[]{:S(2)}, u32[]{:S(2)}) collective-permute-start(bf16[2752,128]{1,0:T(8,128)(2,1)S(1)} %get-tuple-element.220), channel_id=1, source_target_pairs={{0,4},{4,0},{8,12},{12,8},{16,20},{20,16},{24,28},{28,24},{1,5},{5... | collective-permute-start | bytes 2113544 | tf_op jit(solution)/shard_map/ppermute | solution.py:291
  52.3 28.6 %collective-permute-start.16 = (bf16[2752,128]{1,0:T(8,128)(2,1)}, bf16[2752,128]{1,0:T(8,128)(2,1)}, u32[]{:S(2)}, u32[]{:S(2)}) collective-permute-start(bf16[2752,128]{1,0:T(8,128)(2,1)} %get-tuple-element.227), channel_id=1, source_target_pairs={{0,24},{4,28},{8,0},{12,4},{16,8},{20,12},{24,16},{28,20},{1,25},{... | collective-permute-start | bytes 2113544 | tf_op jit(solution)/shard_map/ppermute | solution.py:290
  53.9 27.0 %collective-permute-start.18 = (bf16[2752,128]{1,0:T(8,128)(2,1)}, bf16[2752,128]{1,0:T(8,128)(2,1)}, u32[]{:S(2)}, u32[]{:S(2)}) collective-permute-start(bf16[2752,128]{1,0:T(8,128)(2,1)} %get-tuple-element.227), channel_id=1, source_target_pairs={{0,4},{4,0},{8,12},{12,8},{16,20},{20,16},{24,28},{28,24},{1,5},{5... | collective-permute-start | bytes 2113544 | tf_op jit(solution)/shard_map/ppermute | solution.py:291
  62.5 29.2 %collective-permute-start.17 = (bf16[2752,128]{1,0:T(8,128)(2,1)}, bf16[2752,128]{1,0:T(8,128)(2,1)}, u32[]{:S(2)}, u32[]{:S(2)}) collective-permute-start(bf16[2752,128]{1,0:T(8,128)(2,1)} %get-tuple-element.228), channel_id=1, source_target_pairs={{0,24},{4,28},{8,0},{12,4},{16,8},{20,12},{24,16},{28,20},{1,25},{... | collective-permute-start | bytes 2113544 | tf_op jit(solution)/shard_map/ppermute | solution.py:290
  66.9 27.0 %collective-permute-start.19 = (bf16[2752,128]{1,0:T(8,128)(2,1)}, bf16[2752,128]{1,0:T(8,128)(2,1)}, u32[]{:S(2)}, u32[]{:S(2)}) collective-permute-start(bf16[2752,128]{1,0:T(8,128)(2,1)} %get-tuple-element.228), channel_id=1, source_target_pairs={{0,4},{4,0},{8,12},{12,8},{16,20},{20,16},{24,28},{28,24},{1,5},{5... | collective-permute-start | bytes 2113544 | tf_op jit(solution)/shard_map/ppermute | solution.py:291
  74.2 6.2 %collective-permute-start.12 = (f32[320,128]{1,0:T(8,128)S(1)}, f32[320,128]{1,0:T(8,128)S(1)}, u32[]{:S(2)}, u32[]{:S(2)}) collective-permute-start(f32[320,128]{1,0:T(8,128)S(1)} %get-tuple-element.214), channel_id=1, source_target_pairs={{0,2},{1,3},{2,0},{3,1},{4,6},{5,7},{6,4},{7,5},{8,10},{9,11},{10,... | collective-permute-start | bytes 491528 | tf_op jit(solution)/shard_map/ppermute | solution.py:307
  80.4 9.8 %collective-permute-start.15 = (f32[448,128]{1,0:T(8,128)}, f32[448,128]{1,0:T(8,128)S(1)}, u32[]{:S(2)}, u32[]{:S(2)}) collective-permute-start(f32[448,128]{1,0:T(8,128)} %get-tuple-element.222), channel_id=1, source_target_pairs={{0,2},{1,3},{2,0},{3,1},{4,6},{5,7},{6,4},{7,5},{8,10},{9,11},{10,... | collective-permute-start | bytes 688136 | tf_op jit(solution)/shard_map/ppermute | solution.py:307
  85.9 2.1 %collective-permute-start.5 = (f32[2,576,128]{2,1,0:T(8,128)S(1)}, f32[2,576,128]{2,1,0:T(8,128)S(1)}, u32[]{:S(2)}, u32[]{:S(2)}) collective-permute-start(f32[2,576,128]{2,1,0:T(8,128)S(1)} %get-tuple-element.151), channel_id=1, source_target_pairs={{0,1},{1,0},{2,3},{3,2},{4,5},{5,4},{6,7},{7,6},{8,9},{9,8},{10,11... | collective-permute-start | bytes 1769480 | tf_op jit(solution)/shard_map/cond/branch_1_fun/ppermute | solution.py:275
  88.7 14.1 %collective-permute-start.20 = (f32[576,128]{1,0:T(8,128)}, f32[576,128]{1,0:T(8,128)S(1)}, u32[]{:S(2)}, u32[]{:S(2)}) collective-permute-start(f32[576,128]{1,0:T(8,128)} %get-tuple-element.237), channel_id=1, source_target_pairs={{0,2},{1,3},{2,0},{3,1},{4,6},{5,7},{6,4},{7,5},{8,10},{9,11},{10,... | collective-permute-start | bytes 884744 | tf_op jit(solution)/shard_map/ppermute | solution.py:307
  99.3 2.3 %collective-permute-start.4 = (f32[2,704,128]{2,1,0:T(8,128)S(1)}, f32[2,704,128]{2,1,0:T(8,128)S(1)}, u32[]{:S(2)}, u32[]{:S(2)}) collective-permute-start(f32[2,704,128]{2,1,0:T(8,128)S(1)} %get-tuple-element.138), channel_id=1, source_target_pairs={{0,1},{1,0},{2,3},{3,2},{4,5},{5,4},{6,7},{7,6},{8,9},{9,8},{10,11... | collective-permute-start | bytes 2162696 | tf_op jit(solution)/shard_map/cond/branch_1_fun/ppermute | solution.py:275
  102.4 10.7 %collective-permute-start.21 = (f32[704,128]{1,0:T(8,128)}, f32[704,128]{1,0:T(8,128)S(1)}, u32[]{:S(2)}, u32[]{:S(2)}) collective-permute-start(f32[704,128]{1,0:T(8,128)} %copy-done.7), channel_id=1, source_target_pairs={{0,2},{1,3},{2,0},{3,1},{4,6},{5,7},{6,4},{7,5},{8,10},{9,11},{10,... | collective-permute-start | bytes 1081352 | tf_op jit(solution)/shard_map/ppermute | solution.py:307
  104.7 14.9 %collective-permute-start.22 = (f32[672,128]{1,0:T(8,128)S(1)}, f32[672,128]{1,0:T(8,128)S(1)}, u32[]{:S(2)}, u32[]{:S(2)}) collective-permute-start(f32[672,128]{1,0:T(8,128)S(1)} %get-tuple-element.240), channel_id=1, source_target_pairs={{0,8},{4,12},{8,16},{12,20},{16,24},{20,28},{24,0},{28,4},{1,9},{5... | collective-permute-start | bytes 1032200 | tf_op jit(solution)/shard_map/ppermute | solution.py:348
  113.1 7.7 %collective-permute-start.24 = (f32[352,128]{1,0:T(8,128)S(1)}, f32[352,128]{1,0:T(8,128)S(1)}, u32[]{:S(2)}, u32[]{:S(2)}) collective-permute-start(f32[352,128]{1,0:T(8,128)S(1)} %get-tuple-element.242), channel_id=1, source_target_pairs={{0,8},{4,12},{8,16},{12,20},{16,24},{20,28},{24,0},{28,4},{1,9},{5... | collective-permute-start | bytes 540680 | tf_op jit(solution)/shard_map/ppermute | solution.py:348
  113.2 6.4 %collective-permute-start.23 = (f32[288,128]{1,0:T(8,128)S(1)}, f32[288,128]{1,0:T(8,128)S(1)}, u32[]{:S(2)}, u32[]{:S(2)}) collective-permute-start(f32[288,128]{1,0:T(8,128)S(1)} %get-tuple-element.241), channel_id=1, source_target_pairs={{0,4},{4,0},{8,12},{12,8},{16,20},{20,16},{24,28},{28,24},{1,5},{5... | collective-permute-start | bytes 442376 | tf_op jit(solution)/shard_map/ppermute | solution.py:348
  113.6 7.2 %collective-permute-start.25 = (f32[224,128]{1,0:T(8,128)S(1)}, f32[224,128]{1,0:T(8,128)S(1)}, u32[]{:S(2)}, u32[]{:S(2)}) collective-permute-start(f32[224,128]{1,0:T(8,128)S(1)} %get-tuple-element.243), channel_id=1, source_target_pairs={{0,4},{4,0},{8,12},{12,8},{16,20},{20,16},{24,28},{28,24},{1,5},{5... | collective-permute-start | bytes 344072 | tf_op jit(solution)/shard_map/ppermute | solution.py:348
  (17 other events, 154.6 us)

commit v6 on v5

--- a/solution.py
+++ b/solution.py
@@ -12,11 +12,12 @@
 WID = 4
 UNIT = 128
 SUB = UNIT // WID
+WHOLE = 3
 VMEM_LIMIT = 24 << 20
-PIECES = ['A', '0', 'kS', '1', 'kA', '2', '3', 'k0', 'k1', 'k2', 'k3']
-GATES = {'R1': ['RA'], 'O1': ['OA'], 'R2': ['RA'], 'O2': ['OA'], 'R3': ['R1'], 'O3': ['O1'], 'KA': ['SS'], 'K0': ['SS'], 'K1': ['SA'], 'K2': ['S0'], 'K3': ['S0', 'S1'], 'SA': [], 'S0': ['SA'], 'S1': [], 'S2': [], 'S3': ['S0', 'S1'], 'G0': [], 'G1': []}
+PIECES = ["A", "0", "kS", "1", "kA", "2", "3", "k0", "4", "k1", "k2", "k3", "k4"]
+GATES = {"R1": ["RA"], "O1": ["OA"], "R2": ["RA"], "O2": ["OA"], "R3": ["R1"], "O3": ["O1"], "R4": ["R2"], "O4": ["O2"], "KA": ["SS"], "K0": ["SS"], "K1": ["SA"], "K2": ["S0"], "K3": ["S0", "S1"], "K4": ["S1"], "S0": ["SA"]}
 PLAIN = []
-GROUPS = [[0, 1, 2], [3]]
+GROUPS = [[0, 1, 2, 3], [4]]
 SMEM = pl.BlockSpec(memory_space=pltpu.SMEM)
 VMEM = pl.BlockSpec(memory_space=pltpu.VMEM)
 
@@ -28,7 +29,7 @@
         in_specs=[SMEM] * scalars + [memory] * (len(args) - scalars),
         out_specs=jax.tree.map(lambda _: VMEM, outs),
         scratch_shapes=scratch,
-        cost_estimate=pl.CostEstimate(flops=2000000000, bytes_accessed=2000000, transcendentals=0),
+        cost_estimate=pl.CostEstimate(flops=0, bytes_accessed=0, transcendentals=0),
         compiler_params=pltpu.CompilerParams(vmem_limit_bytes=VMEM_LIMIT),
     )(*args)
 
@@ -61,44 +62,90 @@
     return block[:, b * UNIT : (b + 1) * UNIT]
 
 
-def step_layout(step, units):
-    fresh = [(step, b) for b in range(step + 1)] + [(a, step) for a in range(step)]
-    at, spot = UNIT, {("rt", step): 0}
-    for a, b in fresh:
-        spot[("tt", b, a)] = at
-        at += SUB
-    n_ring = at
-    for a, b in fresh:
-        spot[("tj", a, b)] = at
-        at += SUB
-    n_swap = at
-    for b in range(WID):
-        spot[("rj", step, b)] = at
-        at += SUB
-    return spot, n_ring, n_swap, at
+def step_layouts():
+    layouts = []
+    for step in range(WHOLE + 2):
+        half = step - WHOLE
+        if half < 0:
+            names = [(step, b) for b in range(step + 1)] + [(a, step) for a in range(step)]
+            rt, size = UNIT, SUB
+        else:
+            names = [(step, b) for b in range(WHOLE)] + [(step, "p")] + [(a, step) for a in range(WHOLE)] + [("p", step)] * half
+            rt, size = UNIT // 2, SUB // 2
+        tt = [(("tt", b, a), size) for a, b in names]
+        tj = [(("tj", a, b), size) for a, b in names]
+        rj = [(("rj", step, b), size) for b in range(WID)]
+        spot, at, ends = {}, 0, []
+        for part in ([(("rt", step), rt)] + tt, tj, rj):
+            for name, rows in part:
+                spot[name] = (at, rows)
+                at += rows
+            ends.append(at)
+        layouts.append((spot, *ends))
+    return layouts
+
+
+def pack(block):
+    n = block.shape[0] // 2
+    return jnp.concatenate([block[:n], block[n:]], axis=1)
+
+
+def unpack(block):
+    return jnp.concatenate([block[:, : UNIT // 2], block[:, UNIT // 2 :]], axis=0)
 
 
 def put_ring(place_ref, keep, send, spot, base, step, block):
     columns = [lanes(block, b) for b in range(WID)]
-    put(place_ref, keep, send, base + spot[("rt", step)], [c.T for c in columns])
+    quarters = [pack(c.T) if step >= WHOLE else c.T for c in columns]
+    put(place_ref, keep, send, base + spot[("rt", step)][0], quarters)
     for b in range(WID):
-        put(place_ref, keep, send, base + spot[("rj", step, b)], split_rows(columns[b]))
+        put(place_ref, keep, send, base + spot[("rj", step, b)][0], split_rows(columns[b]))
 
 
 def put_third(place_ref, keep, send, spot, base, a, b, block):
-    put(place_ref, keep, send, base + spot[("tj", a, b)], split_rows(block))
-    put(place_ref, keep, send, base + spot[("tt", b, a)], split_rows(block.T))
+    put(place_ref, keep, send, base + spot[("tj", a, b)][0], split_rows(block))
+    put(place_ref, keep, send, base + spot[("tt", b, a)][0], split_rows(block.T))
+
+
+def put_half(place_ref, keep, send, spot, base, first, second, tall, wide, block):
+    put(place_ref, keep, send, base + spot[(tall, first, second)][0], split_rows(block))
+    turned = block.T
+    if second == "p":
+        parts = [split_rows(x) for x in (turned[: UNIT // 2], turned[UNIT // 2 :])]
+        quarters = [jnp.concatenate([parts[0][q], parts[1][q]], axis=0) for q in range(WID)]
+    else:
+        quarters = split_rows(turned)
+    put(place_ref, keep, send, base + spot[(wide, second, first)][0], [pack(q) for q in quarters])
+
+
+def put_halves(place_ref, keep, send, spot, base, step, by_chosen, by_other):
+    for b in range(WHOLE):
+        put_half(place_ref, keep, send, spot, base, step, b, "tj", "tt", lanes(by_chosen, b))
+        put_half(place_ref, keep, send, spot, base, step, b, "tt", "tj", lanes(by_other, b))
+    put_half(place_ref, keep, send, spot, base, step, "p", "tj", "tt", lanes(by_chosen, WHOLE))
+    if step > WHOLE:
+        put_half(place_ref, keep, send, spot, base, step, "p", "tt", "tj", lanes(by_other, WHOLE))
 
 
 def reorder_kernel(g_ref, *outs):
-    units = len(outs)
     tokens = g_ref.shape[1]
+    half = g_ref.shape[0] // 2
     source = lax.broadcasted_iota(jnp.int32, (tokens, UNIT), 0)
     lane = lax.broadcasted_iota(jnp.int32, (tokens, UNIT), 1)
-    for c, out in enumerate(outs):
+
+    def pick(wanted):
+        return jnp.where(source == wanted, 1.0, 0.0).astype(jnp.bfloat16)
+
+    for c in range(WHOLE):
         wanted = (lane // SUB) * UNIT + c * SUB + lane % SUB
-        pick = jnp.where(source == wanted, 1.0, 0.0).astype(jnp.bfloat16)
-        out[...] = dot(g_ref[...], pick, ((1,), (0,))).astype(jnp.bfloat16)
+        outs[c][...] = dot(g_ref[...], pick(wanted), ((1,), (0,))).astype(jnp.bfloat16)
+    size = SUB // 2
+    for h in range(2):
+        inner = lane % (UNIT // 2)
+        wanted = (inner // size) * UNIT + WHOLE * SUB + h * size + inner % size
+        upper = dot(g_ref[:half, :], pick(jnp.where(lane < UNIT // 2, wanted, -1)), ((1,), (0,)))
+        lower = dot(g_ref[half:, :], pick(jnp.where(lane < UNIT // 2, -1, wanted)), ((1,), (0,)))
+        outs[WHOLE + h][...] = (upper + lower).astype(jnp.bfloat16)
 
 
 def self_kernel(place_ref, a_ref, g_ref, keep, send):
@@ -110,26 +157,34 @@
 
 
 def acts_kernel(layouts, place_ref, own_ref, ring_ref, other_ref, keep, send):
-    units = len(layouts)
     even = place_ref[0] == 0
 
     def arrival(x):
-        return jnp.concatenate([x[q * UNIT + c * SUB : q * UNIT + (c + 1) * SUB] for c in range(units) for q in range(WID)], axis=0)
+        spans = [(q * UNIT + c * SUB, SUB) for c in range(WHOLE) for q in range(WID)]
+        spans += [(q * UNIT + WHOLE * SUB + h * (SUB // 2), SUB // 2) for h in range(2) for q in range(WID)]
+        return jnp.concatenate([x[at : at + size] for at, size in spans], axis=0)
 
     own, ring, other = own_ref[...], ring_ref[...], other_ref[...]
     chosen = arrival(jnp.where(even, ring, own))
-    ring = arrival(ring)
-    other = arrival(other)
+    ring = row_dot(arrival(ring), own)
+    third = row_dot(chosen, arrival(other))
     base = 0
-    for c, (spot, _, _, size) in enumerate(layouts):
-        put_ring(place_ref, keep, send, spot, base, c, row_dot(ring[c * UNIT : (c + 1) * UNIT], own))
-        base += size
-    for a in range(units):
-        block = row_dot(chosen[a * UNIT : (a + 1) * UNIT], other)
-        for b in range(units):
-            step = max(a, b)
-            base = sum(layouts[s][3] for s in range(step))
-            put_third(place_ref, keep, send, layouts[step][0], base, a, b, lanes(block, b))
+    for c, layout in enumerate(layouts):
+        spot = layout[0]
+        if c < WHOLE:
+            rows = slice(c * UNIT, (c + 1) * UNIT)
+            put_ring(place_ref, keep, send, spot, base, c, ring[rows])
+            for b in range(c + 1):
+                put_third(place_ref, keep, send, spot, base, c, b, lanes(third[rows], b))
+            for a in range(c):
+                put_third(place_ref, keep, send, spot, base, a, c, lanes(third[a * UNIT : (a + 1) * UNIT], c))
+        else:
+            first = (c - WHOLE) * (UNIT // 2)
+            rows = slice(WHOLE * UNIT + first, WHOLE * UNIT + first + UNIT // 2)
+            put_ring(place_ref, keep, send, spot, base, c, ring[rows])
+            by_other = lanes(third, WHOLE).T[first : first + UNIT // 2]
+            put_halves(place_ref, keep, send, spot, base, c, third[rows], by_other)
+        base += layout[3]
 
 
 def grads_kernel(step, spot, place_ref, own_hbm, *refs):
@@ -178,6 +233,69 @@
             put_third(place_ref, keep, send, spot, 0, a, step, block[a * UNIT : (a + 1) * UNIT])
 
 
+def halves_kernel(step, spot, place_ref, own_hbm, *refs):
+    n = step - WHOLE + 1
+    count = WHOLE + n
+    mine, ring, other, scratch = refs[:count], refs[count : 2 * count], refs[2 * count : 3 * count], refs[3 * count :]
+    keep, send, own, fresh, chosen, others, chosen_part, other_part, sems = scratch
+    even = place_ref[0] == 0
+    deep = own.shape[0] // 2
+    size = UNIT // 2
+
+    def home(whole, part, a):
+        return whole.at[:, a * UNIT : (a + 1) * UNIT] if a < WHOLE else part.at[a - WHOLE]
+
+    copies = [
+        pltpu.make_async_copy(ring[step], fresh, sems.at[0]),
+        pltpu.make_async_copy(own_hbm.at[:deep], own.at[:deep], sems.at[1]),
+        pltpu.make_async_copy(own_hbm.at[deep:], own.at[deep:], sems.at[2]),
+    ]
+    third = [pltpu.make_async_copy(other[a], home(others, other_part, a), sems.at[3 + a]) for a in range(count)]
+    from_ring = [pltpu.make_async_copy(ring[a], home(chosen, chosen_part, a), sems.at[3 + count + a]) for a in range(count)]
+    from_mine = [pltpu.make_async_copy(mine[a], home(chosen, chosen_part, a), sems.at[3 + count + a]) for a in range(count)]
+    for copy in copies:
+        copy.start()
+
+    @pl.when(even)
+    def _():
+        for copy in from_ring:
+            copy.start()
+
+    @pl.when(jnp.logical_not(even))
+    def _():
+        for copy in from_mine:
+            copy.start()
+
+    for copy in third:
+        copy.start()
+
+    def against(turned, right):
+        return dot(turned[:size], right[:deep, :], ((1,), (0,))) + dot(turned[size:], right[deep:, :], ((1,), (0,)))
+
+    def against_half(turned, right):
+        return dot(turned[:size], right, ((1,), (0,)))[:, :size] + dot(turned[size:], right, ((1,), (0,)))[:, size:]
+
+    def product_of(turned, whole, part):
+        halves = [against_half(turned, part[h]) for h in range(n)]
+        return jnp.concatenate([against(turned, whole), halves[0], halves[-1]], axis=1)
+
+    for copy in copies:
+        copy.wait()
+    put_ring(place_ref, keep, send, spot, 0, step, against(fresh[...].T, own))
+    for copy in from_ring + third:
+        copy.wait()
+    by_chosen = product_of(chosen_part[n - 1].T, others, other_part)
+    by_other = product_of(other_part[n - 1].T, chosen, chosen_part)
+    put_halves(place_ref, keep, send, spot, 0, step, by_chosen, by_other)
+
+
+def halves_scratch(own, n):
+    deep = own.shape[0]
+    arrays = [pltpu.VMEM((deep, own.shape[1]), jnp.bfloat16), pltpu.VMEM((deep // 2, UNIT), jnp.bfloat16)]
+    arrays += [pltpu.VMEM((deep, WHOLE * UNIT), jnp.bfloat16)] * 2 + [pltpu.VMEM((n, deep // 2, UNIT), jnp.bfloat16)] * 2
+    return (*arrays, pltpu.SemaphoreType.DMA((3 + 2 * (WHOLE + n),)))
+
+
 def grads_scratch(own, n):
     deep = own.shape[0]
     arrays = [pltpu.VMEM((deep, width), jnp.bfloat16) for width in (own.shape[1], UNIT, n * UNIT, n * UNIT)]
@@ -204,12 +322,12 @@
 
 
 def final_kernel(layouts, groups, place_ref, lengths_ref, *refs):
-    units = len(layouts)
+    count = len(layouts)
     selves, acts, out = refs[:2], refs[2:4], refs[-1]
-    grads = [refs[4 + 2 * c : 6 + 2 * c] for c in range(units)]
+    grads = [refs[4 + 2 * c : 6 + 2 * c] for c in range(count)]
     returned = {}
     for i, steps in enumerate(groups):
-        ring, swap = refs[4 + 2 * units + 2 * i : 6 + 2 * units + 2 * i]
+        ring, swap = refs[4 + 2 * count + 2 * i : 6 + 2 * count + 2 * i]
         ring_at = swap_at = 0
         for c in steps:
             _, n_ring, n_swap, _ = layouts[c]
@@ -224,41 +342,63 @@
     columns = width * UNIT + lax.broadcasted_iota(jnp.int32, (UNIT, UNIT), 1)
     line = lax.broadcasted_iota(jnp.int32, (UNIT, UNIT), 0)
 
-    def block(where, name, step):
-        spot = layouts[step][0][name]
-        size = UNIT if name[0] == "rt" else SUB
+    def block(where, *name):
+        step = max(x for x in name[1 : 2 if name[0] == "rj" else 3] if x != "p")
+        at, size = layouts[step][0][name]
         if where == "local":
-            base = sum(layouts[s][3] for s in range(step))
-            return product(acts, grads[step], base + spot, spot, size)
+            base = sum(layout[3] for layout in layouts[:step])
+            return product(acts, grads[step], base + at, at, size)
         ring, ring_at, swap, swap_at = returned[step]
-        ref, at = (ring, ring_at + spot) if where == "ring" else (swap, swap_at + spot)
+        ref, at = (ring, ring_at + at) if where == "ring" else (swap, swap_at + at)
         return ref[at : at + size, :]
+
+    def beside(left, right):
+        return jnp.concatenate([unpack(left), unpack(right)], axis=1)
+
+    def third(where, kind, c):
+        one, two = WHOLE, WHOLE + 1
+        if c < WHOLE:
+            rows = [block(where, kind, a, c) for a in (*range(WHOLE), one, two)]
+        else:
+            rows = [beside(block(where, kind, a, one), block(where, kind, a, two)) for a in range(WHOLE)]
+            if kind == "tt":
+                rows.append(beside(block(where, kind, "p", one), block(where, kind, "p", two))[: SUB // 2])
+            else:
+                crossed = unpack(block(where, kind, "p", two))[: SUB // 2]
+                rows.append(jnp.concatenate([block(where, kind, one, "p")[:, : UNIT // 2], crossed], axis=1))
+            rows.append(block(where, kind, two, "p"))
+        return jnp.concatenate(rows, axis=0)
 
     def natural(offset, b, tile, there):
         live = (b * UNIT + line < here) & (columns < there)
         out[offset, b * UNIT : (b + 1) * UNIT, :] = jnp.where(live, tile.T, 0.0)
 
     def arrival(offset, c, tile, there):
-        token_at = (line // SUB) * UNIT + c * SUB + line % SUB
+        if c < WHOLE:
+            token_at = (line // SUB) * UNIT + c * SUB + line % SUB
+            spans = [(q * SUB, q * UNIT + c * SUB, SUB) for q in range(WID)]
+        else:
+            size = SUB // 2
+            inner = line % (UNIT // 2)
+            token_at = (inner // size) * UNIT + c * SUB + (line // (UNIT // 2)) * size + inner % size
+            spans = [(h * (UNIT // 2) + q * size, q * UNIT + c * SUB + h * size, size) for h in range(2) for q in range(WID)]
         tile = jnp.where((token_at < here) & (columns < there), tile.T, 0.0)
-        for q in range(WID):
-            first = q * UNIT + c * SUB
-            out[offset, first : first + SUB, :] = tile[q * SUB : (q + 1) * SUB]
+        for at, first, size in spans:
+            out[offset, first : first + size, :] = tile[at : at + size]
 
     there = [lengths_ref[lax.rem(token + offset + total - 2, total)] for offset in range(5)]
-    for c in range(units):
-        arrival(0, c, block("ring", ("rt", c), c), there[0])
-        tt = [jnp.concatenate([block(r, ("tt", a, c), max(a, c)) for a in range(units)], axis=0) for r in ("ring", "local")]
-        arrival(1, c, jnp.where(even, tt[0], tt[1]), there[1])
-        arrival(3, c, jnp.concatenate([block("swap", ("tj", a, c), max(a, c)) for a in range(units)], axis=0), there[3])
+    for c in range(WHOLE + 1):
+        rt = block("ring", "rt", c) if c < WHOLE else beside(block("ring", "rt", WHOLE), block("ring", "rt", WHOLE + 1))
+        arrival(0, c, rt, there[0])
+        arrival(1, c, jnp.where(even, third("ring", "tt", c), third("local", "tt", c)), there[1])
+        arrival(3, c, third("swap", "tj", c), there[3])
     for b in range(WID):
         natural(2, b, product(selves, selves, b * UNIT, (WID + b) * UNIT, UNIT), there[2])
-        natural(4, b, jnp.concatenate([block("local", ("rj", c, b), c) for c in range(units)], axis=0), there[4])
+        natural(4, b, jnp.concatenate([block("local", "rj", c, b) for c in range(WHOLE + 2)], axis=0), there[4])
 
 
 def shards(acts, grads, lengths):
     rows = acts.shape[0]
-    units = rows // UNIT
     length = lax.axis_size("tok")
     token = lax.axis_index("tok")
     width = lax.axis_index("wid")
@@ -266,7 +406,7 @@
     swap = [(i, i ^ 1) for i in range(length)]
     down = [(i, (i - 2) % length) for i in range(length)]
     up = [(i, (i + 2) % length) for i in range(length)]
-    layouts = [step_layout(c, units) for c in range(units)]
+    layouts = step_layouts()
 
     def floats(n):
         return (jax.ShapeDtypeStruct((2, n, UNIT), jnp.float32),) * 2
@@ -275,7 +415,9 @@
         return lax.ppermute(send, "wid", [(w, w ^ 1) for w in range(WID)])
 
     own_g = grads.T
-    mine = list(call(reorder_kernel, (jax.ShapeDtypeStruct((grads.shape[1], UNIT), jnp.bfloat16),) * units, own_g))
+    deep = grads.shape[1]
+    shapes = [jax.ShapeDtypeStruct((deep if c < WHOLE else deep // 2, UNIT), jnp.bfloat16) for c in range(WHOLE + 2)]
+    mine = call(reorder_kernel, tuple(shapes), own_g)
     alive = jnp.max(lengths) > 0
     seen = {}
 
@@ -307,19 +449,12 @@
         seen["S" + name] = lax.ppermute(after(far, GATES.get("S" + name)), "wid", [(w, w ^ 2) for w in range(WID)])
         return near
 
-    def pair(c):
-        if str(c) in PIECES:
-            return seen["R%d" % c], seen["O%d" % c]
-        return tuple(jnp.concatenate([seen["%s%d%s" % (side, c, half)] for half in "ab"], axis=0) for side in "RO")
-
     near = {}
     for piece in PIECES:
         if piece == "A":
             start(piece, acts)
-        elif piece[0] in "0123":
-            chunk = mine[int(piece[0])]
-            cut = chunk.shape[0] // 2
-            start(piece, {"": chunk, "a": chunk[:cut], "b": chunk[cut:]}[piece[1:]])
+        elif piece.isdigit():
+            start(piece, mine[int(piece)])
         elif piece == "kS":
             near["S"] = exchange("S", self_kernel, 2 * WID * UNIT, acts, own_g)
         elif piece == "kA":
@@ -328,11 +463,13 @@
         else:
             c = int(piece[1])
             spot, size = layouts[c][0], layouts[c][3]
-            pairs = [pair(a) for a in range(c + 1)]
+            kernel, scratch = grads_kernel, grads_scratch(own_g, c + 1)
+            if c >= WHOLE:
+                kernel, scratch = halves_kernel, halves_scratch(own_g, c - WHOLE + 1)
+            arrived = [seen["%s%d" % (side, a)] for side in "RO" for a in range(c + 1)]
             near[c] = seen["N%d" % c] = exchange(
-                piece[1], lambda *refs, c=c, spot=spot: grads_kernel(c, spot, *refs),
-                size, own_g, *mine[: c + 1], *[p[0] for p in pairs], *[p[1] for p in pairs],
-                memory=pl.BlockSpec(memory_space=pl.ANY), scratch=grads_scratch(own_g, c + 1),
+                piece[1], lambda *refs, c=c, spot=spot, kernel=kernel: kernel(c, spot, *refs),
+                size, own_g, *mine[: c + 1], *arrived, memory=pl.BlockSpec(memory_space=pl.ANY), scratch=scratch,
             )
 
     returned = []
@@ -347,7 +484,7 @@
         )
         returned += [lax.ppermute(ring, "tok", up), lax.ppermute(swapped, "tok", swap)]
 
-    grams = sum([[near[c], seen["S%d" % c]] for c in range(units)], [])
+    grams = sum([[near[c], seen["S%d" % c]] for c in range(WHOLE + 2)], [])
     out = call(
         lambda *refs: final_kernel(layouts, GROUPS, *refs),
         jax.ShapeDtypeStruct((5, rows, UNIT), jnp.float32),

time: 123 us -> 136 us (1.11)
  Pallas kernels: 36.9 us -> 44.5 us
  starting transfers between devices: 28.1 us -> 31.8 us
    pallas_call x10 -> x11, Pallas kernels: 36.9 us -> 44.5 us  [call(): pl.pallas_call(kernel, out_shape=outs, in_specs=[SMEM] * scalars + [memor...]
    ppermute x2, waiting for transfers between devices: 5.49 us -> 2.88 us  [shards(): lax.ppermute(swapped, 'tok', swap)]
    ppermute x5 -> x6, waiting for transfers between devices: 9.87 us -> 12.3 us  [start(): lax.ppermute(after(chunk, GATES.get('R' + name)), 'tok', down)]
    ppermute x5 -> x6, starting transfers between devices: 14.3 us -> 16.5 us  [start(): lax.ppermute(after(chunk, GATES.get('R' + name)), 'tok', down)]
    ppermute x2, waiting for transfers between devices: 0.01 us -> 2.07 us  [shards(): lax.ppermute(ring, 'tok', up)]
    ppermute x6 -> x7, waiting for transfers between devices: 19.5 us -> 17.6 us  [exchange(): lax.ppermute(after(far, GATES.get('S' + name)), 'wid', [(w, w ^ 2) for w...]
    add x6 -> x7, other arithmetic: 2.03 us -> 3.38 us  [summed(): return (keep[0] + arrived[0], keep[1] + arrived[1])]
    ppermute x5 -> x6, starting transfers between devices: 5.08 us -> 6.35 us  [start(): lax.ppermute(after(chunk, GATES.get('O' + name)), 'tok', swap)]
  transfers between devices with their start and end apart: 26 -> 30, of which waited for: 15 -> 17; matrix products, arithmetic and copies ran while one was open for 3% -> 4% of each run, Pallas kernels for 28% -> 30%
where the time goes in v6:
time: 136 us
  waiting for transfers between devices  52.5 us (39%)
  Pallas kernels  44.5 us (33%)
  starting transfers between devices  31.8 us (23%)
  other arithmetic  4.7 us (3%)
  local copies, waits for them, and re-layouts  1.55 us (1%)
    pallas_call x11, Pallas kernels, call(): pl.pallas_call(kernel, out_shape=outs, in_specs=[SMEM] * scalars + [memor...  44.5 us
    ppermute x7, waiting for transfers between devices, exchange(): lax.ppermute(after(far, GATES.get('S' + name)), 'wid', [(w, w ^ 2) for w...  17.6 us
    ppermute x6, starting transfers between devices, start(): lax.ppermute(after(chunk, GATES.get('R' + name)), 'tok', down)  16.5 us
    ppermute x7, waiting for transfers between devices, over_core(): return lax.ppermute(send, 'wid', [(w, w ^ 1) for w in range(WID)])  15.6 us
    ppermute x6, waiting for transfers between devices, start(): lax.ppermute(after(chunk, GATES.get('R' + name)), 'tok', down)  12.3 us
    ppermute x6, starting transfers between devices, start(): lax.ppermute(after(chunk, GATES.get('O' + name)), 'tok', swap)  6.35 us
    ppermute x7, starting transfers between devices, exchange(): lax.ppermute(after(far, GATES.get('S' + name)), 'wid', [(w, w ^ 2) for w...  5.31 us
    add x7, other arithmetic, summed(): return (keep[0] + arrived[0], keep[1] + arrived[1])  3.38 us
  transfers between devices with their start and end apart: 30, of which 17 were waited for; matrix products, arithmetic and copies ran while one was open for 4% of the time, Pallas kernels for 30%

profile of v6, /device:TPU:0, one launch (start us, length us, event | category | flops | bytes accessed | tf_op | source)
XLA Modules:
  0.0 136.0 jit_solution(9821079826629192281)
XLA Ops:
  2.9 3.6 %collective-permute-start.8 = (bf16[512,1024]{1,0:T(8,128)(2,1)}, bf16[512,1024]{1,0:T(8,128)(2,1)}, u32[]{:S(2)}, u32[]{:S(2)}) collective-permute-start(bf16[512,1024]{1,0:T(8,128)(2,1)} %param.17), channel_id=1, source_target_pairs={{0,24},{4,28},{8,0},{12,4},{16,8},{20,12},{24,16},{28,20},{1,25},{... | collective-permute-start | bytes 3145736 | tf_op jit(solution)/shard_map/ppermute | solution.py:432
  8.6 7.3 %conditional.7 = (f32[1024,128]{1,0:T(8,128)S(1)}, f32[1024,128]{1,0:T(8,128)S(1)}) conditional(s32[]{:T(128)} %convert_element_type.2, () %tuple.76, (s32[5]{0:T(128)S(1)}, bf16[512,1024]{1,0:T(8,128)(2,1)}, bf16[2752,512]{1,0:T(8,128)(2,1)}) %tuple.126), branch_computations={%region_1.2_spmd, %region_2.3_spmd} | conditional | flops 262144 | bytes 7340088 | solution.py:448
  8.6 4.5 %branch_1_fun.7 = (f32[2,1024,128]{2,1,0:T(8,128)S(1)}, f32[2,1024,128]{2,1,0:T(8,128)S(1)}) custom-call(s32[5]{0:T(128)S(1)} %get-tuple-element.129.place_ref, bf16[512,1024]{1,0:T(8,128)(2,1)} %get-tuple-element.130.a_ref, bf16[2752,512]{1,0:T(8,128)(2,1)} %get-tuple-element.131.g_ref), custom_call_target="tpu_custom_call" | custom-call | tf_op jit(solution)/shard_map/cond/branch_1_fun/pallas_call | solution.py:26
  17.5 6.4 %shard_map.37 = (bf16[2752,128]{1,0:T(8,128)(2,1)S(1)}, bf16[2752,128]{1,0:T(8,128)(2,1)}, bf16[2752,128]{1,0:T(8,128)(2,1)}, bf16[1376,128]{1,0:T(8,128)(2,1)S(1)}, bf16[1376,128]{1,0:T(8,128)(2,1)}) custom-call(bf16[2752,512]{1,0:T(8,128)(2,1)} %bitcast.36), custom_call_target="tpu_custom_call" | custom-call | tf_op jit(solution)/shard_map/pallas_call | solution.py:26
  24.9 5.0 %collective-permute-done.7.refs_3_ = f32[1024,128]{1,0:T(8,128)S(1)} collective-permute-done((f32[1024,128]{1,0:T(8,128)S(1)}, f32[1024,128]{1,0:T(8,128)S(1)}, u32[]{:S(2)}, u32[]{:S(2)}) %collective-permute-start.7) | collective-permute-done | bytes 524320 | tf_op jit(solution)/shard_map/ppermute | solution.py:449
  30.5 9.5 %conditional.8 = (f32[2080,128]{1,0:T(8,128)}, f32[2080,128]{1,0:T(8,128)}) conditional(s32[]{:T(128)} %convert_element_type.2, () %tuple.80, (s32[5]{0:T(128)S(1)}, bf16[512,1024]{1,0:T(8,128)(2,1)S(1)}, bf16[512,1024]{1,0:T(8,128)(2,1)}, bf16[512,1024]{1,0:T(8,128)(2,1)}) %tuple.133), branch_computations={%region_3.4_spmd, %region_4.5_spmd} | conditional | flops 532480 | bytes 14909496 | solution.py:448
  30.5 3.7 %branch_1_fun.8 = (f32[2,2080,128]{2,1,0:T(8,128)S(1)}, f32[2,2080,128]{2,1,0:T(8,128)S(1)}) custom-call(s32[5]{0:T(128)S(1)} %get-tuple-element.134.refs_0_, bf16[512,1024]{1,0:T(8,128)(2,1)S(1)} %get-tuple-element.135.refs_1_, bf16[512,1024]{1,0:T(8,128)(2,1)} %get-tuple-element.136.refs_2_, bf16[512,1024]{1,0:T(8,128)(2,1)} %get-tuple-element.137.refs_3_), custom_call_target="tpu_custom_call" | custom-call | tf_op jit(solution)/shard_map/cond/branch_1_fun/pallas_call | solution.py:26
  34.3 4.2 %collective-permute-done.1 = f32[2,2080,128]{2,1,0:T(8,128)S(1)} collective-permute-done((f32[2,2080,128]{2,1,0:T(8,128)S(1)}, f32[2,2080,128]{2,1,0:T(8,128)S(1)}, u32[]{:S(2)}, u32[]{:S(2)}) %collective-permute-start.1) | collective-permute-done | bytes 2129952 | tf_op jit(solution)/shard_map/cond/branch_1_fun/ppermute | solution.py:415
  41.5 4.3 %collective-permute-start.14 = (bf16[2752,128]{1,0:T(8,128)(2,1)}, bf16[2752,128]{1,0:T(8,128)(2,1)}, u32[]{:S(2)}, u32[]{:S(2)}) collective-permute-start(bf16[2752,128]{1,0:T(8,128)(2,1)} %get-tuple-element.279), channel_id=1, source_target_pairs={{0,24},{4,28},{8,0},{12,4},{16,8},{20,12},{24,16},{28,20},{1,25},{... | collective-permute-start | bytes 2113544 | tf_op jit(solution)/shard_map/ppermute | solution.py:432
  46.3 5.5 %conditional.9 = (f32[320,128]{1,0:T(8,128)S(1)}, f32[320,128]{1,0:T(8,128)S(1)}) conditional(s32[]{:T(128)} %convert_element_type.2, () %tuple.84, (s32[5]{0:T(128)S(1)}, bf16[2752,512]{1,0:T(8,128)(2,1)}, bf16[2752,128]{1,0:T(8,128)(2,1)S(1)}, bf16[2752,128]{1,0:T(8,128)(2,1)}, bf16[2752,128]{1,0:T(8,128)(2,1)}) %tuple.127), branch_computations={%region_5.6_spmd, %region_6.7_spmd} | conditional | flops 81920 | bytes 2293816 | solution.py:448
  46.4 3.7 %branch_1_fun.9 = (f32[2,320,128]{2,1,0:T(8,128)S(1)}, f32[2,320,128]{2,1,0:T(8,128)S(1)}) custom-call(s32[5]{0:T(128)S(1)} %get-tuple-element.140.refs_0_, bf16[2752,512]{1,0:T(8,128)(2,1)} %get-tuple-element.141.refs_1_, bf16[2752,128]{1,0:T(8,128)(2,1)S(1)} %get-tuple-element.142.refs_2_, bf16[2752,128]{1,0:T(8,128)(2,1)} %get-tuple-element.143.refs_3_, ...), custom_call_target="tpu_custom_call" | custom-call | tf_op jit(solution)/shard_map/cond/branch_1_fun/pallas_call | solution.py:26
  53.4 8.9 %collective-permute-done.14 = bf16[2752,128]{1,0:T(8,128)(2,1)} collective-permute-done((bf16[2752,128]{1,0:T(8,128)(2,1)}, bf16[2752,128]{1,0:T(8,128)(2,1)}, u32[]{:S(2)}, u32[]{:S(2)}) %collective-permute-start.14) | collective-permute-done | bytes 704544 | tf_op jit(solution)/shard_map/ppermute | solution.py:432
  62.3 4.3 %collective-permute-start.20 = (bf16[1376,128]{1,0:T(8,128)(2,1)S(1)}, bf16[1376,128]{1,0:T(8,128)(2,1)}, u32[]{:S(2)}, u32[]{:S(2)}) collective-permute-start(bf16[1376,128]{1,0:T(8,128)(2,1)S(1)} %get-tuple-element.297), channel_id=1, source_target_pairs={{0,24},{4,28},{8,0},{12,4},{16,8},{20,12},{24,16},{28,20},{1,25},{... | collective-permute-start | bytes 1056776 | tf_op jit(solution)/shard_map/ppermute | solution.py:432
  67.1 6.8 %conditional.10 = (f32[448,128]{1,0:T(8,128)}, f32[448,128]{1,0:T(8,128)}) conditional(s32[]{:T(128)} %convert_element_type.2, () %tuple.89, (s32[5]{0:T(128)S(1)}, bf16[2752,512]{1,0:T(8,128)(2,1)}, bf16[2752,128]{1,0:T(8,128)(2,1)S(1)}, bf16[2752,128]{1,0:T(8,128)(2,1)}, bf16[2752,128]{1,0:T(8,128)(2,1)}, /*index=5*/bf16[2752,128]{1,0:T(8,128)(2,1)}, ...), branch_computations={%region_7.8_spmd, %region_8.9_spmd} | conditional | flops 114688 | bytes 3211320 | solution.py:448
  67.1 4.1 %branch_1_fun.10 = (f32[2,448,128]{2,1,0:T(8,128)S(1)}, f32[2,448,128]{2,1,0:T(8,128)S(1)}) custom-call(s32[5]{0:T(128)S(1)} %get-tuple-element.147.refs_0_, bf16[2752,512]{1,0:T(8,128)(2,1)} %get-tuple-element.148.refs_1_, bf16[2752,128]{1,0:T(8,128)(2,1)S(1)} %get-tuple-element.149.refs_2_, bf16[2752,128]{1,0:T(8,128)(2,1)} %get-tuple-element.150.refs_3_, ...), custom_call_target="tpu_custom_call" | custom-call | tf_op jit(solution)/shard_map/cond/branch_1_fun/pallas_call | solution.py:26
  81.0 7.8 %conditional.11 = (f32[576,128]{1,0:T(8,128)S(1)}, f32[576,128]{1,0:T(8,128)}) conditional(s32[]{:T(128)} %convert_element_type.2, () %tuple.95, (s32[5]{0:T(128)S(1)}, bf16[2752,512]{1,0:T(8,128)(2,1)}, bf16[2752,128]{1,0:T(8,128)(2,1)S(1)}, bf16[2752,128]{1,0:T(8,128)(2,1)}, bf16[2752,128]{1,0:T(8,128)(2,1)}, ...), branch_computations={%region_9.10_spmd, %region_10.11_spmd} | conditional | flops 147456 | bytes 4128824 | solution.py:448
  81.0 5.0 %branch_1_fun.11 = (f32[2,576,128]{2,1,0:T(8,128)S(1)}, f32[2,576,128]{2,1,0:T(8,128)S(1)}) custom-call(s32[5]{0:T(128)S(1)} %get-tuple-element.157.refs_0_, bf16[2752,512]{1,0:T(8,128)(2,1)} %get-tuple-element.158.refs_1_, bf16[2752,128]{1,0:T(8,128)(2,1)S(1)} %get-tuple-element.159.refs_2_, bf16[2752,128]{1,0:T(8,128)(2,1)} %get-tuple-element.160.refs_3_, ...), custom_call_target="tpu_custom_call" | custom-call | tf_op jit(solution)/shard_map/cond/branch_1_fun/pallas_call | solution.py:26
  90.0 3.9 %collective-permute-start.23 = (bf16[1376,128]{1,0:T(8,128)(2,1)}, bf16[1376,128]{1,0:T(8,128)(2,1)}, u32[]{:S(2)}, u32[]{:S(2)}) collective-permute-start(bf16[1376,128]{1,0:T(8,128)(2,1)} %get-tuple-element.302), channel_id=1, source_target_pairs={{0,24},{4,28},{8,0},{12,4},{16,8},{20,12},{24,16},{28,20},{1,25},{... | collective-permute-start | bytes 1056776 | tf_op jit(solution)/shard_map/ppermute | solution.py:432
  94.2 7.2 %conditional.12 = (f32[352,128]{1,0:T(8,128)S(1)}, f32[352,128]{1,0:T(8,128)S(1)}) conditional(s32[]{:T(128)} %convert_element_type.2, () %tuple.101, (s32[5]{0:T(128)S(1)}, bf16[2752,512]{1,0:T(8,128)(2,1)}, bf16[2752,128]{1,0:T(8,128)(2,1)S(1)}, bf16[2752,128]{1,0:T(8,128)(2,1)}, bf16[2752,128]{1,0:T(8,128)(2,1)}, ...), branch_computations={%region_11.12_spmd, %region_12.13_spmd} | conditional | flops 90112 | bytes 2523192 | solution.py:448
  94.2 5.3 %branch_1_fun.12 = (f32[2,352,128]{2,1,0:T(8,128)S(1)}, f32[2,352,128]{2,1,0:T(8,128)S(1)}) custom-call(s32[5]{0:T(128)S(1)} %get-tuple-element.170.refs_0_, bf16[2752,512]{1,0:T(8,128)(2,1)} %get-tuple-element.171.refs_1_, bf16[2752,128]{1,0:T(8,128)(2,1)S(1)} %get-tuple-element.172.refs_2_, bf16[2752,128]{1,0:T(8,128)(2,1)} %get-tuple-element.173.refs_3_, ...), custom_call_target="tpu_custom_call" | custom-call | tf_op jit(solution)/shard_map/cond/branch_1_fun/pallas_call | solution.py:26
  101.7 6.3 %collective-permute-done.22.refs_9_.refs_13_ = f32[352,128]{1,0:T(8,128)S(1)} collective-permute-done((f32[352,128]{1,0:T(8,128)S(1)}, f32[352,128]{1,0:T(8,128)S(1)}, u32[]{:S(2)}, u32[]{:S(2)}) %collective-permute-start.22) | collective-permute-done | bytes 180256 | tf_op jit(solution)/shard_map/ppermute | solution.py:449
  110.6 7.2 %conditional.13 = (f32[384,128]{1,0:T(8,128)S(1)}, f32[384,128]{1,0:T(8,128)S(1)}) conditional(s32[]{:T(128)} %convert_element_type.2, () %tuple.103, (s32[5]{0:T(128)S(1)}, bf16[2752,512]{1,0:T(8,128)(2,1)S(1)}, bf16[2752,128]{1,0:T(8,128)(2,1)S(1)}, bf16[2752,128]{1,0:T(8,128)(2,1)}, bf16[2752,128]{1,0:T(8,128)(2,1)}, ...), branch_computations={%region_13.14_spmd, %region_14.15_spmd} | conditional | flops 98304 | bytes 2752568 | solution.py:448
  110.6 5.3 %branch_1_fun.13 = (f32[2,384,128]{2,1,0:T(8,128)S(1)}, f32[2,384,128]{2,1,0:T(8,128)S(1)}) custom-call(s32[5]{0:T(128)S(1)} %get-tuple-element.186.refs_0_, bf16[2752,512]{1,0:T(8,128)(2,1)S(1)} %get-tuple-element.187.refs_1_, bf16[2752,128]{1,0:T(8,128)(2,1)S(1)} %get-tuple-element.188.refs_2_, bf16[2752,128]{1,0:T(8,128)(2,1)} %get-tuple-element.189.refs_3_, ...), custom_call_target="tpu_custom_call" | custom-call | tf_op jit(solution)/shard_map/cond/branch_1_fun/pallas_call | solution.py:26
  119.6 5.2 %collective-permute-done.25.refs_3_.refs_15_ = f32[384,128]{1,0:T(8,128)S(1)} collective-permute-done((f32[384,128]{1,0:T(8,128)S(1)}, f32[384,128]{1,0:T(8,128)S(1)}, u32[]{:S(2)}, u32[]{:S(2)}) %collective-permute-start.25) | collective-permute-done | bytes 196640 | tf_op jit(solution)/shard_map/ppermute | solution.py:449
  (91 shorter events, 51.3 us)
Async XLA Ops:
  0.0 30.0 %collective-permute-start.9 = (bf16[512,1024]{1,0:T(8,128)(2,1)}, bf16[512,1024]{1,0:T(8,128)(2,1)}, u32[]{:S(2)}, u32[]{:S(2)}) collective-permute-start(bf16[512,1024]{1,0:T(8,128)(2,1)} %param.17), channel_id=1, source_target_pairs={{0,4},{4,0},{8,12},{12,8},{16,20},{20,16},{24,28},{28,24},{1,5},{5... | collective-permute-start | bytes 3145736 | tf_op jit(solution)/shard_map/ppermute | solution.py:433
  2.9 27.5 %collective-permute-start.8 = (bf16[512,1024]{1,0:T(8,128)(2,1)}, bf16[512,1024]{1,0:T(8,128)(2,1)}, u32[]{:S(2)}, u32[]{:S(2)}) collective-permute-start(bf16[512,1024]{1,0:T(8,128)(2,1)} %param.17), channel_id=1, source_target_pairs={{0,24},{4,28},{8,0},{12,4},{16,8},{20,12},{24,16},{28,20},{1,25},{... | collective-permute-start | bytes 3145736 | tf_op jit(solution)/shard_map/ppermute | solution.py:432
  15.9 14.0 %collective-permute-start.7 = (f32[1024,128]{1,0:T(8,128)S(1)}, f32[1024,128]{1,0:T(8,128)S(1)}, u32[]{:S(2)}, u32[]{:S(2)}) collective-permute-start(f32[1024,128]{1,0:T(8,128)S(1)} %get-tuple-element.258), channel_id=1, source_target_pairs={{0,2},{1,3},{2,0},{3,1},{4,6},{5,7},{6,4},{7,5},{8,10},{9,11},{10,... | collective-permute-start | bytes 1572872 | tf_op jit(solution)/shard_map/ppermute | solution.py:449
  23.9 22.4 %collective-permute-start.11 = (bf16[2752,128]{1,0:T(8,128)(2,1)S(1)}, bf16[2752,128]{1,0:T(8,128)(2,1)}, u32[]{:S(2)}, u32[]{:S(2)}) collective-permute-start(bf16[2752,128]{1,0:T(8,128)(2,1)S(1)} %get-tuple-element.267), channel_id=1, source_target_pairs={{0,4},{4,0},{8,12},{12,8},{16,20},{20,16},{24,28},{28,24},{1,5},{5... | collective-permute-start | bytes 2113544 | tf_op jit(solution)/shard_map/ppermute | solution.py:433
  24.5 21.9 %collective-permute-start.10 = (bf16[2752,128]{1,0:T(8,128)(2,1)S(1)}, bf16[2752,128]{1,0:T(8,128)(2,1)}, u32[]{:S(2)}, u32[]{:S(2)}) collective-permute-start(bf16[2752,128]{1,0:T(8,128)(2,1)S(1)} %get-tuple-element.267), channel_id=1, source_target_pairs={{0,24},{4,28},{8,0},{12,4},{16,8},{20,12},{24,16},{28,20},{1,25},{... | collective-permute-start | bytes 2113544 | tf_op jit(solution)/shard_map/ppermute | solution.py:432
  34.2 4.3 %collective-permute-start.1 = (f32[2,2080,128]{2,1,0:T(8,128)S(1)}, f32[2,2080,128]{2,1,0:T(8,128)S(1)}, u32[]{:S(2)}, u32[]{:S(2)}) collective-permute-start(f32[2,2080,128]{2,1,0:T(8,128)S(1)} %get-tuple-element.139), channel_id=1, source_target_pairs={{0,1},{1,0},{2,3},{3,2},{4,5},{5,4},{6,7},{7,6},{8,9},{9,8},{10,11... | collective-permute-start | bytes 6389768 | tf_op jit(solution)/shard_map/cond/branch_1_fun/ppermute | solution.py:415
  40.0 27.1 %collective-permute-start.12 = (f32[2080,128]{1,0:T(8,128)}, f32[2080,128]{1,0:T(8,128)S(1)}, u32[]{:S(2)}, u32[]{:S(2)}) collective-permute-start(f32[2080,128]{1,0:T(8,128)} %get-tuple-element.269), channel_id=1, source_target_pairs={{0,2},{1,3},{2,0},{3,1},{4,6},{5,7},{6,4},{7,5},{8,10},{9,11},{10,... | collective-permute-start | bytes 3194888 | tf_op jit(solution)/shard_map/ppermute | solution.py:449
  41.5 20.8 %collective-permute-start.14 = (bf16[2752,128]{1,0:T(8,128)(2,1)}, bf16[2752,128]{1,0:T(8,128)(2,1)}, u32[]{:S(2)}, u32[]{:S(2)}) collective-permute-start(bf16[2752,128]{1,0:T(8,128)(2,1)} %get-tuple-element.279), channel_id=1, source_target_pairs={{0,24},{4,28},{8,0},{12,4},{16,8},{20,12},{24,16},{28,20},{1,25},{... | collective-permute-start | bytes 2113544 | tf_op jit(solution)/shard_map/ppermute | solution.py:432
  45.8 20.8 %collective-permute-start.15 = (bf16[2752,128]{1,0:T(8,128)(2,1)}, bf16[2752,128]{1,0:T(8,128)(2,1)}, u32[]{:S(2)}, u32[]{:S(2)}) collective-permute-start(bf16[2752,128]{1,0:T(8,128)(2,1)} %get-tuple-element.279), channel_id=1, source_target_pairs={{0,4},{4,0},{8,12},{12,8},{16,20},{20,16},{24,28},{28,24},{1,5},{5... | collective-permute-start | bytes 2113544 | tf_op jit(solution)/shard_map/ppermute | solution.py:433
  46.3 31.1 %collective-permute-start.17 = (bf16[2752,128]{1,0:T(8,128)(2,1)}, bf16[2752,128]{1,0:T(8,128)(2,1)}, u32[]{:S(2)}, u32[]{:S(2)}) collective-permute-start(bf16[2752,128]{1,0:T(8,128)(2,1)} %get-tuple-element.291), channel_id=1, source_target_pairs={{0,24},{4,28},{8,0},{12,4},{16,8},{20,12},{24,16},{28,20},{1,25},{... | collective-permute-start | bytes 2113544 | tf_op jit(solution)/shard_map/ppermute | solution.py:432
  51.8 28.1 %collective-permute-start.18 = (bf16[2752,128]{1,0:T(8,128)(2,1)}, bf16[2752,128]{1,0:T(8,128)(2,1)}, u32[]{:S(2)}, u32[]{:S(2)}) collective-permute-start(bf16[2752,128]{1,0:T(8,128)(2,1)} %get-tuple-element.291), channel_id=1, source_target_pairs={{0,4},{4,0},{8,12},{12,8},{16,20},{20,16},{24,28},{28,24},{1,5},{5... | collective-permute-start | bytes 2113544 | tf_op jit(solution)/shard_map/ppermute | solution.py:433
  62.3 31.9 %collective-permute-start.20 = (bf16[1376,128]{1,0:T(8,128)(2,1)S(1)}, bf16[1376,128]{1,0:T(8,128)(2,1)}, u32[]{:S(2)}, u32[]{:S(2)}) collective-permute-start(bf16[1376,128]{1,0:T(8,128)(2,1)S(1)} %get-tuple-element.297), channel_id=1, source_target_pairs={{0,24},{4,28},{8,0},{12,4},{16,8},{20,12},{24,16},{28,20},{1,25},{... | collective-permute-start | bytes 1056776 | tf_op jit(solution)/shard_map/ppermute | solution.py:432
  66.6 27.6 %collective-permute-start.21 = (bf16[1376,128]{1,0:T(8,128)(2,1)S(1)}, bf16[1376,128]{1,0:T(8,128)(2,1)}, u32[]{:S(2)}, u32[]{:S(2)}) collective-permute-start(bf16[1376,128]{1,0:T(8,128)(2,1)S(1)} %get-tuple-element.297), channel_id=1, source_target_pairs={{0,4},{4,0},{8,12},{12,8},{16,20},{20,16},{24,28},{28,24},{1,5},{5... | collective-permute-start | bytes 1056776 | tf_op jit(solution)/shard_map/ppermute | solution.py:433
  74.0 7.0 %collective-permute-start.13 = (f32[320,128]{1,0:T(8,128)S(1)}, f32[320,128]{1,0:T(8,128)S(1)}, u32[]{:S(2)}, u32[]{:S(2)}) collective-permute-start(f32[320,128]{1,0:T(8,128)S(1)} %get-tuple-element.273), channel_id=1, source_target_pairs={{0,2},{1,3},{2,0},{3,1},{4,6},{5,7},{6,4},{7,5},{8,10},{9,11},{10,... | collective-permute-start | bytes 491528 | tf_op jit(solution)/shard_map/ppermute | solution.py:449
  77.4 16.6 %collective-permute-start.16 = (f32[448,128]{1,0:T(8,128)}, f32[448,128]{1,0:T(8,128)S(1)}, u32[]{:S(2)}, u32[]{:S(2)}) collective-permute-start(f32[448,128]{1,0:T(8,128)} %get-tuple-element.281), channel_id=1, source_target_pairs={{0,2},{1,3},{2,0},{3,1},{4,6},{5,7},{6,4},{7,5},{8,10},{9,11},{10,... | collective-permute-start | bytes 688136 | tf_op jit(solution)/shard_map/ppermute | solution.py:449
  89.5 18.5 %collective-permute-start.19 = (f32[576,128]{1,0:T(8,128)}, f32[576,128]{1,0:T(8,128)S(1)}, u32[]{:S(2)}, u32[]{:S(2)}) collective-permute-start(f32[576,128]{1,0:T(8,128)} %get-tuple-element.294), channel_id=1, source_target_pairs={{0,2},{1,3},{2,0},{3,1},{4,6},{5,7},{6,4},{7,5},{8,10},{9,11},{10,... | collective-permute-start | bytes 884744 | tf_op jit(solution)/shard_map/ppermute | solution.py:449
  90.0 19.8 %collective-permute-start.23 = (bf16[1376,128]{1,0:T(8,128)(2,1)}, bf16[1376,128]{1,0:T(8,128)(2,1)}, u32[]{:S(2)}, u32[]{:S(2)}) collective-permute-start(bf16[1376,128]{1,0:T(8,128)(2,1)} %get-tuple-element.302), channel_id=1, source_target_pairs={{0,24},{4,28},{8,0},{12,4},{16,8},{20,12},{24,16},{28,20},{1,25},{... | collective-permute-start | bytes 1056776 | tf_op jit(solution)/shard_map/ppermute | solution.py:432
  94.0 15.9 %collective-permute-start.24 = (bf16[1376,128]{1,0:T(8,128)(2,1)}, bf16[1376,128]{1,0:T(8,128)(2,1)}, u32[]{:S(2)}, u32[]{:S(2)}) collective-permute-start(bf16[1376,128]{1,0:T(8,128)(2,1)} %get-tuple-element.302), channel_id=1, source_target_pairs={{0,4},{4,0},{8,12},{12,8},{16,20},{20,16},{24,28},{28,24},{1,5},{5... | collective-permute-start | bytes 1056776 | tf_op jit(solution)/shard_map/ppermute | solution.py:433
  101.4 6.7 %collective-permute-start.22 = (f32[352,128]{1,0:T(8,128)S(1)}, f32[352,128]{1,0:T(8,128)S(1)}, u32[]{:S(2)}, u32[]{:S(2)}) collective-permute-start(f32[352,128]{1,0:T(8,128)S(1)} %get-tuple-element.299), channel_id=1, source_target_pairs={{0,2},{1,3},{2,0},{3,1},{4,6},{5,7},{6,4},{7,5},{8,10},{9,11},{10,... | collective-permute-start | bytes 540680 | tf_op jit(solution)/shard_map/ppermute | solution.py:449
  109.8 22.8 %collective-permute-start.26 = (f32[848,128]{1,0:T(8,128)S(1)}, f32[848,128]{1,0:T(8,128)S(1)}, u32[]{:S(2)}, u32[]{:S(2)}) collective-permute-start(f32[848,128]{1,0:T(8,128)S(1)} %get-tuple-element.305), channel_id=1, source_target_pairs={{0,8},{4,12},{8,16},{12,20},{16,24},{20,28},{24,0},{28,4},{1,9},{5... | collective-permute-start | bytes 1302536 | tf_op jit(solution)/shard_map/ppermute | solution.py:485
  117.8 7.0 %collective-permute-start.25 = (f32[384,128]{1,0:T(8,128)S(1)}, f32[384,128]{1,0:T(8,128)S(1)}, u32[]{:S(2)}, u32[]{:S(2)}) collective-permute-start(f32[384,128]{1,0:T(8,128)S(1)} %get-tuple-element.304), channel_id=1, source_target_pairs={{0,2},{1,3},{2,0},{3,1},{4,6},{5,7},{6,4},{7,5},{8,10},{9,11},{10,... | collective-permute-start | bytes 589832 | tf_op jit(solution)/shard_map/ppermute | solution.py:449
  118.1 14.5 %collective-permute-start.27 = (f32[400,128]{1,0:T(8,128)S(1)}, f32[400,128]{1,0:T(8,128)S(1)}, u32[]{:S(2)}, u32[]{:S(2)}) collective-permute-start(f32[400,128]{1,0:T(8,128)S(1)} %get-tuple-element.306), channel_id=1, source_target_pairs={{0,4},{4,0},{8,12},{12,8},{16,20},{20,16},{24,28},{28,24},{1,5},{5... | collective-permute-start | bytes 614408 | tf_op jit(solution)/shard_map/ppermute | solution.py:485
  126.2 6.5 %collective-permute-start.28 = (f32[192,128]{1,0:T(8,128)S(1)}, f32[192,128]{1,0:T(8,128)S(1)}, u32[]{:S(2)}, u32[]{:S(2)}) collective-permute-start(f32[192,128]{1,0:T(8,128)S(1)} %get-tuple-element.307), channel_id=1, source_target_pairs={{0,8},{4,12},{8,16},{12,20},{16,24},{20,28},{24,0},{28,4},{1,9},{5... | collective-permute-start | bytes 294920 | tf_op jit(solution)/shard_map/ppermute | solution.py:485
  126.2 4.3 %collective-permute-start.29 = (f32[128,128]{1,0:T(8,128)S(1)}, f32[128,128]{1,0:T(8,128)S(1)}, u32[]{:S(2)}, u32[]{:S(2)}) collective-permute-start(f32[128,128]{1,0:T(8,128)S(1)} %get-tuple-element.308), channel_id=1, source_target_pairs={{0,4},{4,0},{8,12},{12,8},{16,20},{20,16},{24,28},{28,24},{1,5},{5... | collective-permute-start | bytes 196616 | tf_op jit(solution)/shard_map/ppermute | solution.py:485
  (20 other events, 242.0 us)

commit v7 on v6

--- a/solution.py
+++ b/solution.py
@@ -13,11 +13,13 @@
 UNIT = 128
 SUB = UNIT // WID
 WHOLE = 3
+STEPS = ((0, 1), (2,), (3,), (4,))
+HALVES = 2
 VMEM_LIMIT = 24 << 20
-PIECES = ["A", "0", "kS", "1", "kA", "2", "3", "k0", "4", "k1", "k2", "k3", "k4"]
-GATES = {"R1": ["RA"], "O1": ["OA"], "R2": ["RA"], "O2": ["OA"], "R3": ["R1"], "O3": ["O1"], "R4": ["R2"], "O4": ["O2"], "KA": ["SS"], "K0": ["SS"], "K1": ["SA"], "K2": ["S0"], "K3": ["S0", "S1"], "K4": ["S1"], "S0": ["SA"]}
+PIECES = ["A", "0", "kS", "1", "kA", "2", "k0", "3", "k1", "k2", "k3"]
+GATES = {"R1": ["RA"], "O1": ["OA"], "R2": ["RA"], "O2": ["OA"], "R3": ["R1"], "O3": ["O1"], "KA": ["SS"], "K0": ["SA"], "K1": ["S0"], "K2": ["S0"], "K3": ["S0"]}
 PLAIN = []
-GROUPS = [[0, 1, 2, 3], [4]]
+GROUPS = [[0, 1, 2]]
 SMEM = pl.BlockSpec(memory_space=pltpu.SMEM)
 VMEM = pl.BlockSpec(memory_space=pltpu.VMEM)
 
@@ -64,19 +66,18 @@
 
 def step_layouts():
     layouts = []
-    for step in range(WHOLE + 2):
-        half = step - WHOLE
-        if half < 0:
-            names = [(step, b) for b in range(step + 1)] + [(a, step) for a in range(step)]
+    for step, ids in enumerate(STEPS):
+        if step < HALVES:
+            names = [(c, b) for c in ids for b in range(ids[-1] + 1)] + [(a, c) for a in range(ids[0]) for c in ids]
             rt, size = UNIT, SUB
         else:
-            names = [(step, b) for b in range(WHOLE)] + [(step, "p")] + [(a, step) for a in range(WHOLE)] + [("p", step)] * half
+            c = ids[0]
+            names = [(c, b) for b in range(WHOLE)] + [(c, "p")] + [(a, c) for a in range(WHOLE)] + [("p", c)] * (c - WHOLE)
             rt, size = UNIT // 2, SUB // 2
-        tt = [(("tt", b, a), size) for a, b in names]
-        tj = [(("tj", a, b), size) for a, b in names]
-        rj = [(("rj", step, b), size) for b in range(WID)]
+        parts = [(("rt", c), rt) for c in ids] + [(("tt", b, a), size) for a, b in names]
+        parts = parts, [(("tj", a, b), size) for a, b in names], [(("rj", c, b), size) for c in ids for b in range(WID)]
         spot, at, ends = {}, 0, []
-        for part in ([(("rt", step), rt)] + tt, tj, rj):
+        for part in parts:
             for name, rows in part:
                 spot[name] = (at, rows)
                 at += rows
@@ -94,12 +95,12 @@
     return jnp.concatenate([block[:, : UNIT // 2], block[:, UNIT // 2 :]], axis=0)
 
 
-def put_ring(place_ref, keep, send, spot, base, step, block):
+def put_ring(place_ref, keep, send, spot, base, c, block):
     columns = [lanes(block, b) for b in range(WID)]
-    quarters = [pack(c.T) if step >= WHOLE else c.T for c in columns]
-    put(place_ref, keep, send, base + spot[("rt", step)][0], quarters)
+    quarters = [pack(column.T) if c >= WHOLE else column.T for column in columns]
+    put(place_ref, keep, send, base + spot[("rt", c)][0], quarters)
     for b in range(WID):
-        put(place_ref, keep, send, base + spot[("rj", step, b)][0], split_rows(columns[b]))
+        put(place_ref, keep, send, base + spot[("rj", c, b)][0], split_rows(columns[b]))
 
 
 def put_third(place_ref, keep, send, spot, base, a, b, block):
@@ -118,13 +119,13 @@
     put(place_ref, keep, send, base + spot[(wide, second, first)][0], [pack(q) for q in quarters])
 
 
-def put_halves(place_ref, keep, send, spot, base, step, by_chosen, by_other):
+def put_halves(place_ref, keep, send, spot, base, c, by_chosen, by_other):
     for b in range(WHOLE):
-        put_half(place_ref, keep, send, spot, base, step, b, "tj", "tt", lanes(by_chosen, b))
-        put_half(place_ref, keep, send, spot, base, step, b, "tt", "tj", lanes(by_other, b))
-    put_half(place_ref, keep, send, spot, base, step, "p", "tj", "tt", lanes(by_chosen, WHOLE))
-    if step > WHOLE:
-        put_half(place_ref, keep, send, spot, base, step, "p", "tt", "tj", lanes(by_other, WHOLE))
+        put_half(place_ref, keep, send, spot, base, c, b, "tj", "tt", lanes(by_chosen, b))
+        put_half(place_ref, keep, send, spot, base, c, b, "tt", "tj", lanes(by_other, b))
+    put_half(place_ref, keep, send, spot, base, c, "p", "tj", "tt", lanes(by_chosen, WHOLE))
+    if c > WHOLE:
+        put_half(place_ref, keep, send, spot, base, c, "p", "tt", "tj", lanes(by_other, WHOLE))
 
 
 def reorder_kernel(g_ref, *outs):
@@ -136,16 +137,18 @@
     def pick(wanted):
         return jnp.where(source == wanted, 1.0, 0.0).astype(jnp.bfloat16)
 
-    for c in range(WHOLE):
-        wanted = (lane // SUB) * UNIT + c * SUB + lane % SUB
-        outs[c][...] = dot(g_ref[...], pick(wanted), ((1,), (0,))).astype(jnp.bfloat16)
+    for step in range(HALVES):
+        for i, c in enumerate(STEPS[step]):
+            wanted = (lane // SUB) * UNIT + c * SUB + lane % SUB
+            chunk = dot(g_ref[...], pick(wanted), ((1,), (0,))).astype(jnp.bfloat16)
+            outs[step][:, i * UNIT : (i + 1) * UNIT] = chunk
     size = SUB // 2
     for h in range(2):
         inner = lane % (UNIT // 2)
         wanted = (inner // size) * UNIT + WHOLE * SUB + h * size + inner % size
         upper = dot(g_ref[:half, :], pick(jnp.where(lane < UNIT // 2, wanted, -1)), ((1,), (0,)))
         lower = dot(g_ref[half:, :], pick(jnp.where(lane < UNIT // 2, -1, wanted)), ((1,), (0,)))
-        outs[WHOLE + h][...] = (upper + lower).astype(jnp.bfloat16)
+        outs[HALVES + h][...] = (upper + lower).astype(jnp.bfloat16)
 
 
 def self_kernel(place_ref, a_ref, g_ref, keep, send):
@@ -169,41 +172,49 @@
     ring = row_dot(arrival(ring), own)
     third = row_dot(chosen, arrival(other))
     base = 0
-    for c, layout in enumerate(layouts):
-        spot = layout[0]
-        if c < WHOLE:
-            rows = slice(c * UNIT, (c + 1) * UNIT)
+    for step, layout in enumerate(layouts):
+        spot, ids = layout[0], STEPS[step]
+        for c in ids:
+            first = c * UNIT if c < WHOLE else WHOLE * UNIT + (c - WHOLE) * (UNIT // 2)
+            rows = slice(first, first + (UNIT if c < WHOLE else UNIT // 2))
             put_ring(place_ref, keep, send, spot, base, c, ring[rows])
-            for b in range(c + 1):
-                put_third(place_ref, keep, send, spot, base, c, b, lanes(third[rows], b))
-            for a in range(c):
-                put_third(place_ref, keep, send, spot, base, a, c, lanes(third[a * UNIT : (a + 1) * UNIT], c))
-        else:
-            first = (c - WHOLE) * (UNIT // 2)
-            rows = slice(WHOLE * UNIT + first, WHOLE * UNIT + first + UNIT // 2)
-            put_ring(place_ref, keep, send, spot, base, c, ring[rows])
-            by_other = lanes(third, WHOLE).T[first : first + UNIT // 2]
-            put_halves(place_ref, keep, send, spot, base, c, third[rows], by_other)
+            if c < WHOLE:
+                for b in range(ids[-1] + 1):
+                    put_third(place_ref, keep, send, spot, base, c, b, lanes(third[rows], b))
+                for a in range(ids[0]):
+                    put_third(place_ref, keep, send, spot, base, a, c, lanes(third[a * UNIT : (a + 1) * UNIT], c))
+            else:
+                by_other = lanes(third, WHOLE).T[first - WHOLE * UNIT : first - WHOLE * UNIT + UNIT // 2]
+                put_halves(place_ref, keep, send, spot, base, c, third[rows], by_other)
         base += layout[3]
+
+
+PARTS = 4
+
+
+def own_copies(own_hbm, own, sems):
+    deep = own.shape[0] // PARTS
+    spans = [pl.ds(k * deep, deep) for k in (0, 2, 1, 3)]
+    return [pltpu.make_async_copy(own_hbm.at[at], own.at[at], sems.at[i]) for i, at in enumerate(spans)]
 
 
 def grads_kernel(step, spot, place_ref, own_hbm, *refs):
     n = step + 1
     mine, ring, other, (keep, send, own, fresh, chosen, others, sems) = refs[:n], refs[n : 2 * n], refs[2 * n : 3 * n], refs[3 * n :]
     even = place_ref[0] == 0
-    half = own.shape[0] // 2
+    deep = own.shape[0] // PARTS
+    ids = STEPS[step]
+    before = ids[0] * UNIT
 
     def column(ref, a):
-        return ref.at[:, a * UNIT : (a + 1) * UNIT]
-
-    copies = [
-        pltpu.make_async_copy(ring[step], fresh, sems.at[0]),
-        pltpu.make_async_copy(own_hbm.at[:half], own.at[:half], sems.at[1]),
-        pltpu.make_async_copy(own_hbm.at[half:], own.at[half:], sems.at[2]),
-    ]
-    third = [pltpu.make_async_copy(other[a], column(others, a), sems.at[3 + a]) for a in range(n)]
-    from_ring = [pltpu.make_async_copy(ring[a], column(chosen, a), sems.at[3 + n + a]) for a in range(n)]
-    from_mine = [pltpu.make_async_copy(mine[a], column(chosen, a), sems.at[3 + n + a]) for a in range(n)]
+        return ref.at[:, STEPS[a][0] * UNIT : (STEPS[a][-1] + 1) * UNIT]
+
+    first = pltpu.make_async_copy(ring[step], fresh, sems.at[PARTS])
+    copies = own_copies(own_hbm, own, sems)
+    third = [pltpu.make_async_copy(other[a], column(others, a), sems.at[PARTS + 1 + a]) for a in range(n)]
+    from_ring = [pltpu.make_async_copy(ring[a], column(chosen, a), sems.at[PARTS + 1 + n + a]) for a in range(n)]
+    from_mine = [pltpu.make_async_copy(mine[a], column(chosen, a), sems.at[PARTS + 1 + n + a]) for a in range(n)]
+    first.start()
     for copy in copies:
         copy.start()
 
@@ -219,23 +230,31 @@
 
     for copy in third:
         copy.start()
-    for copy in copies:
+    first.wait()
+    block = jnp.zeros((len(ids) * UNIT, own.shape[1]), jnp.float32)
+    for copy, k in zip(copies, (0, 2, 1, 3)):
         copy.wait()
-    put_ring(place_ref, keep, send, spot, 0, step, dot(fresh[...].T, own[...], ((1,), (0,))))
+        at = pl.ds(k * deep, deep)
+        block = block + dot(fresh[at, :].T, own[at, :], ((1,), (0,)))
+    for i, c in enumerate(ids):
+        put_ring(place_ref, keep, send, spot, 0, c, block[i * UNIT : (i + 1) * UNIT])
     for copy in from_ring + third:
         copy.wait()
     block = dot(column(chosen, step)[...].T, others[...], ((1,), (0,)))
-    for b in range(n):
-        put_third(place_ref, keep, send, spot, 0, step, b, lanes(block, b))
-    if step:
-        block = dot(column(others, step)[...].T, chosen[:, : step * UNIT], ((1,), (0,))).T
-        for a in range(step):
-            put_third(place_ref, keep, send, spot, 0, a, step, block[a * UNIT : (a + 1) * UNIT])
+    for i, c in enumerate(ids):
+        for b in range(ids[-1] + 1):
+            put_third(place_ref, keep, send, spot, 0, c, b, lanes(block[i * UNIT : (i + 1) * UNIT], b))
+    if before:
+        block = dot(column(others, step)[...].T, chosen[:, :before], ((1,), (0,))).T
+        for a in range(ids[0]):
+            for i, c in enumerate(ids):
+                put_third(place_ref, keep, send, spot, 0, a, c, lanes(block[a * UNIT : (a + 1) * UNIT], i))
 
 
 def halves_kernel(step, spot, place_ref, own_hbm, *refs):
-    n = step - WHOLE + 1
-    count = WHOLE + n
+    n = step - HALVES + 1
+    count = step + 1
+    c = STEPS[step][0]
     mine, ring, other, scratch = refs[:count], refs[count : 2 * count], refs[2 * count : 3 * count], refs[3 * count :]
     keep, send, own, fresh, chosen, others, chosen_part, other_part, sems = scratch
     even = place_ref[0] == 0
@@ -243,16 +262,14 @@
     size = UNIT // 2
 
     def home(whole, part, a):
-        return whole.at[:, a * UNIT : (a + 1) * UNIT] if a < WHOLE else part.at[a - WHOLE]
-
-    copies = [
-        pltpu.make_async_copy(ring[step], fresh, sems.at[0]),
-        pltpu.make_async_copy(own_hbm.at[:deep], own.at[:deep], sems.at[1]),
-        pltpu.make_async_copy(own_hbm.at[deep:], own.at[deep:], sems.at[2]),
-    ]
-    third = [pltpu.make_async_copy(other[a], home(others, other_part, a), sems.at[3 + a]) for a in range(count)]
-    from_ring = [pltpu.make_async_copy(ring[a], home(chosen, chosen_part, a), sems.at[3 + count + a]) for a in range(count)]
-    from_mine = [pltpu.make_async_copy(mine[a], home(chosen, chosen_part, a), sems.at[3 + count + a]) for a in range(count)]
+        return whole.at[:, STEPS[a][0] * UNIT : (STEPS[a][-1] + 1) * UNIT] if a < HALVES else part.at[a - HALVES]
+
+    first = pltpu.make_async_copy(ring[step], fresh, sems.at[PARTS])
+    copies = own_copies(own_hbm, own, sems)
+    third = [pltpu.make_async_copy(other[a], home(others, other_part, a), sems.at[PARTS + 1 + a]) for a in range(count)]
+    from_ring = [pltpu.make_async_copy(ring[a], home(chosen, chosen_part, a), sems.at[PARTS + 1 + count + a]) for a in range(count)]
+    from_mine = [pltpu.make_async_copy(mine[a], home(chosen, chosen_part, a), sems.at[PARTS + 1 + count + a]) for a in range(count)]
+    first.start()
     for copy in copies:
         copy.start()
 
@@ -279,27 +296,34 @@
         halves = [against_half(turned, part[h]) for h in range(n)]
         return jnp.concatenate([against(turned, whole), halves[0], halves[-1]], axis=1)
 
-    for copy in copies:
+    first.wait()
+    part = own.shape[0] // PARTS
+    block = jnp.zeros((size, own.shape[1]), jnp.float32)
+    for i, copy in enumerate(copies):
         copy.wait()
-    put_ring(place_ref, keep, send, spot, 0, step, against(fresh[...].T, own))
+        turned = fresh[(i // 2) * part : (i // 2 + 1) * part, :].T[(i % 2) * size : (i % 2 + 1) * size]
+        k = (i % 2) * 2 + i // 2
+        block = block + dot(turned, own[k * part : (k + 1) * part, :], ((1,), (0,)))
+    put_ring(place_ref, keep, send, spot, 0, c, block)
     for copy in from_ring + third:
         copy.wait()
     by_chosen = product_of(chosen_part[n - 1].T, others, other_part)
     by_other = product_of(other_part[n - 1].T, chosen, chosen_part)
-    put_halves(place_ref, keep, send, spot, 0, step, by_chosen, by_other)
-
-
-def halves_scratch(own, n):
-    deep = own.shape[0]
+    put_halves(place_ref, keep, send, spot, 0, c, by_chosen, by_other)
+
+
+def halves_scratch(own, step):
+    deep, n = own.shape[0], step - HALVES + 1
     arrays = [pltpu.VMEM((deep, own.shape[1]), jnp.bfloat16), pltpu.VMEM((deep // 2, UNIT), jnp.bfloat16)]
     arrays += [pltpu.VMEM((deep, WHOLE * UNIT), jnp.bfloat16)] * 2 + [pltpu.VMEM((n, deep // 2, UNIT), jnp.bfloat16)] * 2
-    return (*arrays, pltpu.SemaphoreType.DMA((3 + 2 * (WHOLE + n),)))
-
-
-def grads_scratch(own, n):
-    deep = own.shape[0]
-    arrays = [pltpu.VMEM((deep, width), jnp.bfloat16) for width in (own.shape[1], UNIT, n * UNIT, n * UNIT)]
-    return (*arrays, pltpu.SemaphoreType.DMA((3 + 2 * n,)))
+    return (*arrays, pltpu.SemaphoreType.DMA((PARTS + 1 + 2 * (step + 1),)))
+
+
+def grads_scratch(own, step):
+    deep, ids = own.shape[0], STEPS[step]
+    widths = (own.shape[1], len(ids) * UNIT, (ids[-1] + 1) * UNIT, (ids[-1] + 1) * UNIT)
+    arrays = [pltpu.VMEM((deep, width), jnp.bfloat16) for width in widths]
+    return (*arrays, pltpu.SemaphoreType.DMA((PARTS + 1 + 2 * (step + 1),)))
 
 
 def product(acts, grads, act_at, grad_at, rows):
@@ -321,17 +345,25 @@
         swap_at += n_swap - n_ring
 
 
+def last_kernel(base, first, *refs):
+    acts, near, far, out = refs[:2], refs[2], refs[3], refs[4]
+    n = out.shape[0]
+    near_part = near.at[first : first + n, :]
+    out[...] = product(acts, (near_part, far), base + first, 0, n)
+
+
 def final_kernel(layouts, groups, place_ref, lengths_ref, *refs):
-    count = len(layouts)
+    last = len(layouts) - 1
     selves, acts, out = refs[:2], refs[2:4], refs[-1]
-    grads = [refs[4 + 2 * c : 6 + 2 * c] for c in range(count)]
-    returned = {}
+    grads = [refs[4 + 2 * c : 6 + 2 * c] for c in range(last)]
+    near, far_ring, far_rest = refs[4 + 2 * last : 7 + 2 * last]
+    rings, swaps = refs[7 + 2 * last : -1 : 2], refs[8 + 2 * last : -1 : 2]
+    returned = {last: (rings[-1], 0, swaps[-1], -layouts[last][1])}
     for i, steps in enumerate(groups):
-        ring, swap = refs[4 + 2 * count + 2 * i : 6 + 2 * count + 2 * i]
         ring_at = swap_at = 0
         for c in steps:
             _, n_ring, n_swap, _ = layouts[c]
-            returned[c] = ring, ring_at, swap, swap_at - n_ring
+            returned[c] = rings[i], ring_at, swaps[i], swap_at - n_ring
             ring_at += n_ring
             swap_at += n_swap - n_ring
     even = place_ref[0] == 0
@@ -342,12 +374,18 @@
     columns = width * UNIT + lax.broadcasted_iota(jnp.int32, (UNIT, UNIT), 1)
     line = lax.broadcasted_iota(jnp.int32, (UNIT, UNIT), 0)
 
+    step_of = {c: step for step, ids in enumerate(STEPS) for c in ids}
+
     def block(where, *name):
-        step = max(x for x in name[1 : 2 if name[0] == "rj" else 3] if x != "p")
+        step = step_of[max(x for x in name[1 : 2 if name[0] == "rj" else 3] if x != "p")]
         at, size = layouts[step][0][name]
         if where == "local":
             base = sum(layout[3] for layout in layouts[:step])
-            return product(acts, grads[step], base + at, at, size)
+            if step < last:
+                return product(acts, grads[step], base + at, at, size)
+            n_ring = layouts[last][1]
+            far, far_at = (far_ring, at) if at < n_ring else (far_rest, at - n_ring)
+            return product(acts, (near.at[at : at + size, :], far.at[far_at : far_at + size, :]), base + at, 0, size)
         ring, ring_at, swap, swap_at = returned[step]
         ref, at = (ring, ring_at + at) if where == "ring" else (swap, swap_at + at)
         return ref[at : at + size, :]
@@ -416,8 +454,8 @@
 
     own_g = grads.T
     deep = grads.shape[1]
-    shapes = [jax.ShapeDtypeStruct((deep if c < WHOLE else deep // 2, UNIT), jnp.bfloat16) for c in range(WHOLE + 2)]
-    mine = call(reorder_kernel, tuple(shapes), own_g)
+    shapes = [(deep, len(ids) * UNIT) if step < HALVES else (deep // 2, UNIT) for step, ids in enumerate(STEPS)]
+    mine = call(reorder_kernel, tuple(jax.ShapeDtypeStruct(shape, jnp.bfloat16) for shape in shapes), own_g)
     alive = jnp.max(lengths) > 0
     seen = {}
 
@@ -432,21 +470,23 @@
         seen["R" + name] = lax.ppermute(after(chunk, GATES.get("R" + name)), "tok", down)
         seen["O" + name] = lax.ppermute(after(chunk, GATES.get("O" + name)), "tok", swap)
 
-    def exchange(name, kernel, n, first, *rest, **options):
+    def exchange(name, kernel, n, first, *rest, cuts=(), **options):
+        spans = list(zip((0, *cuts), (*cuts, n)))
+
         def summed(*args):
             keep, send = call(kernel, floats(n), place, *args, scalars=1, **options)
             arrived = over_core(send)
-            return keep[0] + arrived[0], keep[1] + arrived[1]
+            return keep[0] + arrived[0], *[keep[1, a:b] + arrived[1, a:b] for a, b in spans]
 
         def nothing(*args):
-            return (jnp.zeros((n, UNIT), jnp.float32),) * 2
+            return tuple(jnp.zeros((b - a, UNIT), jnp.float32) for a, b in [(0, n)] + spans)
 
         first = after(first, GATES.get("K" + name))
-        if name in PLAIN:
-            near, far = summed(first, *rest)
-        else:
-            near, far = lax.cond(alive, summed, nothing, first, *rest)
-        seen["S" + name] = lax.ppermute(after(far, GATES.get("S" + name)), "wid", [(w, w ^ 2) for w in range(WID)])
+        run = summed if name in PLAIN else lambda *args: lax.cond(alive, summed, nothing, *args)
+        near, *far = run(first, *rest)
+        for i, x in enumerate(far):
+            label = "S" + name + "xy"[i : i + 1] * (len(far) > 1)
+            seen[label] = lax.ppermute(after(x, GATES.get(label)), "wid", [(w, w ^ 2) for w in range(WID)])
         return near
 
     near = {}
@@ -463,13 +503,14 @@
         else:
             c = int(piece[1])
             spot, size = layouts[c][0], layouts[c][3]
-            kernel, scratch = grads_kernel, grads_scratch(own_g, c + 1)
-            if c >= WHOLE:
-                kernel, scratch = halves_kernel, halves_scratch(own_g, c - WHOLE + 1)
+            kernel, scratch = grads_kernel, grads_scratch
+            if c >= HALVES:
+                kernel, scratch = halves_kernel, halves_scratch
             arrived = [seen["%s%d" % (side, a)] for side in "RO" for a in range(c + 1)]
             near[c] = seen["N%d" % c] = exchange(
                 piece[1], lambda *refs, c=c, spot=spot, kernel=kernel: kernel(c, spot, *refs),
-                size, own_g, *mine[: c + 1], *arrived, memory=pl.BlockSpec(memory_space=pl.ANY), scratch=scratch,
+                size, own_g, *mine[: c + 1], *arrived, memory=pl.BlockSpec(memory_space=pl.ANY), scratch=scratch(own_g, c),
+                cuts=(layouts[c][1],) if c + 1 == len(layouts) else (),
             )
 
     returned = []
@@ -484,11 +525,22 @@
         )
         returned += [lax.ppermute(ring, "tok", up), lax.ppermute(swapped, "tok", swap)]
 
-    grams = sum([[near[c], seen["S%d" % c]] for c in range(WHOLE + 2)], [])
+    last = len(layouts) - 1
+    base = sum(layout[3] for layout in layouts[:last])
+    _, n_ring, n_swap, _ = layouts[last]
+    for first, n, far, move in ((0, n_ring, "S%dx" % last, up), (n_ring, n_swap - n_ring, "S%dy" % last, swap)):
+        tile = call(
+            lambda *refs, first=first: last_kernel(base, first, *refs),
+            jax.ShapeDtypeStruct((n, UNIT), jnp.float32), near["A"], seen["SA"], near[last], seen[far],
+        )
+        returned.append(lax.ppermute(tile, "tok", move))
+
+    grams = sum([[near[c], seen["S%d" % c]] for c in range(last)], [near["A"], seen["SA"]])
+    grams += [near[last], seen["S%dx" % last], seen["S%dy" % last]]
     out = call(
         lambda *refs: final_kernel(layouts, GROUPS, *refs),
         jax.ShapeDtypeStruct((5, rows, UNIT), jnp.float32),
-        place, lengths, near["S"], seen["SS"], near["A"], seen["SA"], *grams, *returned, scalars=2,
+        place, lengths, near["S"], seen["SS"], *grams, *returned, scalars=2,
     )
     return out.transpose(1, 0, 2)
 

time: 136 us -> 142 us (1.044)
  waiting for transfers between devices: 52.5 us -> 63.2 us
  starting transfers between devices: 31.8 us -> 28.2 us
  Pallas kernels: 44.5 us -> 42.6 us
    ppermute x7 -> x9, waiting for transfers between devices: 17.6 us -> 44.6 us  [the longest x7 39.7 us: exchange(): lax.ppermute(after(x, GATES.get(label)), 'wid', [(w, w ^ 2) for w in rang...]
    ppermute x6 -> x5, waiting for transfers between devices: 12.3 us -> 1.48 us  [start(): lax.ppermute(after(chunk, GATES.get('R' + name)), 'tok', down)]
    ppermute x6 -> x5, starting transfers between devices: 16.5 us -> 10.8 us  [start(): lax.ppermute(after(chunk, GATES.get('R' + name)), 'tok', down)]
    ppermute x7 -> x9, starting transfers between devices: 5.31 us -> 10.3 us  [the longest x7 8.74 us: exchange(): lax.ppermute(after(x, GATES.get(label)), 'wid', [(w, w ^ 2) for w in rang...]
    ppermute x2 -> x1, waiting for transfers between devices: 2.88 us -> 0.01 us  [shards(): lax.ppermute(swapped, 'tok', swap)]
    ppermute x2 -> x1, starting transfers between devices: 2.95 us -> 0.84 us  [shards(): lax.ppermute(swapped, 'tok', swap)]
    ppermute x2 -> x1, waiting for transfers between devices: 2.07 us -> 0.01 us  [shards(): lax.ppermute(ring, 'tok', up)]
    pallas_call x11, Pallas kernels: 44.5 us -> 42.6 us  [call(): pl.pallas_call(kernel, out_shape=outs, in_specs=[SMEM] * scalars + [memor...]
  transfers between devices with their start and end apart: 30 -> 27, of which waited for: 17 -> 16; matrix products, arithmetic and copies ran while one was open for 4% -> 3% of each run, Pallas kernels for 30% -> 28%
where the time goes in v7:
time: 142 us
  waiting for transfers between devices  63.2 us (45%)
  Pallas kernels  42.6 us (30%)
  starting transfers between devices  28.2 us (20%)
  other arithmetic  4.1 us (3%)
  local copies, waits for them, and re-layouts  2.57 us (2%)
    pallas_call x11, Pallas kernels, call(): pl.pallas_call(kernel, out_shape=outs, in_specs=[SMEM] * scalars + [memor...  42.6 us
    ppermute x7, waiting for transfers between devices, exchange(): lax.ppermute(after(x, GATES.get(label)), 'wid', [(w, w ^ 2) for w in rang...  39.7 us
    ppermute x6, waiting for transfers between devices, over_core(): return lax.ppermute(send, 'wid', [(w, w ^ 1) for w in range(WID)])  14.5 us
    ppermute x5, starting transfers between devices, start(): lax.ppermute(after(chunk, GATES.get('R' + name)), 'tok', down)  10.8 us
    ppermute x7, starting transfers between devices, exchange(): lax.ppermute(after(x, GATES.get(label)), 'wid', [(w, w ^ 2) for w in rang...  8.74 us
    ppermute x5, starting transfers between devices, start(): lax.ppermute(after(chunk, GATES.get('O' + name)), 'tok', swap)  5.84 us
    ppermute x2, waiting for transfers between devices, shards(): returned.append(lax.ppermute(tile, 'tok', move))  4.9 us
  transfers between devices with their start and end apart: 27, of which 16 were waited for; matrix products, arithmetic and copies ran while one was open for 3% of the time, Pallas kernels for 28%

profile of v7, /device:TPU:0, one launch (start us, length us, event | category | flops | bytes accessed | tf_op | source)
XLA Modules:
  0.0 141.5 jit_solution(1831421387514729332)
XLA Ops:
  0.0 5.0 %collective-permute-start.7 = (bf16[512,1024]{1,0:T(8,128)(2,1)}, bf16[512,1024]{1,0:T(8,128)(2,1)}, u32[]{:S(2)}, u32[]{:S(2)}) collective-permute-start(bf16[512,1024]{1,0:T(8,128)(2,1)} %param.15), channel_id=1, source_target_pairs={{0,24},{4,28},{8,0},{12,4},{16,8},{20,12},{24,16},{28,20},{1,25},{... | collective-permute-start | bytes 3145736 | tf_op jit(solution)/shard_map/ppermute | solution.py:470
  8.5 8.1 %conditional.6 = (f32[1024,128]{1,0:T(8,128)S(1)}, f32[1024,128]{1,0:T(8,128)}) conditional(s32[]{:T(128)} %convert_element_type.2, () %tuple.64, (s32[5]{0:T(128)S(1)}, bf16[512,1024]{1,0:T(8,128)(2,1)}, bf16[2752,512]{1,0:T(8,128)(2,1)}) %tuple.105), branch_computations={%region_1.2_spmd, %region_2.3_spmd} | conditional | flops 262144 | bytes 7340088 | solution.py:485
  8.5 4.5 %branch_1_fun.6 = (f32[2,1024,128]{2,1,0:T(8,128)S(1)}, f32[2,1024,128]{2,1,0:T(8,128)S(1)}) custom-call(s32[5]{0:T(128)S(1)} %get-tuple-element.95.place_ref, bf16[512,1024]{1,0:T(8,128)(2,1)} %get-tuple-element.96.a_ref, bf16[2752,512]{1,0:T(8,128)(2,1)} %get-tuple-element.97.g_ref), custom_call_target="tpu_custom_call" | custom-call | tf_op jit(solution)/shard_map/cond/branch_1_fun/pallas_call | solution.py:28
  13.1 2.6 %collective-permute-done = f32[2,1024,128]{2,1,0:T(8,128)S(1)} collective-permute-done((f32[2,1024,128]{2,1,0:T(8,128)S(1)}, f32[2,1024,128]{2,1,0:T(8,128)S(1)}, u32[]{:S(2)}, u32[]{:S(2)}) %collective-permute-start) | collective-permute-done | bytes 1048608 | tf_op jit(solution)/shard_map/cond/branch_1_fun/ppermute | solution.py:453
  18.1 6.4 %shard_map.37 = (bf16[2752,256]{1,0:T(8,128)(2,1)}, bf16[2752,128]{1,0:T(8,128)(2,1)S(1)}, bf16[1376,128]{1,0:T(8,128)(2,1)S(1)}, bf16[1376,128]{1,0:T(8,128)(2,1)}) custom-call(bf16[2752,512]{1,0:T(8,128)(2,1)} %bitcast.34), custom_call_target="tpu_custom_call" | custom-call | tf_op jit(solution)/shard_map/pallas_call | solution.py:28
  25.5 5.3 %collective-permute-done.6.refs_3_ = f32[1024,128]{1,0:T(8,128)S(1)} collective-permute-done((f32[1024,128]{1,0:T(8,128)}, f32[1024,128]{1,0:T(8,128)S(1)}, u32[]{:S(2)}, u32[]{:S(2)}) %collective-permute-start.6) | collective-permute-done | bytes 524320 | tf_op jit(solution)/shard_map/ppermute | solution.py:489
  31.5 8.2 %conditional.7 = (f32[2080,128]{1,0:T(8,128)S(1)}, f32[2080,128]{1,0:T(8,128)S(1)}) conditional(s32[]{:T(128)} %convert_element_type.2, () %tuple.67, (s32[5]{0:T(128)S(1)}, bf16[512,1024]{1,0:T(8,128)(2,1)S(1)}, bf16[512,1024]{1,0:T(8,128)(2,1)}, bf16[512,1024]{1,0:T(8,128)(2,1)}) %tuple.111), branch_computations={%region_3.4_spmd, %region_4.5_spmd} | conditional | flops 532480 | bytes 14909496 | solution.py:485
  31.5 3.7 %branch_1_fun.7 = (f32[2,2080,128]{2,1,0:T(8,128)S(1)}, f32[2,2080,128]{2,1,0:T(8,128)S(1)}) custom-call(s32[5]{0:T(128)S(1)} %get-tuple-element.100.refs_0_, bf16[512,1024]{1,0:T(8,128)(2,1)S(1)} %get-tuple-element.101.refs_1_, bf16[512,1024]{1,0:T(8,128)(2,1)} %get-tuple-element.102.refs_2_, bf16[512,1024]{1,0:T(8,128)(2,1)} %get-tuple-element.103.refs_3_), custom_call_target="tpu_custom_call" | custom-call | tf_op jit(solution)/shard_map/cond/branch_1_fun/pallas_call | solution.py:28
  35.3 4.2 %collective-permute-done.1 = f32[2,2080,128]{2,1,0:T(8,128)S(1)} collective-permute-done((f32[2,2080,128]{2,1,0:T(8,128)S(1)}, f32[2,2080,128]{2,1,0:T(8,128)S(1)}, u32[]{:S(2)}, u32[]{:S(2)}) %collective-permute-start.1) | collective-permute-done | bytes 2129952 | tf_op jit(solution)/shard_map/cond/branch_1_fun/ppermute | solution.py:453
  45.4 20.8 %collective-permute-done.9.refs_1_.refs_5_ = f32[2080,128]{1,0:T(8,128)S(1)} collective-permute-done((f32[2080,128]{1,0:T(8,128)S(1)}, f32[2080,128]{1,0:T(8,128)S(1)}, u32[]{:S(2)}, u32[]{:S(2)}) %collective-permute-start.9) | collective-permute-done | bytes 1064992 | tf_op jit(solution)/shard_map/ppermute | solution.py:489
  66.2 8.1 %conditional.8 = (f32[768,128]{1,0:T(8,128)}, f32[768,128]{1,0:T(8,128)S(1)}) conditional(s32[]{:T(128)} %convert_element_type.2, () %tuple.72, (s32[5]{0:T(128)S(1)}, bf16[2752,512]{1,0:T(8,128)(2,1)}, bf16[2752,256]{1,0:T(8,128)(2,1)}, bf16[2752,256]{1,0:T(8,128)(2,1)}, bf16[2752,256]{1,0:T(8,128)(2,1)}) %tuple.106), branch_computations={%region_5.6_spmd, %region_6.7_spmd} | conditional | flops 196608 | bytes 5505080 | solution.py:485
  66.2 5.0 %branch_1_fun.8 = (f32[2,768,128]{2,1,0:T(8,128)S(1)}, f32[2,768,128]{2,1,0:T(8,128)S(1)}) custom-call(s32[5]{0:T(128)S(1)} %get-tuple-element.106.refs_0_, bf16[2752,512]{1,0:T(8,128)(2,1)} %get-tuple-element.107.refs_1_, bf16[2752,256]{1,0:T(8,128)(2,1)} %get-tuple-element.108.refs_2_, bf16[2752,256]{1,0:T(8,128)(2,1)} %get-tuple-element.109.refs_3_, ...), custom_call_target="tpu_custom_call" | custom-call | tf_op jit(solution)/shard_map/cond/branch_1_fun/pallas_call | solution.py:28
  79.9 6.6 %collective-permute-done.12.refs_3_.refs_7_ = f32[768,128]{1,0:T(8,128)S(1)} collective-permute-done((f32[768,128]{1,0:T(8,128)}, f32[768,128]{1,0:T(8,128)S(1)}, u32[]{:S(2)}, u32[]{:S(2)}) %collective-permute-start.12) | collective-permute-done | bytes 393248 | tf_op jit(solution)/shard_map/ppermute | solution.py:489
  86.5 7.8 %conditional.9 = (f32[576,128]{1,0:T(8,128)}, f32[576,128]{1,0:T(8,128)S(1)}) conditional(s32[]{:T(128)} %convert_element_type.2, () %tuple.77, (s32[5]{0:T(128)S(1)}, bf16[2752,512]{1,0:T(8,128)(2,1)}, bf16[2752,256]{1,0:T(8,128)(2,1)}, bf16[2752,128]{1,0:T(8,128)(2,1)S(1)}, bf16[2752,256]{1,0:T(8,128)(2,1)}, /*index=5*/bf16[2752,128]{1,0:T(8,128)(2,1)}, ...), branch_computations={%region_7.8_spmd, %region_8.9_spmd} | conditional | flops 147456 | bytes 4128824 | solution.py:485
  86.5 4.9 %branch_1_fun.9 = (f32[2,576,128]{2,1,0:T(8,128)S(1)}, f32[2,576,128]{2,1,0:T(8,128)S(1)}) custom-call(s32[5]{0:T(128)S(1)} %get-tuple-element.113.refs_0_, bf16[2752,512]{1,0:T(8,128)(2,1)} %get-tuple-element.114.refs_1_, bf16[2752,256]{1,0:T(8,128)(2,1)} %get-tuple-element.115.refs_2_, bf16[2752,128]{1,0:T(8,128)(2,1)S(1)} %get-tuple-element.116.refs_3_, ...), custom_call_target="tpu_custom_call" | custom-call | tf_op jit(solution)/shard_map/cond/branch_1_fun/pallas_call | solution.py:28
  96.5 7.2 %conditional.10 = (f32[352,128]{1,0:T(8,128)S(1)}, f32[352,128]{1,0:T(8,128)S(1)}) conditional(s32[]{:T(128)} %convert_element_type.2, () %tuple.81, (s32[5]{0:T(128)S(1)}, bf16[2752,512]{1,0:T(8,128)(2,1)}, bf16[2752,256]{1,0:T(8,128)(2,1)}, bf16[2752,128]{1,0:T(8,128)(2,1)S(1)}, bf16[1376,128]{1,0:T(8,128)(2,1)S(1)}, ...), branch_computations={%region_9.10_spmd, %region_10.11_spmd} | conditional | flops 90112 | bytes 2523192 | solution.py:485
  96.6 5.4 %branch_1_fun.10 = (f32[2,352,128]{2,1,0:T(8,128)S(1)}, f32[2,352,128]{2,1,0:T(8,128)S(1)}) custom-call(s32[5]{0:T(128)S(1)} %get-tuple-element.123.refs_0_, bf16[2752,512]{1,0:T(8,128)(2,1)} %get-tuple-element.124.refs_1_, bf16[2752,256]{1,0:T(8,128)(2,1)} %get-tuple-element.125.refs_2_, bf16[2752,128]{1,0:T(8,128)(2,1)S(1)} %get-tuple-element.126.refs_3_, ...), custom_call_target="tpu_custom_call" | custom-call | tf_op jit(solution)/shard_map/cond/branch_1_fun/pallas_call | solution.py:28
  107.0 3.5 %collective-permute-done.18.refs_7_.refs_11_ = f32[352,128]{1,0:T(8,128)S(1)} collective-permute-done((f32[352,128]{1,0:T(8,128)S(1)}, f32[352,128]{1,0:T(8,128)S(1)}, u32[]{:S(2)}, u32[]{:S(2)}) %collective-permute-start.18) | collective-permute-done | bytes 180256 | tf_op jit(solution)/shard_map/ppermute | solution.py:489
  110.4 2.4 %shard_map.38 = (f32[848,128]{1,0:T(8,128)S(1)}, f32[400,128]{1,0:T(8,128)}) custom-call(f32[2080,128]{1,0:T(8,128)} %copy-done.2, f32[2080,128]{1,0:T(8,128)S(1)} %collective-permute-done.9.refs_1_.refs_5_, f32[768,128]{1,0:T(8,128)} %get-tuple-element.203.refs_2_.refs_6_, f32[768,128]{1,0:T(8,128)S(1)} %collective-permute-done.12.refs_3_.refs_7_, ...), custom_call_target="tpu_custom_call" | custom-call | tf_op jit(solution)/shard_map/pallas_call | solution.py:28
  117.1 7.7 %conditional.11 = (f32[384,128]{1,0:T(8,128)S(1)}, f32[192,128]{1,0:T(8,128)S(1)}, f32[192,128]{1,0:T(8,128)S(1)}) conditional(s32[]{:T(128)} %convert_element_type.2, () %tuple.85, (s32[5]{0:T(128)S(1)}, bf16[2752,512]{1,0:T(8,128)(2,1)S(1)}, bf16[2752,256]{1,0:T(8,128)(2,1)}, bf16[2752,128]{1,0:T(8,128)(2,1)S(1)}, bf16[1376,128]{1,0:T(8,128)(2,1)}, ...), branch_computations={%region_11.12_spmd, %region_12.13_spmd} | conditional | flops 98304 | bytes 2752576 | solution.py:485
  117.1 5.8 %branch_1_fun.11 = (f32[2,384,128]{2,1,0:T(8,128)S(1)}, f32[2,384,128]{2,1,0:T(8,128)S(1)}) custom-call(s32[5]{0:T(128)S(1)} %get-tuple-element.136.refs_0_, bf16[2752,512]{1,0:T(8,128)(2,1)S(1)} %get-tuple-element.137.refs_1_, bf16[2752,256]{1,0:T(8,128)(2,1)} %get-tuple-element.138.refs_2_, bf16[2752,128]{1,0:T(8,128)(2,1)S(1)} %get-tuple-element.139.refs_3_, ...), custom_call_target="tpu_custom_call" | custom-call | tf_op jit(solution)/shard_map/cond/branch_1_fun/pallas_call | solution.py:28
  126.9 3.6 %collective-permute-done.21.refs_3_.refs_13_ = f32[192,128]{1,0:T(8,128)S(1)} collective-permute-done((f32[192,128]{1,0:T(8,128)S(1)}, f32[192,128]{1,0:T(8,128)S(1)}, u32[]{:S(2)}, u32[]{:S(2)}) %collective-permute-start.21) | collective-permute-done | bytes 98336 | tf_op jit(solution)/shard_map/ppermute | solution.py:489
  133.4 3.5 %collective-permute-done.26.refs_18_ = f32[128,128]{1,0:T(8,128)S(1)} collective-permute-done((f32[128,128]{1,0:T(8,128)S(1)}, f32[128,128]{1,0:T(8,128)S(1)}, u32[]{:S(2)}, u32[]{:S(2)}) %collective-permute-start.26) | collective-permute-done | bytes 65568 | tf_op jit(solution)/shard_map/ppermute | solution.py:536
  138.4 3.1 %shard_map.41 = f32[5,512,128]{2,1,0:T(8,128)} custom-call(s32[5]{0:T(128)S(1)} %stack.23.refs_0_, s32[8]{0:T(128)S(1)} %copy-done, f32[1024,128]{1,0:T(8,128)S(1)} %copy-done.8, f32[1024,128]{1,0:T(8,128)S(1)} %collective-permute-done.6.refs_3_, f32[2080,128]{1,0:T(8,128)S(1)} %copy-done.3, f32[2080,128]{1,0:T(8,128)S(1)} %collective-permute-done.9.refs_1_.refs_5_, ...), custom_call_target="tpu_custom_call" | custom-call | tf_op jit(solution)/shard_map/pallas_call | solution.py:28
  (84 shorter events, 44.4 us)
Async XLA Ops:
  0.0 30.8 %collective-permute-start.7 = (bf16[512,1024]{1,0:T(8,128)(2,1)}, bf16[512,1024]{1,0:T(8,128)(2,1)}, u32[]{:S(2)}, u32[]{:S(2)}) collective-permute-start(bf16[512,1024]{1,0:T(8,128)(2,1)} %param.15), channel_id=1, source_target_pairs={{0,24},{4,28},{8,0},{12,4},{16,8},{20,12},{24,16},{28,20},{1,25},{... | collective-permute-start | bytes 3145736 | tf_op jit(solution)/shard_map/ppermute | solution.py:470
  5.0 26.4 %collective-permute-start.8 = (bf16[512,1024]{1,0:T(8,128)(2,1)}, bf16[512,1024]{1,0:T(8,128)(2,1)}, u32[]{:S(2)}, u32[]{:S(2)}) collective-permute-start(bf16[512,1024]{1,0:T(8,128)(2,1)} %param.15), channel_id=1, source_target_pairs={{0,4},{4,0},{8,12},{12,8},{16,20},{20,16},{24,28},{28,24},{1,5},{5... | collective-permute-start | bytes 3145736 | tf_op jit(solution)/shard_map/ppermute | solution.py:471
  13.0 2.7 %collective-permute-start = (f32[2,1024,128]{2,1,0:T(8,128)S(1)}, f32[2,1024,128]{2,1,0:T(8,128)S(1)}, u32[]{:S(2)}, u32[]{:S(2)}) collective-permute-start(f32[2,1024,128]{2,1,0:T(8,128)S(1)} %get-tuple-element.99), channel_id=1, source_target_pairs={{0,1},{1,0},{2,3},{3,2},{4,5},{5,4},{6,7},{7,6},{8,9},{9,8},{10,11... | collective-permute-start | bytes 3145736 | tf_op jit(solution)/shard_map/cond/branch_1_fun/ppermute | solution.py:453
  16.6 14.2 %collective-permute-start.6 = (f32[1024,128]{1,0:T(8,128)}, f32[1024,128]{1,0:T(8,128)S(1)}, u32[]{:S(2)}, u32[]{:S(2)}) collective-permute-start(f32[1024,128]{1,0:T(8,128)} %get-tuple-element.192), channel_id=1, source_target_pairs={{0,2},{1,3},{2,0},{3,1},{4,6},{5,7},{6,4},{7,5},{8,10},{9,11},{10,... | collective-permute-start | bytes 1572872 | tf_op jit(solution)/shard_map/ppermute | solution.py:489
  24.5 41.7 %collective-permute-start.10 = (bf16[2752,256]{1,0:T(8,128)(2,1)}, bf16[2752,256]{1,0:T(8,128)(2,1)}, u32[]{:S(2)}, u32[]{:S(2)}) collective-permute-start(bf16[2752,256]{1,0:T(8,128)(2,1)} %get-tuple-element.202), channel_id=1, source_target_pairs={{0,24},{4,28},{8,0},{12,4},{16,8},{20,12},{24,16},{28,20},{1,25},{... | collective-permute-start | bytes 4227080 | tf_op jit(solution)/shard_map/ppermute | solution.py:470
  25.0 41.2 %collective-permute-start.11 = (bf16[2752,256]{1,0:T(8,128)(2,1)}, bf16[2752,256]{1,0:T(8,128)(2,1)}, u32[]{:S(2)}, u32[]{:S(2)}) collective-permute-start(bf16[2752,256]{1,0:T(8,128)(2,1)} %get-tuple-element.202), channel_id=1, source_target_pairs={{0,4},{4,0},{8,12},{12,8},{16,20},{20,16},{24,28},{28,24},{1,5},{5... | collective-permute-start | bytes 4227080 | tf_op jit(solution)/shard_map/ppermute | solution.py:471
  35.2 4.3 %collective-permute-start.1 = (f32[2,2080,128]{2,1,0:T(8,128)S(1)}, f32[2,2080,128]{2,1,0:T(8,128)S(1)}, u32[]{:S(2)}, u32[]{:S(2)}) collective-permute-start(f32[2,2080,128]{2,1,0:T(8,128)S(1)} %get-tuple-element.105), channel_id=1, source_target_pairs={{0,1},{1,0},{2,3},{3,2},{4,5},{5,4},{6,7},{7,6},{8,9},{9,8},{10,11... | collective-permute-start | bytes 6389768 | tf_op jit(solution)/shard_map/cond/branch_1_fun/ppermute | solution.py:453
  40.6 25.6 %collective-permute-start.9 = (f32[2080,128]{1,0:T(8,128)S(1)}, f32[2080,128]{1,0:T(8,128)S(1)}, u32[]{:S(2)}, u32[]{:S(2)}) collective-permute-start(f32[2080,128]{1,0:T(8,128)S(1)} %get-tuple-element.199), channel_id=1, source_target_pairs={{0,2},{1,3},{2,0},{3,1},{4,6},{5,7},{6,4},{7,5},{8,10},{9,11},{10,... | collective-permute-start | bytes 3194888 | tf_op jit(solution)/shard_map/ppermute | solution.py:489
  42.2 37.7 %collective-permute-start.13 = (bf16[2752,128]{1,0:T(8,128)(2,1)S(1)}, bf16[2752,128]{1,0:T(8,128)(2,1)}, u32[]{:S(2)}, u32[]{:S(2)}) collective-permute-start(bf16[2752,128]{1,0:T(8,128)(2,1)S(1)} %get-tuple-element.212), channel_id=1, source_target_pairs={{0,24},{4,28},{8,0},{12,4},{16,8},{20,12},{24,16},{28,20},{1,25},{... | collective-permute-start | bytes 2113544 | tf_op jit(solution)/shard_map/ppermute | solution.py:470
  43.9 36.0 %collective-permute-start.14 = (bf16[2752,128]{1,0:T(8,128)(2,1)S(1)}, bf16[2752,128]{1,0:T(8,128)(2,1)}, u32[]{:S(2)}, u32[]{:S(2)}) collective-permute-start(bf16[2752,128]{1,0:T(8,128)(2,1)S(1)} %get-tuple-element.212), channel_id=1, source_target_pairs={{0,4},{4,0},{8,12},{12,8},{16,20},{20,16},{24,28},{28,24},{1,5},{5... | collective-permute-start | bytes 2113544 | tf_op jit(solution)/shard_map/ppermute | solution.py:471
  71.2 2.4 %collective-permute-start.2 = (f32[2,768,128]{2,1,0:T(8,128)S(1)}, f32[2,768,128]{2,1,0:T(8,128)S(1)}, u32[]{:S(2)}, u32[]{:S(2)}) collective-permute-start(f32[2,768,128]{2,1,0:T(8,128)S(1)} %get-tuple-element.112), channel_id=1, source_target_pairs={{0,1},{1,0},{2,3},{3,2},{4,5},{5,4},{6,7},{7,6},{8,9},{9,8},{10,11... | collective-permute-start | bytes 2359304 | tf_op jit(solution)/shard_map/cond/branch_1_fun/ppermute | solution.py:453
  75.1 11.4 %collective-permute-start.12 = (f32[768,128]{1,0:T(8,128)}, f32[768,128]{1,0:T(8,128)S(1)}, u32[]{:S(2)}, u32[]{:S(2)}) collective-permute-start(f32[768,128]{1,0:T(8,128)} %copy-done.12), channel_id=1, source_target_pairs={{0,2},{1,3},{2,0},{3,1},{4,6},{5,7},{6,4},{7,5},{8,10},{9,11},{10,... | collective-permute-start | bytes 1179656 | tf_op jit(solution)/shard_map/ppermute | solution.py:489
  76.6 19.9 %collective-permute-start.16 = (bf16[1376,128]{1,0:T(8,128)(2,1)S(1)}, bf16[1376,128]{1,0:T(8,128)(2,1)}, u32[]{:S(2)}, u32[]{:S(2)}) collective-permute-start(bf16[1376,128]{1,0:T(8,128)(2,1)S(1)} %get-tuple-element.219), channel_id=1, source_target_pairs={{0,24},{4,28},{8,0},{12,4},{16,8},{20,12},{24,16},{28,20},{1,25},{... | collective-permute-start | bytes 1056776 | tf_op jit(solution)/shard_map/ppermute | solution.py:470
  78.4 18.1 %collective-permute-start.17 = (bf16[1376,128]{1,0:T(8,128)(2,1)S(1)}, bf16[1376,128]{1,0:T(8,128)(2,1)}, u32[]{:S(2)}, u32[]{:S(2)}) collective-permute-start(bf16[1376,128]{1,0:T(8,128)(2,1)S(1)} %get-tuple-element.219), channel_id=1, source_target_pairs={{0,4},{4,0},{8,12},{12,8},{16,20},{20,16},{24,28},{28,24},{1,5},{5... | collective-permute-start | bytes 1056776 | tf_op jit(solution)/shard_map/ppermute | solution.py:471
  95.0 15.4 %collective-permute-start.15 = (f32[576,128]{1,0:T(8,128)}, f32[576,128]{1,0:T(8,128)S(1)}, u32[]{:S(2)}, u32[]{:S(2)}) collective-permute-start(f32[576,128]{1,0:T(8,128)} %copy-done.13), channel_id=1, source_target_pairs={{0,2},{1,3},{2,0},{3,1},{4,6},{5,7},{6,4},{7,5},{8,10},{9,11},{10,... | collective-permute-start | bytes 884744 | tf_op jit(solution)/shard_map/ppermute | solution.py:489
  103.8 6.7 %collective-permute-start.18 = (f32[352,128]{1,0:T(8,128)S(1)}, f32[352,128]{1,0:T(8,128)S(1)}, u32[]{:S(2)}, u32[]{:S(2)}) collective-permute-start(f32[352,128]{1,0:T(8,128)S(1)} %get-tuple-element.221), channel_id=1, source_target_pairs={{0,2},{1,3},{2,0},{3,1},{4,6},{5,7},{6,4},{7,5},{8,10},{9,11},{10,... | collective-permute-start | bytes 540680 | tf_op jit(solution)/shard_map/ppermute | solution.py:489
  104.4 10.8 %collective-permute-start.19 = (bf16[1376,128]{1,0:T(8,128)(2,1)}, bf16[1376,128]{1,0:T(8,128)(2,1)S(1)}, u32[]{:S(2)}, u32[]{:S(2)}) collective-permute-start(bf16[1376,128]{1,0:T(8,128)(2,1)} %get-tuple-element.224), channel_id=1, source_target_pairs={{0,24},{4,28},{8,0},{12,4},{16,8},{20,12},{24,16},{28,20},{1,25},{... | collective-permute-start | bytes 1056776 | tf_op jit(solution)/shard_map/ppermute | solution.py:470
  106.1 11.0 %collective-permute-start.20 = (bf16[1376,128]{1,0:T(8,128)(2,1)}, bf16[1376,128]{1,0:T(8,128)(2,1)S(1)}, u32[]{:S(2)}, u32[]{:S(2)}) collective-permute-start(bf16[1376,128]{1,0:T(8,128)(2,1)} %get-tuple-element.224), channel_id=1, source_target_pairs={{0,4},{4,0},{8,12},{12,8},{16,20},{20,16},{24,28},{28,24},{1,5},{5... | collective-permute-start | bytes 1056776 | tf_op jit(solution)/shard_map/ppermute | solution.py:471
  112.8 25.5 %collective-permute-start.23 = (f32[848,128]{1,0:T(8,128)S(1)}, f32[848,128]{1,0:T(8,128)S(1)}, u32[]{:S(2)}, u32[]{:S(2)}) collective-permute-start(f32[848,128]{1,0:T(8,128)S(1)} %get-tuple-element.228), channel_id=1, source_target_pairs={{0,8},{4,12},{8,16},{12,20},{16,24},{20,28},{24,0},{28,4},{1,9},{5... | collective-permute-start | bytes 1302536 | tf_op jit(solution)/shard_map/ppermute | solution.py:526
  112.8 25.5 %collective-permute-start.24 = (f32[400,128]{1,0:T(8,128)}, f32[400,128]{1,0:T(8,128)S(1)}, u32[]{:S(2)}, u32[]{:S(2)}) collective-permute-start(f32[400,128]{1,0:T(8,128)} %get-tuple-element.229), channel_id=1, source_target_pairs={{0,4},{4,0},{8,12},{12,8},{16,20},{20,16},{24,28},{28,24},{1,5},{5... | collective-permute-start | bytes 614408 | tf_op jit(solution)/shard_map/ppermute | solution.py:526
  124.8 5.7 %collective-permute-start.21 = (f32[192,128]{1,0:T(8,128)S(1)}, f32[192,128]{1,0:T(8,128)S(1)}, u32[]{:S(2)}, u32[]{:S(2)}) collective-permute-start(f32[192,128]{1,0:T(8,128)S(1)} %get-tuple-element.226), channel_id=1, source_target_pairs={{0,2},{1,3},{2,0},{3,1},{4,6},{5,7},{6,4},{7,5},{8,10},{9,11},{10,... | collective-permute-start | bytes 294920 | tf_op jit(solution)/shard_map/ppermute | solution.py:489
  126.8 5.8 %collective-permute-start.22 = (f32[192,128]{1,0:T(8,128)S(1)}, f32[192,128]{1,0:T(8,128)S(1)}, u32[]{:S(2)}, u32[]{:S(2)}) collective-permute-start(f32[192,128]{1,0:T(8,128)S(1)} %get-tuple-element.227), channel_id=1, source_target_pairs={{0,2},{1,3},{2,0},{3,1},{4,6},{5,7},{6,4},{7,5},{8,10},{9,11},{10,... | collective-permute-start | bytes 294920 | tf_op jit(solution)/shard_map/ppermute | solution.py:489
  131.9 6.5 %collective-permute-start.25 = (f32[192,128]{1,0:T(8,128)S(1)}, f32[192,128]{1,0:T(8,128)S(1)}, u32[]{:S(2)}, u32[]{:S(2)}) collective-permute-start(f32[192,128]{1,0:T(8,128)S(1)} %shard_map.39), channel_id=1, source_target_pairs={{0,8},{4,12},{8,16},{12,20},{16,24},{20,28},{24,0},{28,4},{1,9},{5... | collective-permute-start | bytes 294920 | tf_op jit(solution)/shard_map/ppermute | solution.py:536
  132.6 4.3 %collective-permute-start.26 = (f32[128,128]{1,0:T(8,128)S(1)}, f32[128,128]{1,0:T(8,128)S(1)}, u32[]{:S(2)}, u32[]{:S(2)}) collective-permute-start(f32[128,128]{1,0:T(8,128)S(1)} %shard_map.40), channel_id=1, source_target_pairs={{0,4},{4,0},{8,12},{12,8},{16,20},{20,16},{24,28},{28,24},{1,5},{5... | collective-permute-start | bytes 196616 | tf_op jit(solution)/shard_map/ppermute | solution.py:536
  (17 other events, 218.8 us)

commit v8 on v5

--- a/solution.py
+++ b/solution.py
@@ -13,10 +13,10 @@
 UNIT = 128
 SUB = UNIT // WID
 VMEM_LIMIT = 24 << 20
-PIECES = ['A', '0', 'kS', '1', 'kA', '2', '3', 'k0', 'k1', 'k2', 'k3']
-GATES = {'R1': ['RA'], 'O1': ['OA'], 'R2': ['RA'], 'O2': ['OA'], 'R3': ['R1'], 'O3': ['O1'], 'KA': ['SS'], 'K0': ['SS'], 'K1': ['SA'], 'K2': ['S0'], 'K3': ['S0', 'S1'], 'SA': [], 'S0': ['SA'], 'S1': [], 'S2': [], 'S3': ['S0', 'S1'], 'G0': [], 'G1': []}
+PIECES = ['A', '0', 'kS', '1', 'kA', '2', 'k0', '3', 'k1', 'g0', 'k2', 'g1', 'k3']
+GATES = {'R1': ['RA'], 'O1': ['OA'], 'R2': ['RA'], 'O2': ['OA'], 'R3': ['R1'], 'O3': ['O1'], 'KA': [], 'K0': ['SS'], 'K1': ['SS'], 'K2': ['S0'], 'K3': ['V0'], 'SA': [], 'S0': [], 'S1': ['S0'], 'S2': [], 'S3x': [], 'S3y': ['V1'], 'G0': ['R2'], 'G1': []}
 PLAIN = []
-GROUPS = [[0, 1, 2], [3]]
+GROUPS = [[0, 1], [2]]
 SMEM = pl.BlockSpec(memory_space=pltpu.SMEM)
 VMEM = pl.BlockSpec(memory_space=pltpu.VMEM)
 
@@ -132,23 +132,30 @@
             put_third(place_ref, keep, send, layouts[step][0], base, a, b, lanes(block, b))
 
 
+PARTS = 4
+
+
+def own_copies(own_hbm, own, sems):
+    deep = own.shape[0] // PARTS
+    spans = [pl.ds(k * deep, deep) for k in (0, 2, 1, 3)]
+    return [pltpu.make_async_copy(own_hbm.at[at], own.at[at], sems.at[i]) for i, at in enumerate(spans)]
+
+
 def grads_kernel(step, spot, place_ref, own_hbm, *refs):
     n = step + 1
     mine, ring, other, (keep, send, own, fresh, chosen, others, sems) = refs[:n], refs[n : 2 * n], refs[2 * n : 3 * n], refs[3 * n :]
     even = place_ref[0] == 0
-    half = own.shape[0] // 2
+    deep = own.shape[0] // PARTS
 
     def column(ref, a):
         return ref.at[:, a * UNIT : (a + 1) * UNIT]
 
-    copies = [
-        pltpu.make_async_copy(ring[step], fresh, sems.at[0]),
-        pltpu.make_async_copy(own_hbm.at[:half], own.at[:half], sems.at[1]),
-        pltpu.make_async_copy(own_hbm.at[half:], own.at[half:], sems.at[2]),
-    ]
-    third = [pltpu.make_async_copy(other[a], column(others, a), sems.at[3 + a]) for a in range(n)]
-    from_ring = [pltpu.make_async_copy(ring[a], column(chosen, a), sems.at[3 + n + a]) for a in range(n)]
-    from_mine = [pltpu.make_async_copy(mine[a], column(chosen, a), sems.at[3 + n + a]) for a in range(n)]
+    first = pltpu.make_async_copy(ring[step], fresh, sems.at[PARTS])
+    copies = own_copies(own_hbm, own, sems)
+    third = [pltpu.make_async_copy(other[a], column(others, a), sems.at[PARTS + 1 + a]) for a in range(n)]
+    from_ring = [pltpu.make_async_copy(ring[a], column(chosen, a), sems.at[PARTS + 1 + n + a]) for a in range(n)]
+    from_mine = [pltpu.make_async_copy(mine[a], column(chosen, a), sems.at[PARTS + 1 + n + a]) for a in range(n)]
+    first.start()
     for copy in copies:
         copy.start()
 
@@ -164,9 +171,13 @@
 
     for copy in third:
         copy.start()
-    for copy in copies:
+    first.wait()
+    block = jnp.zeros((UNIT, own.shape[1]), jnp.float32)
+    for copy, k in zip(copies, (0, 2, 1, 3)):
         copy.wait()
-    put_ring(place_ref, keep, send, spot, 0, step, dot(fresh[...].T, own[...], ((1,), (0,))))
+        at = pl.ds(k * deep, deep)
+        block = block + dot(fresh[at, :].T, own[at, :], ((1,), (0,)))
+    put_ring(place_ref, keep, send, spot, 0, step, block)
     for copy in from_ring + third:
         copy.wait()
     block = dot(column(chosen, step)[...].T, others[...], ((1,), (0,)))
@@ -181,7 +192,7 @@
 def grads_scratch(own, n):
     deep = own.shape[0]
     arrays = [pltpu.VMEM((deep, width), jnp.bfloat16) for width in (own.shape[1], UNIT, n * UNIT, n * UNIT)]
-    return (*arrays, pltpu.SemaphoreType.DMA((3 + 2 * n,)))
+    return (*arrays, pltpu.SemaphoreType.DMA((PARTS + 1 + 2 * n,)))
 
 
 def product(acts, grads, act_at, grad_at, rows):
@@ -203,17 +214,26 @@
         swap_at += n_swap - n_ring
 
 
+def last_kernel(base, first, *refs):
+    acts, near, far, out = refs[:2], refs[2], refs[3], refs[4]
+    n = out.shape[0]
+    near_part = near.at[first : first + n, :]
+    out[...] = product(acts, (near_part, far), base + first, 0, n)
+
+
 def final_kernel(layouts, groups, place_ref, lengths_ref, *refs):
     units = len(layouts)
+    last = units - 1
     selves, acts, out = refs[:2], refs[2:4], refs[-1]
-    grads = [refs[4 + 2 * c : 6 + 2 * c] for c in range(units)]
-    returned = {}
+    grads = [refs[4 + 2 * c : 6 + 2 * c] for c in range(last)]
+    near, far_ring, far_rest = refs[4 + 2 * last : 7 + 2 * last]
+    rings, swaps = refs[7 + 2 * last : -1 : 2], refs[8 + 2 * last : -1 : 2]
+    returned = {last: (rings[-1], 0, swaps[-1], -layouts[last][1])}
     for i, steps in enumerate(groups):
-        ring, swap = refs[4 + 2 * units + 2 * i : 6 + 2 * units + 2 * i]
         ring_at = swap_at = 0
         for c in steps:
             _, n_ring, n_swap, _ = layouts[c]
-            returned[c] = ring, ring_at, swap, swap_at - n_ring
+            returned[c] = rings[i], ring_at, swaps[i], swap_at - n_ring
             ring_at += n_ring
             swap_at += n_swap - n_ring
     even = place_ref[0] == 0
@@ -229,7 +249,11 @@
         size = UNIT if name[0] == "rt" else SUB
         if where == "local":
             base = sum(layouts[s][3] for s in range(step))
-            return product(acts, grads[step], base + spot, spot, size)
+            if step < last:
+                return product(acts, grads[step], base + spot, spot, size)
+            n_ring = layouts[last][1]
+            far, at = (far_ring, spot) if spot < n_ring else (far_rest, spot - n_ring)
+            return product(acts, (near.at[spot : spot + size, :], far.at[at : at + size, :]), base + spot, 0, size)
         ring, ring_at, swap, swap_at = returned[step]
         ref, at = (ring, ring_at + spot) if where == "ring" else (swap, swap_at + spot)
         return ref[at : at + size, :]
@@ -290,21 +314,23 @@
         seen["R" + name] = lax.ppermute(after(chunk, GATES.get("R" + name)), "tok", down)
         seen["O" + name] = lax.ppermute(after(chunk, GATES.get("O" + name)), "tok", swap)
 
-    def exchange(name, kernel, n, first, *rest, **options):
+    def exchange(name, kernel, n, first, *rest, cuts=(), **options):
+        spans = list(zip((0, *cuts), (*cuts, n)))
+
         def summed(*args):
             keep, send = call(kernel, floats(n), place, *args, scalars=1, **options)
             arrived = over_core(send)
-            return keep[0] + arrived[0], keep[1] + arrived[1]
+            return keep[0] + arrived[0], *[keep[1, a:b] + arrived[1, a:b] for a, b in spans]
 
         def nothing(*args):
-            return (jnp.zeros((n, UNIT), jnp.float32),) * 2
+            return tuple(jnp.zeros((b - a, UNIT), jnp.float32) for a, b in [(0, n)] + spans)
 
         first = after(first, GATES.get("K" + name))
-        if name in PLAIN:
-            near, far = summed(first, *rest)
-        else:
-            near, far = lax.cond(alive, summed, nothing, first, *rest)
-        seen["S" + name] = lax.ppermute(after(far, GATES.get("S" + name)), "wid", [(w, w ^ 2) for w in range(WID)])
+        run = summed if name in PLAIN else lambda *args: lax.cond(alive, summed, nothing, *args)
+        near, *far = run(first, *rest)
+        for i, x in enumerate(far):
+            label = "S" + name + "xy"[i : i + 1] * (len(far) > 1)
+            seen[label] = lax.ppermute(after(x, GATES.get(label)), "wid", [(w, w ^ 2) for w in range(WID)])
         return near
 
     def pair(c):
@@ -313,6 +339,20 @@
         return tuple(jnp.concatenate([seen["%s%d%s" % (side, c, half)] for half in "ab"], axis=0) for side in "RO")
 
     near = {}
+
+    def send_back(i, steps):
+        sizes = [sum(layouts[c][1] for c in steps), sum(layouts[c][2] - layouts[c][1] for c in steps)]
+        first = after(near[steps[0]], GATES.get("G%d" % i))
+        grams = sum([[first if c == steps[0] else near[c], seen["S%d" % c]] for c in steps], [])
+        ring, swapped = call(
+            lambda *refs: return_kernel(layouts, steps, *refs),
+            tuple(jax.ShapeDtypeStruct((n, UNIT), jnp.float32) for n in sizes),
+            near["A"], seen["SA"], *grams,
+        )
+        seen["V%d" % i] = ring
+        seen["U%d" % i] = lax.ppermute(ring, "tok", up)
+        seen["X%d" % i] = lax.ppermute(swapped, "tok", swap)
+
     for piece in PIECES:
         if piece == "A":
             start(piece, acts)
@@ -320,6 +360,8 @@
             chunk = mine[int(piece[0])]
             cut = chunk.shape[0] // 2
             start(piece, {"": chunk, "a": chunk[:cut], "b": chunk[cut:]}[piece[1:]])
+        elif piece[0] == "g":
+            send_back(int(piece[1:]), GROUPS[int(piece[1:])])
         elif piece == "kS":
             near["S"] = exchange("S", self_kernel, 2 * WID * UNIT, acts, own_g)
         elif piece == "kA":
@@ -333,25 +375,29 @@
                 piece[1], lambda *refs, c=c, spot=spot: grads_kernel(c, spot, *refs),
                 size, own_g, *mine[: c + 1], *[p[0] for p in pairs], *[p[1] for p in pairs],
                 memory=pl.BlockSpec(memory_space=pl.ANY), scratch=grads_scratch(own_g, c + 1),
+                cuts=(layouts[c][1],) if c + 1 == units else (),
             )
 
     returned = []
-    for i, steps in enumerate(GROUPS):
-        sizes = [sum(layouts[c][1] for c in steps), sum(layouts[c][2] - layouts[c][1] for c in steps)]
-        first = after(near[steps[0]], GATES.get("G%d" % i))
-        grams = sum([[first if c == steps[0] else near[c], seen["S%d" % c]] for c in steps], [])
-        ring, swapped = call(
-            lambda *refs, steps=steps: return_kernel(layouts, steps, *refs),
-            tuple(jax.ShapeDtypeStruct((n, UNIT), jnp.float32) for n in sizes),
-            near["A"], seen["SA"], *grams,
+    for i in range(len(GROUPS)):
+        returned += [seen["U%d" % i], seen["X%d" % i]]
+
+    last = units - 1
+    base = sum(layout[3] for layout in layouts[:last])
+    _, n_ring, n_swap, _ = layouts[last]
+    for first, n, far, move in ((0, n_ring, "S%dx" % last, up), (n_ring, n_swap - n_ring, "S%dy" % last, swap)):
+        tile = call(
+            lambda *refs, first=first: last_kernel(base, first, *refs),
+            jax.ShapeDtypeStruct((n, UNIT), jnp.float32), near["A"], seen["SA"], near[last], seen[far],
         )
-        returned += [lax.ppermute(ring, "tok", up), lax.ppermute(swapped, "tok", swap)]
-
-    grams = sum([[near[c], seen["S%d" % c]] for c in range(units)], [])
+        returned.append(lax.ppermute(tile, "tok", move))
+
+    grams = sum([[near[c], seen["S%d" % c]] for c in range(last)], [near["A"], seen["SA"]])
+    grams += [near[last], seen["S%dx" % last], seen["S%dy" % last]]
     out = call(
         lambda *refs: final_kernel(layouts, GROUPS, *refs),
         jax.ShapeDtypeStruct((5, rows, UNIT), jnp.float32),
-        place, lengths, near["S"], seen["SS"], near["A"], seen["SA"], *grams, *returned, scalars=2,
+        place, lengths, near["S"], seen["SS"], *grams, *returned, scalars=2,
     )
     return out.transpose(1, 0, 2)
 

time: 123 us -> 119 us (0.967)
  waiting for transfers between devices: 51.4 us -> 40.8 us
  starting transfers between devices: 28.1 us -> 34 us
  Pallas kernels: 36.9 us -> 38.5 us
    ppermute x10 -> x13, waiting for transfers between devices: 25 us -> 12.8 us  [the longest x7 8.7 us: exchange(): lax.ppermute(after(x, GATES.get(label)), 'wid', [(w, w ^ 2) for w in rang...]
    ppermute x10 -> x13, starting transfers between devices: 8.33 us -> 13.1 us  [the longest x7 9.75 us: exchange(): lax.ppermute(after(x, GATES.get(label)), 'wid', [(w, w ^ 2) for w in rang...]
    ppermute x5, waiting for transfers between devices: 2.21 us -> 5.42 us  [start(): lax.ppermute(after(chunk, GATES.get('O' + name)), 'tok', swap)]
    pallas_call x10 -> x12, Pallas kernels: 36.9 us -> 38.5 us  [call(): pl.pallas_call(kernel, out_shape=outs, in_specs=[SMEM] * scalars + [memor...]
    ppermute x5, waiting for transfers between devices: 9.87 us -> 8.24 us  [start(): lax.ppermute(after(chunk, GATES.get('R' + name)), 'tok', down)]
    ppermute x5, starting transfers between devices: 5.08 us -> 6.36 us  [start(): lax.ppermute(after(chunk, GATES.get('O' + name)), 'tok', swap)]
    add x6 -> x7, other arithmetic: 2.03 us -> 3.03 us  [the longest x6 2.98 us: summed(): keep[1, a:b] + arrived[1, a:b]]
  transfers between devices with their start and end apart: 26 -> 29, of which waited for: 15 -> 15; matrix products, arithmetic and copies ran while one was open for 3% -> 3% of each run, Pallas kernels for 28% -> 31%
where the time goes in v8:
time: 119 us
  waiting for transfers between devices  40.8 us (34%)
  Pallas kernels  38.5 us (32%)
  starting transfers between devices  34 us (29%)
  other arithmetic  3.69 us (3%)
    pallas_call x12, Pallas kernels, call(): pl.pallas_call(kernel, out_shape=outs, in_specs=[SMEM] * scalars + [memor...  38.5 us
    ppermute x6, waiting for transfers between devices, over_core(): return lax.ppermute(send, 'wid', [(w, w ^ 1) for w in range(WID)])  14.4 us
    ppermute x5, starting transfers between devices, start(): lax.ppermute(after(chunk, GATES.get('R' + name)), 'tok', down)  14.1 us
    ppermute x7, starting transfers between devices, exchange(): lax.ppermute(after(x, GATES.get(label)), 'wid', [(w, w ^ 2) for w in rang...  9.75 us
    ppermute x7, waiting for transfers between devices, exchange(): lax.ppermute(after(x, GATES.get(label)), 'wid', [(w, w ^ 2) for w in rang...  8.7 us
    ppermute x5, waiting for transfers between devices, start(): lax.ppermute(after(chunk, GATES.get('R' + name)), 'tok', down)  8.24 us
    ppermute x5, starting transfers between devices, start(): lax.ppermute(after(chunk, GATES.get('O' + name)), 'tok', swap)  6.36 us
    ppermute x5, waiting for transfers between devices, start(): lax.ppermute(after(chunk, GATES.get('O' + name)), 'tok', swap)  5.42 us
  transfers between devices with their start and end apart: 29, of which 15 were waited for; matrix products, arithmetic and copies ran while one was open for 3% of the time, Pallas kernels for 31%

profile of v8, /device:TPU:0, one launch (start us, length us, event | category | flops | bytes accessed | tf_op | source)
XLA Modules:
  0.0 119.0 jit_solution(4754319743964971646)
XLA Ops:
  0.0 5.0 %collective-permute-start.7 = (bf16[512,1024]{1,0:T(8,128)(2,1)}, bf16[512,1024]{1,0:T(8,128)(2,1)}, u32[]{:S(2)}, u32[]{:S(2)}) collective-permute-start(bf16[512,1024]{1,0:T(8,128)(2,1)} %param.15), channel_id=1, source_target_pairs={{0,24},{4,28},{8,0},{12,4},{16,8},{20,12},{24,16},{28,20},{1,25},{... | collective-permute-start | bytes 3145736 | tf_op jit(solution)/shard_map/ppermute | solution.py:314
  6.5 6.0 %shard_map.37 = (bf16[2752,128]{1,0:T(8,128)(2,1)S(1)}, bf16[2752,128]{1,0:T(8,128)(2,1)S(1)}, bf16[2752,128]{1,0:T(8,128)(2,1)}, bf16[2752,128]{1,0:T(8,128)(2,1)}) custom-call(bf16[2752,512]{1,0:T(8,128)(2,1)} %bitcast.33), custom_call_target="tpu_custom_call" | custom-call | flops 2000000000 | bytes 2000000 | tf_op jit(solution)/shard_map/pallas_call | solution.py:25
  14.4 7.3 %conditional.6 = (f32[1024,128]{1,0:T(8,128)S(1)}, f32[1024,128]{1,0:T(8,128)S(1)}) conditional(s32[]{:T(128)} %convert_element_type.2, () %tuple.66, (s32[5]{0:T(128)S(1)}, bf16[512,1024]{1,0:T(8,128)(2,1)}, bf16[2752,512]{1,0:T(8,128)(2,1)}) %tuple.109), branch_computations={%region_1.2_spmd, %region_2.3_spmd} | conditional | flops 2000262144 | bytes 9340088 | solution.py:329
  14.4 4.5 %branch_1_fun.6 = (f32[2,1024,128]{2,1,0:T(8,128)S(1)}, f32[2,1024,128]{2,1,0:T(8,128)S(1)}) custom-call(s32[5]{0:T(128)S(1)} %get-tuple-element.95.place_ref, bf16[512,1024]{1,0:T(8,128)(2,1)} %get-tuple-element.96.a_ref, bf16[2752,512]{1,0:T(8,128)(2,1)} %get-tuple-element.97.g_ref), custom_call_target="tpu_custom_call" | custom-call | flops 2000000000 | bytes 2000000 | tf_op jit(solution)/shard_map/cond/branch_1_fun/pallas_call | solution.py:25
  19.0 2.6 %collective-permute-done = f32[2,1024,128]{2,1,0:T(8,128)S(1)} collective-permute-done((f32[2,1024,128]{2,1,0:T(8,128)S(1)}, f32[2,1024,128]{2,1,0:T(8,128)S(1)}, u32[]{:S(2)}, u32[]{:S(2)}) %collective-permute-start) | collective-permute-done | bytes 1048608 | tf_op jit(solution)/shard_map/cond/branch_1_fun/ppermute | solution.py:299
  24.6 4.3 %collective-permute-done.7 = bf16[512,1024]{1,0:T(8,128)(2,1)} collective-permute-done((bf16[512,1024]{1,0:T(8,128)(2,1)}, bf16[512,1024]{1,0:T(8,128)(2,1)}, u32[]{:S(2)}, u32[]{:S(2)}) %collective-permute-start.7) | collective-permute-done | bytes 1048608 | tf_op jit(solution)/shard_map/ppermute | solution.py:314
  28.9 4.3 %collective-permute-start.12 = (bf16[2752,128]{1,0:T(8,128)(2,1)S(1)}, bf16[2752,128]{1,0:T(8,128)(2,1)}, u32[]{:S(2)}, u32[]{:S(2)}) collective-permute-start(bf16[2752,128]{1,0:T(8,128)(2,1)S(1)} %get-tuple-element.211), channel_id=1, source_target_pairs={{0,24},{4,28},{8,0},{12,4},{16,8},{20,12},{24,16},{28,20},{1,25},{... | collective-permute-start | bytes 2113544 | tf_op jit(solution)/shard_map/ppermute | solution.py:314
  33.2 10.3 %conditional.7 = (f32[2048,128]{1,0:T(8,128)S(1)}, f32[2048,128]{1,0:T(8,128)}) conditional(s32[]{:T(128)} %convert_element_type.2, () %tuple.70, (s32[5]{0:T(128)S(1)}, bf16[512,1024]{1,0:T(8,128)(2,1)}, bf16[512,1024]{1,0:T(8,128)(2,1)}, bf16[512,1024]{1,0:T(8,128)(2,1)}) %tuple.73), branch_computations={%region_3.4_spmd, %region_4.5_spmd} | conditional | flops 2000524288 | bytes 16680120 | solution.py:329
  33.2 4.9 %branch_1_fun.7 = (f32[2,2048,128]{2,1,0:T(8,128)S(1)}, f32[2,2048,128]{2,1,0:T(8,128)S(1)}) custom-call(s32[5]{0:T(128)S(1)} %get-tuple-element.100.refs_0_, bf16[512,1024]{1,0:T(8,128)(2,1)} %get-tuple-element.101.refs_1_, bf16[512,1024]{1,0:T(8,128)(2,1)} %get-tuple-element.102.refs_2_, bf16[512,1024]{1,0:T(8,128)(2,1)} %get-tuple-element.103.refs_3_), custom_call_target="tpu_custom_call" | custom-call | flops 2000000000 | bytes 2000000 | tf_op jit(solution)/shard_map/cond/branch_1_fun/pallas_call | solution.py:25
  38.2 4.1 %collective-permute-done.1 = f32[2,2048,128]{2,1,0:T(8,128)S(1)} collective-permute-done((f32[2,2048,128]{2,1,0:T(8,128)S(1)}, f32[2,2048,128]{2,1,0:T(8,128)S(1)}, u32[]{:S(2)}, u32[]{:S(2)}) %collective-permute-start.1) | collective-permute-done | bytes 2097184 | tf_op jit(solution)/shard_map/cond/branch_1_fun/ppermute | solution.py:299
  48.3 5.2 %conditional.8 = (f32[320,128]{1,0:T(8,128)S(1)}, f32[320,128]{1,0:T(8,128)S(1)}) conditional(s32[]{:T(128)} %convert_element_type.2, () %tuple.74, (s32[5]{0:T(128)S(1)}, bf16[2752,512]{1,0:T(8,128)(2,1)}, bf16[2752,128]{1,0:T(8,128)(2,1)S(1)}, bf16[2752,128]{1,0:T(8,128)(2,1)}, bf16[2752,128]{1,0:T(8,128)(2,1)}) %tuple.110), branch_computations={%region_5.6_spmd, %region_6.7_spmd} | conditional | flops 2000081920 | bytes 4293816 | solution.py:329
  48.3 3.5 %branch_1_fun.8 = (f32[2,320,128]{2,1,0:T(8,128)S(1)}, f32[2,320,128]{2,1,0:T(8,128)S(1)}) custom-call(s32[5]{0:T(128)S(1)} %get-tuple-element.106.refs_0_, bf16[2752,512]{1,0:T(8,128)(2,1)} %get-tuple-element.107.refs_1_, bf16[2752,128]{1,0:T(8,128)(2,1)S(1)} %get-tuple-element.108.refs_2_, bf16[2752,128]{1,0:T(8,128)(2,1)} %get-tuple-element.109.refs_3_, ...), custom_call_target="tpu_custom_call" | custom-call | flops 2000000000 | bytes 2000000 | tf_op jit(solution)/shard_map/cond/branch_1_fun/pallas_call | solution.py:25
  55.1 3.9 %collective-permute-done.12 = bf16[2752,128]{1,0:T(8,128)(2,1)} collective-permute-done((bf16[2752,128]{1,0:T(8,128)(2,1)S(1)}, bf16[2752,128]{1,0:T(8,128)(2,1)}, u32[]{:S(2)}, u32[]{:S(2)}) %collective-permute-start.12) | collective-permute-done | bytes 704544 | tf_op jit(solution)/shard_map/ppermute | solution.py:314
  62.3 6.8 %conditional.9 = (f32[448,128]{1,0:T(8,128)S(1)}, f32[448,128]{1,0:T(8,128)}) conditional(s32[]{:T(128)} %convert_element_type.2, () %tuple.76, (s32[5]{0:T(128)S(1)}, bf16[2752,512]{1,0:T(8,128)(2,1)}, bf16[2752,128]{1,0:T(8,128)(2,1)S(1)}, bf16[2752,128]{1,0:T(8,128)(2,1)S(1)}, bf16[2752,128]{1,0:T(8,128)(2,1)}, ...), branch_computations={%region_7.8_spmd, %region_8.9_spmd} | conditional | flops 2000114688 | bytes 5211320 | solution.py:329
  62.3 4.1 %branch_1_fun.9 = (f32[2,448,128]{2,1,0:T(8,128)S(1)}, f32[2,448,128]{2,1,0:T(8,128)S(1)}) custom-call(s32[5]{0:T(128)S(1)} %get-tuple-element.113.refs_0_, bf16[2752,512]{1,0:T(8,128)(2,1)} %get-tuple-element.114.refs_1_, bf16[2752,128]{1,0:T(8,128)(2,1)S(1)} %get-tuple-element.115.refs_2_, bf16[2752,128]{1,0:T(8,128)(2,1)S(1)} %get-tuple-element.116.refs_3_, ...), custom_call_target="tpu_custom_call" | custom-call | flops 2000000000 | bytes 2000000 | tf_op jit(solution)/shard_map/cond/branch_1_fun/pallas_call | solution.py:25
  69.1 2.6 %collective-permute-start.19 = (bf16[2752,128]{1,0:T(8,128)(2,1)}, bf16[2752,128]{1,0:T(8,128)(2,1)}, u32[]{:S(2)}, u32[]{:S(2)}) collective-permute-start(bf16[2752,128]{1,0:T(8,128)(2,1)} %get-tuple-element.230), channel_id=1, source_target_pairs={{0,24},{4,28},{8,0},{12,4},{16,8},{20,12},{24,16},{28,20},{1,25},{... | collective-permute-start | bytes 2113544 | tf_op jit(solution)/shard_map/ppermute | solution.py:314
  77.4 7.8 %conditional.10 = (f32[576,128]{1,0:T(8,128)S(1)}, f32[576,128]{1,0:T(8,128)}) conditional(s32[]{:T(128)} %convert_element_type.2, () %tuple.82, (s32[5]{0:T(128)S(1)}, bf16[2752,512]{1,0:T(8,128)(2,1)}, bf16[2752,128]{1,0:T(8,128)(2,1)S(1)}, bf16[2752,128]{1,0:T(8,128)(2,1)S(1)}, bf16[2752,128]{1,0:T(8,128)(2,1)}, ...), branch_computations={%region_9.10_spmd, %region_10.11_spmd} | conditional | flops 2000147456 | bytes 6128824 | solution.py:329
  77.4 4.9 %branch_1_fun.10 = (f32[2,576,128]{2,1,0:T(8,128)S(1)}, f32[2,576,128]{2,1,0:T(8,128)S(1)}) custom-call(s32[5]{0:T(128)S(1)} %get-tuple-element.123.refs_0_, bf16[2752,512]{1,0:T(8,128)(2,1)} %get-tuple-element.124.refs_1_, bf16[2752,128]{1,0:T(8,128)(2,1)S(1)} %get-tuple-element.125.refs_2_, bf16[2752,128]{1,0:T(8,128)(2,1)S(1)} %get-tuple-element.126.refs_3_, ...), custom_call_target="tpu_custom_call" | custom-call | flops 2000000000 | bytes 2000000 | tf_op jit(solution)/shard_map/cond/branch_1_fun/pallas_call | solution.py:25
  89.5 2.8 %collective-permute-done.20 = bf16[2752,128]{1,0:T(8,128)(2,1)} collective-permute-done((bf16[2752,128]{1,0:T(8,128)(2,1)}, bf16[2752,128]{1,0:T(8,128)(2,1)}, u32[]{:S(2)}, u32[]{:S(2)}) %collective-permute-start.20) | collective-permute-done | bytes 704544 | tf_op jit(solution)/shard_map/ppermute | solution.py:315
  92.3 7.9 %conditional.11 = (f32[704,128]{1,0:T(8,128)S(1)}, f32[352,128]{1,0:T(8,128)S(1)}, f32[352,128]{1,0:T(8,128)S(1)}) conditional(s32[]{:T(128)} %convert_element_type.2, () %tuple.87, (s32[5]{0:T(128)S(1)}, bf16[2752,512]{1,0:T(8,128)(2,1)S(1)}, bf16[2752,128]{1,0:T(8,128)(2,1)S(1)}, bf16[2752,128]{1,0:T(8,128)(2,1)S(1)}, ...), branch_computations={%region_11.12_spmd, %region_12.13_spmd} | conditional | flops 2000180224 | bytes 7046336 | solution.py:329
  92.3 5.5 %branch_1_fun.11 = (f32[2,704,128]{2,1,0:T(8,128)S(1)}, f32[2,704,128]{2,1,0:T(8,128)S(1)}) custom-call(s32[5]{0:T(128)S(1)} %get-tuple-element.136.refs_0_, bf16[2752,512]{1,0:T(8,128)(2,1)S(1)} %get-tuple-element.137.refs_1_, bf16[2752,128]{1,0:T(8,128)(2,1)S(1)} %get-tuple-element.138.refs_2_, bf16[2752,128]{1,0:T(8,128)(2,1)S(1)} %get-tuple-element.139.refs_3_, ...), custom_call_target="tpu_custom_call" | custom-call | flops 2000000000 | bytes 2000000 | tf_op jit(solution)/shard_map/cond/branch_1_fun/pallas_call | solution.py:25
  103.9 3.8 %collective-permute-done.21.refs_3_.refs_13_ = f32[352,128]{1,0:T(8,128)S(1)} collective-permute-done((f32[352,128]{1,0:T(8,128)S(1)}, f32[352,128]{1,0:T(8,128)S(1)}, u32[]{:S(2)}, u32[]{:S(2)}) %collective-permute-start.21) | collective-permute-done | bytes 180256 | tf_op jit(solution)/shard_map/ppermute | solution.py:333
  107.8 2.9 %collective-permute-done.22.refs_3_.refs_14_ = f32[352,128]{1,0:T(8,128)S(1)} collective-permute-done((f32[352,128]{1,0:T(8,128)S(1)}, f32[352,128]{1,0:T(8,128)S(1)}, u32[]{:S(2)}, u32[]{:S(2)}) %collective-permute-start.22) | collective-permute-done | bytes 180256 | tf_op jit(solution)/shard_map/ppermute | solution.py:333
  112.8 4.1 %collective-permute-done.26.refs_18_ = f32[160,128]{1,0:T(8,128)S(1)} collective-permute-done((f32[160,128]{1,0:T(8,128)S(1)}, f32[160,128]{1,0:T(8,128)S(1)}, u32[]{:S(2)}, u32[]{:S(2)}) %collective-permute-start.26) | collective-permute-done | bytes 81952 | tf_op jit(solution)/shard_map/ppermute | solution.py:354
  (93 shorter events, 44.1 us)
Async XLA Ops:
  0.0 28.9 %collective-permute-start.7 = (bf16[512,1024]{1,0:T(8,128)(2,1)}, bf16[512,1024]{1,0:T(8,128)(2,1)}, u32[]{:S(2)}, u32[]{:S(2)}) collective-permute-start(bf16[512,1024]{1,0:T(8,128)(2,1)} %param.15), channel_id=1, source_target_pairs={{0,24},{4,28},{8,0},{12,4},{16,8},{20,12},{24,16},{28,20},{1,25},{... | collective-permute-start | bytes 3145736 | tf_op jit(solution)/shard_map/ppermute | solution.py:314
  5.0 28.2 %collective-permute-start.8 = (bf16[512,1024]{1,0:T(8,128)(2,1)}, bf16[512,1024]{1,0:T(8,128)(2,1)}, u32[]{:S(2)}, u32[]{:S(2)}) collective-permute-start(bf16[512,1024]{1,0:T(8,128)(2,1)} %param.15), channel_id=1, source_target_pairs={{0,4},{4,0},{8,12},{12,8},{16,20},{20,16},{24,28},{28,24},{1,5},{5... | collective-permute-start | bytes 3145736 | tf_op jit(solution)/shard_map/ppermute | solution.py:315
  12.6 34.0 %collective-permute-start.10 = (bf16[2752,128]{1,0:T(8,128)(2,1)S(1)}, bf16[2752,128]{1,0:T(8,128)(2,1)}, u32[]{:S(2)}, u32[]{:S(2)}) collective-permute-start(bf16[2752,128]{1,0:T(8,128)(2,1)S(1)} %get-tuple-element.205), channel_id=1, source_target_pairs={{0,24},{4,28},{8,0},{12,4},{16,8},{20,12},{24,16},{28,20},{1,25},{... | collective-permute-start | bytes 2113544 | tf_op jit(solution)/shard_map/ppermute | solution.py:314
  22.6 22.5 %collective-permute-start.6 = (f32[1024,128]{1,0:T(8,128)S(1)}, f32[1024,128]{1,0:T(8,128)S(1)}, u32[]{:S(2)}, u32[]{:S(2)}) collective-permute-start(f32[1024,128]{1,0:T(8,128)S(1)} %get-tuple-element.196), channel_id=1, source_target_pairs={{0,2},{1,3},{2,0},{3,1},{4,6},{5,7},{6,4},{7,5},{8,10},{9,11},{10,... | collective-permute-start | bytes 1572872 | tf_op jit(solution)/shard_map/ppermute | solution.py:333
  24.1 24.2 %collective-permute-start.11 = (bf16[2752,128]{1,0:T(8,128)(2,1)S(1)}, bf16[2752,128]{1,0:T(8,128)(2,1)}, u32[]{:S(2)}, u32[]{:S(2)}) collective-permute-start(bf16[2752,128]{1,0:T(8,128)(2,1)S(1)} %get-tuple-element.205), channel_id=1, source_target_pairs={{0,4},{4,0},{8,12},{12,8},{16,20},{20,16},{24,28},{28,24},{1,5},{5... | collective-permute-start | bytes 2113544 | tf_op jit(solution)/shard_map/ppermute | solution.py:315
  28.9 30.1 %collective-permute-start.12 = (bf16[2752,128]{1,0:T(8,128)(2,1)S(1)}, bf16[2752,128]{1,0:T(8,128)(2,1)}, u32[]{:S(2)}, u32[]{:S(2)}) collective-permute-start(bf16[2752,128]{1,0:T(8,128)(2,1)S(1)} %get-tuple-element.211), channel_id=1, source_target_pairs={{0,24},{4,28},{8,0},{12,4},{16,8},{20,12},{24,16},{28,20},{1,25},{... | collective-permute-start | bytes 2113544 | tf_op jit(solution)/shard_map/ppermute | solution.py:314
  38.1 4.2 %collective-permute-start.1 = (f32[2,2048,128]{2,1,0:T(8,128)S(1)}, f32[2,2048,128]{2,1,0:T(8,128)S(1)}, u32[]{:S(2)}, u32[]{:S(2)}) collective-permute-start(f32[2,2048,128]{2,1,0:T(8,128)S(1)} %get-tuple-element.105), channel_id=1, source_target_pairs={{0,1},{1,0},{2,3},{3,2},{4,5},{5,4},{6,7},{7,6},{8,9},{9,8},{10,11... | collective-permute-start | bytes 6291464 | tf_op jit(solution)/shard_map/cond/branch_1_fun/ppermute | solution.py:299
  43.6 18.7 %collective-permute-start.13 = (bf16[2752,128]{1,0:T(8,128)(2,1)S(1)}, bf16[2752,128]{1,0:T(8,128)(2,1)}, u32[]{:S(2)}, u32[]{:S(2)}) collective-permute-start(bf16[2752,128]{1,0:T(8,128)(2,1)S(1)} %get-tuple-element.211), channel_id=1, source_target_pairs={{0,4},{4,0},{8,12},{12,8},{16,20},{20,16},{24,28},{28,24},{1,5},{5... | collective-permute-start | bytes 2113544 | tf_op jit(solution)/shard_map/ppermute | solution.py:315
  45.1 41.7 %collective-permute-start.9 = (f32[2048,128]{1,0:T(8,128)}, f32[2048,128]{1,0:T(8,128)S(1)}, u32[]{:S(2)}, u32[]{:S(2)}) collective-permute-start(f32[2048,128]{1,0:T(8,128)} %get-tuple-element.203), channel_id=1, source_target_pairs={{0,2},{1,3},{2,0},{3,1},{4,6},{5,7},{6,4},{7,5},{8,10},{9,11},{10,... | collective-permute-start | bytes 3145736 | tf_op jit(solution)/shard_map/ppermute | solution.py:333
  46.6 28.4 %collective-permute-start.16 = (bf16[2752,128]{1,0:T(8,128)(2,1)}, bf16[2752,128]{1,0:T(8,128)(2,1)}, u32[]{:S(2)}, u32[]{:S(2)}) collective-permute-start(bf16[2752,128]{1,0:T(8,128)(2,1)} %get-tuple-element.223), channel_id=1, source_target_pairs={{0,24},{4,28},{8,0},{12,4},{16,8},{20,12},{24,16},{28,20},{1,25},{... | collective-permute-start | bytes 2113544 | tf_op jit(solution)/shard_map/ppermute | solution.py:314
  53.5 23.9 %collective-permute-start.17 = (bf16[2752,128]{1,0:T(8,128)(2,1)}, bf16[2752,128]{1,0:T(8,128)(2,1)}, u32[]{:S(2)}, u32[]{:S(2)}) collective-permute-start(bf16[2752,128]{1,0:T(8,128)(2,1)} %get-tuple-element.223), channel_id=1, source_target_pairs={{0,4},{4,0},{8,12},{12,8},{16,20},{20,16},{24,28},{28,24},{1,5},{5... | collective-permute-start | bytes 2113544 | tf_op jit(solution)/shard_map/ppermute | solution.py:315
  59.0 14.7 %collective-permute-start.14 = (f32[320,128]{1,0:T(8,128)S(1)}, f32[320,128]{1,0:T(8,128)S(1)}, u32[]{:S(2)}, u32[]{:S(2)}) collective-permute-start(f32[320,128]{1,0:T(8,128)S(1)} %get-tuple-element.214), channel_id=1, source_target_pairs={{0,2},{1,3},{2,0},{3,1},{4,6},{5,7},{6,4},{7,5},{8,10},{9,11},{10,... | collective-permute-start | bytes 491528 | tf_op jit(solution)/shard_map/ppermute | solution.py:333
  69.1 20.5 %collective-permute-start.19 = (bf16[2752,128]{1,0:T(8,128)(2,1)}, bf16[2752,128]{1,0:T(8,128)(2,1)}, u32[]{:S(2)}, u32[]{:S(2)}) collective-permute-start(bf16[2752,128]{1,0:T(8,128)(2,1)} %get-tuple-element.230), channel_id=1, source_target_pairs={{0,24},{4,28},{8,0},{12,4},{16,8},{20,12},{24,16},{28,20},{1,25},{... | collective-permute-start | bytes 2113544 | tf_op jit(solution)/shard_map/ppermute | solution.py:314
  73.7 18.6 %collective-permute-start.20 = (bf16[2752,128]{1,0:T(8,128)(2,1)}, bf16[2752,128]{1,0:T(8,128)(2,1)}, u32[]{:S(2)}, u32[]{:S(2)}) collective-permute-start(bf16[2752,128]{1,0:T(8,128)(2,1)} %get-tuple-element.230), channel_id=1, source_target_pairs={{0,4},{4,0},{8,12},{12,8},{16,20},{20,16},{24,28},{28,24},{1,5},{5... | collective-permute-start | bytes 2113544 | tf_op jit(solution)/shard_map/ppermute | solution.py:315
  75.0 11.7 %collective-permute-start.15 = (f32[448,128]{1,0:T(8,128)}, f32[448,128]{1,0:T(8,128)S(1)}, u32[]{:S(2)}, u32[]{:S(2)}) collective-permute-start(f32[448,128]{1,0:T(8,128)} %get-tuple-element.218), channel_id=1, source_target_pairs={{0,2},{1,3},{2,0},{3,1},{4,6},{5,7},{6,4},{7,5},{8,10},{9,11},{10,... | collective-permute-start | bytes 688136 | tf_op jit(solution)/shard_map/ppermute | solution.py:333
  85.2 16.7 %collective-permute-start.18 = (f32[576,128]{1,0:T(8,128)}, f32[576,128]{1,0:T(8,128)S(1)}, u32[]{:S(2)}, u32[]{:S(2)}) collective-permute-start(f32[576,128]{1,0:T(8,128)} %get-tuple-element.225), channel_id=1, source_target_pairs={{0,2},{1,3},{2,0},{3,1},{4,6},{5,7},{6,4},{7,5},{8,10},{9,11},{10,... | collective-permute-start | bytes 884744 | tf_op jit(solution)/shard_map/ppermute | solution.py:333
  88.3 28.6 %collective-permute-start.23 = (f32[384,128]{1,0:T(8,128)S(1)}, f32[384,128]{1,0:T(8,128)S(1)}, u32[]{:S(2)}, u32[]{:S(2)}) collective-permute-start(f32[384,128]{1,0:T(8,128)S(1)} %get-tuple-element.227), channel_id=1, source_target_pairs={{0,8},{4,12},{8,16},{12,20},{16,24},{20,28},{24,0},{28,4},{1,9},{5... | collective-permute-start | bytes 589832 | tf_op jit(solution)/shard_map/ppermute | solution.py:353
  88.4 23.6 %collective-permute-start.24 = (f32[128,128]{1,0:T(8,128)S(1)}, f32[128,128]{1,0:T(8,128)S(1)}, u32[]{:S(2)}, u32[]{:S(2)}) collective-permute-start(f32[128,128]{1,0:T(8,128)S(1)} %get-tuple-element.236), channel_id=1, source_target_pairs={{0,4},{4,0},{8,12},{12,8},{16,20},{20,16},{24,28},{28,24},{1,5},{5... | collective-permute-start | bytes 196616 | tf_op jit(solution)/shard_map/ppermute | solution.py:354
  100.2 7.5 %collective-permute-start.21 = (f32[352,128]{1,0:T(8,128)S(1)}, f32[352,128]{1,0:T(8,128)S(1)}, u32[]{:S(2)}, u32[]{:S(2)}) collective-permute-start(f32[352,128]{1,0:T(8,128)S(1)} %get-tuple-element.232), channel_id=1, source_target_pairs={{0,2},{1,3},{2,0},{3,1},{4,6},{5,7},{6,4},{7,5},{8,10},{9,11},{10,... | collective-permute-start | bytes 540680 | tf_op jit(solution)/shard_map/ppermute | solution.py:333
  103.3 13.6 %collective-permute-start.25 = (f32[288,128]{1,0:T(8,128)S(1)}, f32[288,128]{1,0:T(8,128)S(1)}, u32[]{:S(2)}, u32[]{:S(2)}) collective-permute-start(f32[288,128]{1,0:T(8,128)S(1)} %get-tuple-element.234), channel_id=1, source_target_pairs={{0,8},{4,12},{8,16},{12,20},{16,24},{20,28},{24,0},{28,4},{1,9},{5... | collective-permute-start | bytes 442376 | tf_op jit(solution)/shard_map/ppermute | solution.py:353
  103.4 7.3 %collective-permute-start.22 = (f32[352,128]{1,0:T(8,128)S(1)}, f32[352,128]{1,0:T(8,128)S(1)}, u32[]{:S(2)}, u32[]{:S(2)}) collective-permute-start(f32[352,128]{1,0:T(8,128)S(1)} %get-tuple-element.235), channel_id=1, source_target_pairs={{0,2},{1,3},{2,0},{3,1},{4,6},{5,7},{6,4},{7,5},{8,10},{9,11},{10,... | collective-permute-start | bytes 540680 | tf_op jit(solution)/shard_map/ppermute | solution.py:333
  107.7 9.2 %collective-permute-start.27 = (f32[352,128]{1,0:T(8,128)S(1)}, f32[352,128]{1,0:T(8,128)S(1)}, u32[]{:S(2)}, u32[]{:S(2)}) collective-permute-start(f32[352,128]{1,0:T(8,128)S(1)} %shard_map.40), channel_id=1, source_target_pairs={{0,8},{4,12},{8,16},{12,20},{16,24},{20,28},{24,0},{28,4},{1,9},{5... | collective-permute-start | bytes 540680 | tf_op jit(solution)/shard_map/ppermute | solution.py:393
  110.7 6.2 %collective-permute-start.28 = (f32[224,128]{1,0:T(8,128)S(1)}, f32[224,128]{1,0:T(8,128)S(1)}, u32[]{:S(2)}, u32[]{:S(2)}) collective-permute-start(f32[224,128]{1,0:T(8,128)S(1)} %shard_map.41), channel_id=1, source_target_pairs={{0,4},{4,0},{8,12},{12,8},{16,20},{20,16},{24,28},{28,24},{1,5},{5... | collective-permute-start | bytes 344072 | tf_op jit(solution)/shard_map/ppermute | solution.py:393
  112.0 4.9 %collective-permute-start.26 = (f32[160,128]{1,0:T(8,128)S(1)}, f32[160,128]{1,0:T(8,128)S(1)}, u32[]{:S(2)}, u32[]{:S(2)}) collective-permute-start(f32[160,128]{1,0:T(8,128)S(1)} %get-tuple-element.237), channel_id=1, source_target_pairs={{0,4},{4,0},{8,12},{12,8},{16,20},{20,16},{24,28},{28,24},{1,5},{5... | collective-permute-start | bytes 245768 | tf_op jit(solution)/shard_map/ppermute | solution.py:354
  (21 other events, 167.9 us)

commit v9 on v8

--- a/solution.py
+++ b/solution.py
@@ -14,7 +14,7 @@
 SUB = UNIT // WID
 VMEM_LIMIT = 24 << 20
 PIECES = ['A', '0', 'kS', '1', 'kA', '2', 'k0', '3', 'k1', 'g0', 'k2', 'g1', 'k3']
-GATES = {'R1': ['RA'], 'O1': ['OA'], 'R2': ['RA'], 'O2': ['OA'], 'R3': ['R1'], 'O3': ['O1'], 'KA': [], 'K0': ['SS'], 'K1': ['SS'], 'K2': ['S0'], 'K3': ['V0'], 'SA': [], 'S0': [], 'S1': ['S0'], 'S2': [], 'S3x': [], 'S3y': ['V1'], 'G0': ['R2'], 'G1': []}
+GATES = {'R1': ['RA'], 'O1': ['OA'], 'R2': ['RA'], 'O2': ['OA'], 'R3': ['R0'], 'O3': ['O0'], 'KA': [], 'K0': ['SS'], 'K1': ['SS'], 'K2': ['S0'], 'K3': ['V0'], 'SA': [], 'S0': [], 'S1': ['S0'], 'S2': ['S1'], 'S3x': [], 'S3y': [], 'S3z': ['S3x'], 'G0': [], 'G1': []}
 PLAIN = []
 GROUPS = [[0, 1], [2]]
 SMEM = pl.BlockSpec(memory_space=pltpu.SMEM)
@@ -251,8 +251,8 @@
             base = sum(layouts[s][3] for s in range(step))
             if step < last:
                 return product(acts, grads[step], base + spot, spot, size)
-            n_ring = layouts[last][1]
-            far, at = (far_ring, spot) if spot < n_ring else (far_rest, spot - n_ring)
+            _, n_ring, n_swap, _ = layouts[last]
+            far, at = (far_ring, spot) if spot < n_ring else (far_rest, spot - n_swap)
             return product(acts, (near.at[spot : spot + size, :], far.at[at : at + size, :]), base + spot, 0, size)
         ring, ring_at, swap, swap_at = returned[step]
         ref, at = (ring, ring_at + spot) if where == "ring" else (swap, swap_at + spot)
@@ -329,7 +329,7 @@
         run = summed if name in PLAIN else lambda *args: lax.cond(alive, summed, nothing, *args)
         near, *far = run(first, *rest)
         for i, x in enumerate(far):
-            label = "S" + name + "xy"[i : i + 1] * (len(far) > 1)
+            label = "S" + name + "xyz"[i : i + 1] * (len(far) > 1)
             seen[label] = lax.ppermute(after(x, GATES.get(label)), "wid", [(w, w ^ 2) for w in range(WID)])
         return near
 
@@ -375,7 +375,7 @@
                 piece[1], lambda *refs, c=c, spot=spot: grads_kernel(c, spot, *refs),
                 size, own_g, *mine[: c + 1], *[p[0] for p in pairs], *[p[1] for p in pairs],
                 memory=pl.BlockSpec(memory_space=pl.ANY), scratch=grads_scratch(own_g, c + 1),
-                cuts=(layouts[c][1],) if c + 1 == units else (),
+                cuts=layouts[c][1:3] if c + 1 == units else (),
             )
 
     returned = []
@@ -393,7 +393,7 @@
         returned.append(lax.ppermute(tile, "tok", move))
 
     grams = sum([[near[c], seen["S%d" % c]] for c in range(last)], [near["A"], seen["SA"]])
-    grams += [near[last], seen["S%dx" % last], seen["S%dy" % last]]
+    grams += [near[last], seen["S%dx" % last], seen["S%dz" % last]]
     out = call(
         lambda *refs: final_kernel(layouts, GROUPS, *refs),
         jax.ShapeDtypeStruct((5, rows, UNIT), jnp.float32),

time: 119 us -> 117 us (0.983)
  waiting for transfers between devices: 40.8 us -> 38.5 us
  starting transfers between devices: 34 us -> 35.3 us
    ppermute x2, waiting for transfers between devices: 4.09 us -> 0.01 us  [send_back(): seen['X%d' % i] = lax.ppermute(swapped, 'tok', swap)]
    ppermute x2, waiting for transfers between devices: 0.01 us -> 1.7 us  [shards(): returned.append(lax.ppermute(tile, 'tok', move))]
    ppermute x7 -> x8, starting transfers between devices: 9.75 us -> 11.2 us  [exchange(): lax.ppermute(after(x, GATES.get(label)), 'wid', [(w, w ^ 2) for w in rang...]
    ppermute x7 -> x8, waiting for transfers between devices: 8.7 us -> 7.38 us  [exchange(): lax.ppermute(after(x, GATES.get(label)), 'wid', [(w, w ^ 2) for w in rang...]
    add x6 -> x8, other arithmetic: 2.98 us -> 3.81 us  [summed(): keep[1, a:b] + arrived[1, a:b]]
  transfers between devices with their start and end apart: 29 -> 30, of which waited for: 15 -> 16; matrix products, arithmetic and copies ran while one was open for 3% -> 4% of each run, Pallas kernels for 31% -> 30%
where the time goes in v9:
time: 117 us
  waiting for transfers between devices  38.5 us (33%)
  Pallas kernels  37.8 us (32%)
  starting transfers between devices  35.3 us (30%)
  other arithmetic  4.53 us (4%)
    pallas_call x12, Pallas kernels, call(): pl.pallas_call(kernel, out_shape=outs, in_specs=[SMEM] * scalars + [memor...  37.8 us
    ppermute x6, waiting for transfers between devices, over_core(): return lax.ppermute(send, 'wid', [(w, w ^ 1) for w in range(WID)])  14.4 us
    ppermute x5, starting transfers between devices, start(): lax.ppermute(after(chunk, GATES.get('R' + name)), 'tok', down)  14 us
    ppermute x8, starting transfers between devices, exchange(): lax.ppermute(after(x, GATES.get(label)), 'wid', [(w, w ^ 2) for w in rang...  11.2 us
    ppermute x5, waiting for transfers between devices, start(): lax.ppermute(after(chunk, GATES.get('R' + name)), 'tok', down)  9.08 us
    ppermute x8, waiting for transfers between devices, exchange(): lax.ppermute(after(x, GATES.get(label)), 'wid', [(w, w ^ 2) for w in rang...  7.38 us
    ppermute x5, starting transfers between devices, start(): lax.ppermute(after(chunk, GATES.get('O' + name)), 'tok', swap)  6.31 us
    ppermute x5, waiting for transfers between devices, start(): lax.ppermute(after(chunk, GATES.get('O' + name)), 'tok', swap)  5.96 us
  transfers between devices with their start and end apart: 30, of which 16 were waited for; matrix products, arithmetic and copies ran while one was open for 4% of the time, Pallas kernels for 30%

profile of v9, /device:TPU:0, one launch (start us, length us, event | category | flops | bytes accessed | tf_op | source)
XLA Modules:
  0.0 117.3 jit_solution(13285732272234493415)
XLA Ops:
  0.0 5.0 %collective-permute-start.7 = (bf16[512,1024]{1,0:T(8,128)(2,1)}, bf16[512,1024]{1,0:T(8,128)(2,1)}, u32[]{:S(2)}, u32[]{:S(2)}) collective-permute-start(bf16[512,1024]{1,0:T(8,128)(2,1)} %param.15), channel_id=1, source_target_pairs={{0,24},{4,28},{8,0},{12,4},{16,8},{20,12},{24,16},{28,20},{1,25},{... | collective-permute-start | bytes 3145736 | tf_op jit(solution)/shard_map/ppermute | solution.py:314
  6.5 6.2 %shard_map.37 = (bf16[2752,128]{1,0:T(8,128)(2,1)S(1)}, bf16[2752,128]{1,0:T(8,128)(2,1)}, bf16[2752,128]{1,0:T(8,128)(2,1)}, bf16[2752,128]{1,0:T(8,128)(2,1)}) custom-call(bf16[2752,512]{1,0:T(8,128)(2,1)} %bitcast.35), custom_call_target="tpu_custom_call" | custom-call | flops 2000000000 | bytes 2000000 | tf_op jit(solution)/shard_map/pallas_call | solution.py:25
  14.5 7.3 %conditional.6 = (f32[1024,128]{1,0:T(8,128)S(1)}, f32[1024,128]{1,0:T(8,128)}) conditional(s32[]{:T(128)} %convert_element_type.2, () %tuple.66, (s32[5]{0:T(128)S(1)}, bf16[512,1024]{1,0:T(8,128)(2,1)}, bf16[2752,512]{1,0:T(8,128)(2,1)S(1)}) %tuple.111), branch_computations={%region_1.2_spmd, %region_2.3_spmd} | conditional | flops 2000262144 | bytes 9340088 | solution.py:329
  14.5 3.6 %branch_1_fun.6 = (f32[2,1024,128]{2,1,0:T(8,128)S(1)}, f32[2,1024,128]{2,1,0:T(8,128)S(1)}) custom-call(s32[5]{0:T(128)S(1)} %get-tuple-element.95.place_ref, bf16[512,1024]{1,0:T(8,128)(2,1)} %get-tuple-element.96.a_ref, bf16[2752,512]{1,0:T(8,128)(2,1)S(1)} %get-tuple-element.97.g_ref), custom_call_target="tpu_custom_call" | custom-call | flops 2000000000 | bytes 2000000 | tf_op jit(solution)/shard_map/cond/branch_1_fun/pallas_call | solution.py:25
  18.2 2.6 %collective-permute-done = f32[2,1024,128]{2,1,0:T(8,128)S(1)} collective-permute-done((f32[2,1024,128]{2,1,0:T(8,128)S(1)}, f32[2,1024,128]{2,1,0:T(8,128)S(1)}, u32[]{:S(2)}, u32[]{:S(2)}) %collective-permute-start) | collective-permute-done | bytes 1048608 | tf_op jit(solution)/shard_map/cond/branch_1_fun/ppermute | solution.py:299
  23.9 5.0 %collective-permute-done.7 = bf16[512,1024]{1,0:T(8,128)(2,1)} collective-permute-done((bf16[512,1024]{1,0:T(8,128)(2,1)}, bf16[512,1024]{1,0:T(8,128)(2,1)}, u32[]{:S(2)}, u32[]{:S(2)}) %collective-permute-start.7) | collective-permute-done | bytes 1048608 | tf_op jit(solution)/shard_map/ppermute | solution.py:314
  28.9 4.3 %collective-permute-start.12 = (bf16[2752,128]{1,0:T(8,128)(2,1)}, bf16[2752,128]{1,0:T(8,128)(2,1)}, u32[]{:S(2)}, u32[]{:S(2)}) collective-permute-start(bf16[2752,128]{1,0:T(8,128)(2,1)} %get-tuple-element.214), channel_id=1, source_target_pairs={{0,24},{4,28},{8,0},{12,4},{16,8},{20,12},{24,16},{28,20},{1,25},{... | collective-permute-start | bytes 2113544 | tf_op jit(solution)/shard_map/ppermute | solution.py:314
  33.2 10.4 %conditional.7 = (f32[2048,128]{1,0:T(8,128)S(1)}, f32[2048,128]{1,0:T(8,128)}) conditional(s32[]{:T(128)} %convert_element_type.2, () %tuple.70, (s32[5]{0:T(128)S(1)}, bf16[512,1024]{1,0:T(8,128)(2,1)}, bf16[512,1024]{1,0:T(8,128)(2,1)}, bf16[512,1024]{1,0:T(8,128)(2,1)}) %tuple.73), branch_computations={%region_3.4_spmd, %region_4.5_spmd} | conditional | flops 2000524288 | bytes 16680120 | solution.py:329
  33.2 4.9 %branch_1_fun.7 = (f32[2,2048,128]{2,1,0:T(8,128)S(1)}, f32[2,2048,128]{2,1,0:T(8,128)S(1)}) custom-call(s32[5]{0:T(128)S(1)} %get-tuple-element.100.refs_0_, bf16[512,1024]{1,0:T(8,128)(2,1)} %get-tuple-element.101.refs_1_, bf16[512,1024]{1,0:T(8,128)(2,1)} %get-tuple-element.102.refs_2_, bf16[512,1024]{1,0:T(8,128)(2,1)} %get-tuple-element.103.refs_3_), custom_call_target="tpu_custom_call" | custom-call | flops 2000000000 | bytes 2000000 | tf_op jit(solution)/shard_map/cond/branch_1_fun/pallas_call | solution.py:25
  38.3 4.1 %collective-permute-done.1 = f32[2,2048,128]{2,1,0:T(8,128)S(1)} collective-permute-done((f32[2,2048,128]{2,1,0:T(8,128)S(1)}, f32[2,2048,128]{2,1,0:T(8,128)S(1)}, u32[]{:S(2)}, u32[]{:S(2)}) %collective-permute-start.1) | collective-permute-done | bytes 2097184 | tf_op jit(solution)/shard_map/cond/branch_1_fun/ppermute | solution.py:299
  48.3 5.2 %conditional.8 = (f32[320,128]{1,0:T(8,128)S(1)}, f32[320,128]{1,0:T(8,128)S(1)}) conditional(s32[]{:T(128)} %convert_element_type.2, () %tuple.74, (s32[5]{0:T(128)S(1)}, bf16[2752,512]{1,0:T(8,128)(2,1)}, bf16[2752,128]{1,0:T(8,128)(2,1)S(1)}, bf16[2752,128]{1,0:T(8,128)(2,1)}, bf16[2752,128]{1,0:T(8,128)(2,1)}) %tuple.108), branch_computations={%region_5.6_spmd, %region_6.7_spmd} | conditional | flops 2000081920 | bytes 4293816 | solution.py:329
  48.3 3.5 %branch_1_fun.8 = (f32[2,320,128]{2,1,0:T(8,128)S(1)}, f32[2,320,128]{2,1,0:T(8,128)S(1)}) custom-call(s32[5]{0:T(128)S(1)} %get-tuple-element.106.refs_0_, bf16[2752,512]{1,0:T(8,128)(2,1)} %get-tuple-element.107.refs_1_, bf16[2752,128]{1,0:T(8,128)(2,1)S(1)} %get-tuple-element.108.refs_2_, bf16[2752,128]{1,0:T(8,128)(2,1)} %get-tuple-element.109.refs_3_, ...), custom_call_target="tpu_custom_call" | custom-call | flops 2000000000 | bytes 2000000 | tf_op jit(solution)/shard_map/cond/branch_1_fun/pallas_call | solution.py:25
  55.1 4.0 %collective-permute-done.12 = bf16[2752,128]{1,0:T(8,128)(2,1)} collective-permute-done((bf16[2752,128]{1,0:T(8,128)(2,1)}, bf16[2752,128]{1,0:T(8,128)(2,1)}, u32[]{:S(2)}, u32[]{:S(2)}) %collective-permute-start.12) | collective-permute-done | bytes 704544 | tf_op jit(solution)/shard_map/ppermute | solution.py:314
  62.4 6.8 %conditional.9 = (f32[448,128]{1,0:T(8,128)S(1)}, f32[448,128]{1,0:T(8,128)}) conditional(s32[]{:T(128)} %convert_element_type.2, () %tuple.76, (s32[5]{0:T(128)S(1)}, bf16[2752,512]{1,0:T(8,128)(2,1)}, bf16[2752,128]{1,0:T(8,128)(2,1)S(1)}, bf16[2752,128]{1,0:T(8,128)(2,1)S(1)}, bf16[2752,128]{1,0:T(8,128)(2,1)}, ...), branch_computations={%region_7.8_spmd, %region_8.9_spmd} | conditional | flops 2000114688 | bytes 5211320 | solution.py:329
  62.4 4.1 %branch_1_fun.9 = (f32[2,448,128]{2,1,0:T(8,128)S(1)}, f32[2,448,128]{2,1,0:T(8,128)S(1)}) custom-call(s32[5]{0:T(128)S(1)} %get-tuple-element.113.refs_0_, bf16[2752,512]{1,0:T(8,128)(2,1)} %get-tuple-element.114.refs_1_, bf16[2752,128]{1,0:T(8,128)(2,1)S(1)} %get-tuple-element.115.refs_2_, bf16[2752,128]{1,0:T(8,128)(2,1)S(1)} %get-tuple-element.116.refs_3_, ...), custom_call_target="tpu_custom_call" | custom-call | flops 2000000000 | bytes 2000000 | tf_op jit(solution)/shard_map/cond/branch_1_fun/pallas_call | solution.py:25
  69.2 2.5 %collective-permute-start.19 = (bf16[2752,128]{1,0:T(8,128)(2,1)}, bf16[2752,128]{1,0:T(8,128)(2,1)}, u32[]{:S(2)}, u32[]{:S(2)}) collective-permute-start(bf16[2752,128]{1,0:T(8,128)(2,1)} %get-tuple-element.232), channel_id=1, source_target_pairs={{0,24},{4,28},{8,0},{12,4},{16,8},{20,12},{24,16},{28,20},{1,25},{... | collective-permute-start | bytes 2113544 | tf_op jit(solution)/shard_map/ppermute | solution.py:314
  71.7 2.1 %collective-permute-done.14.refs_3_.refs_7_ = f32[320,128]{1,0:T(8,128)S(1)} collective-permute-done((f32[320,128]{1,0:T(8,128)S(1)}, f32[320,128]{1,0:T(8,128)S(1)}, u32[]{:S(2)}, u32[]{:S(2)}) %collective-permute-start.14) | collective-permute-done | bytes 163872 | tf_op jit(solution)/shard_map/ppermute | solution.py:333
  77.5 7.8 %conditional.10 = (f32[576,128]{1,0:T(8,128)S(1)}, f32[576,128]{1,0:T(8,128)}) conditional(s32[]{:T(128)} %convert_element_type.2, () %tuple.82, (s32[5]{0:T(128)S(1)}, bf16[2752,512]{1,0:T(8,128)(2,1)}, bf16[2752,128]{1,0:T(8,128)(2,1)S(1)}, bf16[2752,128]{1,0:T(8,128)(2,1)S(1)}, bf16[2752,128]{1,0:T(8,128)(2,1)}, ...), branch_computations={%region_9.10_spmd, %region_10.11_spmd} | conditional | flops 2000147456 | bytes 6128824 | solution.py:329
  77.5 4.9 %branch_1_fun.10 = (f32[2,576,128]{2,1,0:T(8,128)S(1)}, f32[2,576,128]{2,1,0:T(8,128)S(1)}) custom-call(s32[5]{0:T(128)S(1)} %get-tuple-element.123.refs_0_, bf16[2752,512]{1,0:T(8,128)(2,1)} %get-tuple-element.124.refs_1_, bf16[2752,128]{1,0:T(8,128)(2,1)S(1)} %get-tuple-element.125.refs_2_, bf16[2752,128]{1,0:T(8,128)(2,1)S(1)} %get-tuple-element.126.refs_3_, ...), custom_call_target="tpu_custom_call" | custom-call | flops 2000000000 | bytes 2000000 | tf_op jit(solution)/shard_map/cond/branch_1_fun/pallas_call | solution.py:25
  88.5 3.3 %collective-permute-done.20 = bf16[2752,128]{1,0:T(8,128)(2,1)} collective-permute-done((bf16[2752,128]{1,0:T(8,128)(2,1)}, bf16[2752,128]{1,0:T(8,128)(2,1)}, u32[]{:S(2)}, u32[]{:S(2)}) %collective-permute-start.20) | collective-permute-done | bytes 704544 | tf_op jit(solution)/shard_map/ppermute | solution.py:315
  91.8 7.9 %conditional.11 = (f32[704,128]{1,0:T(8,128)S(1)}, f32[352,128]{1,0:T(8,128)S(1)}, f32[224,128]{1,0:T(8,128)S(1)}, f32[128,128]{1,0:T(8,128)S(1)}) conditional(s32[]{:T(128)} %convert_element_type.2, () %tuple.87, (s32[5]{0:T(128)S(1)}, bf16[2752,512]{1,0:T(8,128)(2,1)S(1)}, bf16[2752,128]{1,0:T(8,128)(2,1)S(1)}, bf16[2752,128]{1,0:T(8,128)(2,1)S(1)}, ...), branch_computations={%region_11.12_spmd, %region_12.13_spmd} | conditional | flops 2000180224 | bytes 7046344 | solution.py:329
  91.8 5.5 %branch_1_fun.11 = (f32[2,704,128]{2,1,0:T(8,128)S(1)}, f32[2,704,128]{2,1,0:T(8,128)S(1)}) custom-call(s32[5]{0:T(128)S(1)} %get-tuple-element.136.refs_0_, bf16[2752,512]{1,0:T(8,128)(2,1)S(1)} %get-tuple-element.137.refs_1_, bf16[2752,128]{1,0:T(8,128)(2,1)S(1)} %get-tuple-element.138.refs_2_, bf16[2752,128]{1,0:T(8,128)(2,1)S(1)} %get-tuple-element.139.refs_3_, ...), custom_call_target="tpu_custom_call" | custom-call | flops 2000000000 | bytes 2000000 | tf_op jit(solution)/shard_map/cond/branch_1_fun/pallas_call | solution.py:25
  97.4 2.2 %collective-permute-done.5 = f32[2,704,128]{2,1,0:T(8,128)S(1)} collective-permute-done((f32[2,704,128]{2,1,0:T(8,128)S(1)}, f32[2,704,128]{2,1,0:T(8,128)S(1)}, u32[]{:S(2)}, u32[]{:S(2)}) %collective-permute-start.5) | collective-permute-done | bytes 720928 | tf_op jit(solution)/shard_map/cond/branch_1_fun/ppermute | solution.py:299
  104.4 2.7 %collective-permute-done.21.refs_3_.refs_13_ = f32[352,128]{1,0:T(8,128)S(1)} collective-permute-done((f32[352,128]{1,0:T(8,128)S(1)}, f32[352,128]{1,0:T(8,128)S(1)}, u32[]{:S(2)}, u32[]{:S(2)}) %collective-permute-start.21) | collective-permute-done | bytes 180256 | tf_op jit(solution)/shard_map/ppermute | solution.py:333
  (99 shorter events, 45.6 us)
Async XLA Ops:
  0.0 28.9 %collective-permute-start.7 = (bf16[512,1024]{1,0:T(8,128)(2,1)}, bf16[512,1024]{1,0:T(8,128)(2,1)}, u32[]{:S(2)}, u32[]{:S(2)}) collective-permute-start(bf16[512,1024]{1,0:T(8,128)(2,1)} %param.15), channel_id=1, source_target_pairs={{0,24},{4,28},{8,0},{12,4},{16,8},{20,12},{24,16},{28,20},{1,25},{... | collective-permute-start | bytes 3145736 | tf_op jit(solution)/shard_map/ppermute | solution.py:314
  5.0 28.2 %collective-permute-start.8 = (bf16[512,1024]{1,0:T(8,128)(2,1)}, bf16[512,1024]{1,0:T(8,128)(2,1)}, u32[]{:S(2)}, u32[]{:S(2)}) collective-permute-start(bf16[512,1024]{1,0:T(8,128)(2,1)} %param.15), channel_id=1, source_target_pairs={{0,4},{4,0},{8,12},{12,8},{16,20},{20,16},{24,28},{28,24},{1,5},{5... | collective-permute-start | bytes 3145736 | tf_op jit(solution)/shard_map/ppermute | solution.py:315
  12.7 34.0 %collective-permute-start.10 = (bf16[2752,128]{1,0:T(8,128)(2,1)S(1)}, bf16[2752,128]{1,0:T(8,128)(2,1)}, u32[]{:S(2)}, u32[]{:S(2)}) collective-permute-start(bf16[2752,128]{1,0:T(8,128)(2,1)S(1)} %get-tuple-element.207), channel_id=1, source_target_pairs={{0,24},{4,28},{8,0},{12,4},{16,8},{20,12},{24,16},{28,20},{1,25},{... | collective-permute-start | bytes 2113544 | tf_op jit(solution)/shard_map/ppermute | solution.py:314
  21.8 23.3 %collective-permute-start.6 = (f32[1024,128]{1,0:T(8,128)}, f32[1024,128]{1,0:T(8,128)S(1)}, u32[]{:S(2)}, u32[]{:S(2)}) collective-permute-start(f32[1024,128]{1,0:T(8,128)} %get-tuple-element.198), channel_id=1, source_target_pairs={{0,2},{1,3},{2,0},{3,1},{4,6},{5,7},{6,4},{7,5},{8,10},{9,11},{10,... | collective-permute-start | bytes 1572872 | tf_op jit(solution)/shard_map/ppermute | solution.py:333
  23.4 25.0 %collective-permute-start.11 = (bf16[2752,128]{1,0:T(8,128)(2,1)S(1)}, bf16[2752,128]{1,0:T(8,128)(2,1)}, u32[]{:S(2)}, u32[]{:S(2)}) collective-permute-start(bf16[2752,128]{1,0:T(8,128)(2,1)S(1)} %get-tuple-element.207), channel_id=1, source_target_pairs={{0,4},{4,0},{8,12},{12,8},{16,20},{20,16},{24,28},{28,24},{1,5},{5... | collective-permute-start | bytes 2113544 | tf_op jit(solution)/shard_map/ppermute | solution.py:315
  28.9 30.2 %collective-permute-start.12 = (bf16[2752,128]{1,0:T(8,128)(2,1)}, bf16[2752,128]{1,0:T(8,128)(2,1)}, u32[]{:S(2)}, u32[]{:S(2)}) collective-permute-start(bf16[2752,128]{1,0:T(8,128)(2,1)} %get-tuple-element.214), channel_id=1, source_target_pairs={{0,24},{4,28},{8,0},{12,4},{16,8},{20,12},{24,16},{28,20},{1,25},{... | collective-permute-start | bytes 2113544 | tf_op jit(solution)/shard_map/ppermute | solution.py:314
  43.6 18.7 %collective-permute-start.13 = (bf16[2752,128]{1,0:T(8,128)(2,1)S(1)}, bf16[2752,128]{1,0:T(8,128)(2,1)}, u32[]{:S(2)}, u32[]{:S(2)}) collective-permute-start(bf16[2752,128]{1,0:T(8,128)(2,1)S(1)} %copy-done.3), channel_id=1, source_target_pairs={{0,4},{4,0},{8,12},{12,8},{16,20},{20,16},{24,28},{28,24},{1,5},{5... | collective-permute-start | bytes 2113544 | tf_op jit(solution)/shard_map/ppermute | solution.py:315
  45.1 41.6 %collective-permute-start.9 = (f32[2048,128]{1,0:T(8,128)}, f32[2048,128]{1,0:T(8,128)S(1)}, u32[]{:S(2)}, u32[]{:S(2)}) collective-permute-start(f32[2048,128]{1,0:T(8,128)} %get-tuple-element.205), channel_id=1, source_target_pairs={{0,2},{1,3},{2,0},{3,1},{4,6},{5,7},{6,4},{7,5},{8,10},{9,11},{10,... | collective-permute-start | bytes 3145736 | tf_op jit(solution)/shard_map/ppermute | solution.py:333
  46.7 28.4 %collective-permute-start.15 = (bf16[2752,128]{1,0:T(8,128)(2,1)}, bf16[2752,128]{1,0:T(8,128)(2,1)}, u32[]{:S(2)}, u32[]{:S(2)}) collective-permute-start(bf16[2752,128]{1,0:T(8,128)(2,1)} %get-tuple-element.223), channel_id=1, source_target_pairs={{0,24},{4,28},{8,0},{12,4},{16,8},{20,12},{24,16},{28,20},{1,25},{... | collective-permute-start | bytes 2113544 | tf_op jit(solution)/shard_map/ppermute | solution.py:314
  53.5 23.9 %collective-permute-start.16 = (bf16[2752,128]{1,0:T(8,128)(2,1)}, bf16[2752,128]{1,0:T(8,128)(2,1)}, u32[]{:S(2)}, u32[]{:S(2)}) collective-permute-start(bf16[2752,128]{1,0:T(8,128)(2,1)} %get-tuple-element.223), channel_id=1, source_target_pairs={{0,4},{4,0},{8,12},{12,8},{16,20},{20,16},{24,28},{28,24},{1,5},{5... | collective-permute-start | bytes 2113544 | tf_op jit(solution)/shard_map/ppermute | solution.py:315
  59.1 14.7 %collective-permute-start.14 = (f32[320,128]{1,0:T(8,128)S(1)}, f32[320,128]{1,0:T(8,128)S(1)}, u32[]{:S(2)}, u32[]{:S(2)}) collective-permute-start(f32[320,128]{1,0:T(8,128)S(1)} %get-tuple-element.216), channel_id=1, source_target_pairs={{0,2},{1,3},{2,0},{3,1},{4,6},{5,7},{6,4},{7,5},{8,10},{9,11},{10,... | collective-permute-start | bytes 491528 | tf_op jit(solution)/shard_map/ppermute | solution.py:333
  69.2 19.3 %collective-permute-start.19 = (bf16[2752,128]{1,0:T(8,128)(2,1)}, bf16[2752,128]{1,0:T(8,128)(2,1)}, u32[]{:S(2)}, u32[]{:S(2)}) collective-permute-start(bf16[2752,128]{1,0:T(8,128)(2,1)} %get-tuple-element.232), channel_id=1, source_target_pairs={{0,24},{4,28},{8,0},{12,4},{16,8},{20,12},{24,16},{28,20},{1,25},{... | collective-permute-start | bytes 2113544 | tf_op jit(solution)/shard_map/ppermute | solution.py:314
  73.8 18.0 %collective-permute-start.20 = (bf16[2752,128]{1,0:T(8,128)(2,1)}, bf16[2752,128]{1,0:T(8,128)(2,1)}, u32[]{:S(2)}, u32[]{:S(2)}) collective-permute-start(bf16[2752,128]{1,0:T(8,128)(2,1)} %get-tuple-element.232), channel_id=1, source_target_pairs={{0,4},{4,0},{8,12},{12,8},{16,20},{20,16},{24,28},{28,24},{1,5},{5... | collective-permute-start | bytes 2113544 | tf_op jit(solution)/shard_map/ppermute | solution.py:315
  75.0 10.2 %collective-permute-start.17 = (f32[448,128]{1,0:T(8,128)}, f32[448,128]{1,0:T(8,128)S(1)}, u32[]{:S(2)}, u32[]{:S(2)}) collective-permute-start(f32[448,128]{1,0:T(8,128)} %get-tuple-element.225), channel_id=1, source_target_pairs={{0,2},{1,3},{2,0},{3,1},{4,6},{5,7},{6,4},{7,5},{8,10},{9,11},{10,... | collective-permute-start | bytes 688136 | tf_op jit(solution)/shard_map/ppermute | solution.py:333
  85.3 17.6 %collective-permute-start.18 = (f32[576,128]{1,0:T(8,128)}, f32[576,128]{1,0:T(8,128)S(1)}, u32[]{:S(2)}, u32[]{:S(2)}) collective-permute-start(f32[576,128]{1,0:T(8,128)} %get-tuple-element.228), channel_id=1, source_target_pairs={{0,2},{1,3},{2,0},{3,1},{4,6},{5,7},{6,4},{7,5},{8,10},{9,11},{10,... | collective-permute-start | bytes 884744 | tf_op jit(solution)/shard_map/ppermute | solution.py:333
  88.4 22.5 %collective-permute-start.23 = (f32[384,128]{1,0:T(8,128)S(1)}, f32[384,128]{1,0:T(8,128)S(1)}, u32[]{:S(2)}, u32[]{:S(2)}) collective-permute-start(f32[384,128]{1,0:T(8,128)S(1)} %get-tuple-element.229), channel_id=1, source_target_pairs={{0,8},{4,12},{8,16},{12,20},{16,24},{20,28},{24,0},{28,4},{1,9},{5... | collective-permute-start | bytes 589832 | tf_op jit(solution)/shard_map/ppermute | solution.py:353
  99.7 7.5 %collective-permute-start.21 = (f32[352,128]{1,0:T(8,128)S(1)}, f32[352,128]{1,0:T(8,128)S(1)}, u32[]{:S(2)}, u32[]{:S(2)}) collective-permute-start(f32[352,128]{1,0:T(8,128)S(1)} %get-tuple-element.235), channel_id=1, source_target_pairs={{0,2},{1,3},{2,0},{3,1},{4,6},{5,7},{6,4},{7,5},{8,10},{9,11},{10,... | collective-permute-start | bytes 540680 | tf_op jit(solution)/shard_map/ppermute | solution.py:333
  101.3 8.8 %collective-permute-start.24 = (f32[128,128]{1,0:T(8,128)S(1)}, f32[128,128]{1,0:T(8,128)S(1)}, u32[]{:S(2)}, u32[]{:S(2)}) collective-permute-start(f32[128,128]{1,0:T(8,128)S(1)} %get-tuple-element.238), channel_id=1, source_target_pairs={{0,4},{4,0},{8,12},{12,8},{16,20},{20,16},{24,28},{28,24},{1,5},{5... | collective-permute-start | bytes 196616 | tf_op jit(solution)/shard_map/ppermute | solution.py:354
  102.4 6.4 %collective-permute-start.28 = (f32[224,128]{1,0:T(8,128)S(1)}, f32[224,128]{1,0:T(8,128)S(1)}, u32[]{:S(2)}, u32[]{:S(2)}) collective-permute-start(f32[224,128]{1,0:T(8,128)S(1)} %get-tuple-element.241), channel_id=1, source_target_pairs={{0,2},{1,3},{2,0},{3,1},{4,6},{5,7},{6,4},{7,5},{8,10},{9,11},{10,... | collective-permute-start | bytes 344072 | tf_op jit(solution)/shard_map/ppermute | solution.py:333
  104.3 10.8 %collective-permute-start.25 = (f32[288,128]{1,0:T(8,128)S(1)}, f32[288,128]{1,0:T(8,128)S(1)}, u32[]{:S(2)}, u32[]{:S(2)}) collective-permute-start(f32[288,128]{1,0:T(8,128)S(1)} %get-tuple-element.239), channel_id=1, source_target_pairs={{0,8},{4,12},{8,16},{12,20},{16,24},{20,28},{24,0},{28,4},{1,9},{5... | collective-permute-start | bytes 442376 | tf_op jit(solution)/shard_map/ppermute | solution.py:353
  107.2 8.0 %collective-permute-start.27 = (f32[352,128]{1,0:T(8,128)S(1)}, f32[352,128]{1,0:T(8,128)S(1)}, u32[]{:S(2)}, u32[]{:S(2)}) collective-permute-start(f32[352,128]{1,0:T(8,128)S(1)} %shard_map.40), channel_id=1, source_target_pairs={{0,8},{4,12},{8,16},{12,20},{16,24},{20,28},{24,0},{28,4},{1,9},{5... | collective-permute-start | bytes 540680 | tf_op jit(solution)/shard_map/ppermute | solution.py:393
  108.8 5.3 %collective-permute-start.29 = (f32[224,128]{1,0:T(8,128)S(1)}, f32[224,128]{1,0:T(8,128)S(1)}, u32[]{:S(2)}, u32[]{:S(2)}) collective-permute-start(f32[224,128]{1,0:T(8,128)S(1)} %shard_map.41), channel_id=1, source_target_pairs={{0,4},{4,0},{8,12},{12,8},{16,20},{20,16},{24,28},{28,24},{1,5},{5... | collective-permute-start | bytes 344072 | tf_op jit(solution)/shard_map/ppermute | solution.py:393
  110.0 5.2 %collective-permute-start.26 = (f32[160,128]{1,0:T(8,128)S(1)}, f32[160,128]{1,0:T(8,128)S(1)}, u32[]{:S(2)}, u32[]{:S(2)}) collective-permute-start(f32[160,128]{1,0:T(8,128)S(1)} %get-tuple-element.240), channel_id=1, source_target_pairs={{0,4},{4,0},{8,12},{12,8},{16,20},{20,16},{24,28},{28,24},{1,5},{5... | collective-permute-start | bytes 245768 | tf_op jit(solution)/shard_map/ppermute | solution.py:354
  110.9 4.3 %collective-permute-start.22 = (f32[128,128]{1,0:T(8,128)S(1)}, f32[128,128]{1,0:T(8,128)S(1)}, u32[]{:S(2)}, u32[]{:S(2)}) collective-permute-start(f32[128,128]{1,0:T(8,128)S(1)} %get-tuple-element.237), channel_id=1, source_target_pairs={{0,2},{1,3},{2,0},{3,1},{4,6},{5,7},{6,4},{7,5},{8,10},{9,11},{10,... | collective-permute-start | bytes 196616 | tf_op jit(solution)/shard_map/ppermute | solution.py:333
  (23 other events, 124.5 us)

commit v10 on v9

--- a/solution.py
+++ b/solution.py
@@ -132,12 +132,12 @@
             put_third(place_ref, keep, send, layouts[step][0], base, a, b, lanes(block, b))
 
 
-PARTS = 4
+PARTS = 1
 
 
 def own_copies(own_hbm, own, sems):
     deep = own.shape[0] // PARTS
-    spans = [pl.ds(k * deep, deep) for k in (0, 2, 1, 3)]
+    spans = [pl.ds(k * deep, deep) for k in range(PARTS)]
     return [pltpu.make_async_copy(own_hbm.at[at], own.at[at], sems.at[i]) for i, at in enumerate(spans)]
 
 
@@ -173,7 +173,7 @@
         copy.start()
     first.wait()
     block = jnp.zeros((UNIT, own.shape[1]), jnp.float32)
-    for copy, k in zip(copies, (0, 2, 1, 3)):
+    for copy, k in zip(copies, range(PARTS)):
         copy.wait()
         at = pl.ds(k * deep, deep)
         block = block + dot(fresh[at, :].T, own[at, :], ((1,), (0,)))

time: 117 us -> 117 us (level)
  no operation moved by 1% of the time
where the time goes in v10:
time: 117 us
  waiting for transfers between devices  38.3 us (33%)
  Pallas kernels  37.4 us (32%)
  starting transfers between devices  35.3 us (30%)
  other arithmetic  4.53 us (4%)
    pallas_call x12, Pallas kernels, call(): pl.pallas_call(kernel, out_shape=outs, in_specs=[SMEM] * scalars + [memor...  37.4 us
    ppermute x6, waiting for transfers between devices, over_core(): return lax.ppermute(send, 'wid', [(w, w ^ 1) for w in range(WID)])  14.4 us
    ppermute x5, starting transfers between devices, start(): lax.ppermute(after(chunk, GATES.get('R' + name)), 'tok', down)  14 us
    ppermute x8, starting transfers between devices, exchange(): lax.ppermute(after(x, GATES.get(label)), 'wid', [(w, w ^ 2) for w in rang...  11.2 us
    ppermute x5, waiting for transfers between devices, start(): lax.ppermute(after(chunk, GATES.get('R' + name)), 'tok', down)  8.81 us
    ppermute x8, waiting for transfers between devices, exchange(): lax.ppermute(after(x, GATES.get(label)), 'wid', [(w, w ^ 2) for w in rang...  7.4 us
    ppermute x5, starting transfers between devices, start(): lax.ppermute(after(chunk, GATES.get('O' + name)), 'tok', swap)  6.3 us
    ppermute x5, waiting for transfers between devices, start(): lax.ppermute(after(chunk, GATES.get('O' + name)), 'tok', swap)  5.98 us
  transfers between devices with their start and end apart: 30, of which 16 were waited for; matrix products, arithmetic and copies ran while one was open for 4% of the time, Pallas kernels for 30%

profile of v10, /device:TPU:0, one launch (start us, length us, event | category | flops | bytes accessed | tf_op | source)
XLA Modules:
  0.0 116.6 jit_solution(7127027257404707516)
XLA Ops:
  0.0 5.0 %collective-permute-start.7 = (bf16[512,1024]{1,0:T(8,128)(2,1)}, bf16[512,1024]{1,0:T(8,128)(2,1)}, u32[]{:S(2)}, u32[]{:S(2)}) collective-permute-start(bf16[512,1024]{1,0:T(8,128)(2,1)} %param.15), channel_id=1, source_target_pairs={{0,24},{4,28},{8,0},{12,4},{16,8},{20,12},{24,16},{28,20},{1,25},{... | collective-permute-start | bytes 3145736 | tf_op jit(solution)/shard_map/ppermute | solution.py:314
  6.5 6.2 %shard_map.37 = (bf16[2752,128]{1,0:T(8,128)(2,1)S(1)}, bf16[2752,128]{1,0:T(8,128)(2,1)}, bf16[2752,128]{1,0:T(8,128)(2,1)}, bf16[2752,128]{1,0:T(8,128)(2,1)}) custom-call(bf16[2752,512]{1,0:T(8,128)(2,1)} %bitcast.35), custom_call_target="tpu_custom_call" | custom-call | flops 2000000000 | bytes 2000000 | tf_op jit(solution)/shard_map/pallas_call | solution.py:25
  14.5 7.3 %conditional.6 = (f32[1024,128]{1,0:T(8,128)S(1)}, f32[1024,128]{1,0:T(8,128)}) conditional(s32[]{:T(128)} %convert_element_type.2, () %tuple.66, (s32[5]{0:T(128)S(1)}, bf16[512,1024]{1,0:T(8,128)(2,1)}, bf16[2752,512]{1,0:T(8,128)(2,1)S(1)}) %tuple.111), branch_computations={%region_1.2_spmd, %region_2.3_spmd} | conditional | flops 2000262144 | bytes 9340088 | solution.py:329
  14.5 3.6 %branch_1_fun.6 = (f32[2,1024,128]{2,1,0:T(8,128)S(1)}, f32[2,1024,128]{2,1,0:T(8,128)S(1)}) custom-call(s32[5]{0:T(128)S(1)} %get-tuple-element.95.place_ref, bf16[512,1024]{1,0:T(8,128)(2,1)} %get-tuple-element.96.a_ref, bf16[2752,512]{1,0:T(8,128)(2,1)S(1)} %get-tuple-element.97.g_ref), custom_call_target="tpu_custom_call" | custom-call | flops 2000000000 | bytes 2000000 | tf_op jit(solution)/shard_map/cond/branch_1_fun/pallas_call | solution.py:25
  18.2 2.6 %collective-permute-done = f32[2,1024,128]{2,1,0:T(8,128)S(1)} collective-permute-done((f32[2,1024,128]{2,1,0:T(8,128)S(1)}, f32[2,1024,128]{2,1,0:T(8,128)S(1)}, u32[]{:S(2)}, u32[]{:S(2)}) %collective-permute-start) | collective-permute-done | bytes 1048608 | tf_op jit(solution)/shard_map/cond/branch_1_fun/ppermute | solution.py:299
  23.9 5.0 %collective-permute-done.7 = bf16[512,1024]{1,0:T(8,128)(2,1)} collective-permute-done((bf16[512,1024]{1,0:T(8,128)(2,1)}, bf16[512,1024]{1,0:T(8,128)(2,1)}, u32[]{:S(2)}, u32[]{:S(2)}) %collective-permute-start.7) | collective-permute-done | bytes 1048608 | tf_op jit(solution)/shard_map/ppermute | solution.py:314
  28.9 4.3 %collective-permute-start.12 = (bf16[2752,128]{1,0:T(8,128)(2,1)}, bf16[2752,128]{1,0:T(8,128)(2,1)}, u32[]{:S(2)}, u32[]{:S(2)}) collective-permute-start(bf16[2752,128]{1,0:T(8,128)(2,1)} %get-tuple-element.214), channel_id=1, source_target_pairs={{0,24},{4,28},{8,0},{12,4},{16,8},{20,12},{24,16},{28,20},{1,25},{... | collective-permute-start | bytes 2113544 | tf_op jit(solution)/shard_map/ppermute | solution.py:314
  33.2 10.4 %conditional.7 = (f32[2048,128]{1,0:T(8,128)S(1)}, f32[2048,128]{1,0:T(8,128)}) conditional(s32[]{:T(128)} %convert_element_type.2, () %tuple.70, (s32[5]{0:T(128)S(1)}, bf16[512,1024]{1,0:T(8,128)(2,1)}, bf16[512,1024]{1,0:T(8,128)(2,1)}, bf16[512,1024]{1,0:T(8,128)(2,1)}) %tuple.73), branch_computations={%region_3.4_spmd, %region_4.5_spmd} | conditional | flops 2000524288 | bytes 16680120 | solution.py:329
  33.2 4.9 %branch_1_fun.7 = (f32[2,2048,128]{2,1,0:T(8,128)S(1)}, f32[2,2048,128]{2,1,0:T(8,128)S(1)}) custom-call(s32[5]{0:T(128)S(1)} %get-tuple-element.100.refs_0_, bf16[512,1024]{1,0:T(8,128)(2,1)} %get-tuple-element.101.refs_1_, bf16[512,1024]{1,0:T(8,128)(2,1)} %get-tuple-element.102.refs_2_, bf16[512,1024]{1,0:T(8,128)(2,1)} %get-tuple-element.103.refs_3_), custom_call_target="tpu_custom_call" | custom-call | flops 2000000000 | bytes 2000000 | tf_op jit(solution)/shard_map/cond/branch_1_fun/pallas_call | solution.py:25
  38.3 4.1 %collective-permute-done.1 = f32[2,2048,128]{2,1,0:T(8,128)S(1)} collective-permute-done((f32[2,2048,128]{2,1,0:T(8,128)S(1)}, f32[2,2048,128]{2,1,0:T(8,128)S(1)}, u32[]{:S(2)}, u32[]{:S(2)}) %collective-permute-start.1) | collective-permute-done | bytes 2097184 | tf_op jit(solution)/shard_map/cond/branch_1_fun/ppermute | solution.py:299
  48.3 5.5 %conditional.8 = (f32[320,128]{1,0:T(8,128)S(1)}, f32[320,128]{1,0:T(8,128)S(1)}) conditional(s32[]{:T(128)} %convert_element_type.2, () %tuple.74, (s32[5]{0:T(128)S(1)}, bf16[2752,512]{1,0:T(8,128)(2,1)}, bf16[2752,128]{1,0:T(8,128)(2,1)S(1)}, bf16[2752,128]{1,0:T(8,128)(2,1)}, bf16[2752,128]{1,0:T(8,128)(2,1)}) %tuple.108), branch_computations={%region_5.6_spmd, %region_6.7_spmd} | conditional | flops 2000081920 | bytes 4293816 | solution.py:329
  48.3 3.7 %branch_1_fun.8 = (f32[2,320,128]{2,1,0:T(8,128)S(1)}, f32[2,320,128]{2,1,0:T(8,128)S(1)}) custom-call(s32[5]{0:T(128)S(1)} %get-tuple-element.106.refs_0_, bf16[2752,512]{1,0:T(8,128)(2,1)} %get-tuple-element.107.refs_1_, bf16[2752,128]{1,0:T(8,128)(2,1)S(1)} %get-tuple-element.108.refs_2_, bf16[2752,128]{1,0:T(8,128)(2,1)} %get-tuple-element.109.refs_3_, ...), custom_call_target="tpu_custom_call" | custom-call | flops 2000000000 | bytes 2000000 | tf_op jit(solution)/shard_map/cond/branch_1_fun/pallas_call | solution.py:25
  55.4 3.8 %collective-permute-done.12 = bf16[2752,128]{1,0:T(8,128)(2,1)} collective-permute-done((bf16[2752,128]{1,0:T(8,128)(2,1)}, bf16[2752,128]{1,0:T(8,128)(2,1)}, u32[]{:S(2)}, u32[]{:S(2)}) %collective-permute-start.12) | collective-permute-done | bytes 704544 | tf_op jit(solution)/shard_map/ppermute | solution.py:314
  62.4 6.7 %conditional.9 = (f32[448,128]{1,0:T(8,128)S(1)}, f32[448,128]{1,0:T(8,128)}) conditional(s32[]{:T(128)} %convert_element_type.2, () %tuple.76, (s32[5]{0:T(128)S(1)}, bf16[2752,512]{1,0:T(8,128)(2,1)}, bf16[2752,128]{1,0:T(8,128)(2,1)S(1)}, bf16[2752,128]{1,0:T(8,128)(2,1)S(1)}, bf16[2752,128]{1,0:T(8,128)(2,1)}, ...), branch_computations={%region_7.8_spmd, %region_8.9_spmd} | conditional | flops 2000114688 | bytes 5211320 | solution.py:329
  62.4 4.1 %branch_1_fun.9 = (f32[2,448,128]{2,1,0:T(8,128)S(1)}, f32[2,448,128]{2,1,0:T(8,128)S(1)}) custom-call(s32[5]{0:T(128)S(1)} %get-tuple-element.113.refs_0_, bf16[2752,512]{1,0:T(8,128)(2,1)} %get-tuple-element.114.refs_1_, bf16[2752,128]{1,0:T(8,128)(2,1)S(1)} %get-tuple-element.115.refs_2_, bf16[2752,128]{1,0:T(8,128)(2,1)S(1)} %get-tuple-element.116.refs_3_, ...), custom_call_target="tpu_custom_call" | custom-call | flops 2000000000 | bytes 2000000 | tf_op jit(solution)/shard_map/cond/branch_1_fun/pallas_call | solution.py:25
  69.1 2.5 %collective-permute-start.19 = (bf16[2752,128]{1,0:T(8,128)(2,1)}, bf16[2752,128]{1,0:T(8,128)(2,1)}, u32[]{:S(2)}, u32[]{:S(2)}) collective-permute-start(bf16[2752,128]{1,0:T(8,128)(2,1)} %get-tuple-element.232), channel_id=1, source_target_pairs={{0,24},{4,28},{8,0},{12,4},{16,8},{20,12},{24,16},{28,20},{1,25},{... | collective-permute-start | bytes 2113544 | tf_op jit(solution)/shard_map/ppermute | solution.py:314
  71.7 2.1 %collective-permute-done.14.refs_3_.refs_7_ = f32[320,128]{1,0:T(8,128)S(1)} collective-permute-done((f32[320,128]{1,0:T(8,128)S(1)}, f32[320,128]{1,0:T(8,128)S(1)}, u32[]{:S(2)}, u32[]{:S(2)}) %collective-permute-start.14) | collective-permute-done | bytes 163872 | tf_op jit(solution)/shard_map/ppermute | solution.py:333
  77.5 7.8 %conditional.10 = (f32[576,128]{1,0:T(8,128)S(1)}, f32[576,128]{1,0:T(8,128)}) conditional(s32[]{:T(128)} %convert_element_type.2, () %tuple.82, (s32[5]{0:T(128)S(1)}, bf16[2752,512]{1,0:T(8,128)(2,1)}, bf16[2752,128]{1,0:T(8,128)(2,1)S(1)}, bf16[2752,128]{1,0:T(8,128)(2,1)S(1)}, bf16[2752,128]{1,0:T(8,128)(2,1)}, ...), branch_computations={%region_9.10_spmd, %region_10.11_spmd} | conditional | flops 2000147456 | bytes 6128824 | solution.py:329
  77.5 4.9 %branch_1_fun.10 = (f32[2,576,128]{2,1,0:T(8,128)S(1)}, f32[2,576,128]{2,1,0:T(8,128)S(1)}) custom-call(s32[5]{0:T(128)S(1)} %get-tuple-element.123.refs_0_, bf16[2752,512]{1,0:T(8,128)(2,1)} %get-tuple-element.124.refs_1_, bf16[2752,128]{1,0:T(8,128)(2,1)S(1)} %get-tuple-element.125.refs_2_, bf16[2752,128]{1,0:T(8,128)(2,1)S(1)} %get-tuple-element.126.refs_3_, ...), custom_call_target="tpu_custom_call" | custom-call | flops 2000000000 | bytes 2000000 | tf_op jit(solution)/shard_map/cond/branch_1_fun/pallas_call | solution.py:25
  88.5 3.3 %collective-permute-done.20 = bf16[2752,128]{1,0:T(8,128)(2,1)} collective-permute-done((bf16[2752,128]{1,0:T(8,128)(2,1)}, bf16[2752,128]{1,0:T(8,128)(2,1)}, u32[]{:S(2)}, u32[]{:S(2)}) %collective-permute-start.20) | collective-permute-done | bytes 704544 | tf_op jit(solution)/shard_map/ppermute | solution.py:315
  91.8 7.2 %conditional.11 = (f32[704,128]{1,0:T(8,128)S(1)}, f32[352,128]{1,0:T(8,128)S(1)}, f32[224,128]{1,0:T(8,128)S(1)}, f32[128,128]{1,0:T(8,128)S(1)}) conditional(s32[]{:T(128)} %convert_element_type.2, () %tuple.87, (s32[5]{0:T(128)S(1)}, bf16[2752,512]{1,0:T(8,128)(2,1)S(1)}, bf16[2752,128]{1,0:T(8,128)(2,1)S(1)}, bf16[2752,128]{1,0:T(8,128)(2,1)S(1)}, ...), branch_computations={%region_11.12_spmd, %region_12.13_spmd} | conditional | flops 2000180224 | bytes 7046344 | solution.py:329
  91.8 4.8 %branch_1_fun.11 = (f32[2,704,128]{2,1,0:T(8,128)S(1)}, f32[2,704,128]{2,1,0:T(8,128)S(1)}) custom-call(s32[5]{0:T(128)S(1)} %get-tuple-element.136.refs_0_, bf16[2752,512]{1,0:T(8,128)(2,1)S(1)} %get-tuple-element.137.refs_1_, bf16[2752,128]{1,0:T(8,128)(2,1)S(1)} %get-tuple-element.138.refs_2_, bf16[2752,128]{1,0:T(8,128)(2,1)S(1)} %get-tuple-element.139.refs_3_, ...), custom_call_target="tpu_custom_call" | custom-call | flops 2000000000 | bytes 2000000 | tf_op jit(solution)/shard_map/cond/branch_1_fun/pallas_call | solution.py:25
  96.7 2.2 %collective-permute-done.5 = f32[2,704,128]{2,1,0:T(8,128)S(1)} collective-permute-done((f32[2,704,128]{2,1,0:T(8,128)S(1)}, f32[2,704,128]{2,1,0:T(8,128)S(1)}, u32[]{:S(2)}, u32[]{:S(2)}) %collective-permute-start.5) | collective-permute-done | bytes 720928 | tf_op jit(solution)/shard_map/cond/branch_1_fun/ppermute | solution.py:299
  103.8 2.7 %collective-permute-done.21.refs_3_.refs_13_ = f32[352,128]{1,0:T(8,128)S(1)} collective-permute-done((f32[352,128]{1,0:T(8,128)S(1)}, f32[352,128]{1,0:T(8,128)S(1)}, u32[]{:S(2)}, u32[]{:S(2)}) %collective-permute-start.21) | collective-permute-done | bytes 180256 | tf_op jit(solution)/shard_map/ppermute | solution.py:333
  (99 shorter events, 45.6 us)
Async XLA Ops:
  0.0 28.9 %collective-permute-start.7 = (bf16[512,1024]{1,0:T(8,128)(2,1)}, bf16[512,1024]{1,0:T(8,128)(2,1)}, u32[]{:S(2)}, u32[]{:S(2)}) collective-permute-start(bf16[512,1024]{1,0:T(8,128)(2,1)} %param.15), channel_id=1, source_target_pairs={{0,24},{4,28},{8,0},{12,4},{16,8},{20,12},{24,16},{28,20},{1,25},{... | collective-permute-start | bytes 3145736 | tf_op jit(solution)/shard_map/ppermute | solution.py:314
  5.0 28.2 %collective-permute-start.8 = (bf16[512,1024]{1,0:T(8,128)(2,1)}, bf16[512,1024]{1,0:T(8,128)(2,1)}, u32[]{:S(2)}, u32[]{:S(2)}) collective-permute-start(bf16[512,1024]{1,0:T(8,128)(2,1)} %param.15), channel_id=1, source_target_pairs={{0,4},{4,0},{8,12},{12,8},{16,20},{20,16},{24,28},{28,24},{1,5},{5... | collective-permute-start | bytes 3145736 | tf_op jit(solution)/shard_map/ppermute | solution.py:315
  12.7 34.0 %collective-permute-start.10 = (bf16[2752,128]{1,0:T(8,128)(2,1)S(1)}, bf16[2752,128]{1,0:T(8,128)(2,1)}, u32[]{:S(2)}, u32[]{:S(2)}) collective-permute-start(bf16[2752,128]{1,0:T(8,128)(2,1)S(1)} %get-tuple-element.207), channel_id=1, source_target_pairs={{0,24},{4,28},{8,0},{12,4},{16,8},{20,12},{24,16},{28,20},{1,25},{... | collective-permute-start | bytes 2113544 | tf_op jit(solution)/shard_map/ppermute | solution.py:314
  21.8 23.3 %collective-permute-start.6 = (f32[1024,128]{1,0:T(8,128)}, f32[1024,128]{1,0:T(8,128)S(1)}, u32[]{:S(2)}, u32[]{:S(2)}) collective-permute-start(f32[1024,128]{1,0:T(8,128)} %get-tuple-element.198), channel_id=1, source_target_pairs={{0,2},{1,3},{2,0},{3,1},{4,6},{5,7},{6,4},{7,5},{8,10},{9,11},{10,... | collective-permute-start | bytes 1572872 | tf_op jit(solution)/shard_map/ppermute | solution.py:333
  23.4 25.0 %collective-permute-start.11 = (bf16[2752,128]{1,0:T(8,128)(2,1)S(1)}, bf16[2752,128]{1,0:T(8,128)(2,1)}, u32[]{:S(2)}, u32[]{:S(2)}) collective-permute-start(bf16[2752,128]{1,0:T(8,128)(2,1)S(1)} %get-tuple-element.207), channel_id=1, source_target_pairs={{0,4},{4,0},{8,12},{12,8},{16,20},{20,16},{24,28},{28,24},{1,5},{5... | collective-permute-start | bytes 2113544 | tf_op jit(solution)/shard_map/ppermute | solution.py:315
  28.9 30.2 %collective-permute-start.12 = (bf16[2752,128]{1,0:T(8,128)(2,1)}, bf16[2752,128]{1,0:T(8,128)(2,1)}, u32[]{:S(2)}, u32[]{:S(2)}) collective-permute-start(bf16[2752,128]{1,0:T(8,128)(2,1)} %get-tuple-element.214), channel_id=1, source_target_pairs={{0,24},{4,28},{8,0},{12,4},{16,8},{20,12},{24,16},{28,20},{1,25},{... | collective-permute-start | bytes 2113544 | tf_op jit(solution)/shard_map/ppermute | solution.py:314
  43.6 18.7 %collective-permute-start.13 = (bf16[2752,128]{1,0:T(8,128)(2,1)S(1)}, bf16[2752,128]{1,0:T(8,128)(2,1)}, u32[]{:S(2)}, u32[]{:S(2)}) collective-permute-start(bf16[2752,128]{1,0:T(8,128)(2,1)S(1)} %copy-done.3), channel_id=1, source_target_pairs={{0,4},{4,0},{8,12},{12,8},{16,20},{20,16},{24,28},{28,24},{1,5},{5... | collective-permute-start | bytes 2113544 | tf_op jit(solution)/shard_map/ppermute | solution.py:315
  45.1 41.6 %collective-permute-start.9 = (f32[2048,128]{1,0:T(8,128)}, f32[2048,128]{1,0:T(8,128)S(1)}, u32[]{:S(2)}, u32[]{:S(2)}) collective-permute-start(f32[2048,128]{1,0:T(8,128)} %get-tuple-element.205), channel_id=1, source_target_pairs={{0,2},{1,3},{2,0},{3,1},{4,6},{5,7},{6,4},{7,5},{8,10},{9,11},{10,... | collective-permute-start | bytes 3145736 | tf_op jit(solution)/shard_map/ppermute | solution.py:333
  46.7 28.4 %collective-permute-start.15 = (bf16[2752,128]{1,0:T(8,128)(2,1)}, bf16[2752,128]{1,0:T(8,128)(2,1)}, u32[]{:S(2)}, u32[]{:S(2)}) collective-permute-start(bf16[2752,128]{1,0:T(8,128)(2,1)} %get-tuple-element.223), channel_id=1, source_target_pairs={{0,24},{4,28},{8,0},{12,4},{16,8},{20,12},{24,16},{28,20},{1,25},{... | collective-permute-start | bytes 2113544 | tf_op jit(solution)/shard_map/ppermute | solution.py:314
  53.8 23.7 %collective-permute-start.16 = (bf16[2752,128]{1,0:T(8,128)(2,1)}, bf16[2752,128]{1,0:T(8,128)(2,1)}, u32[]{:S(2)}, u32[]{:S(2)}) collective-permute-start(bf16[2752,128]{1,0:T(8,128)(2,1)} %get-tuple-element.223), channel_id=1, source_target_pairs={{0,4},{4,0},{8,12},{12,8},{16,20},{20,16},{24,28},{28,24},{1,5},{5... | collective-permute-start | bytes 2113544 | tf_op jit(solution)/shard_map/ppermute | solution.py:315
  59.1 14.7 %collective-permute-start.14 = (f32[320,128]{1,0:T(8,128)S(1)}, f32[320,128]{1,0:T(8,128)S(1)}, u32[]{:S(2)}, u32[]{:S(2)}) collective-permute-start(f32[320,128]{1,0:T(8,128)S(1)} %get-tuple-element.216), channel_id=1, source_target_pairs={{0,2},{1,3},{2,0},{3,1},{4,6},{5,7},{6,4},{7,5},{8,10},{9,11},{10,... | collective-permute-start | bytes 491528 | tf_op jit(solution)/shard_map/ppermute | solution.py:333
  69.1 19.3 %collective-permute-start.19 = (bf16[2752,128]{1,0:T(8,128)(2,1)}, bf16[2752,128]{1,0:T(8,128)(2,1)}, u32[]{:S(2)}, u32[]{:S(2)}) collective-permute-start(bf16[2752,128]{1,0:T(8,128)(2,1)} %get-tuple-element.232), channel_id=1, source_target_pairs={{0,24},{4,28},{8,0},{12,4},{16,8},{20,12},{24,16},{28,20},{1,25},{... | collective-permute-start | bytes 2113544 | tf_op jit(solution)/shard_map/ppermute | solution.py:314
  73.8 18.0 %collective-permute-start.20 = (bf16[2752,128]{1,0:T(8,128)(2,1)}, bf16[2752,128]{1,0:T(8,128)(2,1)}, u32[]{:S(2)}, u32[]{:S(2)}) collective-permute-start(bf16[2752,128]{1,0:T(8,128)(2,1)} %get-tuple-element.232), channel_id=1, source_target_pairs={{0,4},{4,0},{8,12},{12,8},{16,20},{20,16},{24,28},{28,24},{1,5},{5... | collective-permute-start | bytes 2113544 | tf_op jit(solution)/shard_map/ppermute | solution.py:315
  75.0 10.2 %collective-permute-start.17 = (f32[448,128]{1,0:T(8,128)}, f32[448,128]{1,0:T(8,128)S(1)}, u32[]{:S(2)}, u32[]{:S(2)}) collective-permute-start(f32[448,128]{1,0:T(8,128)} %get-tuple-element.225), channel_id=1, source_target_pairs={{0,2},{1,3},{2,0},{3,1},{4,6},{5,7},{6,4},{7,5},{8,10},{9,11},{10,... | collective-permute-start | bytes 688136 | tf_op jit(solution)/shard_map/ppermute | solution.py:333
  85.2 17.0 %collective-permute-start.18 = (f32[576,128]{1,0:T(8,128)}, f32[576,128]{1,0:T(8,128)S(1)}, u32[]{:S(2)}, u32[]{:S(2)}) collective-permute-start(f32[576,128]{1,0:T(8,128)} %get-tuple-element.228), channel_id=1, source_target_pairs={{0,2},{1,3},{2,0},{3,1},{4,6},{5,7},{6,4},{7,5},{8,10},{9,11},{10,... | collective-permute-start | bytes 884744 | tf_op jit(solution)/shard_map/ppermute | solution.py:333
  88.4 21.9 %collective-permute-start.23 = (f32[384,128]{1,0:T(8,128)S(1)}, f32[384,128]{1,0:T(8,128)S(1)}, u32[]{:S(2)}, u32[]{:S(2)}) collective-permute-start(f32[384,128]{1,0:T(8,128)S(1)} %get-tuple-element.229), channel_id=1, source_target_pairs={{0,8},{4,12},{8,16},{12,20},{16,24},{20,28},{24,0},{28,4},{1,9},{5... | collective-permute-start | bytes 589832 | tf_op jit(solution)/shard_map/ppermute | solution.py:353
  99.0 7.5 %collective-permute-start.21 = (f32[352,128]{1,0:T(8,128)S(1)}, f32[352,128]{1,0:T(8,128)S(1)}, u32[]{:S(2)}, u32[]{:S(2)}) collective-permute-start(f32[352,128]{1,0:T(8,128)S(1)} %get-tuple-element.235), channel_id=1, source_target_pairs={{0,2},{1,3},{2,0},{3,1},{4,6},{5,7},{6,4},{7,5},{8,10},{9,11},{10,... | collective-permute-start | bytes 540680 | tf_op jit(solution)/shard_map/ppermute | solution.py:333
  100.6 8.8 %collective-permute-start.24 = (f32[128,128]{1,0:T(8,128)S(1)}, f32[128,128]{1,0:T(8,128)S(1)}, u32[]{:S(2)}, u32[]{:S(2)}) collective-permute-start(f32[128,128]{1,0:T(8,128)S(1)} %get-tuple-element.238), channel_id=1, source_target_pairs={{0,4},{4,0},{8,12},{12,8},{16,20},{20,16},{24,28},{28,24},{1,5},{5... | collective-permute-start | bytes 196616 | tf_op jit(solution)/shard_map/ppermute | solution.py:354
  101.8 6.4 %collective-permute-start.28 = (f32[224,128]{1,0:T(8,128)S(1)}, f32[224,128]{1,0:T(8,128)S(1)}, u32[]{:S(2)}, u32[]{:S(2)}) collective-permute-start(f32[224,128]{1,0:T(8,128)S(1)} %get-tuple-element.241), channel_id=1, source_target_pairs={{0,2},{1,3},{2,0},{3,1},{4,6},{5,7},{6,4},{7,5},{8,10},{9,11},{10,... | collective-permute-start | bytes 344072 | tf_op jit(solution)/shard_map/ppermute | solution.py:333
  103.7 10.8 %collective-permute-start.25 = (f32[288,128]{1,0:T(8,128)S(1)}, f32[288,128]{1,0:T(8,128)S(1)}, u32[]{:S(2)}, u32[]{:S(2)}) collective-permute-start(f32[288,128]{1,0:T(8,128)S(1)} %get-tuple-element.239), channel_id=1, source_target_pairs={{0,8},{4,12},{8,16},{12,20},{16,24},{20,28},{24,0},{28,4},{1,9},{5... | collective-permute-start | bytes 442376 | tf_op jit(solution)/shard_map/ppermute | solution.py:353
  106.6 8.0 %collective-permute-start.27 = (f32[352,128]{1,0:T(8,128)S(1)}, f32[352,128]{1,0:T(8,128)S(1)}, u32[]{:S(2)}, u32[]{:S(2)}) collective-permute-start(f32[352,128]{1,0:T(8,128)S(1)} %shard_map.40), channel_id=1, source_target_pairs={{0,8},{4,12},{8,16},{12,20},{16,24},{20,28},{24,0},{28,4},{1,9},{5... | collective-permute-start | bytes 540680 | tf_op jit(solution)/shard_map/ppermute | solution.py:393
  108.2 5.3 %collective-permute-start.29 = (f32[224,128]{1,0:T(8,128)S(1)}, f32[224,128]{1,0:T(8,128)S(1)}, u32[]{:S(2)}, u32[]{:S(2)}) collective-permute-start(f32[224,128]{1,0:T(8,128)S(1)} %shard_map.41), channel_id=1, source_target_pairs={{0,4},{4,0},{8,12},{12,8},{16,20},{20,16},{24,28},{28,24},{1,5},{5... | collective-permute-start | bytes 344072 | tf_op jit(solution)/shard_map/ppermute | solution.py:393
  109.4 5.2 %collective-permute-start.26 = (f32[160,128]{1,0:T(8,128)S(1)}, f32[160,128]{1,0:T(8,128)S(1)}, u32[]{:S(2)}, u32[]{:S(2)}) collective-permute-start(f32[160,128]{1,0:T(8,128)S(1)} %get-tuple-element.240), channel_id=1, source_target_pairs={{0,4},{4,0},{8,12},{12,8},{16,20},{20,16},{24,28},{28,24},{1,5},{5... | collective-permute-start | bytes 245768 | tf_op jit(solution)/shard_map/ppermute | solution.py:354
  110.3 4.3 %collective-permute-start.22 = (f32[128,128]{1,0:T(8,128)S(1)}, f32[128,128]{1,0:T(8,128)S(1)}, u32[]{:S(2)}, u32[]{:S(2)}) collective-permute-start(f32[128,128]{1,0:T(8,128)S(1)} %get-tuple-element.237), channel_id=1, source_target_pairs={{0,2},{1,3},{2,0},{3,1},{4,6},{5,7},{6,4},{7,5},{8,10},{9,11},{10,... | collective-permute-start | bytes 196616 | tf_op jit(solution)/shard_map/ppermute | solution.py:333
  (23 other events, 124.4 us)

commit v11 on v10

--- a/solution.py
+++ b/solution.py
@@ -153,7 +153,7 @@
     first = pltpu.make_async_copy(ring[step], fresh, sems.at[PARTS])
     copies = own_copies(own_hbm, own, sems)
     third = [pltpu.make_async_copy(other[a], column(others, a), sems.at[PARTS + 1 + a]) for a in range(n)]
-    from_ring = [pltpu.make_async_copy(ring[a], column(chosen, a), sems.at[PARTS + 1 + n + a]) for a in range(n)]
+    from_ring = [pltpu.make_async_copy(ring[a], column(chosen, a), sems.at[PARTS + 1 + n + a]) for a in range(step)]
     from_mine = [pltpu.make_async_copy(mine[a], column(chosen, a), sems.at[PARTS + 1 + n + a]) for a in range(n)]
     first.start()
     for copy in copies:
@@ -161,7 +161,7 @@
 
     @pl.when(even)
     def _():
-        for copy in from_ring:
+        for copy in from_ring[:step]:
             copy.start()
 
     @pl.when(jnp.logical_not(even))
@@ -178,9 +178,15 @@
         at = pl.ds(k * deep, deep)
         block = block + dot(fresh[at, :].T, own[at, :], ((1,), (0,)))
     put_ring(place_ref, keep, send, spot, 0, step, block)
-    for copy in from_ring + third:
+    for copy in from_ring[:step] + third:
         copy.wait()
-    block = dot(column(chosen, step)[...].T, others[...], ((1,), (0,)))
+
+    @pl.when(jnp.logical_not(even))
+    def _():
+        from_mine[step].wait()
+
+    newest = jnp.where(even, fresh[...], column(chosen, step)[...])
+    block = dot(newest.T, others[...], ((1,), (0,)))
     for b in range(n):
         put_third(place_ref, keep, send, spot, 0, step, b, lanes(block, b))
     if step:

time: 117 us -> 117 us (level)
  transfers between devices with their start and end apart: 30 -> 30, of which waited for: 16 -> 17; matrix products, arithmetic and copies ran while one was open for 4% -> 4% of each run, Pallas kernels for 30% -> 30%
where the time goes in v11:
time: 117 us
  waiting for transfers between devices  38.5 us (33%)
  Pallas kernels  37 us (32%)
  starting transfers between devices  35.6 us (30%)
  other arithmetic  4.53 us (4%)
    pallas_call x12, Pallas kernels, call(): pl.pallas_call(kernel, out_shape=outs, in_specs=[SMEM] * scalars + [memor...  37 us
    ppermute x6, waiting for transfers between devices, over_core(): return lax.ppermute(send, 'wid', [(w, w ^ 1) for w in range(WID)])  14.4 us
    ppermute x5, starting transfers between devices, start(): lax.ppermute(after(chunk, GATES.get('R' + name)), 'tok', down)  14 us
    ppermute x8, starting transfers between devices, exchange(): lax.ppermute(after(x, GATES.get(label)), 'wid', [(w, w ^ 2) for w in rang...  11.2 us
    ppermute x5, waiting for transfers between devices, start(): lax.ppermute(after(chunk, GATES.get('R' + name)), 'tok', down)  8.78 us
    ppermute x8, waiting for transfers between devices, exchange(): lax.ppermute(after(x, GATES.get(label)), 'wid', [(w, w ^ 2) for w in rang...  7.29 us
    ppermute x5, starting transfers between devices, start(): lax.ppermute(after(chunk, GATES.get('O' + name)), 'tok', swap)  6.32 us
    ppermute x5, waiting for transfers between devices, start(): lax.ppermute(after(chunk, GATES.get('O' + name)), 'tok', swap)  6.17 us
  transfers between devices with their start and end apart: 30, of which 17 were waited for; matrix products, arithmetic and copies ran while one was open for 4% of the time, Pallas kernels for 30%

profile of v11, /device:TPU:0, one launch (start us, length us, event | category | flops | bytes accessed | tf_op | source)
XLA Modules:
  0.0 116.7 jit_solution(14857426686952798409)
XLA Ops:
  0.0 5.0 %collective-permute-start.7 = (bf16[512,1024]{1,0:T(8,128)(2,1)}, bf16[512,1024]{1,0:T(8,128)(2,1)}, u32[]{:S(2)}, u32[]{:S(2)}) collective-permute-start(bf16[512,1024]{1,0:T(8,128)(2,1)} %param.15), channel_id=1, source_target_pairs={{0,24},{4,28},{8,0},{12,4},{16,8},{20,12},{24,16},{28,20},{1,25},{... | collective-permute-start | bytes 3145736 | tf_op jit(solution)/shard_map/ppermute | solution.py:320
  6.5 6.2 %shard_map.37 = (bf16[2752,128]{1,0:T(8,128)(2,1)S(1)}, bf16[2752,128]{1,0:T(8,128)(2,1)}, bf16[2752,128]{1,0:T(8,128)(2,1)}, bf16[2752,128]{1,0:T(8,128)(2,1)}) custom-call(bf16[2752,512]{1,0:T(8,128)(2,1)} %bitcast.35), custom_call_target="tpu_custom_call" | custom-call | flops 2000000000 | bytes 2000000 | tf_op jit(solution)/shard_map/pallas_call | solution.py:25
  14.5 7.3 %conditional.6 = (f32[1024,128]{1,0:T(8,128)S(1)}, f32[1024,128]{1,0:T(8,128)}) conditional(s32[]{:T(128)} %convert_element_type.2, () %tuple.66, (s32[5]{0:T(128)S(1)}, bf16[512,1024]{1,0:T(8,128)(2,1)}, bf16[2752,512]{1,0:T(8,128)(2,1)S(1)}) %tuple.111), branch_computations={%region_1.2_spmd, %region_2.3_spmd} | conditional | flops 2000262144 | bytes 9340088 | solution.py:335
  14.5 3.6 %branch_1_fun.6 = (f32[2,1024,128]{2,1,0:T(8,128)S(1)}, f32[2,1024,128]{2,1,0:T(8,128)S(1)}) custom-call(s32[5]{0:T(128)S(1)} %get-tuple-element.95.place_ref, bf16[512,1024]{1,0:T(8,128)(2,1)} %get-tuple-element.96.a_ref, bf16[2752,512]{1,0:T(8,128)(2,1)S(1)} %get-tuple-element.97.g_ref), custom_call_target="tpu_custom_call" | custom-call | flops 2000000000 | bytes 2000000 | tf_op jit(solution)/shard_map/cond/branch_1_fun/pallas_call | solution.py:25
  18.2 2.6 %collective-permute-done = f32[2,1024,128]{2,1,0:T(8,128)S(1)} collective-permute-done((f32[2,1024,128]{2,1,0:T(8,128)S(1)}, f32[2,1024,128]{2,1,0:T(8,128)S(1)}, u32[]{:S(2)}, u32[]{:S(2)}) %collective-permute-start) | collective-permute-done | bytes 1048608 | tf_op jit(solution)/shard_map/cond/branch_1_fun/ppermute | solution.py:305
  23.9 5.0 %collective-permute-done.7 = bf16[512,1024]{1,0:T(8,128)(2,1)} collective-permute-done((bf16[512,1024]{1,0:T(8,128)(2,1)}, bf16[512,1024]{1,0:T(8,128)(2,1)}, u32[]{:S(2)}, u32[]{:S(2)}) %collective-permute-start.7) | collective-permute-done | bytes 1048608 | tf_op jit(solution)/shard_map/ppermute | solution.py:320
  28.9 4.3 %collective-permute-start.12 = (bf16[2752,128]{1,0:T(8,128)(2,1)}, bf16[2752,128]{1,0:T(8,128)(2,1)}, u32[]{:S(2)}, u32[]{:S(2)}) collective-permute-start(bf16[2752,128]{1,0:T(8,128)(2,1)} %get-tuple-element.214), channel_id=1, source_target_pairs={{0,24},{4,28},{8,0},{12,4},{16,8},{20,12},{24,16},{28,20},{1,25},{... | collective-permute-start | bytes 2113544 | tf_op jit(solution)/shard_map/ppermute | solution.py:320
  33.2 10.4 %conditional.7 = (f32[2048,128]{1,0:T(8,128)S(1)}, f32[2048,128]{1,0:T(8,128)}) conditional(s32[]{:T(128)} %convert_element_type.2, () %tuple.70, (s32[5]{0:T(128)S(1)}, bf16[512,1024]{1,0:T(8,128)(2,1)}, bf16[512,1024]{1,0:T(8,128)(2,1)}, bf16[512,1024]{1,0:T(8,128)(2,1)}) %tuple.73), branch_computations={%region_3.4_spmd, %region_4.5_spmd} | conditional | flops 2000524288 | bytes 16680120 | solution.py:335
  33.2 4.9 %branch_1_fun.7 = (f32[2,2048,128]{2,1,0:T(8,128)S(1)}, f32[2,2048,128]{2,1,0:T(8,128)S(1)}) custom-call(s32[5]{0:T(128)S(1)} %get-tuple-element.100.refs_0_, bf16[512,1024]{1,0:T(8,128)(2,1)} %get-tuple-element.101.refs_1_, bf16[512,1024]{1,0:T(8,128)(2,1)} %get-tuple-element.102.refs_2_, bf16[512,1024]{1,0:T(8,128)(2,1)} %get-tuple-element.103.refs_3_), custom_call_target="tpu_custom_call" | custom-call | flops 2000000000 | bytes 2000000 | tf_op jit(solution)/shard_map/cond/branch_1_fun/pallas_call | solution.py:25
  38.3 4.1 %collective-permute-done.1 = f32[2,2048,128]{2,1,0:T(8,128)S(1)} collective-permute-done((f32[2,2048,128]{2,1,0:T(8,128)S(1)}, f32[2,2048,128]{2,1,0:T(8,128)S(1)}, u32[]{:S(2)}, u32[]{:S(2)}) %collective-permute-start.1) | collective-permute-done | bytes 2097184 | tf_op jit(solution)/shard_map/cond/branch_1_fun/ppermute | solution.py:305
  48.3 5.5 %conditional.8 = (f32[320,128]{1,0:T(8,128)S(1)}, f32[320,128]{1,0:T(8,128)S(1)}) conditional(s32[]{:T(128)} %convert_element_type.2, () %tuple.74, (s32[5]{0:T(128)S(1)}, bf16[2752,512]{1,0:T(8,128)(2,1)}, bf16[2752,128]{1,0:T(8,128)(2,1)S(1)}, bf16[2752,128]{1,0:T(8,128)(2,1)}, bf16[2752,128]{1,0:T(8,128)(2,1)}) %tuple.108), branch_computations={%region_5.6_spmd, %region_6.7_spmd} | conditional | flops 2000081920 | bytes 4293816 | solution.py:335
  48.3 3.8 %branch_1_fun.8 = (f32[2,320,128]{2,1,0:T(8,128)S(1)}, f32[2,320,128]{2,1,0:T(8,128)S(1)}) custom-call(s32[5]{0:T(128)S(1)} %get-tuple-element.106.refs_0_, bf16[2752,512]{1,0:T(8,128)(2,1)} %get-tuple-element.107.refs_1_, bf16[2752,128]{1,0:T(8,128)(2,1)S(1)} %get-tuple-element.108.refs_2_, bf16[2752,128]{1,0:T(8,128)(2,1)} %get-tuple-element.109.refs_3_, ...), custom_call_target="tpu_custom_call" | custom-call | flops 2000000000 | bytes 2000000 | tf_op jit(solution)/shard_map/cond/branch_1_fun/pallas_call | solution.py:25
  55.4 3.7 %collective-permute-done.12 = bf16[2752,128]{1,0:T(8,128)(2,1)} collective-permute-done((bf16[2752,128]{1,0:T(8,128)(2,1)}, bf16[2752,128]{1,0:T(8,128)(2,1)}, u32[]{:S(2)}, u32[]{:S(2)}) %collective-permute-start.12) | collective-permute-done | bytes 704544 | tf_op jit(solution)/shard_map/ppermute | solution.py:320
  62.4 6.7 %conditional.9 = (f32[448,128]{1,0:T(8,128)S(1)}, f32[448,128]{1,0:T(8,128)}) conditional(s32[]{:T(128)} %convert_element_type.2, () %tuple.76, (s32[5]{0:T(128)S(1)}, bf16[2752,512]{1,0:T(8,128)(2,1)}, bf16[2752,128]{1,0:T(8,128)(2,1)S(1)}, bf16[2752,128]{1,0:T(8,128)(2,1)S(1)}, bf16[2752,128]{1,0:T(8,128)(2,1)}, ...), branch_computations={%region_7.8_spmd, %region_8.9_spmd} | conditional | flops 2000114688 | bytes 5211320 | solution.py:335
  62.4 4.0 %branch_1_fun.9 = (f32[2,448,128]{2,1,0:T(8,128)S(1)}, f32[2,448,128]{2,1,0:T(8,128)S(1)}) custom-call(s32[5]{0:T(128)S(1)} %get-tuple-element.113.refs_0_, bf16[2752,512]{1,0:T(8,128)(2,1)} %get-tuple-element.114.refs_1_, bf16[2752,128]{1,0:T(8,128)(2,1)S(1)} %get-tuple-element.115.refs_2_, bf16[2752,128]{1,0:T(8,128)(2,1)S(1)} %get-tuple-element.116.refs_3_, ...), custom_call_target="tpu_custom_call" | custom-call | flops 2000000000 | bytes 2000000 | tf_op jit(solution)/shard_map/cond/branch_1_fun/pallas_call | solution.py:25
  69.0 2.5 %collective-permute-start.19 = (bf16[2752,128]{1,0:T(8,128)(2,1)}, bf16[2752,128]{1,0:T(8,128)(2,1)}, u32[]{:S(2)}, u32[]{:S(2)}) collective-permute-start(bf16[2752,128]{1,0:T(8,128)(2,1)} %get-tuple-element.232), channel_id=1, source_target_pairs={{0,24},{4,28},{8,0},{12,4},{16,8},{20,12},{24,16},{28,20},{1,25},{... | collective-permute-start | bytes 2113544 | tf_op jit(solution)/shard_map/ppermute | solution.py:320
  71.6 2.2 %collective-permute-done.14.refs_3_.refs_7_ = f32[320,128]{1,0:T(8,128)S(1)} collective-permute-done((f32[320,128]{1,0:T(8,128)S(1)}, f32[320,128]{1,0:T(8,128)S(1)}, u32[]{:S(2)}, u32[]{:S(2)}) %collective-permute-start.14) | collective-permute-done | bytes 163872 | tf_op jit(solution)/shard_map/ppermute | solution.py:339
  77.5 7.6 %conditional.10 = (f32[576,128]{1,0:T(8,128)S(1)}, f32[576,128]{1,0:T(8,128)}) conditional(s32[]{:T(128)} %convert_element_type.2, () %tuple.82, (s32[5]{0:T(128)S(1)}, bf16[2752,512]{1,0:T(8,128)(2,1)}, bf16[2752,128]{1,0:T(8,128)(2,1)S(1)}, bf16[2752,128]{1,0:T(8,128)(2,1)S(1)}, bf16[2752,128]{1,0:T(8,128)(2,1)}, ...), branch_computations={%region_9.10_spmd, %region_10.11_spmd} | conditional | flops 2000147456 | bytes 6128824 | solution.py:335
  77.5 4.7 %branch_1_fun.10 = (f32[2,576,128]{2,1,0:T(8,128)S(1)}, f32[2,576,128]{2,1,0:T(8,128)S(1)}) custom-call(s32[5]{0:T(128)S(1)} %get-tuple-element.123.refs_0_, bf16[2752,512]{1,0:T(8,128)(2,1)} %get-tuple-element.124.refs_1_, bf16[2752,128]{1,0:T(8,128)(2,1)S(1)} %get-tuple-element.125.refs_2_, bf16[2752,128]{1,0:T(8,128)(2,1)S(1)} %get-tuple-element.126.refs_3_, ...), custom_call_target="tpu_custom_call" | custom-call | flops 2000000000 | bytes 2000000 | tf_op jit(solution)/shard_map/cond/branch_1_fun/pallas_call | solution.py:25
  88.3 3.5 %collective-permute-done.20 = bf16[2752,128]{1,0:T(8,128)(2,1)} collective-permute-done((bf16[2752,128]{1,0:T(8,128)(2,1)}, bf16[2752,128]{1,0:T(8,128)(2,1)}, u32[]{:S(2)}, u32[]{:S(2)}) %collective-permute-start.20) | collective-permute-done | bytes 704544 | tf_op jit(solution)/shard_map/ppermute | solution.py:321
  91.8 7.1 %conditional.11 = (f32[704,128]{1,0:T(8,128)S(1)}, f32[352,128]{1,0:T(8,128)S(1)}, f32[224,128]{1,0:T(8,128)S(1)}, f32[128,128]{1,0:T(8,128)S(1)}) conditional(s32[]{:T(128)} %convert_element_type.2, () %tuple.87, (s32[5]{0:T(128)S(1)}, bf16[2752,512]{1,0:T(8,128)(2,1)S(1)}, bf16[2752,128]{1,0:T(8,128)(2,1)S(1)}, bf16[2752,128]{1,0:T(8,128)(2,1)S(1)}, ...), branch_computations={%region_11.12_spmd, %region_12.13_spmd} | conditional | flops 2000180224 | bytes 7046344 | solution.py:335
  91.8 4.7 %branch_1_fun.11 = (f32[2,704,128]{2,1,0:T(8,128)S(1)}, f32[2,704,128]{2,1,0:T(8,128)S(1)}) custom-call(s32[5]{0:T(128)S(1)} %get-tuple-element.136.refs_0_, bf16[2752,512]{1,0:T(8,128)(2,1)S(1)} %get-tuple-element.137.refs_1_, bf16[2752,128]{1,0:T(8,128)(2,1)S(1)} %get-tuple-element.138.refs_2_, bf16[2752,128]{1,0:T(8,128)(2,1)S(1)} %get-tuple-element.139.refs_3_, ...), custom_call_target="tpu_custom_call" | custom-call | flops 2000000000 | bytes 2000000 | tf_op jit(solution)/shard_map/cond/branch_1_fun/pallas_call | solution.py:25
  96.6 2.2 %collective-permute-done.5 = f32[2,704,128]{2,1,0:T(8,128)S(1)} collective-permute-done((f32[2,704,128]{2,1,0:T(8,128)S(1)}, f32[2,704,128]{2,1,0:T(8,128)S(1)}, u32[]{:S(2)}, u32[]{:S(2)}) %collective-permute-start.5) | collective-permute-done | bytes 720928 | tf_op jit(solution)/shard_map/cond/branch_1_fun/ppermute | solution.py:305
  103.8 2.5 %collective-permute-done.21.refs_3_.refs_13_ = f32[352,128]{1,0:T(8,128)S(1)} collective-permute-done((f32[352,128]{1,0:T(8,128)S(1)}, f32[352,128]{1,0:T(8,128)S(1)}, u32[]{:S(2)}, u32[]{:S(2)}) %collective-permute-start.21) | collective-permute-done | bytes 180256 | tf_op jit(solution)/shard_map/ppermute | solution.py:339
  (99 shorter events, 46.0 us)
Async XLA Ops:
  0.0 28.9 %collective-permute-start.7 = (bf16[512,1024]{1,0:T(8,128)(2,1)}, bf16[512,1024]{1,0:T(8,128)(2,1)}, u32[]{:S(2)}, u32[]{:S(2)}) collective-permute-start(bf16[512,1024]{1,0:T(8,128)(2,1)} %param.15), channel_id=1, source_target_pairs={{0,24},{4,28},{8,0},{12,4},{16,8},{20,12},{24,16},{28,20},{1,25},{... | collective-permute-start | bytes 3145736 | tf_op jit(solution)/shard_map/ppermute | solution.py:320
  5.0 28.2 %collective-permute-start.8 = (bf16[512,1024]{1,0:T(8,128)(2,1)}, bf16[512,1024]{1,0:T(8,128)(2,1)}, u32[]{:S(2)}, u32[]{:S(2)}) collective-permute-start(bf16[512,1024]{1,0:T(8,128)(2,1)} %param.15), channel_id=1, source_target_pairs={{0,4},{4,0},{8,12},{12,8},{16,20},{20,16},{24,28},{28,24},{1,5},{5... | collective-permute-start | bytes 3145736 | tf_op jit(solution)/shard_map/ppermute | solution.py:321
  12.7 34.0 %collective-permute-start.10 = (bf16[2752,128]{1,0:T(8,128)(2,1)S(1)}, bf16[2752,128]{1,0:T(8,128)(2,1)}, u32[]{:S(2)}, u32[]{:S(2)}) collective-permute-start(bf16[2752,128]{1,0:T(8,128)(2,1)S(1)} %get-tuple-element.207), channel_id=1, source_target_pairs={{0,24},{4,28},{8,0},{12,4},{16,8},{20,12},{24,16},{28,20},{1,25},{... | collective-permute-start | bytes 2113544 | tf_op jit(solution)/shard_map/ppermute | solution.py:320
  21.8 23.3 %collective-permute-start.6 = (f32[1024,128]{1,0:T(8,128)}, f32[1024,128]{1,0:T(8,128)S(1)}, u32[]{:S(2)}, u32[]{:S(2)}) collective-permute-start(f32[1024,128]{1,0:T(8,128)} %get-tuple-element.198), channel_id=1, source_target_pairs={{0,2},{1,3},{2,0},{3,1},{4,6},{5,7},{6,4},{7,5},{8,10},{9,11},{10,... | collective-permute-start | bytes 1572872 | tf_op jit(solution)/shard_map/ppermute | solution.py:339
  23.4 25.0 %collective-permute-start.11 = (bf16[2752,128]{1,0:T(8,128)(2,1)S(1)}, bf16[2752,128]{1,0:T(8,128)(2,1)}, u32[]{:S(2)}, u32[]{:S(2)}) collective-permute-start(bf16[2752,128]{1,0:T(8,128)(2,1)S(1)} %get-tuple-element.207), channel_id=1, source_target_pairs={{0,4},{4,0},{8,12},{12,8},{16,20},{20,16},{24,28},{28,24},{1,5},{5... | collective-permute-start | bytes 2113544 | tf_op jit(solution)/shard_map/ppermute | solution.py:321
  28.9 30.2 %collective-permute-start.12 = (bf16[2752,128]{1,0:T(8,128)(2,1)}, bf16[2752,128]{1,0:T(8,128)(2,1)}, u32[]{:S(2)}, u32[]{:S(2)}) collective-permute-start(bf16[2752,128]{1,0:T(8,128)(2,1)} %get-tuple-element.214), channel_id=1, source_target_pairs={{0,24},{4,28},{8,0},{12,4},{16,8},{20,12},{24,16},{28,20},{1,25},{... | collective-permute-start | bytes 2113544 | tf_op jit(solution)/shard_map/ppermute | solution.py:320
  43.6 18.7 %collective-permute-start.13 = (bf16[2752,128]{1,0:T(8,128)(2,1)S(1)}, bf16[2752,128]{1,0:T(8,128)(2,1)}, u32[]{:S(2)}, u32[]{:S(2)}) collective-permute-start(bf16[2752,128]{1,0:T(8,128)(2,1)S(1)} %copy-done.3), channel_id=1, source_target_pairs={{0,4},{4,0},{8,12},{12,8},{16,20},{20,16},{24,28},{28,24},{1,5},{5... | collective-permute-start | bytes 2113544 | tf_op jit(solution)/shard_map/ppermute | solution.py:321
  45.1 41.4 %collective-permute-start.9 = (f32[2048,128]{1,0:T(8,128)}, f32[2048,128]{1,0:T(8,128)S(1)}, u32[]{:S(2)}, u32[]{:S(2)}) collective-permute-start(f32[2048,128]{1,0:T(8,128)} %get-tuple-element.205), channel_id=1, source_target_pairs={{0,2},{1,3},{2,0},{3,1},{4,6},{5,7},{6,4},{7,5},{8,10},{9,11},{10,... | collective-permute-start | bytes 3145736 | tf_op jit(solution)/shard_map/ppermute | solution.py:339
  46.7 28.4 %collective-permute-start.15 = (bf16[2752,128]{1,0:T(8,128)(2,1)}, bf16[2752,128]{1,0:T(8,128)(2,1)}, u32[]{:S(2)}, u32[]{:S(2)}) collective-permute-start(bf16[2752,128]{1,0:T(8,128)(2,1)} %get-tuple-element.223), channel_id=1, source_target_pairs={{0,24},{4,28},{8,0},{12,4},{16,8},{20,12},{24,16},{28,20},{1,25},{... | collective-permute-start | bytes 2113544 | tf_op jit(solution)/shard_map/ppermute | solution.py:320
  53.8 23.7 %collective-permute-start.16 = (bf16[2752,128]{1,0:T(8,128)(2,1)}, bf16[2752,128]{1,0:T(8,128)(2,1)}, u32[]{:S(2)}, u32[]{:S(2)}) collective-permute-start(bf16[2752,128]{1,0:T(8,128)(2,1)} %get-tuple-element.223), channel_id=1, source_target_pairs={{0,4},{4,0},{8,12},{12,8},{16,20},{20,16},{24,28},{28,24},{1,5},{5... | collective-permute-start | bytes 2113544 | tf_op jit(solution)/shard_map/ppermute | solution.py:321
  59.1 14.7 %collective-permute-start.14 = (f32[320,128]{1,0:T(8,128)S(1)}, f32[320,128]{1,0:T(8,128)S(1)}, u32[]{:S(2)}, u32[]{:S(2)}) collective-permute-start(f32[320,128]{1,0:T(8,128)S(1)} %get-tuple-element.216), channel_id=1, source_target_pairs={{0,2},{1,3},{2,0},{3,1},{4,6},{5,7},{6,4},{7,5},{8,10},{9,11},{10,... | collective-permute-start | bytes 491528 | tf_op jit(solution)/shard_map/ppermute | solution.py:339
  69.0 19.2 %collective-permute-start.19 = (bf16[2752,128]{1,0:T(8,128)(2,1)}, bf16[2752,128]{1,0:T(8,128)(2,1)}, u32[]{:S(2)}, u32[]{:S(2)}) collective-permute-start(bf16[2752,128]{1,0:T(8,128)(2,1)} %get-tuple-element.232), channel_id=1, source_target_pairs={{0,24},{4,28},{8,0},{12,4},{16,8},{20,12},{24,16},{28,20},{1,25},{... | collective-permute-start | bytes 2113544 | tf_op jit(solution)/shard_map/ppermute | solution.py:320
  73.8 18.0 %collective-permute-start.20 = (bf16[2752,128]{1,0:T(8,128)(2,1)}, bf16[2752,128]{1,0:T(8,128)(2,1)}, u32[]{:S(2)}, u32[]{:S(2)}) collective-permute-start(bf16[2752,128]{1,0:T(8,128)(2,1)} %get-tuple-element.232), channel_id=1, source_target_pairs={{0,4},{4,0},{8,12},{12,8},{16,20},{20,16},{24,28},{28,24},{1,5},{5... | collective-permute-start | bytes 2113544 | tf_op jit(solution)/shard_map/ppermute | solution.py:321
  75.0 10.0 %collective-permute-start.17 = (f32[448,128]{1,0:T(8,128)}, f32[448,128]{1,0:T(8,128)S(1)}, u32[]{:S(2)}, u32[]{:S(2)}) collective-permute-start(f32[448,128]{1,0:T(8,128)} %get-tuple-element.225), channel_id=1, source_target_pairs={{0,2},{1,3},{2,0},{3,1},{4,6},{5,7},{6,4},{7,5},{8,10},{9,11},{10,... | collective-permute-start | bytes 688136 | tf_op jit(solution)/shard_map/ppermute | solution.py:339
  85.1 17.2 %collective-permute-start.18 = (f32[576,128]{1,0:T(8,128)}, f32[576,128]{1,0:T(8,128)S(1)}, u32[]{:S(2)}, u32[]{:S(2)}) collective-permute-start(f32[576,128]{1,0:T(8,128)} %get-tuple-element.228), channel_id=1, source_target_pairs={{0,2},{1,3},{2,0},{3,1},{4,6},{5,7},{6,4},{7,5},{8,10},{9,11},{10,... | collective-permute-start | bytes 884744 | tf_op jit(solution)/shard_map/ppermute | solution.py:339
  88.2 21.9 %collective-permute-start.23 = (f32[384,128]{1,0:T(8,128)S(1)}, f32[384,128]{1,0:T(8,128)S(1)}, u32[]{:S(2)}, u32[]{:S(2)}) collective-permute-start(f32[384,128]{1,0:T(8,128)S(1)} %get-tuple-element.229), channel_id=1, source_target_pairs={{0,8},{4,12},{8,16},{12,20},{16,24},{20,28},{24,0},{28,4},{1,9},{5... | collective-permute-start | bytes 589832 | tf_op jit(solution)/shard_map/ppermute | solution.py:359
  98.9 7.5 %collective-permute-start.21 = (f32[352,128]{1,0:T(8,128)S(1)}, f32[352,128]{1,0:T(8,128)S(1)}, u32[]{:S(2)}, u32[]{:S(2)}) collective-permute-start(f32[352,128]{1,0:T(8,128)S(1)} %get-tuple-element.235), channel_id=1, source_target_pairs={{0,2},{1,3},{2,0},{3,1},{4,6},{5,7},{6,4},{7,5},{8,10},{9,11},{10,... | collective-permute-start | bytes 540680 | tf_op jit(solution)/shard_map/ppermute | solution.py:339
  100.4 9.0 %collective-permute-start.24 = (f32[128,128]{1,0:T(8,128)S(1)}, f32[128,128]{1,0:T(8,128)S(1)}, u32[]{:S(2)}, u32[]{:S(2)}) collective-permute-start(f32[128,128]{1,0:T(8,128)S(1)} %get-tuple-element.238), channel_id=1, source_target_pairs={{0,4},{4,0},{8,12},{12,8},{16,20},{20,16},{24,28},{28,24},{1,5},{5... | collective-permute-start | bytes 196616 | tf_op jit(solution)/shard_map/ppermute | solution.py:360
  101.8 6.2 %collective-permute-start.28 = (f32[224,128]{1,0:T(8,128)S(1)}, f32[224,128]{1,0:T(8,128)S(1)}, u32[]{:S(2)}, u32[]{:S(2)}) collective-permute-start(f32[224,128]{1,0:T(8,128)S(1)} %get-tuple-element.241), channel_id=1, source_target_pairs={{0,2},{1,3},{2,0},{3,1},{4,6},{5,7},{6,4},{7,5},{8,10},{9,11},{10,... | collective-permute-start | bytes 344072 | tf_op jit(solution)/shard_map/ppermute | solution.py:339
  103.7 10.6 %collective-permute-start.25 = (f32[288,128]{1,0:T(8,128)S(1)}, f32[288,128]{1,0:T(8,128)S(1)}, u32[]{:S(2)}, u32[]{:S(2)}) collective-permute-start(f32[288,128]{1,0:T(8,128)S(1)} %get-tuple-element.239), channel_id=1, source_target_pairs={{0,8},{4,12},{8,16},{12,20},{16,24},{20,28},{24,0},{28,4},{1,9},{5... | collective-permute-start | bytes 442376 | tf_op jit(solution)/shard_map/ppermute | solution.py:359
  106.4 8.2 %collective-permute-start.27 = (f32[352,128]{1,0:T(8,128)S(1)}, f32[352,128]{1,0:T(8,128)S(1)}, u32[]{:S(2)}, u32[]{:S(2)}) collective-permute-start(f32[352,128]{1,0:T(8,128)S(1)} %shard_map.40), channel_id=1, source_target_pairs={{0,8},{4,12},{8,16},{12,20},{16,24},{20,28},{24,0},{28,4},{1,9},{5... | collective-permute-start | bytes 540680 | tf_op jit(solution)/shard_map/ppermute | solution.py:399
  108.0 5.3 %collective-permute-start.29 = (f32[224,128]{1,0:T(8,128)S(1)}, f32[224,128]{1,0:T(8,128)S(1)}, u32[]{:S(2)}, u32[]{:S(2)}) collective-permute-start(f32[224,128]{1,0:T(8,128)S(1)} %shard_map.41), channel_id=1, source_target_pairs={{0,4},{4,0},{8,12},{12,8},{16,20},{20,16},{24,28},{28,24},{1,5},{5... | collective-permute-start | bytes 344072 | tf_op jit(solution)/shard_map/ppermute | solution.py:399
  109.4 5.0 %collective-permute-start.26 = (f32[160,128]{1,0:T(8,128)S(1)}, f32[160,128]{1,0:T(8,128)S(1)}, u32[]{:S(2)}, u32[]{:S(2)}) collective-permute-start(f32[160,128]{1,0:T(8,128)S(1)} %get-tuple-element.240), channel_id=1, source_target_pairs={{0,4},{4,0},{8,12},{12,8},{16,20},{20,16},{24,28},{28,24},{1,5},{5... | collective-permute-start | bytes 245768 | tf_op jit(solution)/shard_map/ppermute | solution.py:360
  110.1 4.3 %collective-permute-start.22 = (f32[128,128]{1,0:T(8,128)S(1)}, f32[128,128]{1,0:T(8,128)S(1)}, u32[]{:S(2)}, u32[]{:S(2)}) collective-permute-start(f32[128,128]{1,0:T(8,128)S(1)} %get-tuple-element.237), channel_id=1, source_target_pairs={{0,2},{1,3},{2,0},{3,1},{4,6},{5,7},{6,4},{7,5},{8,10},{9,11},{10,... | collective-permute-start | bytes 196616 | tf_op jit(solution)/shard_map/ppermute | solution.py:339
  (23 other events, 125.8 us)
